TPU v7x, 32 devices: a whole 2x2x4 slice. The times are simulated.
32 devices in a mesh: gx: 2 (over y), gy: 4 (over z), gz: 4 (over x, core).
Axes of the slice: x: 2, y: 2, z: 4, core: 2. Of those that a mesh axis runs over, the one named last changes fastest.
Arguments:
- state: float32 [1024, 5, 4096], P(('gx', 'gy', 'gz')), may hold values from -1 to 5.75, as said below
- send_slots: int32 [3, 32, 8], P(None, ('gx', 'gy', 'gz')), may hold values from 0 to 32, as said below
- recv_slots: int32 [3, 32, 8], P(None, ('gx', 'gy', 'gz')), may hold values from 0 to 32, as said below
- owner_slot: int32 [256], replicated, may hold values from 0 to 31, as said below
Outputs:
- new_state: float32 [1024, 5, 4096], P(('gx', 'gy', 'gz'))
Inputs may be any that keep to these rules, and one draw needn't show every extreme that they name: `state`: in every slot that holds a block at the start, density lies in 1 to 2, each velocity component in -0.5 to 0.5 and pressure in 1 to 2; slots holding no block carry values that no output reads. `send_slots`: at each level and device, the entries under 32 come first, are distinct, and name slots that hold a block at the start of that level; the rest equal 32. At most 8 are named, and at each level one device names exactly 8. `recv_slots`: at each level and device, the entries under 32 come first, are as many as the partner names in send_slots at that level, are distinct, and name slots that hold no block once the device's own sent slots are emptied; the rest equal 32. After the three levels, each device holds exactly the 8 blocks of its box (the blocks of the second step's rule), block b in slot owner_slot[b]; its other slots hold no block.
All inputs are finite; a program needn't handle non-finite values.
Results may differ from a plain program's by a relative error of at most 0.0003.
Values sent between devices are 32-bit elements; how exact they have to be, the bound alone decides.
No kernel may reach another device: no remote copies, remote signals or barrier semaphores. Data moves between devices by JAX's collectives and lax.ppermute only.
A program may use at most 64 MiB of HBM per device.

v0:
```python
import functools

import jax
import jax.numpy as jnp
from jax import lax
from jax.experimental import pallas as pl
from jax.experimental.pallas import tpu as pltpu
from jax.sharding import PartitionSpec as P

gamma_ratio = 1.4
time_step = 0.05
LANES = 128
SUB = 8
NF = 5
FIELDS = range(NF)
AXES = ("gx", "gy", "gz")

VMEM = pltpu.VMEM
SMEM = pltpu.SMEM
HBM = pltpu.HBM
f32 = jnp.float32


def whole(space):
    return pl.BlockSpec(memory_space=space)


def params():
    return pltpu.CompilerParams(vmem_limit_bytes=16 * 1024 * 1024)


def cost(flops, moved):
    return pl.CostEstimate(flops=flops, bytes_accessed=moved, transcendentals=0)


def split_units(units):
    first, last = units // 10, 3 * units // 20
    middle = units - first - last
    sizes = [first] + [middle // 3 + (i < middle % 3) for i in range(3)] + [last]
    starts = [sum(sizes[:i]) for i in range(len(sizes) + 1)]
    return list(zip(starts[:-1], starts[1:]))


def from_state(state, tag, unit, slots, rows):
    slab, field = unit // NF, unit % NF
    groups = slots // SUB
    base = (tag // SUB) * (rows * SUB) + lax.rem(tag, SUB)
    start = base + (field * groups * rows + slab * SUB) * SUB
    return state[pl.ds(start, SUB, stride=SUB), :]


def pick(tag, unit, local, state, arrived, slots, rows, moves):
    value = from_state(state, jnp.minimum(tag, slots - 1), unit, slots, rows)
    for level, ref in enumerate(arrived):
        base = slots + level * moves
        index = jnp.clip(tag - base, 0, moves - 1)
        value = jnp.where(tag >= base, ref[index, local * SUB : (local + 1) * SUB, :], value)
    return value


def first_kernel(send, state, *outs, pieces, slots, rows, moves):
    for k in range(moves):
        slot = jnp.minimum(send[0, 0, k], slots - 1)
        for (begin, end), out in zip(pieces, outs):
            for unit in range(begin, end):
                at = (unit - begin) * SUB
                out[k, at : at + SUB, :] = from_state(state, slot, unit, slots, rows)


def tags_kernel(send, recv, own, tags, *, slots, moves, occ):
    def find(slot, levels):
        tag = slot
        for level in range(levels):
            for j in range(moves):
                tag = jnp.where(recv[level, 0, j] == slot, slots + level * moves + j, tag)
        return tag

    def one(k, carry):
        for level in (1, 2):
            slot = jnp.minimum(send[level, 0, k], slots - 1)
            tags[(level - 1) * moves + k] = find(slot, level)
        return carry

    lax.fori_loop(0, moves, one, 0)

    def last(b, carry):
        tags[2 * moves + b] = find(own[b], 3)
        return carry

    lax.fori_loop(0, occ, last, 0)


def pick_kernel(tags, state, *refs, plan, given, passed, slots, rows, moves):
    arrived = refs[:given]
    outs = refs[given + passed :]
    for (level, begin, end, which), out in zip(plan, outs):
        sources = [arrived[i] for i in which]
        for k in range(moves):
            tag = tags[(level - 1) * moves + k]
            for unit in range(begin, end):
                local = unit - begin
                out[k, local * SUB : (local + 1) * SUB, :] = pick(
                    tag, unit, local, state, sources, slots, rows, moves
                )


def primitives(cons):
    density = cons[0]
    inverse = 1.0 / density
    vel = [cons[1] * inverse, cons[2] * inverse, cons[3] * inverse]
    kinetic = cons[1] * vel[0] + cons[2] * vel[1] + cons[3] * vel[2]
    pressure = (gamma_ratio - 1.0) * (cons[4] - 0.5 * kinetic)
    return [density, vel[0], vel[1], vel[2], pressure]


def half_minmod(lower, upper):
    both = jnp.maximum(0.0, jnp.minimum(lower, upper)) + jnp.minimum(
        0.0, jnp.maximum(lower, upper)
    )
    return 0.5 * both


def half_slopes(before, here, after):
    return [half_minmod(h - b, a - h) for b, h, a in zip(before, here, after)]


def plus(a, b):
    return [x + y for x, y in zip(a, b)]


def minus(a, b):
    return [x - y for x, y in zip(a, b)]


def side_terms(prim, normal):
    density, vel, pressure = prim[0], prim[1:4], prim[4]
    along = vel[normal]
    mom = [density * v for v in vel]
    kinetic = mom[0] * vel[0] + mom[1] * vel[1] + mom[2] * vel[2]
    energy = pressure * (1.0 / (gamma_ratio - 1.0)) + 0.5 * kinetic
    flux = [m * along for m in mom]
    flux[normal] = flux[normal] + pressure
    scaled = gamma_ratio * pressure
    speed = jnp.abs(along) + scaled * lax.rsqrt(scaled * density)
    return [density] + mom + [energy], [mom[normal]] + flux + [(energy + pressure) * along], speed


def twice_flux(left, right, normal):
    left_cons, left_flux, left_speed = side_terms(left, normal)
    right_cons, right_flux, right_speed = side_terms(right, normal)
    speed = jnp.maximum(left_speed, right_speed)
    return [
        (fl + fr) - speed * (ur - ul)
        for fl, fr, ul, ur in zip(left_flux, right_flux, left_cons, right_cons)
    ]


def lane_of():
    return lax.broadcasted_iota(jnp.int32, (SUB, LANES), 1)


def sub_of():
    return lax.broadcasted_iota(jnp.int32, (SUB, LANES), 0)


def lane_roll(value, amount):
    amount = amount % LANES
    return value if amount == 0 else pltpu.roll(value, amount, 1)


class Shape:
    def __init__(self, rows, edge):
        self.rows, self.edge = rows, edge
        self.halves = rows // edge
        self.width = 2 * edge
        self.fit = LANES // self.width
        self.slabs = rows // SUB
        self.pad = 2 * self.halves

    def at(self, f, row):
        start = (f * self.rows + row) * SUB
        return pl.ds(start if isinstance(start, int) else pl.multiple_of(start, SUB), SUB)

    def across(self, f, slab, sub):
        return pl.ds((f * self.rows + slab * SUB) * SUB + sub, SUB, stride=SUB)

    def grid(self):
        return jax.ShapeDtypeStruct((NF * self.rows * SUB, LANES), f32)

    def faces(self):
        x = jax.ShapeDtypeStruct((NF, self.pad, SUB, LANES), f32)
        y = jax.ShapeDtypeStruct((NF, self.edge // self.fit, SUB, LANES), f32)
        z = jax.ShapeDtypeStruct((NF, self.rows, LANES), f32)
        return [x, x, y, y, z, z]


def send_slab(shape, prim, y_lo, y_hi, z_lo, z_hi, slab):
    lane = lane_of()
    halves = shape.halves
    for f in FIELDS:
        lo = hi = None
        for k in range(shape.fit):
            row = slab * SUB + k * halves
            below = lane_roll(prim[shape.at(f, row), :], shape.width * k)
            above = lane_roll(prim[shape.at(f, row + halves - 1), :], shape.width * (k + 1))
            if lo is None:
                lo, hi = below, above
            else:
                mine = lane >= shape.width * k
                lo = jnp.where(mine, below, lo)
                hi = jnp.where(mine, above, hi)
        y_lo[f, slab] = lo
        y_hi[f, slab] = hi
        to = pl.ds(slab * SUB, SUB) if isinstance(slab, int) else pl.ds(
            pl.multiple_of(slab * SUB, SUB), SUB
        )
        z_lo[f, to, :] = prim[shape.across(f, slab, 0), :]
        z_hi[f, to, :] = prim[shape.across(f, slab, SUB - 1), :]


def send_x(shape, prim, x_lo, x_hi):
    for f in FIELDS:
        for i in range(shape.pad):
            x_lo[f, i] = prim[shape.at(f, i), :]
            x_hi[f, i] = prim[shape.at(f, shape.rows - shape.pad + i), :]


def assemble_kernel(tags, state, *refs, pieces, slots, moves, occ, shape):
    count = 3 * len(pieces)
    given = refs[:count]
    field, prim, x_lo, x_hi, y_lo, y_hi, z_lo, z_hi, held = refs[count:]
    rows = shape.rows
    units = NF * shape.slabs
    for b in range(occ):
        tag = tags[2 * moves + b]
        for number, (begin, end) in enumerate(pieces):
            sources = given[3 * number : 3 * number + 3]
            for unit in range(begin, end):
                at = (b * units + unit) * SUB
                held[at : at + SUB, :] = pick(
                    tag, unit, unit - begin, state, sources, slots, rows, moves
                )
    for slab in range(shape.slabs):
        for i in range(SUB):
            row = slab * SUB + i
            cons = [
                held[pl.ds((slab * NF + f) * SUB + i, occ, stride=units * SUB), :] for f in FIELDS
            ]
            for f, (c, w) in enumerate(zip(cons, primitives(cons))):
                field[shape.at(f, row), :] = c
                prim[shape.at(f, row), :] = w
        send_slab(shape, prim, y_lo, y_hi, z_lo, z_hi, slab)
    send_x(shape, prim, x_lo, x_hi)


def sweep_z_kernel(prim, z_lo, z_hi, z_prev, z_next, total, below_z, flux_z, over_z, right_z, *, shape):
    edge, rows = shape.edge, shape.rows

    def ghost(a, carry):
        at = pl.ds(pl.multiple_of(a * SUB, SUB), SUB)
        low = [z_lo[f, at, :] for f in FIELDS]
        high = [z_hi[f, at, :] for f in FIELDS]
        prev = [z_prev[f, at, :] for f in FIELDS]
        after = [z_next[f, at, :] for f in FIELDS]
        below = [lane_roll(v, -(edge - 1)) for v in prev]
        before = [lane_roll(v, -(edge - 2)) for v in prev]
        second = [lane_roll(v, -1) for v in low]
        left = plus(below, half_slopes(before, below, low))
        right = minus(low, half_slopes(below, low, second))
        flux = twice_flux(left, right, 2)
        last = [lane_roll(v, -(edge - 1)) for v in high]
        beyond = [lane_roll(v, -1) for v in after]
        over = minus(after, half_slopes(last, after, beyond))
        for f in FIELDS:
            below_z[f, at, :] = below[f]
            flux_z[f, at, :] = flux[f]
            over_z[f, at, :] = lane_roll(after[f], edge - 1)
            right_z[f, at, :] = lane_roll(over[f], edge - 1)
        return carry

    lax.fori_loop(0, shape.slabs, ghost, 0)
    z_of = lax.rem(lane_of(), edge)
    sub = sub_of()
    first_z, last_z = z_of == 0, z_of == edge - 1
    first_sub, last_sub = sub == 0, sub == SUB - 1

    def up(value, insert):
        across = pltpu.roll(lane_roll(value, edge - 1), SUB - 1, 0)
        across = jnp.where(last_sub, insert, across)
        return jnp.where(last_z, across, lane_roll(value, -1))

    def down(value, insert):
        across = pltpu.roll(lane_roll(value, -(edge - 1)), 1, 0)
        across = jnp.where(first_sub, insert, across)
        return jnp.where(first_z, across, lane_roll(value, 1))

    def body(row, carry):
        def insert(ref, f):
            return jnp.broadcast_to(ref[f, pl.ds(row, 1), :], (SUB, LANES))

        left, right = [], []
        for f in FIELDS:
            mine = prim[shape.at(f, row), :]
            shift = half_minmod(
                mine - down(mine, insert(below_z, f)), up(mine, insert(over_z, f)) - mine
            )
            left.append(mine + shift)
            right.append(up(mine - shift, insert(right_z, f)))
        flux = twice_flux(left, right, 2)
        for f in FIELDS:
            total[shape.at(f, row), :] = flux[f] - down(flux[f], insert(flux_z, f))
        return carry

    lax.fori_loop(0, rows, body, 0, unroll=2)


def sweep_x_kernel(prim, x_prev, x_next, sofar, total, wide, *, shape):
    rows, halves, pad = shape.rows, shape.halves, shape.pad
    for f in FIELDS:
        for i in range(pad):
            wide[f, i] = x_prev[f, i]
            wide[f, pad + rows + i] = x_next[f, i]

        def copy(r, carry, f=f):
            wide[f, pad + r] = prim[shape.at(f, r), :]
            return carry

        lax.fori_loop(0, rows, copy, 0, unroll=8)

    for h in range(halves):
        cells = [[wide[f, i * halves + h] for f in FIELDS] for i in range(4)]
        left = plus(cells[1], half_slopes(*cells[0:3]))
        shift = half_slopes(*cells[1:4])
        flux = twice_flux(left, minus(cells[2], shift), 0)
        keep = plus(cells[2], shift)

        def body(x, carry, h=h):
            below, left = carry
            here, one, two = (
                [wide[f, pad + (x + i) * halves + h] for f in FIELDS] for i in range(3)
            )
            shift = half_slopes(here, one, two)
            flux = twice_flux(left, minus(one, shift), 0)
            row = x * halves + h
            for f in FIELDS:
                at = shape.at(f, row)
                total[at, :] = sofar[at, :] + (flux[f] - below[f])
            return flux, plus(one, shift)

        lax.fori_loop(0, shape.edge, body, (flux, keep), unroll=4)


def sweep_y(prim, y_lo, y_hi, y_prev, y_next, sofar, ghost_prim, ghost_flux, shape, finish, after_slab):
    edge, halves, fit, width = shape.edge, shape.halves, shape.fit, shape.width
    lane = lane_of()
    upper = lax.rem(lane, width) >= edge

    def ghost(q, carry):
        low = [y_lo[f, q] for f in FIELDS]
        high = [y_hi[f, q] for f in FIELDS]
        below = [y_prev[f, q] for f in FIELDS]
        after = [y_next[f, q] for f in FIELDS]
        before = [lane_roll(v, edge) for v in below]
        first = [lane_roll(v, edge) for v in low]
        left = plus(below, half_slopes(before, below, first))
        right = minus(first, half_slopes(below, first, low))
        flux = twice_flux(left, right, 1)
        last = [lane_roll(v, -edge) for v in high]
        beyond = [lane_roll(v, -edge) for v in after]
        over = minus(after, half_slopes(last, after, beyond))
        for f in FIELDS:
            ghost_prim[f, q] = jnp.where(upper, below[f], after[f])
            ghost_flux[f, q] = jnp.where(upper, flux[f], over[f])
        return carry

    lax.fori_loop(0, edge // fit, ghost, 0)
    top_lanes = lane >= LANES - edge
    low_lanes = lane < edge

    def up(values, insert):
        rolled = [lane_roll(v, -edge) for v in values]
        follow = rolled[1:] + [insert]
        return [jnp.where(top_lanes, n, r) for r, n in zip(rolled, follow)]

    def down(values, insert):
        rolled = [lane_roll(v, edge) for v in values]
        lead = [insert] + rolled[:-1]
        return [jnp.where(low_lanes, n, r) for r, n in zip(rolled, lead)]

    def body(q, carry):
        for k in range(fit):
            turn = -(width * k + edge)
            base = (q * fit + k) * halves
            left = [[None] * NF for _ in range(halves)]
            right = [[None] * NF for _ in range(halves)]
            for f in FIELDS:
                mine = [prim[shape.at(f, base + h), :] for h in range(halves)]
                ghost = lane_roll(ghost_prim[f, q], turn)
                over, under = up(mine, ghost), down(mine, ghost)
                shift = [half_minmod(m - d, u - m) for m, d, u in zip(mine, under, over)]
                above = up(minus(mine, shift), lane_roll(ghost_flux[f, q], turn))
                for h in range(halves):
                    left[h][f] = mine[h] + shift[h]
                    right[h][f] = above[h]
            fluxes = [twice_flux(left[h], right[h], 1) for h in range(halves)]
            total = [[None] * NF for _ in range(halves)]
            for f in FIELDS:
                mine = [fluxes[h][f] for h in range(halves)]
                under = down(mine, lane_roll(ghost_flux[f, q], turn))
                for h in range(halves):
                    total[h][f] = sofar[shape.at(f, base + h), :] + (mine[h] - under[h])
            for h in range(halves):
                finish(base + h, total[h])
        after_slab(q)
        return carry

    lax.fori_loop(0, edge // fit, body, 0)


def sweep_y_one_kernel(field, prim, y_lo, y_hi, y_prev, y_next, sofar, *refs, shape):
    one, one_prim, x_lo, x_hi, out_y_lo, out_y_hi, z_lo, z_hi = refs[:8]

    def finish(row, total):
        cons = [field[shape.at(f, row), :] - (0.5 * time_step) * total[f] for f in FIELDS]
        for f, (c, w) in enumerate(zip(cons, primitives(cons))):
            one[shape.at(f, row), :] = c
            one_prim[shape.at(f, row), :] = w

    def after_slab(q):
        send_slab(shape, one_prim, out_y_lo, out_y_hi, z_lo, z_hi, q)

    sweep_y(prim, y_lo, y_hi, y_prev, y_next, sofar, *refs[8:], shape, finish, after_slab)
    send_x(shape, one_prim, x_lo, x_hi)


def sweep_y_two_kernel(own, field, one, prim, y_lo, y_hi, y_prev, y_next, sofar, out,
                       ghost_prim, ghost_flux, result, canvas, sems, *, shape, occ, groups):
    rows = shape.rows
    span = SUB * SUB

    def clear(i, carry):
        canvas[pl.ds(pl.multiple_of(i * SUB, SUB), SUB), :] = jnp.zeros((SUB, LANES), f32)
        return carry

    lax.fori_loop(0, NF * groups * rows, clear, 0, unroll=16)

    def finish(row, total):
        for f in FIELDS:
            at = shape.at(f, row)
            advanced = one[at, :] - (0.5 * time_step) * total[f]
            result[at, :] = 0.5 * field[at, :] + 0.5 * advanced

    def copy(part):
        begin = part * span if isinstance(part, int) else pl.multiple_of(part * span, span)
        return [
            pltpu.make_async_copy(
                canvas.at[pl.ds(i * rows * SUB + begin, span), :],
                out.at[pl.ds(i * rows * SUB + begin, span), :],
                sems.at[part, i],
            )
            for i in range(NF * groups)
        ]

    def after_slab(q):
        for b in range(occ):
            slot = own[b]
            base = (slot // SUB) * (rows * SUB) + lax.rem(slot, SUB) + q * span
            for f in FIELDS:
                canvas[pl.ds(base + f * groups * rows * SUB, SUB, stride=SUB), :] = result[
                    shape.across(f, q, b), :
                ]
        for c in copy(q):
            c.start()

    sweep_y(prim, y_lo, y_hi, y_prev, y_next, sofar, ghost_prim, ghost_flux, shape, finish, after_slab)
    for part in range(shape.slabs):
        for c in copy(part):
            c.wait()


def shards(state, send_slots, recv_slots, owner_slot):
    slots, _, cells = state.shape
    moves = send_slots.shape[2]
    size_x, size_y, size_z = (lax.axis_size(axis) for axis in AXES)
    occ = owner_slot.shape[0] // (size_x * size_y * size_z)
    edge = round(cells ** (1 / 3))
    rows = cells // LANES
    groups = slots // SUB
    shape = Shape(rows, edge)
    pieces = split_units(NF * shape.slabs)
    count = len(pieces)

    bit_z = size_z.bit_length() - 2
    bit_y = bit_z + size_y.bit_length() - 1
    bit_x = bit_y + size_x.bit_length() - 1
    pair_bits = (bit_x, bit_y, bit_z)

    def swapped(value, level):
        mask = 2 ** pair_bits[level]
        pairs = [(source, source ^ mask) for source in range(lax.axis_size(AXES))]
        return lax.ppermute(value, AXES, pairs)

    rows_of_state = (
        state.reshape(groups, SUB, NF, rows, LANES)
        .transpose(2, 0, 3, 1, 4)
        .reshape(NF * groups * rows * SUB, LANES)
    )
    device = lax.axis_index(AXES)
    own = lax.dynamic_slice(owner_slot, (device * occ,), (occ,))
    sizes = dict(slots=slots, moves=moves)

    def message(p):
        begin, end = pieces[p]
        return jax.ShapeDtypeStruct((moves, (end - begin) * SUB, LANES), f32)

    sent = pl.pallas_call(
        functools.partial(first_kernel, pieces=pieces, rows=rows, **sizes),
        out_shape=[message(p) for p in range(count)],
        in_specs=[whole(SMEM), whole(VMEM)],
        out_specs=[whole(VMEM)] * count,
        compiler_params=params(),
        name="pack_first",
    )(send_slots, rows_of_state)

    tags = pl.pallas_call(
        functools.partial(tags_kernel, occ=occ, **sizes),
        out_shape=jax.ShapeDtypeStruct((2 * moves + occ,), jnp.int32),
        in_specs=[whole(SMEM)] * 3,
        out_specs=whole(SMEM),
        compiler_params=params(),
        name="block_tags",
    )(send_slots, recv_slots, own)

    got = [[None] * count for _ in range(3)]

    def make(wanted, through):
        arrays, plan, shapes = [], [], []
        for level, p in wanted:
            which = []
            for earlier in range(level):
                which.append(len(arrays))
                arrays.append(got[earlier][p])
            plan.append((level, *pieces[p], tuple(which)))
            shapes.append(message(p))
        given, passed, made = len(arrays), len(through), len(wanted)
        outs = pl.pallas_call(
            functools.partial(
                pick_kernel, plan=tuple(plan), given=given, passed=passed, rows=rows, **sizes
            ),
            out_shape=shapes + [jax.ShapeDtypeStruct(t.shape, f32) for t in through],
            in_specs=[whole(SMEM)] + [whole(VMEM)] * (1 + given) + [whole(pl.ANY)] * passed,
            out_specs=[whole(VMEM)] * made + [whole(pl.ANY)] * passed,
            input_output_aliases={2 + given + i: made + i for i in range(passed)},
            compiler_params=params(),
            name="pick_" + "_".join("%d%d" % w for w in wanted),
        )(tags, rows_of_state, *arrays, *through)
        return outs[:made], outs[made:]

    ahead = 2
    for p in range(ahead):
        got[0][p] = swapped(sent[p], 0)
    for step in range(count + ahead):
        wanted = []
        if step < count:
            wanted.append((1, step))
        if step >= ahead:
            wanted.append((2, step - ahead))
        through = sent[step + ahead : step + ahead + 1]
        made, passed = make(wanted, list(through))
        for (level, p), value in zip(wanted, made):
            got[level][p] = swapped(value, level)
        if passed:
            got[0][step + ahead] = swapped(passed[0], 0)

    grid = shape.grid()
    produced = [grid, grid] + shape.faces()
    sources = [got[level][p] for p in range(count) for level in range(3)]
    made = pl.pallas_call(
        functools.partial(assemble_kernel, pieces=pieces, occ=occ, shape=shape, **sizes),
        out_shape=produced,
        in_specs=[whole(SMEM)] + [whole(VMEM)] * (1 + len(sources)),
        out_specs=[whole(VMEM)] * len(produced),
        scratch_shapes=[VMEM((occ * NF * rows, LANES), f32)],
        compiler_params=params(),
        name="assemble",
    )(tags, rows_of_state, *sources)

    def ring(value, axis, step):
        size = lax.axis_size(axis)
        return lax.ppermute(value, axis, [(i, (i + step) % size) for i in range(size)])

    def flux_sums(prim, x_lo, x_hi, y_lo, y_hi, z_lo, z_hi):
        y_prev, y_next = ring(y_hi, "gy", 1), ring(y_lo, "gy", -1)
        z_prev, z_next = ring(z_hi, "gz", 1), ring(z_lo, "gz", -1)
        if size_x == 2:
            x_prev, x_next = ring(jnp.stack([x_hi, x_lo]), "gx", 1)
        else:
            x_prev, x_next = ring(x_hi, "gx", 1), ring(x_lo, "gx", -1)
        ghost = VMEM((NF, rows, LANES), f32)
        total = pl.pallas_call(
            functools.partial(sweep_z_kernel, shape=shape),
            out_shape=grid,
            in_specs=[whole(VMEM)] * 5,
            out_specs=whole(VMEM),
            scratch_shapes=[ghost] * 4,
            compiler_params=params(),
            name="sweep_z",
        )(prim, z_lo, z_hi, z_prev, z_next)
        total = pl.pallas_call(
            functools.partial(sweep_x_kernel, shape=shape),
            out_shape=grid,
            in_specs=[whole(VMEM)] * 4,
            out_specs=whole(VMEM),
            scratch_shapes=[VMEM((NF, rows + 2 * shape.pad, SUB, LANES), f32)],
            input_output_aliases={3: 0},
            compiler_params=params(),
            name="sweep_x",
        )(prim, x_prev, x_next, total)
        return y_lo, y_hi, y_prev, y_next, total

    packed = VMEM(shape.faces()[2].shape, f32)
    field, prim = made[0], made[1]
    sums = flux_sums(prim, *made[2:])
    made = pl.pallas_call(
        functools.partial(sweep_y_one_kernel, shape=shape),
        out_shape=produced,
        in_specs=[whole(VMEM)] * 7,
        out_specs=[whole(VMEM)] * len(produced),
        scratch_shapes=[packed] * 2,
        compiler_params=params(),
        name="sweep_y_one",
    )(field, prim, *sums)
    one, one_prim = made[0], made[1]
    sums = flux_sums(one_prim, *made[2:])
    state_rows = NF * groups * rows * SUB
    out = pl.pallas_call(
        functools.partial(sweep_y_two_kernel, shape=shape, occ=occ, groups=groups),
        out_shape=jax.ShapeDtypeStruct((state_rows, LANES), f32),
        in_specs=[whole(SMEM)] + [whole(VMEM)] * 8,
        out_specs=whole(HBM),
        scratch_shapes=[packed] * 2
        + [
            VMEM(grid.shape, f32),
            VMEM((state_rows, LANES), f32),
            pltpu.SemaphoreType.DMA((shape.slabs, NF * groups)),
        ],
        compiler_params=params(),
        name="sweep_y_two",
    )(own, field, one, one_prim, *sums)
    return (
        out.reshape(NF, groups, rows, SUB, LANES)
        .transpose(1, 3, 0, 2, 4)
        .reshape(slots, NF, cells)
    )


def solution(mesh):
    placed = (
        P(AXES, None, None),
        P(None, AXES, None),
        P(None, AXES, None),
        P(),
    )
    return jax.shard_map(
        shards,
        mesh=mesh,
        in_specs=placed,
        out_specs=P(AXES, None, None),
        check_vma=False,
    )
```

profile of v0, /device:TPU:0, one launch (start us, length us, event | category | flops | bytes accessed | tf_op | source)
XLA Modules:
  0.0 89.5 jit_solution(16400914719828425464)
XLA Ops:
  0.0 1.8 %copy-done = f32[32,5,4096]{2,0,1:T(8,128)S(1)} copy-done((f32[32,5,4096]{2,0,1:T(8,128)S(1)}, f32[32,5,4096]{2,0,1:T(8,128)}, u32[]{:S(2)}) %copy-start) | copy-done | bytes 2621464
  1.8 0.7 copy-done.2
  2.4 0.8 pack_first.1
  3.2 3.0 %collective-permute-start.4 = (f32[8,40,128]{2,1,0:T(8,128)S(1)}, f32[8,40,128]{2,1,0:T(8,128)S(1)}, u32[]{:S(2)}, u32[]{:S(2)}) collective-permute-start(f32[8,40,128]{2,1,0:T(8,128)S(1)} %get-tuple-element.43), channel_id=1, source_target_pairs={{0,16},{1,17},{2,18},{3,19},{4,20},{5,21},{6,22},{7,23},{8,24},{9,... | collective-permute-start | bytes 491528 | tf_op jit(solution)/shard_map/ppermute | solution.py:501
  6.2 0.1 collective-permute-start
  6.3 0.1 dynamic_slice.3.own
  6.4 1.6 %block_tags.1.tags = s32[24]{0:T(128)S(1)} custom-call(s32[3,1,8]{2,1,0:T(1,128)S(1)} %copy-done.3, s32[3,1,8]{2,1,0:T(1,128)S(1)} %copy-done.4, s32[8]{0:T(128)S(1)} %dynamic_slice.3.own), custom_call_target="tpu_custom_call" | custom-call | tf_op jit(solution)/shard_map/block_tags/pallas_call | solution.py:525
  8.0 3.8 %collective-permute-done.refs_0_.refs_1_ = f32[8,16,128]{2,1,0:T(8,128)S(1)} collective-permute-done((f32[8,16,128]{2,1,0:T(8,128)S(1)}, f32[8,16,128]{2,1,0:T(8,128)S(1)}, u32[]{:S(2)}, u32[]{:S(2)}) %collective-permute-start) | collective-permute-done | bytes 65568 | tf_op jit(solution)/shard_map/ppermute | solution.py:501
  11.8 0.6 pick_10.1
  12.5 1.8 %collective-permute-start.2 = (f32[8,40,128]{2,1,0:T(8,128)S(1)}, f32[8,40,128]{2,1,0:T(8,128)S(1)}, u32[]{:S(2)}, u32[]{:S(2)}) collective-permute-start(f32[8,40,128]{2,1,0:T(8,128)S(1)} %get-tuple-element.40), channel_id=1, source_target_pairs={{0,16},{1,17},{2,18},{3,19},{4,20},{5,21},{6,22},{7,23},{8,24},{9,... | collective-permute-start | bytes 491528 | tf_op jit(solution)/shard_map/ppermute | solution.py:501
  14.3 0.0 collective-permute-done.4.refs_0_.refs_1_.refs_3_
  14.3 0.6 pick_11.1
  14.9 2.7 %collective-permute-start.5 = (f32[8,40,128]{2,1,0:T(8,128)S(1)}, f32[8,40,128]{2,1,0:T(8,128)S(1)}, u32[]{:S(2)}, u32[]{:S(2)}) collective-permute-start(f32[8,40,128]{2,1,0:T(8,128)S(1)} %get-tuple-element.45), channel_id=1, source_target_pairs={{0,8},{1,9},{2,10},{3,11},{4,12},{5,13},{6,14},{7,15},{8,0},{9,1},... | collective-permute-start | bytes 491528 | tf_op jit(solution)/shard_map/ppermute | solution.py:501
  17.6 0.5 collective-permute-start.6
  18.1 0.1 collective-permute-start.1
  18.2 8.8 %collective-permute-done.1.refs_2_.refs_1_ = f32[8,16,128]{2,1,0:T(8,128)S(1)} collective-permute-done((f32[8,16,128]{2,1,0:T(8,128)S(1)}, f32[8,16,128]{2,1,0:T(8,128)S(1)}, u32[]{:S(2)}, u32[]{:S(2)}) %collective-permute-start.1) | collective-permute-done | bytes 65568 | tf_op jit(solution)/shard_map/ppermute | solution.py:501
  27.0 0.0 collective-permute-done.2.refs_0_.refs_1_.refs_6_
  27.0 0.7 pick_12_20.1
  27.7 0.1 collective-permute-start.8
  27.8 0.0 collective-permute-done.5.refs_2_.refs_4_
  27.8 0.0 collective-permute-done.6.refs_0_.refs_9_
  27.8 0.7 pick_13_21.1
  28.5 3.0 %collective-permute-start.11 = (f32[8,40,128]{2,1,0:T(8,128)S(1)}, f32[8,40,128]{2,1,0:T(8,128)S(1)}, u32[]{:S(2)}, u32[]{:S(2)}) collective-permute-start(f32[8,40,128]{2,1,0:T(8,128)S(1)} %get-tuple-element.51), channel_id=1, source_target_pairs={{0,8},{1,9},{2,10},{3,11},{4,12},{5,13},{6,14},{7,15},{8,0},{9,1},... | collective-permute-start | bytes 491528 | tf_op jit(solution)/shard_map/ppermute | solution.py:501
  31.5 0.6 collective-permute-start.9
  32.1 4.0 %collective-permute-done.9.refs_0_.refs_12_ = f32[8,24,128]{2,1,0:T(8,128)S(1)} collective-permute-done((f32[8,24,128]{2,1,0:T(8,128)S(1)}, f32[8,24,128]{2,1,0:T(8,128)S(1)}, u32[]{:S(2)}, u32[]{:S(2)}) %collective-permute-start.9) | collective-permute-done | bytes 98336 | tf_op jit(solution)/shard_map/ppermute | solution.py:501
  36.1 6.7 %collective-permute-done.8.refs_2_.refs_7_ = f32[8,40,128]{2,1,0:T(8,128)S(1)} collective-permute-done((f32[8,40,128]{2,1,0:T(8,128)S(1)}, f32[8,40,128]{2,1,0:T(8,128)S(1)}, u32[]{:S(2)}, u32[]{:S(2)}) %collective-permute-start.8) | collective-permute-done | bytes 163872 | tf_op jit(solution)/shard_map/ppermute | solution.py:501
  42.8 0.7 pick_14_22.1
  43.5 0.1 collective-permute-start.13
  43.6 1.6 %collective-permute-start.7 = (f32[8,40,128]{2,1,0:T(8,128)S(1)}, f32[8,40,128]{2,1,0:T(8,128)S(1)}, u32[]{:S(2)}, u32[]{:S(2)}) collective-permute-start(f32[8,40,128]{2,1,0:T(8,128)S(1)} %get-tuple-element.47), channel_id=1, source_target_pairs={{0,2},{1,3},{2,0},{3,1},{4,6},{5,7},{6,4},{7,5},{8,10},{9,11},{10,... | collective-permute-start | bytes 491528 | tf_op jit(solution)/shard_map/ppermute | solution.py:501
  45.2 0.5 collective-permute-start.10
  45.7 1.7 %collective-permute-done.11.refs_1_.refs_10_ = f32[8,40,128]{2,1,0:T(8,128)S(1)} collective-permute-done((f32[8,40,128]{2,1,0:T(8,128)S(1)}, f32[8,40,128]{2,1,0:T(8,128)S(1)}, u32[]{:S(2)}, u32[]{:S(2)}) %collective-permute-start.11) | collective-permute-done | bytes 163872 | tf_op jit(solution)/shard_map/ppermute | solution.py:501
  47.4 0.6 pick_23.1
  48.1 1.6 %collective-permute-start.12 = (f32[8,40,128]{2,1,0:T(8,128)S(1)}, f32[8,40,128]{2,1,0:T(8,128)S(1)}, u32[]{:S(2)}, u32[]{:S(2)}) collective-permute-start(f32[8,40,128]{2,1,0:T(8,128)S(1)} %pick_23.1), channel_id=1, source_target_pairs={{0,2},{1,3},{2,0},{3,1},{4,6},{5,7},{6,4},{7,5},{8,10},{9,11},{10,... | collective-permute-start | bytes 491528 | tf_op jit(solution)/shard_map/ppermute | solution.py:501
  49.6 0.0 collective-permute-done.13.refs_1_.refs_13_
  49.6 0.6 pick_24.1
  50.3 1.1 %collective-permute-start.14 = (f32[8,24,128]{2,1,0:T(8,128)S(1)}, f32[8,24,128]{2,1,0:T(8,128)S(1)}, u32[]{:S(2)}, u32[]{:S(2)}) collective-permute-start(f32[8,24,128]{2,1,0:T(8,128)S(1)} %pick_24.1), channel_id=1, source_target_pairs={{0,2},{1,3},{2,0},{3,1},{4,6},{5,7},{6,4},{7,5},{8,10},{9,11},{10,... | collective-permute-start | bytes 294920 | tf_op jit(solution)/shard_map/ppermute | solution.py:501
  51.3 1.0 %collective-permute-start.3 = (f32[8,16,128]{2,1,0:T(8,128)S(1)}, f32[8,16,128]{2,1,0:T(8,128)S(1)}, u32[]{:S(2)}, u32[]{:S(2)}) collective-permute-start(f32[8,16,128]{2,1,0:T(8,128)S(1)} %get-tuple-element.42), channel_id=1, source_target_pairs={{0,2},{1,3},{2,0},{3,1},{4,6},{5,7},{6,4},{7,5},{8,10},{9,11},{10,... | collective-permute-start | bytes 196616 | tf_op jit(solution)/shard_map/ppermute | solution.py:501
  52.4 3.8 %collective-permute-done.3.refs_2_ = f32[8,16,128]{2,1,0:T(8,128)S(1)} collective-permute-done((f32[8,16,128]{2,1,0:T(8,128)S(1)}, f32[8,16,128]{2,1,0:T(8,128)S(1)}, u32[]{:S(2)}, u32[]{:S(2)}) %collective-permute-start.3) | collective-permute-done | bytes 65568 | tf_op jit(solution)/shard_map/ppermute | solution.py:501
  56.1 0.0 collective-permute-done.7.refs_5_
  56.1 0.0 collective-permute-done.14.refs_14_
  56.1 0.0 collective-permute-done.12.refs_11_
  56.1 1.5 %assemble.1 = (f32[1280,128]{1,0:T(8,128)S(1)}, f32[1280,128]{1,0:T(8,128)S(1)}, f32[5,4,8,128]{3,2,1,0:T(8,128)S(1)}, f32[5,4,8,128]{3,2,1,0:T(8,128)S(1)}, f32...) custom-call(s32[24]{0:T(128)S(1)} %block_tags.1.tags, ...), custom_call_target="tpu_custom_call" | custom-call | tf_op jit(solution)/shard_map/assemble/pallas_call | solution.py:578
  57.7 1.0 %collective-permute-start.17 = (f32[2,5,4,8,128]{4,3,2,1,0:T(8,128)S(1)}, f32[2,5,4,8,128]{4,3,2,1,0:T(8,128)S(1)}, u32[]{:S(2)}, u32[]{:S(2)}) collective-permute-start(f32[2,5,4,8,128]{4,3,2,1,0:T(8,128)S(1)} %pad_maximum_fusion), channel_id=1, source_target_pairs={{0,16},{16,0},{1,17},{17,1},{2,18},{18,2},{3,19},{19,3},{4,20},{20... | collective-permute-start | bytes 491528 | tf_op jit(solution)/shard_map/ppermute | solution.py:590
  58.6 0.5 collective-permute-start.18
  59.1 4.2 %collective-permute-start.16 = (f32[5,4,8,128]{3,2,1,0:T(8,128)S(1)}, f32[5,4,8,128]{3,2,1,0:T(8,128)S(1)}, u32[]{:S(2)}, u32[]{:S(2)}) collective-permute-start(f32[5,4,8,128]{3,2,1,0:T(8,128)S(1)} %get-tuple-element.55.y_lo), channel_id=1, source_target_pairs={{0,12},{4,0},{8,4},{12,8},{1,13},{5,1},{9,5},{13,9},{2,14},{6,2},{... | collective-permute-start | bytes 245768 | tf_op jit(solution)/shard_map/ppermute | solution.py:590
  63.3 0.2 collective-permute-start.15
  63.5 5.1 %sweep_z.2.sofar = f32[1280,128]{1,0:T(8,128)S(1)} custom-call(f32[1280,128]{1,0:T(8,128)S(1)} %get-tuple-element.54.prim, f32[5,32,128]{2,1,0:T(8,128)S(1)} %get-tuple-element.59.z_lo, f32[5,32,128]{2,1,0:T(8,128)S(1)} %get-tuple-element.60.z_hi, f32[5,32,128]{2,1,0:T(8,128)S(1)} %collective-permute-done.18.z_prev, ...), custom_call_target="tpu_custom_call" | custom-call | tf_op jit(solution)/shard_map/sweep_z/pallas_call | solution.py:600
  68.7 0.0 collective-permute-done.17
  68.7 1.0 %sweep_x.2.sofar = f32[1280,128]{1,0:T(8,128)S(1)} custom-call(f32[1280,128]{1,0:T(8,128)S(1)} %get-tuple-element.54.prim, f32[5,4,8,128]{3,2,1,0:T(8,128)S(1)} %get-tuple-element.72.x_prev, f32[5,4,8,128]{3,2,1,0:T(8,128)S(1)} %get-tuple-element.71.x_next, f32[1280,128]{1,0:T(8,128)S(1)} %sweep_z.2.sofar), custom_call_target="tpu_custom_call", output_to_operand_aliasing={{}: (3, {})} | custom-call | tf_op jit(solution)/shard_map/sweep_x/pallas_call | solution.py:609
  69.7 0.0 collective-permute-done.16.y_next
  69.7 0.4 collective-permute-done.15.y_prev
  70.1 2.3 %sweep_y_one.1 = (f32[1280,128]{1,0:T(8,128)S(1)}, f32[1280,128]{1,0:T(8,128)S(1)}, f32[5,4,8,128]{3,2,1,0:T(8,128)S(1)}, f32[5,4,8,128]{3,2,1,0:T(8,128)S(1)}, ...) custom-call(f32[1280,128]{1,0:T(8,128)S(1)} %get-tuple-element.53.fi, ...), custom_call_target="tpu_custom_call" | custom-call | tf_op jit(solution)/shard_map/sweep_y_one/pallas_call | solution.py:624
  72.4 1.6 %collective-permute-start.22 = (f32[2,5,4,8,128]{4,3,2,1,0:T(8,128)S(1)}, f32[2,5,4,8,128]{4,3,2,1,0:T(8,128)S(1)}, u32[]{:S(2)}, u32[]{:S(2)}) collective-permute-start(f32[2,5,4,8,128]{4,3,2,1,0:T(8,128)S(1)} %pad_maximum_fusion.1), channel_id=1, source_target_pairs={{0,16},{16,0},{1,17},{17,1},{2,18},{18,2},{3,19},{19,3},{4,20},{20... | collective-permute-start | bytes 491528 | tf_op jit(solution)/shard_map/ppermute | solution.py:590
  74.0 0.1 collective-permute-start.24
  74.1 0.4 collective-permute-start.23
  74.5 3.4 %collective-permute-start.21 = (f32[5,4,8,128]{3,2,1,0:T(8,128)S(1)}, f32[5,4,8,128]{3,2,1,0:T(8,128)S(1)}, u32[]{:S(2)}, u32[]{:S(2)}) collective-permute-start(f32[5,4,8,128]{3,2,1,0:T(8,128)S(1)} %get-tuple-element.63.y_lo), channel_id=1, source_target_pairs={{0,12},{4,0},{8,4},{12,8},{1,13},{5,1},{9,5},{13,9},{2,14},{6,2},{... | collective-permute-start | bytes 245768 | tf_op jit(solution)/shard_map/ppermute | solution.py:590
  77.9 0.2 collective-permute-start.20
  78.1 0.0 collective-permute-done.24.z_next
  78.1 0.7 collective-permute-done.23.z_prev
  78.8 5.1 %sweep_z.3.sofar = f32[1280,128]{1,0:T(8,128)S(1)} custom-call(f32[1280,128]{1,0:T(8,128)S(1)} %get-tuple-element.62.prim, f32[5,32,128]{2,1,0:T(8,128)S(1)} %get-tuple-element.67.z_lo, f32[5,32,128]{2,1,0:T(8,128)S(1)} %get-tuple-element.68.z_hi, f32[5,32,128]{2,1,0:T(8,128)S(1)} %collective-permute-done.23.z_prev, ...), custom_call_target="tpu_custom_call" | custom-call | tf_op jit(solution)/shard_map/sweep_z/pallas_call | solution.py:600
  83.9 0.0 collective-permute-done.22
  83.9 1.0 %sweep_x.3.sofar = f32[1280,128]{1,0:T(8,128)S(1)} custom-call(f32[1280,128]{1,0:T(8,128)S(1)} %get-tuple-element.62.prim, f32[5,4,8,128]{3,2,1,0:T(8,128)S(1)} %get-tuple-element.70.x_prev, f32[5,4,8,128]{3,2,1,0:T(8,128)S(1)} %get-tuple-element.69.x_next, f32[1280,128]{1,0:T(8,128)S(1)} %sweep_z.3.sofar), custom_call_target="tpu_custom_call", output_to_operand_aliasing={{}: (3, {})} | custom-call | tf_op jit(solution)/shard_map/sweep_x/pallas_call | solution.py:609
  84.9 0.0 collective-permute-done.21.y_next
  84.9 4.6 %sweep_y_two.1 = f32[5120,128]{1,0:T(8,128)} custom-call(s32[8]{0:T(128)S(1)} %dynamic_slice.3.own, f32[1280,128]{1,0:T(8,128)S(1)} %get-tuple-element.53.field, f32[1280,128]{1,0:T(8,128)S(1)} %get-tuple-element.61.one, f32[1280,128]{1,0:T(8,128)S(1)} %get-tuple-element.62.prim, f32[5,4,8,128]{3,2,1,0:T(8,128)S(1)} %get-tuple-element.63.y_lo, ...), custom_call_target="tpu_custom_call" | custom-call | tf_op jit(solution)/shard_map/sweep_y_two/pallas_call | solution.py:636
  (19 shorter events, 0.1 us)
Async XLA Ops:
  0.0 6.4 %copy-start.3 = (s32[3,1,8]{2,1,0:T(1,128)S(1)}, s32[3,1,8]{2,1,0:T(1,128)}, u32[]{:S(2)}) copy-start(s32[3,1,8]{2,1,0:T(1,128)} %send.3) | copy-start | bytes 292
  0.0 1.8 %copy-start = (f32[32,5,4096]{2,0,1:T(8,128)S(1)}, f32[32,5,4096]{2,0,1:T(8,128)}, u32[]{:S(2)}) copy-start(f32[32,5,4096]{2,0,1:T(8,128)} %param.4) | copy-start | bytes 7864324
  1.8 0.7 copy-start.2
  2.4 3.9 %copy-start.5 = (s32[256]{0:T(256)S(1)}, s32[256]{0:T(256)}, u32[]{:S(2)}) copy-start(s32[256]{0:T(256)} %param.7) | copy-start | bytes 3076
  2.4 4.0 %copy-start.4 = (s32[3,1,8]{2,1,0:T(1,128)S(1)}, s32[3,1,8]{2,1,0:T(1,128)}, u32[]{:S(2)}) copy-start(s32[3,1,8]{2,1,0:T(1,128)} %recv.1) | copy-start | bytes 292
  2.4 9.4 %copy-start.1 = (f32[32,5,4096]{2,0,1:T(8,128)S(1)}, f32[32,5,4096]{2,0,1:T(8,128)}, u32[]{:S(2)}) copy-start(f32[32,5,4096]{2,0,1:T(8,128)} %param.4) | copy-start | bytes 7864324
  3.2 11.1 %collective-permute-start.4 = (f32[8,40,128]{2,1,0:T(8,128)S(1)}, f32[8,40,128]{2,1,0:T(8,128)S(1)}, u32[]{:S(2)}, u32[]{:S(2)}) collective-permute-start(f32[8,40,128]{2,1,0:T(8,128)S(1)} %get-tuple-element.43), channel_id=1, source_target_pairs={{0,16},{1,17},{2,18},{3,19},{4,20},{5,21},{6,22},{7,23},{8,24},{9,... | collective-permute-start | bytes 491528 | tf_op jit(solution)/shard_map/ppermute | solution.py:501
  6.2 5.6 %collective-permute-start = (f32[8,16,128]{2,1,0:T(8,128)S(1)}, f32[8,16,128]{2,1,0:T(8,128)S(1)}, u32[]{:S(2)}, u32[]{:S(2)}) collective-permute-start(f32[8,16,128]{2,1,0:T(8,128)S(1)} %get-tuple-element.37), channel_id=1, source_target_pairs={{0,16},{1,17},{2,18},{3,19},{4,20},{5,21},{6,22},{7,23},{8,24},{9,... | collective-permute-start | bytes 196616 | tf_op jit(solution)/shard_map/ppermute | solution.py:501
  12.5 14.5 %collective-permute-start.2 = (f32[8,40,128]{2,1,0:T(8,128)S(1)}, f32[8,40,128]{2,1,0:T(8,128)S(1)}, u32[]{:S(2)}, u32[]{:S(2)}) collective-permute-start(f32[8,40,128]{2,1,0:T(8,128)S(1)} %get-tuple-element.40), channel_id=1, source_target_pairs={{0,16},{1,17},{2,18},{3,19},{4,20},{5,21},{6,22},{7,23},{8,24},{9,... | collective-permute-start | bytes 491528 | tf_op jit(solution)/shard_map/ppermute | solution.py:501
  14.9 12.9 %collective-permute-start.5 = (f32[8,40,128]{2,1,0:T(8,128)S(1)}, f32[8,40,128]{2,1,0:T(8,128)S(1)}, u32[]{:S(2)}, u32[]{:S(2)}) collective-permute-start(f32[8,40,128]{2,1,0:T(8,128)S(1)} %get-tuple-element.45), channel_id=1, source_target_pairs={{0,8},{1,9},{2,10},{3,11},{4,12},{5,13},{6,14},{7,15},{8,0},{9,1},... | collective-permute-start | bytes 491528 | tf_op jit(solution)/shard_map/ppermute | solution.py:501
  17.6 10.2 %collective-permute-start.6 = (f32[8,40,128]{2,1,0:T(8,128)S(1)}, f32[8,40,128]{2,1,0:T(8,128)S(1)}, u32[]{:S(2)}, u32[]{:S(2)}) collective-permute-start(f32[8,40,128]{2,1,0:T(8,128)S(1)} %get-tuple-element.46), channel_id=1, source_target_pairs={{0,16},{1,17},{2,18},{3,19},{4,20},{5,21},{6,22},{7,23},{8,24},{9,... | collective-permute-start | bytes 491528 | tf_op jit(solution)/shard_map/ppermute | solution.py:501
  18.1 8.9 %collective-permute-start.1 = (f32[8,16,128]{2,1,0:T(8,128)S(1)}, f32[8,16,128]{2,1,0:T(8,128)S(1)}, u32[]{:S(2)}, u32[]{:S(2)}) collective-permute-start(f32[8,16,128]{2,1,0:T(8,128)S(1)} %get-tuple-element.39), channel_id=1, source_target_pairs={{0,8},{1,9},{2,10},{3,11},{4,12},{5,13},{6,14},{7,15},{8,0},{9,1},... | collective-permute-start | bytes 196616 | tf_op jit(solution)/shard_map/ppermute | solution.py:501
  27.7 15.1 %collective-permute-start.8 = (f32[8,40,128]{2,1,0:T(8,128)S(1)}, f32[8,40,128]{2,1,0:T(8,128)S(1)}, u32[]{:S(2)}, u32[]{:S(2)}) collective-permute-start(f32[8,40,128]{2,1,0:T(8,128)S(1)} %get-tuple-element.48), channel_id=1, source_target_pairs={{0,8},{1,9},{2,10},{3,11},{4,12},{5,13},{6,14},{7,15},{8,0},{9,1},... | collective-permute-start | bytes 491528 | tf_op jit(solution)/shard_map/ppermute | solution.py:501
  28.5 18.9 %collective-permute-start.11 = (f32[8,40,128]{2,1,0:T(8,128)S(1)}, f32[8,40,128]{2,1,0:T(8,128)S(1)}, u32[]{:S(2)}, u32[]{:S(2)}) collective-permute-start(f32[8,40,128]{2,1,0:T(8,128)S(1)} %get-tuple-element.51), channel_id=1, source_target_pairs={{0,8},{1,9},{2,10},{3,11},{4,12},{5,13},{6,14},{7,15},{8,0},{9,1},... | collective-permute-start | bytes 491528 | tf_op jit(solution)/shard_map/ppermute | solution.py:501
  31.5 4.6 %collective-permute-start.9 = (f32[8,24,128]{2,1,0:T(8,128)S(1)}, f32[8,24,128]{2,1,0:T(8,128)S(1)}, u32[]{:S(2)}, u32[]{:S(2)}) collective-permute-start(f32[8,24,128]{2,1,0:T(8,128)S(1)} %get-tuple-element.49), channel_id=1, source_target_pairs={{0,16},{1,17},{2,18},{3,19},{4,20},{5,21},{6,22},{7,23},{8,24},{9,... | collective-permute-start | bytes 294920 | tf_op jit(solution)/shard_map/ppermute | solution.py:501
  43.5 6.1 %collective-permute-start.13 = (f32[8,24,128]{2,1,0:T(8,128)S(1)}, f32[8,24,128]{2,1,0:T(8,128)S(1)}, u32[]{:S(2)}, u32[]{:S(2)}) collective-permute-start(f32[8,24,128]{2,1,0:T(8,128)S(1)} %get-tuple-element.52), channel_id=1, source_target_pairs={{0,8},{1,9},{2,10},{3,11},{4,12},{5,13},{6,14},{7,15},{8,0},{9,1},... | collective-permute-start | bytes 294920 | tf_op jit(solution)/shard_map/ppermute | solution.py:501
  43.6 12.5 %collective-permute-start.7 = (f32[8,40,128]{2,1,0:T(8,128)S(1)}, f32[8,40,128]{2,1,0:T(8,128)S(1)}, u32[]{:S(2)}, u32[]{:S(2)}) collective-permute-start(f32[8,40,128]{2,1,0:T(8,128)S(1)} %get-tuple-element.47), channel_id=1, source_target_pairs={{0,2},{1,3},{2,0},{3,1},{4,6},{5,7},{6,4},{7,5},{8,10},{9,11},{10,... | collective-permute-start | bytes 491528 | tf_op jit(solution)/shard_map/ppermute | solution.py:501
  45.2 10.9 %collective-permute-start.10 = (f32[8,40,128]{2,1,0:T(8,128)S(1)}, f32[8,40,128]{2,1,0:T(8,128)S(1)}, u32[]{:S(2)}, u32[]{:S(2)}) collective-permute-start(f32[8,40,128]{2,1,0:T(8,128)S(1)} %get-tuple-element.50), channel_id=1, source_target_pairs={{0,2},{1,3},{2,0},{3,1},{4,6},{5,7},{6,4},{7,5},{8,10},{9,11},{10,... | collective-permute-start | bytes 491528 | tf_op jit(solution)/shard_map/ppermute | solution.py:501
  48.1 8.1 %collective-permute-start.12 = (f32[8,40,128]{2,1,0:T(8,128)S(1)}, f32[8,40,128]{2,1,0:T(8,128)S(1)}, u32[]{:S(2)}, u32[]{:S(2)}) collective-permute-start(f32[8,40,128]{2,1,0:T(8,128)S(1)} %pick_23.1), channel_id=1, source_target_pairs={{0,2},{1,3},{2,0},{3,1},{4,6},{5,7},{6,4},{7,5},{8,10},{9,11},{10,... | collective-permute-start | bytes 491528 | tf_op jit(solution)/shard_map/ppermute | solution.py:501
  50.3 5.9 %collective-permute-start.14 = (f32[8,24,128]{2,1,0:T(8,128)S(1)}, f32[8,24,128]{2,1,0:T(8,128)S(1)}, u32[]{:S(2)}, u32[]{:S(2)}) collective-permute-start(f32[8,24,128]{2,1,0:T(8,128)S(1)} %pick_24.1), channel_id=1, source_target_pairs={{0,2},{1,3},{2,0},{3,1},{4,6},{5,7},{6,4},{7,5},{8,10},{9,11},{10,... | collective-permute-start | bytes 294920 | tf_op jit(solution)/shard_map/ppermute | solution.py:501
  51.3 4.8 %collective-permute-start.3 = (f32[8,16,128]{2,1,0:T(8,128)S(1)}, f32[8,16,128]{2,1,0:T(8,128)S(1)}, u32[]{:S(2)}, u32[]{:S(2)}) collective-permute-start(f32[8,16,128]{2,1,0:T(8,128)S(1)} %get-tuple-element.42), channel_id=1, source_target_pairs={{0,2},{1,3},{2,0},{3,1},{4,6},{5,7},{6,4},{7,5},{8,10},{9,11},{10,... | collective-permute-start | bytes 196616 | tf_op jit(solution)/shard_map/ppermute | solution.py:501
  57.7 11.0 %collective-permute-start.17 = (f32[2,5,4,8,128]{4,3,2,1,0:T(8,128)S(1)}, f32[2,5,4,8,128]{4,3,2,1,0:T(8,128)S(1)}, u32[]{:S(2)}, u32[]{:S(2)}) collective-permute-start(f32[2,5,4,8,128]{4,3,2,1,0:T(8,128)S(1)} %pad_maximum_fusion), channel_id=1, source_target_pairs={{0,16},{16,0},{1,17},{17,1},{2,18},{18,2},{3,19},{19,3},{4,20},{20... | collective-permute-start | bytes 491528 | tf_op jit(solution)/shard_map/ppermute | solution.py:590
  58.6 4.9 %collective-permute-start.19 = (f32[5,32,128]{2,1,0:T(8,128)S(1)}, f32[5,32,128]{2,1,0:T(8,128)S(1)}, u32[]{:S(2)}, u32[]{:S(2)}) collective-permute-start(f32[5,32,128]{2,1,0:T(8,128)S(1)} %get-tuple-element.59.z_lo), channel_id=1, source_target_pairs={{0,3},{1,0},{2,1},{3,2},{4,7},{5,4},{6,5},{7,6},{8,11},{9,8},{10,9... | collective-permute-start | bytes 245768 | tf_op jit(solution)/shard_map/ppermute | solution.py:590
  58.6 4.9 %collective-permute-start.18 = (f32[5,32,128]{2,1,0:T(8,128)S(1)}, f32[5,32,128]{2,1,0:T(8,128)S(1)}, u32[]{:S(2)}, u32[]{:S(2)}) collective-permute-start(f32[5,32,128]{2,1,0:T(8,128)S(1)} %get-tuple-element.60.z_hi), channel_id=1, source_target_pairs={{0,1},{1,2},{2,3},{3,0},{4,5},{5,6},{6,7},{7,4},{8,9},{9,10},{10,1... | collective-permute-start | bytes 245768 | tf_op jit(solution)/shard_map/ppermute | solution.py:590
  59.1 10.6 %collective-permute-start.16 = (f32[5,4,8,128]{3,2,1,0:T(8,128)S(1)}, f32[5,4,8,128]{3,2,1,0:T(8,128)S(1)}, u32[]{:S(2)}, u32[]{:S(2)}) collective-permute-start(f32[5,4,8,128]{3,2,1,0:T(8,128)S(1)} %get-tuple-element.55.y_lo), channel_id=1, source_target_pairs={{0,12},{4,0},{8,4},{12,8},{1,13},{5,1},{9,5},{13,9},{2,14},{6,2},{... | collective-permute-start | bytes 245768 | tf_op jit(solution)/shard_map/ppermute | solution.py:590
  63.3 6.8 %collective-permute-start.15 = (f32[5,4,8,128]{3,2,1,0:T(8,128)S(1)}, f32[5,4,8,128]{3,2,1,0:T(8,128)S(1)}, u32[]{:S(2)}, u32[]{:S(2)}) collective-permute-start(f32[5,4,8,128]{3,2,1,0:T(8,128)S(1)} %get-tuple-element.56.y_hi), channel_id=1, source_target_pairs={{0,4},{4,8},{8,12},{12,0},{1,5},{5,9},{9,13},{13,1},{2,6},{6,10},{... | collective-permute-start | bytes 245768 | tf_op jit(solution)/shard_map/ppermute | solution.py:590
  72.4 11.5 %collective-permute-start.22 = (f32[2,5,4,8,128]{4,3,2,1,0:T(8,128)S(1)}, f32[2,5,4,8,128]{4,3,2,1,0:T(8,128)S(1)}, u32[]{:S(2)}, u32[]{:S(2)}) collective-permute-start(f32[2,5,4,8,128]{4,3,2,1,0:T(8,128)S(1)} %pad_maximum_fusion.1), channel_id=1, source_target_pairs={{0,16},{16,0},{1,17},{17,1},{2,18},{18,2},{3,19},{19,3},{4,20},{20... | collective-permute-start | bytes 491528 | tf_op jit(solution)/shard_map/ppermute | solution.py:590
  74.0 4.1 %collective-permute-start.24 = (f32[5,32,128]{2,1,0:T(8,128)S(1)}, f32[5,32,128]{2,1,0:T(8,128)S(1)}, u32[]{:S(2)}, u32[]{:S(2)}) collective-permute-start(f32[5,32,128]{2,1,0:T(8,128)S(1)} %get-tuple-element.67.z_lo), channel_id=1, source_target_pairs={{0,3},{1,0},{2,1},{3,2},{4,7},{5,4},{6,5},{7,6},{8,11},{9,8},{10,9... | collective-permute-start | bytes 245768 | tf_op jit(solution)/shard_map/ppermute | solution.py:590
  74.1 4.7 %collective-permute-start.23 = (f32[5,32,128]{2,1,0:T(8,128)S(1)}, f32[5,32,128]{2,1,0:T(8,128)S(1)}, u32[]{:S(2)}, u32[]{:S(2)}) collective-permute-start(f32[5,32,128]{2,1,0:T(8,128)S(1)} %get-tuple-element.68.z_hi), channel_id=1, source_target_pairs={{0,1},{1,2},{2,3},{3,0},{4,5},{5,6},{6,7},{7,4},{8,9},{9,10},{10,1... | collective-permute-start | bytes 245768 | tf_op jit(solution)/shard_map/ppermute | solution.py:590
  74.5 10.5 %collective-permute-start.21 = (f32[5,4,8,128]{3,2,1,0:T(8,128)S(1)}, f32[5,4,8,128]{3,2,1,0:T(8,128)S(1)}, u32[]{:S(2)}, u32[]{:S(2)}) collective-permute-start(f32[5,4,8,128]{3,2,1,0:T(8,128)S(1)} %get-tuple-element.63.y_lo), channel_id=1, source_target_pairs={{0,12},{4,0},{8,4},{12,8},{1,13},{5,1},{9,5},{13,9},{2,14},{6,2},{... | collective-permute-start | bytes 245768 | tf_op jit(solution)/shard_map/ppermute | solution.py:590
  77.9 7.1 %collective-permute-start.20 = (f32[5,4,8,128]{3,2,1,0:T(8,128)S(1)}, f32[5,4,8,128]{3,2,1,0:T(8,128)S(1)}, u32[]{:S(2)}, u32[]{:S(2)}) collective-permute-start(f32[5,4,8,128]{3,2,1,0:T(8,128)S(1)} %get-tuple-element.64.y_hi), channel_id=1, source_target_pairs={{0,4},{4,8},{8,12},{12,0},{1,5},{5,9},{9,13},{13,1},{2,6},{6,10},{... | collective-permute-start | bytes 245768 | tf_op jit(solution)/shard_map/ppermute | solution.py:590
where the time goes:
time: 90.5 us; the launch traced here: 89.5 us
  waiting for transfers between devices  29.9 us (33%)
  starting transfers between devices  29.2 us (32%)
  Pallas kernels  27.6 us (30%)
  local copies, waits for them, and re-layouts  2.55 us (3%)
    ppermute x15, waiting for transfers between devices, swapped(): return lax.ppermute(value, AXES, pairs)  28.8 us
    ppermute x15, starting transfers between devices, swapped(): return lax.ppermute(value, AXES, pairs)  17.6 us
    ppermute x10, starting transfers between devices, ring(): lax.ppermute(value, axis, [(i, (i + step) % size) for i in range(size)])  11.6 us
    pallas_call x2, Pallas kernels, flux_sums(): pl.pallas_call(functools.partial(sweep_z_kernel, shape=shape), out_shape=...  10.3 us
    pallas_call x7, Pallas kernels, make(): pl.pallas_call(functools.partial(pick_kernel, plan=tuple(plan), given=giv...  4.67 us
    pallas_call x1, Pallas kernels, shards(): pl.pallas_call(functools.partial(sweep_y_two_kernel, shape=shape, occ=occ...  4.59 us
    unnamed x12, local copies, waits for them, and re-layouts  2.45 us
    pallas_call x1, Pallas kernels, shards(): pl.pallas_call(functools.partial(sweep_y_one_kernel, shape=shape), out_sh...  2.25 us
  transfers between devices with their start and end apart: 25, of which 8 were waited for; matrix products, arithmetic and copies ran while one was open for 0% of the time, Pallas kernels for 21%

commit v1 on v0

--- a/solution.py
+++ b/solution.py
@@ -34,9 +34,9 @@
 
 
 def split_units(units):
-    first, last = units // 10, 3 * units // 20
-    middle = units - first - last
-    sizes = [first] + [middle // 3 + (i < middle % 3) for i in range(3)] + [last]
+    shares = (2, 4, 5, 6)
+    sizes = [units * share // 20 for share in shares]
+    sizes.append(units - sum(sizes))
     starts = [sum(sizes[:i]) for i in range(len(sizes) + 1)]
     return list(zip(starts[:-1], starts[1:]))
 
@@ -58,7 +58,7 @@
     return value
 
 
-def first_kernel(send, state, *outs, pieces, slots, rows, moves):
+def pack_pieces(send, state, outs, pieces, slots, rows, moves):
     for k in range(moves):
         slot = jnp.minimum(send[0, 0, k], slots - 1)
         for (begin, end), out in zip(pieces, outs):
@@ -67,27 +67,54 @@
                 out[k, at : at + SUB, :] = from_state(state, slot, unit, slots, rows)
 
 
-def tags_kernel(send, recv, own, tags, *, slots, moves, occ):
-    def find(slot, levels):
-        tag = slot
-        for level in range(levels):
-            for j in range(moves):
-                tag = jnp.where(recv[level, 0, j] == slot, slots + level * moves + j, tag)
-        return tag
-
-    def one(k, carry):
-        for level in (1, 2):
-            slot = jnp.minimum(send[level, 0, k], slots - 1)
-            tags[(level - 1) * moves + k] = find(slot, level)
-        return carry
-
-    lax.fori_loop(0, moves, one, 0)
-
-    def last(b, carry):
-        tags[2 * moves + b] = find(own[b], 3)
-        return carry
-
-    lax.fori_loop(0, occ, last, 0)
+def first_kernel(send_hbm, state_hbm, out, send, held, sems, *, piece, slots, rows, moves):
+    span = SUB * SUB
+    groups = slots // SUB
+    copies = [pltpu.make_async_copy(send_hbm, send, sems.at[0])]
+    for unit in range(*piece):
+        slab, field = unit // NF, unit % NF
+        for g in range(groups):
+            at = ((field * groups + g) * rows + slab * SUB) * SUB
+            to = ((unit - piece[0]) * groups + g) * span
+            copies.append(
+                pltpu.make_async_copy(
+                    state_hbm.at[pl.ds(at, span), :],
+                    held.at[pl.ds(to, span), :],
+                    sems.at[len(copies)],
+                )
+            )
+    for c in copies:
+        c.start()
+    for c in copies:
+        c.wait()
+    for k in range(moves):
+        slot = jnp.minimum(send[0, 0, k], slots - 1)
+        base = (slot // SUB) * span + lax.rem(slot, SUB)
+        for i in range(piece[1] - piece[0]):
+            out[k, i * SUB : (i + 1) * SUB, :] = held[
+                pl.ds(base + i * groups * span, SUB, stride=SUB), :
+            ]
+
+
+def load_kernel(send, recv, own, state_hbm, *refs, pieces, slots, rows, moves, occ):
+    state, tags = refs[:2]
+    outs = refs[2 : 2 + len(pieces)]
+    where, sem = refs[2 + len(pieces) :]
+    copy = pltpu.make_async_copy(state_hbm, state, sem)
+    copy.start()
+    for slot in range(slots):
+        where[slot] = slot
+    for level in range(3):
+        if level:
+            for k in range(moves):
+                slot = jnp.minimum(send[level, 0, k], slots - 1)
+                tags[(level - 1) * moves + k] = where[slot]
+        for k in range(moves):
+            where[recv[level, 0, k]] = slots + level * moves + k
+    for b in range(occ):
+        tags[2 * moves + b] = where[own[b]]
+    copy.wait()
+    pack_pieces(send, state, outs, pieces, slots, rows, moves)
 
 
 def pick_kernel(tags, state, *refs, plan, given, passed, slots, rows, moves):
@@ -178,14 +205,17 @@
         self.pad = 2 * self.halves
 
     def at(self, f, row):
-        start = (f * self.rows + row) * SUB
+        start = SUB + (f * self.rows + row) * SUB
         return pl.ds(start if isinstance(start, int) else pl.multiple_of(start, SUB), SUB)
 
     def across(self, f, slab, sub):
-        return pl.ds((f * self.rows + slab * SUB) * SUB + sub, SUB, stride=SUB)
+        return pl.ds(SUB + (f * self.rows + slab * SUB) * SUB + sub, SUB, stride=SUB)
+
+    def beside(self, f, row, step):
+        return pl.ds(SUB + (f * self.rows + row) * SUB + step, SUB)
 
     def grid(self):
-        return jax.ShapeDtypeStruct((NF * self.rows * SUB, LANES), f32)
+        return jax.ShapeDtypeStruct(((NF * self.rows + 2) * SUB, LANES), f32)
 
     def faces(self):
         x = jax.ShapeDtypeStruct((NF, self.pad, SUB, LANES), f32)
@@ -225,22 +255,23 @@
             x_hi[f, i] = prim[shape.at(f, shape.rows - shape.pad + i), :]
 
 
-def assemble_kernel(tags, state, *refs, pieces, slots, moves, occ, shape):
-    count = 3 * len(pieces)
-    given = refs[:count]
-    field, prim, x_lo, x_hi, y_lo, y_hi, z_lo, z_hi, held = refs[count:]
-    rows = shape.rows
+def assemble_kernel(tags, state, *refs, pieces, slabs, slots, moves, occ, shape, first):
+    given = refs[: 3 * len(pieces)]
+    rest = refs[len(given) + (0 if first else 7) :]
+    field, prim, y_lo, y_hi, z_lo, z_hi, other = rest[:7]
+    held = rest[7]
     units = NF * shape.slabs
+    begin_unit, end_unit = slabs[0] * NF, slabs[1] * NF
     for b in range(occ):
         tag = tags[2 * moves + b]
         for number, (begin, end) in enumerate(pieces):
             sources = given[3 * number : 3 * number + 3]
-            for unit in range(begin, end):
+            for unit in range(max(begin, begin_unit), min(end, end_unit)):
                 at = (b * units + unit) * SUB
                 held[at : at + SUB, :] = pick(
-                    tag, unit, unit - begin, state, sources, slots, rows, moves
+                    tag, unit, unit - begin, state, sources, slots, shape.rows, moves
                 )
-    for slab in range(shape.slabs):
+    for slab in range(*slabs):
         for i in range(SUB):
             row = slab * SUB + i
             cons = [
@@ -250,10 +281,23 @@
                 field[shape.at(f, row), :] = c
                 prim[shape.at(f, row), :] = w
         send_slab(shape, prim, y_lo, y_hi, z_lo, z_hi, slab)
-    send_x(shape, prim, x_lo, x_hi)
-
-
-def sweep_z_kernel(prim, z_lo, z_hi, z_prev, z_next, total, below_z, flux_z, over_z, right_z, *, shape):
+    if first:
+
+        def clear(i, carry):
+            other[pl.ds(pl.multiple_of(i * SUB, SUB), SUB), :] = jnp.zeros((SUB, LANES), f32)
+            return carry
+
+        lax.fori_loop(0, other.shape[0] // SUB, clear, 0, unroll=16)
+        for f in FIELDS:
+            for i in range(shape.pad):
+                rest[8][f, i] = prim[shape.at(f, i), :]
+    else:
+        for f in FIELDS:
+            for i in range(shape.pad):
+                rest[8][f, i] = prim[shape.at(f, shape.rows - shape.pad + i), :]
+
+
+def sweep_z_kernel(prim, z_lo, z_hi, z_prev, z_next, total, flux_z, right_z, left, right, flux, *, shape):
     edge, rows = shape.edge, shape.rows
 
     def ghost(a, carry):
@@ -265,53 +309,73 @@
         below = [lane_roll(v, -(edge - 1)) for v in prev]
         before = [lane_roll(v, -(edge - 2)) for v in prev]
         second = [lane_roll(v, -1) for v in low]
-        left = plus(below, half_slopes(before, below, low))
-        right = minus(low, half_slopes(below, low, second))
-        flux = twice_flux(left, right, 2)
+        lefts = plus(below, half_slopes(before, below, low))
+        rights = minus(low, half_slopes(below, low, second))
+        fluxes = twice_flux(lefts, rights, 2)
         last = [lane_roll(v, -(edge - 1)) for v in high]
         beyond = [lane_roll(v, -1) for v in after]
         over = minus(after, half_slopes(last, after, beyond))
         for f in FIELDS:
-            below_z[f, at, :] = below[f]
-            flux_z[f, at, :] = flux[f]
-            over_z[f, at, :] = lane_roll(after[f], edge - 1)
-            right_z[f, at, :] = lane_roll(over[f], edge - 1)
+            flux_z[f, at, :] = lane_roll(fluxes[f], edge - 1)
+            right_z[f, at, :] = over[f]
         return carry
 
     lax.fori_loop(0, shape.slabs, ghost, 0)
-    z_of = lax.rem(lane_of(), edge)
+    lane = lane_of()
+    z_of = lax.rem(lane, edge)
     sub = sub_of()
     first_z, last_z = z_of == 0, z_of == edge - 1
     first_sub, last_sub = sub == 0, sub == SUB - 1
-
-    def up(value, insert):
-        across = pltpu.roll(lane_roll(value, edge - 1), SUB - 1, 0)
-        across = jnp.where(last_sub, insert, across)
-        return jnp.where(last_z, across, lane_roll(value, -1))
-
-    def down(value, insert):
-        across = pltpu.roll(lane_roll(value, -(edge - 1)), 1, 0)
-        across = jnp.where(first_sub, insert, across)
-        return jnp.where(first_z, across, lane_roll(value, 1))
-
-    def body(row, carry):
-        def insert(ref, f):
-            return jnp.broadcast_to(ref[f, pl.ds(row, 1), :], (SUB, LANES))
-
-        left, right = [], []
-        for f in FIELDS:
-            mine = prim[shape.at(f, row), :]
-            shift = half_minmod(
-                mine - down(mine, insert(below_z, f)), up(mine, insert(over_z, f)) - mine
-            )
-            left.append(mine + shift)
-            right.append(up(mine - shift, insert(right_z, f)))
-        flux = twice_flux(left, right, 2)
-        for f in FIELDS:
-            total[shape.at(f, row), :] = flux[f] - down(flux[f], insert(flux_z, f))
+    higher = lane - z_of + lax.rem(z_of + 1, edge)
+    lower = lane - z_of + lax.rem(z_of + edge - 1, edge)
+
+    def insert(ref, f, row):
+        return jnp.broadcast_to(ref[f, pl.ds(row, 1), :], (SUB, LANES))
+
+    def up(ref, value, f, row, ghosts):
+        across = ref[shape.beside(f, row, 1), :]
+        across = jnp.where(last_sub, insert(ghosts, f, row), across)
+        return jnp.take_along_axis(jnp.where(first_z, across, value), higher, axis=1)
+
+    def down(ref, value, f, row, ghosts):
+        across = ref[shape.beside(f, row, -1), :]
+        across = jnp.where(first_sub, insert(ghosts, f, row), across)
+        return jnp.take_along_axis(jnp.where(last_z, across, value), lower, axis=1)
+
+    def slopes(slab, carry):
+        for i in range(SUB):
+            row = slab * SUB + i
+            for f in FIELDS:
+                at = shape.at(f, row)
+                mine = prim[at, :]
+                shift = half_minmod(
+                    mine - down(prim, mine, f, row, z_prev), up(prim, mine, f, row, z_next) - mine
+                )
+                left[at, :] = mine + shift
+                right[at, :] = mine - shift
         return carry
 
-    lax.fori_loop(0, rows, body, 0, unroll=2)
+    def fluxes(slab, carry):
+        for i in range(SUB):
+            row = slab * SUB + i
+            lefts = [left[shape.at(f, row), :] for f in FIELDS]
+            rights = [up(right, right[shape.at(f, row), :], f, row, right_z) for f in FIELDS]
+            for f, value in enumerate(twice_flux(lefts, rights, 2)):
+                flux[shape.at(f, row), :] = value
+        return carry
+
+    def differences(slab, carry):
+        for i in range(SUB):
+            row = slab * SUB + i
+            for f in FIELDS:
+                at = shape.at(f, row)
+                mine = flux[at, :]
+                total[at, :] = mine - down(flux, mine, f, row, flux_z)
+        return carry
+
+    lax.fori_loop(0, shape.slabs, slopes, 0)
+    lax.fori_loop(0, shape.slabs, fluxes, 0)
+    lax.fori_loop(0, shape.slabs, differences, 0)
 
 
 def sweep_x_kernel(prim, x_prev, x_next, sofar, total, wide, *, shape):
@@ -350,7 +414,8 @@
         lax.fori_loop(0, shape.edge, body, (flux, keep), unroll=4)
 
 
-def sweep_y(prim, y_lo, y_hi, y_prev, y_next, sofar, ghost_prim, ghost_flux, shape, finish, after_slab):
+def sweep_y(prim, y_lo, y_hi, y_prev, y_next, sofar, ghost_prim, ghost_flux, left, right, flux,
+            shape, finish, after_slab):
     edge, halves, fit, width = shape.edge, shape.halves, shape.fit, shape.width
     lane = lane_of()
     upper = lax.rem(lane, width) >= edge
@@ -362,15 +427,15 @@
         after = [y_next[f, q] for f in FIELDS]
         before = [lane_roll(v, edge) for v in below]
         first = [lane_roll(v, edge) for v in low]
-        left = plus(below, half_slopes(before, below, first))
-        right = minus(first, half_slopes(below, first, low))
-        flux = twice_flux(left, right, 1)
+        lefts = plus(below, half_slopes(before, below, first))
+        rights = minus(first, half_slopes(below, first, low))
+        fluxes = twice_flux(lefts, rights, 1)
         last = [lane_roll(v, -edge) for v in high]
         beyond = [lane_roll(v, -edge) for v in after]
         over = minus(after, half_slopes(last, after, beyond))
         for f in FIELDS:
             ghost_prim[f, q] = jnp.where(upper, below[f], after[f])
-            ghost_flux[f, q] = jnp.where(upper, flux[f], over[f])
+            ghost_flux[f, q] = jnp.where(upper, fluxes[f], over[f])
         return carry
 
     lax.fori_loop(0, edge // fit, ghost, 0)
@@ -387,25 +452,40 @@
         lead = [insert] + rolled[:-1]
         return [jnp.where(low_lanes, n, r) for r, n in zip(rolled, lead)]
 
-    def body(q, carry):
+    def each(q):
         for k in range(fit):
-            turn = -(width * k + edge)
-            base = (q * fit + k) * halves
-            left = [[None] * NF for _ in range(halves)]
-            right = [[None] * NF for _ in range(halves)]
+            yield -(width * k + edge), (q * fit + k) * halves
+
+    def slopes(q, carry):
+        for turn, base in each(q):
             for f in FIELDS:
                 mine = [prim[shape.at(f, base + h), :] for h in range(halves)]
                 ghost = lane_roll(ghost_prim[f, q], turn)
                 over, under = up(mine, ghost), down(mine, ghost)
-                shift = [half_minmod(m - d, u - m) for m, d, u in zip(mine, under, over)]
-                above = up(minus(mine, shift), lane_roll(ghost_flux[f, q], turn))
                 for h in range(halves):
-                    left[h][f] = mine[h] + shift[h]
-                    right[h][f] = above[h]
-            fluxes = [twice_flux(left[h], right[h], 1) for h in range(halves)]
+                    shift = half_minmod(mine[h] - under[h], over[h] - mine[h])
+                    left[shape.at(f, base + h), :] = mine[h] + shift
+                    right[shape.at(f, base + h), :] = mine[h] - shift
+        return carry
+
+    def fluxes(q, carry):
+        for turn, base in each(q):
+            rights = []
+            for f in FIELDS:
+                mine = [right[shape.at(f, base + h), :] for h in range(halves)]
+                rights.append(up(mine, lane_roll(ghost_flux[f, q], turn)))
+            for h in range(halves):
+                lefts = [left[shape.at(f, base + h), :] for f in FIELDS]
+                result = twice_flux(lefts, [rights[f][h] for f in FIELDS], 1)
+                for f in FIELDS:
+                    flux[shape.at(f, base + h), :] = result[f]
+        return carry
+
+    def differences(q, carry):
+        for turn, base in each(q):
             total = [[None] * NF for _ in range(halves)]
             for f in FIELDS:
-                mine = [fluxes[h][f] for h in range(halves)]
+                mine = [flux[shape.at(f, base + h), :] for h in range(halves)]
                 under = down(mine, lane_roll(ghost_flux[f, q], turn))
                 for h in range(halves):
                     total[h][f] = sofar[shape.at(f, base + h), :] + (mine[h] - under[h])
@@ -414,7 +494,9 @@
         after_slab(q)
         return carry
 
-    lax.fori_loop(0, edge // fit, body, 0)
+    lax.fori_loop(0, edge // fit, slopes, 0)
+    lax.fori_loop(0, edge // fit, fluxes, 0)
+    lax.fori_loop(0, edge // fit, differences, 0)
 
 
 def sweep_y_one_kernel(field, prim, y_lo, y_hi, y_prev, y_next, sofar, *refs, shape):
@@ -433,16 +515,11 @@
     send_x(shape, one_prim, x_lo, x_hi)
 
 
-def sweep_y_two_kernel(own, field, one, prim, y_lo, y_hi, y_prev, y_next, sofar, out,
-                       ghost_prim, ghost_flux, result, canvas, sems, *, shape, occ, groups):
+def sweep_y_two_kernel(own, field, one, prim, y_lo, y_hi, y_prev, y_next, sofar, zeros, out,
+                       canvas, *refs, shape, occ, groups):
+    scratch, (result, sems) = refs[:5], refs[5:]
     rows = shape.rows
     span = SUB * SUB
-
-    def clear(i, carry):
-        canvas[pl.ds(pl.multiple_of(i * SUB, SUB), SUB), :] = jnp.zeros((SUB, LANES), f32)
-        return carry
-
-    lax.fori_loop(0, NF * groups * rows, clear, 0, unroll=16)
 
     def finish(row, total):
         for f in FIELDS:
@@ -472,7 +549,7 @@
         for c in copy(q):
             c.start()
 
-    sweep_y(prim, y_lo, y_hi, y_prev, y_next, sofar, ghost_prim, ghost_flux, shape, finish, after_slab)
+    sweep_y(prim, y_lo, y_hi, y_prev, y_next, sofar, *scratch, shape, finish, after_slab)
     for part in range(shape.slabs):
         for c in copy(part):
             c.wait()
@@ -505,6 +582,8 @@
         .transpose(2, 0, 3, 1, 4)
         .reshape(NF * groups * rows * SUB, LANES)
     )
+    rows_of_state = pltpu.with_memory_space_constraint(rows_of_state, HBM)
+    send_there = pltpu.with_memory_space_constraint(send_slots, HBM)
     device = lax.axis_index(AXES)
     own = lax.dynamic_slice(owner_slot, (device * occ,), (occ,))
     sizes = dict(slots=slots, moves=moves)
@@ -513,23 +592,35 @@
         begin, end = pieces[p]
         return jax.ShapeDtypeStruct((moves, (end - begin) * SUB, LANES), f32)
 
-    sent = pl.pallas_call(
-        functools.partial(first_kernel, pieces=pieces, rows=rows, **sizes),
-        out_shape=[message(p) for p in range(count)],
-        in_specs=[whole(SMEM), whole(VMEM)],
-        out_specs=[whole(VMEM)] * count,
+    state_rows = NF * groups * rows * SUB
+    head = pieces[0]
+    sent = [None] * count
+    sent[0] = pl.pallas_call(
+        functools.partial(first_kernel, piece=head, rows=rows, **sizes),
+        out_shape=message(0),
+        in_specs=[whole(HBM)] * 2,
+        out_specs=whole(VMEM),
+        scratch_shapes=[
+            SMEM(send_slots.shape, jnp.int32),
+            VMEM(((head[1] - head[0]) * groups * SUB * SUB, LANES), f32),
+            pltpu.SemaphoreType.DMA((1 + (head[1] - head[0]) * groups,)),
+        ],
         compiler_params=params(),
         name="pack_first",
-    )(send_slots, rows_of_state)
-
-    tags = pl.pallas_call(
-        functools.partial(tags_kernel, occ=occ, **sizes),
-        out_shape=jax.ShapeDtypeStruct((2 * moves + occ,), jnp.int32),
-        in_specs=[whole(SMEM)] * 3,
-        out_specs=whole(SMEM),
+    )(send_there, rows_of_state)
+    rows_of_state, tags, *sent[1:] = pl.pallas_call(
+        functools.partial(load_kernel, pieces=pieces[1:], rows=rows, occ=occ, **sizes),
+        out_shape=[
+            jax.ShapeDtypeStruct((state_rows, LANES), f32),
+            jax.ShapeDtypeStruct((2 * moves + occ,), jnp.int32),
+        ]
+        + [message(p) for p in range(1, count)],
+        in_specs=[whole(SMEM)] * 3 + [whole(HBM)],
+        out_specs=[whole(VMEM), whole(SMEM)] + [whole(VMEM)] * (count - 1),
+        scratch_shapes=[SMEM((slots + SUB,), jnp.int32), pltpu.SemaphoreType.DMA],
         compiler_params=params(),
-        name="block_tags",
-    )(send_slots, recv_slots, own)
+        name="load_state",
+    )(send_slots, recv_slots, own, rows_of_state)
 
     got = [[None] * count for _ in range(3)]
 
@@ -556,34 +647,63 @@
         )(tags, rows_of_state, *arrays, *through)
         return outs[:made], outs[made:]
 
-    ahead = 2
-    for p in range(ahead):
-        got[0][p] = swapped(sent[p], 0)
-    for step in range(count + ahead):
-        wanted = []
-        if step < count:
-            wanted.append((1, step))
-        if step >= ahead:
-            wanted.append((2, step - ahead))
-        through = sent[step + ahead : step + ahead + 1]
-        made, passed = make(wanted, list(through))
+    steps = [
+        ([(1, 0)], [2], []),
+        ([(1, 1), (2, 0)], [3], []),
+        ([(1, 2)], [4], []),
+        ([(1, 3), (2, 1)], [], [0]),
+        ([(1, 4), (2, 2)], [], []),
+        ([(2, 3)], [], [1]),
+        ([(2, 4)], [], [2]),
+    ]
+    got[0][0] = swapped(sent[0], 0)
+    got[0][1] = swapped(sent[1], 0)
+    for wanted, leaving, awaited in steps:
+        through = [sent[p] for p in leaving] + [got[2][p] for p in awaited]
+        made, passed = make(wanted, through)
         for (level, p), value in zip(wanted, made):
             got[level][p] = swapped(value, level)
-        if passed:
-            got[0][step + ahead] = swapped(passed[0], 0)
+        for p, value in zip(leaving, passed):
+            got[0][p] = swapped(value, 0)
+        for p, value in zip(awaited, passed[len(leaving) :]):
+            got[2][p] = value
 
     grid = shape.grid()
-    produced = [grid, grid] + shape.faces()
-    sources = [got[level][p] for p in range(count) for level in range(3)]
-    made = pl.pallas_call(
-        functools.partial(assemble_kernel, pieces=pieces, occ=occ, shape=shape, **sizes),
-        out_shape=produced,
-        in_specs=[whole(SMEM)] + [whole(VMEM)] * (1 + len(sources)),
-        out_specs=[whole(VMEM)] * len(produced),
-        scratch_shapes=[VMEM((occ * NF * rows, LANES), f32)],
-        compiler_params=params(),
-        name="assemble",
-    )(tags, rows_of_state, *sources)
+    face_x, _, face_y, _, face_z, _ = shape.faces()
+    part = [grid, grid, face_y, face_y, face_z, face_z]
+    canvas = jax.ShapeDtypeStruct((state_rows, LANES), f32)
+    full = pieces[-1][0] // NF
+
+    def assemble(slabs, before):
+        first = not before
+        use = [p for p in range(count) if pieces[p][0] < slabs[1] * NF and pieces[p][1] > slabs[0] * NF]
+        sources = [got[level][p] for p in use for level in range(3)]
+        shapes = part + [canvas if first else face_x, face_x]
+        fixed = 2 + len(sources)
+
+        def kernel(tags, state, *refs):
+            lead = refs[: len(sources) + len(before)]
+            outs = refs[len(lead) : len(lead) + 8]
+            assemble_kernel(
+                tags, state, *lead, *outs[:7], refs[-1], outs[7],
+                pieces=[pieces[p] for p in use], slabs=slabs, occ=occ, shape=shape, first=first,
+                **sizes,
+            )
+
+        return pl.pallas_call(
+            kernel,
+            out_shape=shapes,
+            in_specs=[whole(SMEM)] + [whole(VMEM)] * (1 + len(sources)) + [whole(VMEM)] * len(before),
+            out_specs=[whole(VMEM)] * len(shapes),
+            scratch_shapes=[VMEM((occ * NF * rows, LANES), f32)],
+            input_output_aliases={fixed + i: i for i in range(len(before))},
+            compiler_params=params(),
+            name="assemble_%d" % slabs[0],
+        )(tags, rows_of_state, *sources, *before)
+
+    *made, blank, x_lo = assemble((0, full), [])
+    *made, x_lo, x_hi = assemble((full, shape.slabs), [*made, x_lo])
+    made = made[:2] + [x_lo, x_hi] + made[2:]
 
     def ring(value, axis, step):
         size = lax.axis_size(axis)
@@ -597,12 +717,13 @@
         else:
             x_prev, x_next = ring(x_hi, "gx", 1), ring(x_lo, "gx", -1)
         ghost = VMEM((NF, rows, LANES), f32)
+        work = [VMEM(grid.shape, f32)] * 3
         total = pl.pallas_call(
             functools.partial(sweep_z_kernel, shape=shape),
             out_shape=grid,
             in_specs=[whole(VMEM)] * 5,
             out_specs=whole(VMEM),
-            scratch_shapes=[ghost] * 4,
+            scratch_shapes=[ghost] * 2 + work,
             compiler_params=params(),
             name="sweep_z",
         )(prim, z_lo, z_hi, z_prev, z_next)
@@ -618,7 +739,8 @@
         )(prim, x_prev, x_next, total)
         return y_lo, y_hi, y_prev, y_next, total
 
-    packed = VMEM(shape.faces()[2].shape, f32)
+    produced = [grid, grid] + shape.faces()
+    scratch = [VMEM(face_y.shape, f32)] * 2 + [VMEM(grid.shape, f32)] * 3
     field, prim = made[0], made[1]
     sums = flux_sums(prim, *made[2:])
     made = pl.pallas_call(
@@ -626,27 +748,26 @@
         out_shape=produced,
         in_specs=[whole(VMEM)] * 7,
         out_specs=[whole(VMEM)] * len(produced),
-        scratch_shapes=[packed] * 2,
+        scratch_shapes=scratch,
         compiler_params=params(),
         name="sweep_y_one",
     )(field, prim, *sums)
     one, one_prim = made[0], made[1]
     sums = flux_sums(one_prim, *made[2:])
-    state_rows = NF * groups * rows * SUB
-    out = pl.pallas_call(
+    out, _ = pl.pallas_call(
         functools.partial(sweep_y_two_kernel, shape=shape, occ=occ, groups=groups),
-        out_shape=jax.ShapeDtypeStruct((state_rows, LANES), f32),
-        in_specs=[whole(SMEM)] + [whole(VMEM)] * 8,
-        out_specs=whole(HBM),
-        scratch_shapes=[packed] * 2
+        out_shape=[canvas, canvas],
+        in_specs=[whole(SMEM)] + [whole(VMEM)] * 9,
+        out_specs=[whole(HBM), whole(VMEM)],
+        scratch_shapes=scratch
         + [
             VMEM(grid.shape, f32),
-            VMEM((state_rows, LANES), f32),
             pltpu.SemaphoreType.DMA((shape.slabs, NF * groups)),
         ],
+        input_output_aliases={9: 1},
         compiler_params=params(),
         name="sweep_y_two",
-    )(own, field, one, one_prim, *sums)
+    )(own, field, one, one_prim, *sums, blank)
     return (
         out.reshape(NF, groups, rows, SUB, LANES)
         .transpose(1, 3, 0, 2, 4)

time: 90.5 us -> 81.4 us (0.90)
  waiting for transfers between devices: 29.9 us -> 26.4 us
  Pallas kernels: 27.6 us -> 25 us
  local copies, waits for them, and re-layouts: 2.55 us -> 0.11 us
    ppermute x15, waiting for transfers between devices: 28.8 us -> 21.8 us  [swapped(): return lax.ppermute(value, AXES, pairs)]
    pallas_call x2, Pallas kernels: 10.3 us -> 4.75 us  [flux_sums(): pl.pallas_call(functools.partial(sweep_z_kernel, shape=shape), out_shape=...]
    ppermute x15, starting transfers between devices: 17.6 us -> 22.2 us  [swapped(): return lax.ppermute(value, AXES, pairs)]
    ppermute x10, starting transfers between devices: 11.6 us -> 7.27 us  [ring(): lax.ppermute(value, axis, [(i, (i + step) % size) for i in range(size)])]
    ppermute x10, waiting for transfers between devices: 1.08 us -> 4.55 us  [ring(): lax.ppermute(value, axis, [(i, (i + step) % size) for i in range(size)])]
    pallas_call x3 -> x4, Pallas kernels: 3.84 us -> 6.43 us  [the longest x1 3.01 us: shards(): pl.pallas_call(functools.partial(load_kernel, pieces=pieces[1:], rows=row...]
    unnamed x12 -> x6, local copies, waits for them, and re-layouts: 2.45 us -> 0.01 us
  transfers between devices with their start and end apart: 25 -> 25, of which waited for: 8 -> 12; matrix products, arithmetic and copies ran while one was open for 0% -> 0% of each run, Pallas kernels for 21% -> 19%
where the time goes in v1:
time: 81.4 us; the launch traced here: 81.2 us
  starting transfers between devices  29.5 us (36%)
  waiting for transfers between devices  26.4 us (32%)
  Pallas kernels  25 us (31%)
    ppermute x15, starting transfers between devices, swapped(): return lax.ppermute(value, AXES, pairs)  22.2 us
    ppermute x15, waiting for transfers between devices, swapped(): return lax.ppermute(value, AXES, pairs)  21.8 us
    ppermute x10, starting transfers between devices, ring(): lax.ppermute(value, axis, [(i, (i + step) % size) for i in range(size)])  7.27 us
    pallas_call x2, Pallas kernels, flux_sums(): pl.pallas_call(functools.partial(sweep_z_kernel, shape=shape), out_shape=...  4.75 us
    pallas_call x7, Pallas kernels, make(): pl.pallas_call(functools.partial(pick_kernel, plan=tuple(plan), given=giv...  4.67 us
    pallas_call x1, Pallas kernels, shards(): pl.pallas_call(functools.partial(sweep_y_two_kernel, shape=shape, occ=occ...  4.62 us
    ppermute x10, waiting for transfers between devices, ring(): lax.ppermute(value, axis, [(i, (i + step) % size) for i in range(size)])  4.55 us
    pallas_call x1, Pallas kernels, shards(): pl.pallas_call(functools.partial(load_kernel, pieces=pieces[1:], rows=row...  3.01 us
  transfers between devices with their start and end apart: 25, of which 12 were waited for; matrix products, arithmetic and copies ran while one was open for 0% of the time, Pallas kernels for 19%

profile of v1, /device:TPU:0, one launch (start us, length us, event | category | flops | bytes accessed | tf_op | source)
XLA Modules:
  0.0 81.2 jit_solution(10622054854657208212)
XLA Ops:
  0.0 1.0 %pack_first.1 = f32[8,16,128]{2,1,0:T(8,128)S(1)} custom-call(s32[3,1,8]{2,1,0:T(1,128)} %send_hbm.1, f32[5120,128]{1,0:T(8,128)} %bitcast.26), custom_call_target="tpu_custom_call" | custom-call | tf_op jit(solution)/shard_map/pack_first/pallas_call | solution.py:598
  1.0 3.0 %collective-permute-start.1 = (f32[8,16,128]{2,1,0:T(8,128)S(1)}, f32[8,16,128]{2,1,0:T(8,128)S(1)}, u32[]{:S(2)}, u32[]{:S(2)}) collective-permute-start(f32[8,16,128]{2,1,0:T(8,128)S(1)} %pack_first.1), channel_id=1, source_target_pairs={{0,16},{1,17},{2,18},{3,19},{4,20},{5,21},{6,22},{7,23},{8,24},{9,... | collective-permute-start | bytes 196616 | tf_op jit(solution)/shard_map/ppermute | solution.py:578
  4.1 0.1 dynamic_slice.3.own
  4.1 3.0 %load_state.1 = (f32[5120,128]{1,0:T(8,128)S(1)}, s32[24]{0:T(128)S(1)}, f32[8,32,128]{2,1,0:T(8,128)S(1)}, f32[8,40,128]{2,1,0:T(8,128)S(1)}, f32[8,48,128]{2,1,0:T(8,128)S(1)}, /*index=5*/f32[8,24,128]{2,1,0:T(8,128)S(1)}) custom-call(s32[3,1,8]{2,1,0:T(1,128)S(1)} %copy-done, s32[3,1,8]{2,1,0:T(1,128)S(1)} %copy-done.1, s32[8]{0:T(128)S(1)} %dynamic_slice.3.own, ...), custom_call_target="tpu_custom_call" | custom-call | tf_op jit(solution)/shard_map/load_state/pallas_call | solution.py:611
  7.2 0.1 collective-permute-start
  7.3 0.0 collective-permute-done.1.refs_0_.refs_1_
  7.3 0.6 pick_10.1
  7.9 3.1 %collective-permute-start.2 = (f32[8,16,128]{2,1,0:T(8,128)S(1)}, f32[8,16,128]{2,1,0:T(8,128)S(1)}, u32[]{:S(2)}, u32[]{:S(2)}) collective-permute-start(f32[8,16,128]{2,1,0:T(8,128)S(1)} %get-tuple-element.56), channel_id=1, source_target_pairs={{0,8},{1,9},{2,10},{3,11},{4,12},{5,13},{6,14},{7,15},{8,0},{9,1},... | collective-permute-start | bytes 196616 | tf_op jit(solution)/shard_map/ppermute | solution.py:578
  11.0 1.2 %collective-permute-done.refs_0_.refs_1_.refs_3_ = f32[8,32,128]{2,1,0:T(8,128)S(1)} collective-permute-done((f32[8,32,128]{2,1,0:T(8,128)S(1)}, f32[8,32,128]{2,1,0:T(8,128)S(1)}, u32[]{:S(2)}, u32[]{:S(2)}) %collective-permute-start) | collective-permute-done | bytes 131104 | tf_op jit(solution)/shard_map/ppermute | solution.py:578
  12.2 1.4 %collective-permute-done.2.refs_2_.refs_1_ = f32[8,16,128]{2,1,0:T(8,128)S(1)} collective-permute-done((f32[8,16,128]{2,1,0:T(8,128)S(1)}, f32[8,16,128]{2,1,0:T(8,128)S(1)}, u32[]{:S(2)}, u32[]{:S(2)}) %collective-permute-start.2) | collective-permute-done | bytes 65568 | tf_op jit(solution)/shard_map/ppermute | solution.py:578
  13.6 0.7 pick_11_20.1
  14.3 1.6 %collective-permute-start.3 = (f32[8,48,128]{2,1,0:T(8,128)S(1)}, f32[8,48,128]{2,1,0:T(8,128)S(1)}, u32[]{:S(2)}, u32[]{:S(2)}) collective-permute-start(f32[8,48,128]{2,1,0:T(8,128)S(1)} %get-tuple-element.58), channel_id=1, source_target_pairs={{0,16},{1,17},{2,18},{3,19},{4,20},{5,21},{6,22},{7,23},{8,24},{9,... | collective-permute-start | bytes 589832 | tf_op jit(solution)/shard_map/ppermute | solution.py:578
  15.9 0.5 collective-permute-start.9
  16.4 2.6 %collective-permute-start.4 = (f32[8,32,128]{2,1,0:T(8,128)S(1)}, f32[8,32,128]{2,1,0:T(8,128)S(1)}, u32[]{:S(2)}, u32[]{:S(2)}) collective-permute-start(f32[8,32,128]{2,1,0:T(8,128)S(1)} %get-tuple-element.59), channel_id=1, source_target_pairs={{0,8},{1,9},{2,10},{3,11},{4,12},{5,13},{6,14},{7,15},{8,0},{9,1},... | collective-permute-start | bytes 393224 | tf_op jit(solution)/shard_map/ppermute | solution.py:578
  19.1 1.5 %collective-permute-start.5 = (f32[8,16,128]{2,1,0:T(8,128)S(1)}, f32[8,16,128]{2,1,0:T(8,128)S(1)}, u32[]{:S(2)}, u32[]{:S(2)}) collective-permute-start(f32[8,16,128]{2,1,0:T(8,128)S(1)} %get-tuple-element.60), channel_id=1, source_target_pairs={{0,2},{1,3},{2,0},{3,1},{4,6},{5,7},{6,4},{7,5},{8,10},{9,11},{10,... | collective-permute-start | bytes 196616 | tf_op jit(solution)/shard_map/ppermute | solution.py:578
  20.5 2.2 %collective-permute-done.9.refs_0_.refs_1_.refs_6_ = f32[8,40,128]{2,1,0:T(8,128)S(1)} collective-permute-done((f32[8,40,128]{2,1,0:T(8,128)S(1)}, f32[8,40,128]{2,1,0:T(8,128)S(1)}, u32[]{:S(2)}, u32[]{:S(2)}) %collective-permute-start.9) | collective-permute-done | bytes 163872 | tf_op jit(solution)/shard_map/ppermute | solution.py:578
  22.8 0.6 pick_12.1
  23.4 2.8 %collective-permute-start.11 = (f32[8,40,128]{2,1,0:T(8,128)S(1)}, f32[8,40,128]{2,1,0:T(8,128)S(1)}, u32[]{:S(2)}, u32[]{:S(2)}) collective-permute-start(f32[8,40,128]{2,1,0:T(8,128)S(1)} %get-tuple-element.67), channel_id=1, source_target_pairs={{0,8},{1,9},{2,10},{3,11},{4,12},{5,13},{6,14},{7,15},{8,0},{9,1},... | collective-permute-start | bytes 491528 | tf_op jit(solution)/shard_map/ppermute | solution.py:578
  26.2 0.0 collective-permute-done.5.refs_3_
  26.2 0.0 collective-permute-done.4.refs_2_.refs_4_
  26.2 0.0 collective-permute-done.3.refs_0_.refs_9_
  26.2 0.7 pick_13_21.1
  26.9 0.3 collective-permute-start.6
  27.2 1.6 %collective-permute-start.10 = (f32[8,24,128]{2,1,0:T(8,128)S(1)}, f32[8,24,128]{2,1,0:T(8,128)S(1)}, u32[]{:S(2)}, u32[]{:S(2)}) collective-permute-start(f32[8,24,128]{2,1,0:T(8,128)S(1)} %get-tuple-element.66), channel_id=1, source_target_pairs={{0,16},{1,17},{2,18},{3,19},{4,20},{5,21},{6,22},{7,23},{8,24},{9,... | collective-permute-start | bytes 294920 | tf_op jit(solution)/shard_map/ppermute | solution.py:578
  28.8 1.5 %collective-permute-start.7 = (f32[8,32,128]{2,1,0:T(8,128)S(1)}, f32[8,32,128]{2,1,0:T(8,128)S(1)}, u32[]{:S(2)}, u32[]{:S(2)}) collective-permute-start(f32[8,32,128]{2,1,0:T(8,128)S(1)} %get-tuple-element.62), channel_id=1, source_target_pairs={{0,2},{1,3},{2,0},{3,1},{4,6},{5,7},{6,4},{7,5},{8,10},{9,11},{10,... | collective-permute-start | bytes 393224 | tf_op jit(solution)/shard_map/ppermute | solution.py:578
  30.3 1.5 %collective-permute-done.10.refs_0_.refs_3_ = f32[8,24,128]{2,1,0:T(8,128)S(1)} collective-permute-done((f32[8,24,128]{2,1,0:T(8,128)S(1)}, f32[8,24,128]{2,1,0:T(8,128)S(1)}, u32[]{:S(2)}, u32[]{:S(2)}) %collective-permute-start.10) | collective-permute-done | bytes 98336 | tf_op jit(solution)/shard_map/ppermute | solution.py:578
  31.8 5.7 %collective-permute-done.11.refs_2_.refs_7_ = f32[8,40,128]{2,1,0:T(8,128)S(1)} collective-permute-done((f32[8,40,128]{2,1,0:T(8,128)S(1)}, f32[8,40,128]{2,1,0:T(8,128)S(1)}, u32[]{:S(2)}, u32[]{:S(2)}) %collective-permute-start.11) | collective-permute-done | bytes 163872 | tf_op jit(solution)/shard_map/ppermute | solution.py:578
  37.5 0.7 pick_14_22.1
  38.2 1.6 %collective-permute-start.13 = (f32[8,40,128]{2,1,0:T(8,128)S(1)}, f32[8,40,128]{2,1,0:T(8,128)S(1)}, u32[]{:S(2)}, u32[]{:S(2)}) collective-permute-start(f32[8,40,128]{2,1,0:T(8,128)S(1)} %get-tuple-element.69), channel_id=1, source_target_pairs={{0,2},{1,3},{2,0},{3,1},{4,6},{5,7},{6,4},{7,5},{8,10},{9,11},{10,... | collective-permute-start | bytes 491528 | tf_op jit(solution)/shard_map/ppermute | solution.py:578
  39.8 0.0 collective-permute-done.7.refs_2_
  39.8 0.6 pick_23.1
  40.5 1.4 %collective-permute-start.8 = (f32[8,48,128]{2,1,0:T(8,128)S(1)}, f32[8,48,128]{2,1,0:T(8,128)S(1)}, u32[]{:S(2)}, u32[]{:S(2)}) collective-permute-start(f32[8,48,128]{2,1,0:T(8,128)S(1)} %get-tuple-element.63), channel_id=1, source_target_pairs={{0,2},{1,3},{2,0},{3,1},{4,6},{5,7},{6,4},{7,5},{8,10},{9,11},{10,... | collective-permute-start | bytes 589832 | tf_op jit(solution)/shard_map/ppermute | solution.py:578
  41.9 0.0 collective-permute-start.12
  41.9 7.3 %collective-permute-done.12.refs_1_.refs_4_ = f32[8,24,128]{2,1,0:T(8,128)S(1)} collective-permute-done((f32[8,24,128]{2,1,0:T(8,128)S(1)}, f32[8,24,128]{2,1,0:T(8,128)S(1)}, u32[]{:S(2)}, u32[]{:S(2)}) %collective-permute-start.12) | collective-permute-done | bytes 98336 | tf_op jit(solution)/shard_map/ppermute | solution.py:578
  49.2 0.0 collective-permute-done.13.refs_2_
  49.2 0.6 pick_24.1
  49.8 0.6 collective-permute-start.14
  50.4 1.6 %assemble_0.1 = (f32[1296,128]{1,0:T(8,128)S(1)}, f32[1296,128]{1,0:T(8,128)S(1)}, f32[5,4,8,128]{3,2,1,0:T(8,128)S(1)}, f32[5,4,8,128]{3,2,1,0:T(8,128)S(1)}, f...) custom-call(s32[24]{0:T(128)S(1)} %get-tuple-element.52.tags, ...), custom_call_target="tpu_custom_call" | custom-call | tf_op jit(solution)/shard_map/assemble_0/pallas_call | solution.py:693
  52.0 2.5 %collective-permute-done.14.refs_5_ = f32[8,24,128]{2,1,0:T(8,128)S(1)} collective-permute-done((f32[8,24,128]{2,1,0:T(8,128)S(1)}, f32[8,24,128]{2,1,0:T(8,128)S(1)}, u32[]{:S(2)}, u32[]{:S(2)}) %collective-permute-start.14) | collective-permute-done | bytes 98336 | tf_op jit(solution)/shard_map/ppermute | solution.py:578
  54.5 0.9 %assemble_3.1 = (f32[1296,128]{1,0:T(8,128)S(1)}, f32[1296,128]{1,0:T(8,128)S(1)}, f32[5,4,8,128]{3,2,1,0:T(8,128)S(1)}, f32[5,4,8,128]{3,2,1,0:T(8,128)S(1)}, f...) custom-call(s32[24]{0:T(128)S(1)} %get-tuple-element.52.tags, ...), custom_call_target="tpu_custom_call", output_to_operand_aliasing={{0}: (8, {}), {1}: (9, {}), {2}: (10, {}), {3}: (11, {}), {... | custom-call | tf_op jit(solution)/shard_map/assemble_3/pallas_call | solution.py:693
  55.4 1.6 %collective-permute-start.17 = (f32[2,5,4,8,128]{4,3,2,1,0:T(8,128)S(1)}, f32[2,5,4,8,128]{4,3,2,1,0:T(8,128)S(1)}, u32[]{:S(2)}, u32[]{:S(2)}) collective-permute-start(f32[2,5,4,8,128]{4,3,2,1,0:T(8,128)S(1)} %pad_maximum_fusion), channel_id=1, source_target_pairs={{0,16},{16,0},{1,17},{17,1},{2,18},{18,2},{3,19},{19,3},{4,20},{20... | collective-permute-start | bytes 491528 | tf_op jit(solution)/shard_map/ppermute | solution.py:710
  57.0 0.0 collective-permute-start.19
  57.0 0.5 collective-permute-start.18
  57.5 1.8 %collective-permute-start.16 = (f32[5,4,8,128]{3,2,1,0:T(8,128)S(1)}, f32[5,4,8,128]{3,2,1,0:T(8,128)S(1)}, u32[]{:S(2)}, u32[]{:S(2)}) collective-permute-start(f32[5,4,8,128]{3,2,1,0:T(8,128)S(1)} %get-tuple-element.83.y_lo), channel_id=1, source_target_pairs={{0,12},{4,0},{8,4},{12,8},{1,13},{5,1},{9,5},{13,9},{2,14},{6,2},{... | collective-permute-start | bytes 245768 | tf_op jit(solution)/shard_map/ppermute | solution.py:710
  59.2 0.3 collective-permute-start.15
  59.5 0.3 collective-permute-done.19.z_next
  59.8 1.0 %collective-permute-done.18.z_prev = f32[5,32,128]{2,1,0:T(8,128)S(1)} collective-permute-done((f32[5,32,128]{2,1,0:T(8,128)S(1)}, f32[5,32,128]{2,1,0:T(8,128)S(1)}, u32[]{:S(2)}, u32[]{:S(2)}) %collective-permute-start.18) | collective-permute-done | bytes 81952 | tf_op jit(solution)/shard_map/ppermute | solution.py:710
  60.8 2.4 %sweep_z.2.sofar = f32[1296,128]{1,0:T(8,128)S(1)} custom-call(f32[1296,128]{1,0:T(8,128)S(1)} %get-tuple-element.82.prim, f32[5,32,128]{2,1,0:T(8,128)S(1)} %get-tuple-element.87.z_lo, f32[5,32,128]{2,1,0:T(8,128)S(1)} %get-tuple-element.88.z_hi, f32[5,32,128]{2,1,0:T(8,128)S(1)} %collective-permute-done.18.z_prev, ...), custom_call_target="tpu_custom_call" | custom-call | tf_op jit(solution)/shard_map/sweep_z/pallas_call | solution.py:721
  63.2 0.0 collective-permute-done.17
  63.2 1.0 %sweep_x.2.sofar = f32[1296,128]{1,0:T(8,128)S(1)} custom-call(f32[1296,128]{1,0:T(8,128)S(1)} %get-tuple-element.82.prim, f32[5,4,8,128]{3,2,1,0:T(8,128)S(1)} %get-tuple-element.102.x_prev, f32[5,4,8,128]{3,2,1,0:T(8,128)S(1)} %get-tuple-element.101.x_next, f32[1296,128]{1,0:T(8,128)S(1)} %sweep_z.2.sofar), custom_call_target="tpu_custom_call", output_to_operand_aliasing={{}: (3, {})} | custom-call | tf_op jit(solution)/shard_map/sweep_x/pallas_call | solution.py:730
  64.2 1.2 %collective-permute-done.15.y_prev = f32[5,4,8,128]{3,2,1,0:T(8,128)S(1)} collective-permute-done((f32[5,4,8,128]{3,2,1,0:T(8,128)S(1)}, f32[5,4,8,128]{3,2,1,0:T(8,128)S(1)}, u32[]{:S(2)}, u32[]{:S(2)}) %collective-permute-start.15) | collective-permute-done | bytes 81952 | tf_op jit(solution)/shard_map/ppermute | solution.py:710
  65.5 2.5 %sweep_y_one.1 = (f32[1296,128]{1,0:T(8,128)S(1)}, f32[1296,128]{1,0:T(8,128)S(1)}, f32[5,4,8,128]{3,2,1,0:T(8,128)S(1)}, f32[5,4,8,128]{3,2,1,0:T(8,128)S(1)}, ...) custom-call(f32[1296,128]{1,0:T(8,128)S(1)} %get-tuple-element.81.fi, ...), custom_call_target="tpu_custom_call" | custom-call | tf_op jit(solution)/shard_map/sweep_y_one/pallas_call | solution.py:746
  68.0 0.6 collective-permute-start.22
  68.6 0.5 collective-permute-start.24
  69.2 0.0 collective-permute-start.23
  69.2 1.0 %collective-permute-start.21 = (f32[5,4,8,128]{3,2,1,0:T(8,128)S(1)}, f32[5,4,8,128]{3,2,1,0:T(8,128)S(1)}, u32[]{:S(2)}, u32[]{:S(2)}) collective-permute-start(f32[5,4,8,128]{3,2,1,0:T(8,128)S(1)} %get-tuple-element.91.y_lo), channel_id=1, source_target_pairs={{0,12},{4,0},{8,4},{12,8},{1,13},{5,1},{9,5},{13,9},{2,14},{6,2},{... | collective-permute-start | bytes 245768 | tf_op jit(solution)/shard_map/ppermute | solution.py:710
  70.1 1.0 %collective-permute-start.20 = (f32[5,4,8,128]{3,2,1,0:T(8,128)S(1)}, f32[5,4,8,128]{3,2,1,0:T(8,128)S(1)}, u32[]{:S(2)}, u32[]{:S(2)}) collective-permute-start(f32[5,4,8,128]{3,2,1,0:T(8,128)S(1)} %get-tuple-element.92.y_hi), channel_id=1, source_target_pairs={{0,4},{4,8},{8,12},{12,0},{1,5},{5,9},{9,13},{13,1},{2,6},{6,10},{... | collective-permute-start | bytes 245768 | tf_op jit(solution)/shard_map/ppermute | solution.py:710
  71.2 0.7 collective-permute-done.24.z_next
  71.8 1.3 %collective-permute-done.23.z_prev = f32[5,32,128]{2,1,0:T(8,128)S(1)} collective-permute-done((f32[5,32,128]{2,1,0:T(8,128)S(1)}, f32[5,32,128]{2,1,0:T(8,128)S(1)}, u32[]{:S(2)}, u32[]{:S(2)}) %collective-permute-start.23) | collective-permute-done | bytes 81952 | tf_op jit(solution)/shard_map/ppermute | solution.py:710
  73.2 2.4 %sweep_z.3.sofar = f32[1296,128]{1,0:T(8,128)S(1)} custom-call(f32[1296,128]{1,0:T(8,128)S(1)} %get-tuple-element.90.prim, f32[5,32,128]{2,1,0:T(8,128)S(1)} %get-tuple-element.95.z_lo, f32[5,32,128]{2,1,0:T(8,128)S(1)} %get-tuple-element.96.z_hi, f32[5,32,128]{2,1,0:T(8,128)S(1)} %collective-permute-done.23.z_prev, ...), custom_call_target="tpu_custom_call" | custom-call | tf_op jit(solution)/shard_map/sweep_z/pallas_call | solution.py:721
  75.5 0.0 collective-permute-done.22
  75.6 1.0 %sweep_x.3.sofar = f32[1296,128]{1,0:T(8,128)S(1)} custom-call(f32[1296,128]{1,0:T(8,128)S(1)} %get-tuple-element.90.prim, f32[5,4,8,128]{3,2,1,0:T(8,128)S(1)} %get-tuple-element.100.x_prev, f32[5,4,8,128]{3,2,1,0:T(8,128)S(1)} %get-tuple-element.99.x_next, f32[1296,128]{1,0:T(8,128)S(1)} %sweep_z.3.sofar), custom_call_target="tpu_custom_call", output_to_operand_aliasing={{}: (3, {})} | custom-call | tf_op jit(solution)/shard_map/sweep_x/pallas_call | solution.py:730
  76.6 0.0 collective-permute-done.21.y_next
  76.6 4.6 %sweep_y_two.1 = (f32[5120,128]{1,0:T(8,128)}, f32[5120,128]{1,0:T(8,128)S(1)}) custom-call(s32[8]{0:T(128)S(1)} %dynamic_slice.3.own, f32[1296,128]{1,0:T(8,128)S(1)} %get-tuple-element.81.field, f32[1296,128]{1,0:T(8,128)S(1)} %get-tuple-element.89.one, f32[1296,128]{1,0:T(8,128)S(1)} %get-tuple-element.90.prim, ...), custom_call_target="tpu_custom_call", output_to_operand_aliasing={{1}: (9, {})} | custom-call | tf_op jit(solution)/shard_map/sweep_y_two/pallas_call | solution.py:757
  (14 shorter events, 0.1 us)
Async XLA Ops:
  0.0 4.1 %copy-start = (s32[3,1,8]{2,1,0:T(1,128)S(1)}, s32[3,1,8]{2,1,0:T(1,128)}, u32[]{:S(2)}) copy-start(s32[3,1,8]{2,1,0:T(1,128)} %send_hbm.1) | copy-start | bytes 292
  0.0 4.1 %copy-start.2 = (s32[256]{0:T(256)S(1)}, s32[256]{0:T(256)}, u32[]{:S(2)}) copy-start(s32[256]{0:T(256)} %param.7) | copy-start | bytes 3076
  0.0 4.1 %copy-start.1 = (s32[3,1,8]{2,1,0:T(1,128)S(1)}, s32[3,1,8]{2,1,0:T(1,128)}, u32[]{:S(2)}) copy-start(s32[3,1,8]{2,1,0:T(1,128)} %recv.1) | copy-start | bytes 292
  1.0 6.2 %collective-permute-start.1 = (f32[8,16,128]{2,1,0:T(8,128)S(1)}, f32[8,16,128]{2,1,0:T(8,128)S(1)}, u32[]{:S(2)}, u32[]{:S(2)}) collective-permute-start(f32[8,16,128]{2,1,0:T(8,128)S(1)} %pack_first.1), channel_id=1, source_target_pairs={{0,16},{1,17},{2,18},{3,19},{4,20},{5,21},{6,22},{7,23},{8,24},{9,... | collective-permute-start | bytes 196616 | tf_op jit(solution)/shard_map/ppermute | solution.py:578
  7.2 5.0 %collective-permute-start = (f32[8,32,128]{2,1,0:T(8,128)S(1)}, f32[8,32,128]{2,1,0:T(8,128)S(1)}, u32[]{:S(2)}, u32[]{:S(2)}) collective-permute-start(f32[8,32,128]{2,1,0:T(8,128)S(1)} %get-tuple-element.54), channel_id=1, source_target_pairs={{0,16},{1,17},{2,18},{3,19},{4,20},{5,21},{6,22},{7,23},{8,24},{9,... | collective-permute-start | bytes 393224 | tf_op jit(solution)/shard_map/ppermute | solution.py:578
  7.9 5.7 %collective-permute-start.2 = (f32[8,16,128]{2,1,0:T(8,128)S(1)}, f32[8,16,128]{2,1,0:T(8,128)S(1)}, u32[]{:S(2)}, u32[]{:S(2)}) collective-permute-start(f32[8,16,128]{2,1,0:T(8,128)S(1)} %get-tuple-element.56), channel_id=1, source_target_pairs={{0,8},{1,9},{2,10},{3,11},{4,12},{5,13},{6,14},{7,15},{8,0},{9,1},... | collective-permute-start | bytes 196616 | tf_op jit(solution)/shard_map/ppermute | solution.py:578
  14.3 11.8 %collective-permute-start.3 = (f32[8,48,128]{2,1,0:T(8,128)S(1)}, f32[8,48,128]{2,1,0:T(8,128)S(1)}, u32[]{:S(2)}, u32[]{:S(2)}) collective-permute-start(f32[8,48,128]{2,1,0:T(8,128)S(1)} %get-tuple-element.58), channel_id=1, source_target_pairs={{0,16},{1,17},{2,18},{3,19},{4,20},{5,21},{6,22},{7,23},{8,24},{9,... | collective-permute-start | bytes 589832 | tf_op jit(solution)/shard_map/ppermute | solution.py:578
  15.9 6.9 %collective-permute-start.9 = (f32[8,40,128]{2,1,0:T(8,128)S(1)}, f32[8,40,128]{2,1,0:T(8,128)S(1)}, u32[]{:S(2)}, u32[]{:S(2)}) collective-permute-start(f32[8,40,128]{2,1,0:T(8,128)S(1)} %get-tuple-element.64), channel_id=1, source_target_pairs={{0,16},{1,17},{2,18},{3,19},{4,20},{5,21},{6,22},{7,23},{8,24},{9,... | collective-permute-start | bytes 491528 | tf_op jit(solution)/shard_map/ppermute | solution.py:578
  16.4 9.7 %collective-permute-start.4 = (f32[8,32,128]{2,1,0:T(8,128)S(1)}, f32[8,32,128]{2,1,0:T(8,128)S(1)}, u32[]{:S(2)}, u32[]{:S(2)}) collective-permute-start(f32[8,32,128]{2,1,0:T(8,128)S(1)} %get-tuple-element.59), channel_id=1, source_target_pairs={{0,8},{1,9},{2,10},{3,11},{4,12},{5,13},{6,14},{7,15},{8,0},{9,1},... | collective-permute-start | bytes 393224 | tf_op jit(solution)/shard_map/ppermute | solution.py:578
  19.1 7.1 %collective-permute-start.5 = (f32[8,16,128]{2,1,0:T(8,128)S(1)}, f32[8,16,128]{2,1,0:T(8,128)S(1)}, u32[]{:S(2)}, u32[]{:S(2)}) collective-permute-start(f32[8,16,128]{2,1,0:T(8,128)S(1)} %get-tuple-element.60), channel_id=1, source_target_pairs={{0,2},{1,3},{2,0},{3,1},{4,6},{5,7},{6,4},{7,5},{8,10},{9,11},{10,... | collective-permute-start | bytes 196616 | tf_op jit(solution)/shard_map/ppermute | solution.py:578
  23.4 14.1 %collective-permute-start.11 = (f32[8,40,128]{2,1,0:T(8,128)S(1)}, f32[8,40,128]{2,1,0:T(8,128)S(1)}, u32[]{:S(2)}, u32[]{:S(2)}) collective-permute-start(f32[8,40,128]{2,1,0:T(8,128)S(1)} %get-tuple-element.67), channel_id=1, source_target_pairs={{0,8},{1,9},{2,10},{3,11},{4,12},{5,13},{6,14},{7,15},{8,0},{9,1},... | collective-permute-start | bytes 491528 | tf_op jit(solution)/shard_map/ppermute | solution.py:578
  26.9 12.9 %collective-permute-start.6 = (f32[8,48,128]{2,1,0:T(8,128)S(1)}, f32[8,48,128]{2,1,0:T(8,128)S(1)}, u32[]{:S(2)}, u32[]{:S(2)}) collective-permute-start(f32[8,48,128]{2,1,0:T(8,128)S(1)} %get-tuple-element.61), channel_id=1, source_target_pairs={{0,8},{1,9},{2,10},{3,11},{4,12},{5,13},{6,14},{7,15},{8,0},{9,1},... | collective-permute-start | bytes 589832 | tf_op jit(solution)/shard_map/ppermute | solution.py:578
  27.2 4.6 %collective-permute-start.10 = (f32[8,24,128]{2,1,0:T(8,128)S(1)}, f32[8,24,128]{2,1,0:T(8,128)S(1)}, u32[]{:S(2)}, u32[]{:S(2)}) collective-permute-start(f32[8,24,128]{2,1,0:T(8,128)S(1)} %get-tuple-element.66), channel_id=1, source_target_pairs={{0,16},{1,17},{2,18},{3,19},{4,20},{5,21},{6,22},{7,23},{8,24},{9,... | collective-permute-start | bytes 294920 | tf_op jit(solution)/shard_map/ppermute | solution.py:578
  28.8 11.0 %collective-permute-start.7 = (f32[8,32,128]{2,1,0:T(8,128)S(1)}, f32[8,32,128]{2,1,0:T(8,128)S(1)}, u32[]{:S(2)}, u32[]{:S(2)}) collective-permute-start(f32[8,32,128]{2,1,0:T(8,128)S(1)} %get-tuple-element.62), channel_id=1, source_target_pairs={{0,2},{1,3},{2,0},{3,1},{4,6},{5,7},{6,4},{7,5},{8,10},{9,11},{10,... | collective-permute-start | bytes 393224 | tf_op jit(solution)/shard_map/ppermute | solution.py:578
  38.2 11.0 %collective-permute-start.13 = (f32[8,40,128]{2,1,0:T(8,128)S(1)}, f32[8,40,128]{2,1,0:T(8,128)S(1)}, u32[]{:S(2)}, u32[]{:S(2)}) collective-permute-start(f32[8,40,128]{2,1,0:T(8,128)S(1)} %get-tuple-element.69), channel_id=1, source_target_pairs={{0,2},{1,3},{2,0},{3,1},{4,6},{5,7},{6,4},{7,5},{8,10},{9,11},{10,... | collective-permute-start | bytes 491528 | tf_op jit(solution)/shard_map/ppermute | solution.py:578
  40.5 9.9 %collective-permute-start.8 = (f32[8,48,128]{2,1,0:T(8,128)S(1)}, f32[8,48,128]{2,1,0:T(8,128)S(1)}, u32[]{:S(2)}, u32[]{:S(2)}) collective-permute-start(f32[8,48,128]{2,1,0:T(8,128)S(1)} %get-tuple-element.63), channel_id=1, source_target_pairs={{0,2},{1,3},{2,0},{3,1},{4,6},{5,7},{6,4},{7,5},{8,10},{9,11},{10,... | collective-permute-start | bytes 589832 | tf_op jit(solution)/shard_map/ppermute | solution.py:578
  41.9 7.3 %collective-permute-start.12 = (f32[8,24,128]{2,1,0:T(8,128)S(1)}, f32[8,24,128]{2,1,0:T(8,128)S(1)}, u32[]{:S(2)}, u32[]{:S(2)}) collective-permute-start(f32[8,24,128]{2,1,0:T(8,128)S(1)} %get-tuple-element.68), channel_id=1, source_target_pairs={{0,8},{1,9},{2,10},{3,11},{4,12},{5,13},{6,14},{7,15},{8,0},{9,1},... | collective-permute-start | bytes 294920 | tf_op jit(solution)/shard_map/ppermute | solution.py:578
  49.8 4.7 %collective-permute-start.14 = (f32[8,24,128]{2,1,0:T(8,128)S(1)}, f32[8,24,128]{2,1,0:T(8,128)S(1)}, u32[]{:S(2)}, u32[]{:S(2)}) collective-permute-start(f32[8,24,128]{2,1,0:T(8,128)S(1)} %get-tuple-element.70), channel_id=1, source_target_pairs={{0,2},{1,3},{2,0},{3,1},{4,6},{5,7},{6,4},{7,5},{8,10},{9,11},{10,... | collective-permute-start | bytes 294920 | tf_op jit(solution)/shard_map/ppermute | solution.py:578
  55.4 7.8 %collective-permute-start.17 = (f32[2,5,4,8,128]{4,3,2,1,0:T(8,128)S(1)}, f32[2,5,4,8,128]{4,3,2,1,0:T(8,128)S(1)}, u32[]{:S(2)}, u32[]{:S(2)}) collective-permute-start(f32[2,5,4,8,128]{4,3,2,1,0:T(8,128)S(1)} %pad_maximum_fusion), channel_id=1, source_target_pairs={{0,16},{16,0},{1,17},{17,1},{2,18},{18,2},{3,19},{19,3},{4,20},{20... | collective-permute-start | bytes 491528 | tf_op jit(solution)/shard_map/ppermute | solution.py:710
  57.0 2.8 %collective-permute-start.19 = (f32[5,32,128]{2,1,0:T(8,128)S(1)}, f32[5,32,128]{2,1,0:T(8,128)S(1)}, u32[]{:S(2)}, u32[]{:S(2)}) collective-permute-start(f32[5,32,128]{2,1,0:T(8,128)S(1)} %get-tuple-element.87.z_lo), channel_id=1, source_target_pairs={{0,3},{1,0},{2,1},{3,2},{4,7},{5,4},{6,5},{7,6},{8,11},{9,8},{10,9... | collective-permute-start | bytes 245768 | tf_op jit(solution)/shard_map/ppermute | solution.py:710
  57.0 3.9 %collective-permute-start.18 = (f32[5,32,128]{2,1,0:T(8,128)S(1)}, f32[5,32,128]{2,1,0:T(8,128)S(1)}, u32[]{:S(2)}, u32[]{:S(2)}) collective-permute-start(f32[5,32,128]{2,1,0:T(8,128)S(1)} %get-tuple-element.88.z_hi), channel_id=1, source_target_pairs={{0,1},{1,2},{2,3},{3,0},{4,5},{5,6},{6,7},{7,4},{8,9},{9,10},{10,1... | collective-permute-start | bytes 245768 | tf_op jit(solution)/shard_map/ppermute | solution.py:710
  57.5 6.8 %collective-permute-start.16 = (f32[5,4,8,128]{3,2,1,0:T(8,128)S(1)}, f32[5,4,8,128]{3,2,1,0:T(8,128)S(1)}, u32[]{:S(2)}, u32[]{:S(2)}) collective-permute-start(f32[5,4,8,128]{3,2,1,0:T(8,128)S(1)} %get-tuple-element.83.y_lo), channel_id=1, source_target_pairs={{0,12},{4,0},{8,4},{12,8},{1,13},{5,1},{9,5},{13,9},{2,14},{6,2},{... | collective-permute-start | bytes 245768 | tf_op jit(solution)/shard_map/ppermute | solution.py:710
  59.2 6.2 %collective-permute-start.15 = (f32[5,4,8,128]{3,2,1,0:T(8,128)S(1)}, f32[5,4,8,128]{3,2,1,0:T(8,128)S(1)}, u32[]{:S(2)}, u32[]{:S(2)}) collective-permute-start(f32[5,4,8,128]{3,2,1,0:T(8,128)S(1)} %get-tuple-element.84.y_hi), channel_id=1, source_target_pairs={{0,4},{4,8},{8,12},{12,0},{1,5},{5,9},{9,13},{13,1},{2,6},{6,10},{... | collective-permute-start | bytes 245768 | tf_op jit(solution)/shard_map/ppermute | solution.py:710
  68.0 7.5 %collective-permute-start.22 = (f32[2,5,4,8,128]{4,3,2,1,0:T(8,128)S(1)}, f32[2,5,4,8,128]{4,3,2,1,0:T(8,128)S(1)}, u32[]{:S(2)}, u32[]{:S(2)}) collective-permute-start(f32[2,5,4,8,128]{4,3,2,1,0:T(8,128)S(1)} %pad_maximum_fusion.1), channel_id=1, source_target_pairs={{0,16},{16,0},{1,17},{17,1},{2,18},{18,2},{3,19},{19,3},{4,20},{20... | collective-permute-start | bytes 491528 | tf_op jit(solution)/shard_map/ppermute | solution.py:710
  68.6 3.2 %collective-permute-start.24 = (f32[5,32,128]{2,1,0:T(8,128)S(1)}, f32[5,32,128]{2,1,0:T(8,128)S(1)}, u32[]{:S(2)}, u32[]{:S(2)}) collective-permute-start(f32[5,32,128]{2,1,0:T(8,128)S(1)} %get-tuple-element.95.z_lo), channel_id=1, source_target_pairs={{0,3},{1,0},{2,1},{3,2},{4,7},{5,4},{6,5},{7,6},{8,11},{9,8},{10,9... | collective-permute-start | bytes 245768 | tf_op jit(solution)/shard_map/ppermute | solution.py:710
  69.2 4.0 %collective-permute-start.23 = (f32[5,32,128]{2,1,0:T(8,128)S(1)}, f32[5,32,128]{2,1,0:T(8,128)S(1)}, u32[]{:S(2)}, u32[]{:S(2)}) collective-permute-start(f32[5,32,128]{2,1,0:T(8,128)S(1)} %get-tuple-element.96.z_hi), channel_id=1, source_target_pairs={{0,1},{1,2},{2,3},{3,0},{4,5},{5,6},{6,7},{7,4},{8,9},{9,10},{10,1... | collective-permute-start | bytes 245768 | tf_op jit(solution)/shard_map/ppermute | solution.py:710
  69.2 7.4 %collective-permute-start.21 = (f32[5,4,8,128]{3,2,1,0:T(8,128)S(1)}, f32[5,4,8,128]{3,2,1,0:T(8,128)S(1)}, u32[]{:S(2)}, u32[]{:S(2)}) collective-permute-start(f32[5,4,8,128]{3,2,1,0:T(8,128)S(1)} %get-tuple-element.91.y_lo), channel_id=1, source_target_pairs={{0,12},{4,0},{8,4},{12,8},{1,13},{5,1},{9,5},{13,9},{2,14},{6,2},{... | collective-permute-start | bytes 245768 | tf_op jit(solution)/shard_map/ppermute | solution.py:710
  70.1 6.4 %collective-permute-start.20 = (f32[5,4,8,128]{3,2,1,0:T(8,128)S(1)}, f32[5,4,8,128]{3,2,1,0:T(8,128)S(1)}, u32[]{:S(2)}, u32[]{:S(2)}) collective-permute-start(f32[5,4,8,128]{3,2,1,0:T(8,128)S(1)} %get-tuple-element.92.y_hi), channel_id=1, source_target_pairs={{0,4},{4,8},{8,12},{12,0},{1,5},{5,9},{9,13},{13,1},{2,6},{6,10},{... | collective-permute-start | bytes 245768 | tf_op jit(solution)/shard_map/ppermute | solution.py:710

commit v2 on v1

--- a/solution.py
+++ b/solution.py
@@ -33,12 +33,9 @@
     return pl.CostEstimate(flops=flops, bytes_accessed=moved, transcendentals=0)
 
 
-def split_units(units):
-    shares = (2, 4, 5, 6)
-    sizes = [units * share // 20 for share in shares]
-    sizes.append(units - sum(sizes))
-    starts = [sum(sizes[:i]) for i in range(len(sizes) + 1)]
-    return list(zip(starts[:-1], starts[1:]))
+def split_units(units, shares):
+    ends = [units * sum(shares[: i + 1]) // sum(shares) for i in range(len(shares))]
+    return list(zip([0] + ends[:-1], ends))
 
 
 def from_state(state, tag, unit, slots, rows):
@@ -49,22 +46,16 @@
     return state[pl.ds(start, SUB, stride=SUB), :]
 
 
-def pick(tag, unit, local, state, arrived, slots, rows, moves):
+def pick(tag, unit, state, arrived, slots, rows, moves):
     value = from_state(state, jnp.minimum(tag, slots - 1), unit, slots, rows)
-    for level, ref in enumerate(arrived):
+    for level, held in enumerate(arrived):
         base = slots + level * moves
         index = jnp.clip(tag - base, 0, moves - 1)
-        value = jnp.where(tag >= base, ref[index, local * SUB : (local + 1) * SUB, :], value)
+        for (begin, end), ref in held:
+            if begin <= unit < end:
+                at = (unit - begin) * SUB
+                value = jnp.where(tag >= base, ref[index, at : at + SUB, :], value)
     return value
-
-
-def pack_pieces(send, state, outs, pieces, slots, rows, moves):
-    for k in range(moves):
-        slot = jnp.minimum(send[0, 0, k], slots - 1)
-        for (begin, end), out in zip(pieces, outs):
-            for unit in range(begin, end):
-                at = (unit - begin) * SUB
-                out[k, at : at + SUB, :] = from_state(state, slot, unit, slots, rows)
 
 
 def first_kernel(send_hbm, state_hbm, out, send, held, sems, *, piece, slots, rows, moves):
@@ -99,9 +90,16 @@
 def load_kernel(send, recv, own, state_hbm, *refs, pieces, slots, rows, moves, occ):
     state, tags = refs[:2]
     outs = refs[2 : 2 + len(pieces)]
-    where, sem = refs[2 + len(pieces) :]
-    copy = pltpu.make_async_copy(state_hbm, state, sem)
-    copy.start()
+    where, sems = refs[2 + len(pieces) :]
+    span = slots * rows
+    copies = [
+        pltpu.make_async_copy(
+            state_hbm.at[pl.ds(f * span, span), :], state.at[pl.ds(f * span, span), :], sems.at[f]
+        )
+        for f in FIELDS
+    ]
+    for c in copies:
+        c.start()
     for slot in range(slots):
         where[slot] = slot
     for level in range(3):
@@ -113,21 +111,35 @@
             where[recv[level, 0, k]] = slots + level * moves + k
     for b in range(occ):
         tags[2 * moves + b] = where[own[b]]
-    copy.wait()
-    pack_pieces(send, state, outs, pieces, slots, rows, moves)
-
-
-def pick_kernel(tags, state, *refs, plan, given, passed, slots, rows, moves):
-    arrived = refs[:given]
+    for f in FIELDS:
+        copies[f].wait()
+        for k in range(moves):
+            slot = jnp.minimum(send[0, 0, k], slots - 1)
+            for (begin, end), out in zip(pieces, outs):
+                for unit in range(begin, end):
+                    if unit % NF == f:
+                        at = (unit - begin) * SUB
+                        out[k, at : at + SUB, :] = from_state(state, slot, unit, slots, rows)
+
+
+def group_levels(refs, held):
+    levels = [[], [], []]
+    for ref, (level, piece) in zip(refs, held):
+        levels[level].append((piece, ref))
+    return levels
+
+
+def pick_kernel(tags, state, *refs, plan, held, passed, slots, rows, moves):
+    given = len(held)
+    arrived = group_levels(refs[:given], held)
     outs = refs[given + passed :]
-    for (level, begin, end, which), out in zip(plan, outs):
-        sources = [arrived[i] for i in which]
+    for (level, (begin, end)), out in zip(plan, outs):
         for k in range(moves):
             tag = tags[(level - 1) * moves + k]
             for unit in range(begin, end):
-                local = unit - begin
-                out[k, local * SUB : (local + 1) * SUB, :] = pick(
-                    tag, unit, local, state, sources, slots, rows, moves
+                at = (unit - begin) * SUB
+                out[k, at : at + SUB, :] = pick(
+                    tag, unit, state, arrived[:level], slots, rows, moves
                 )
 
 
@@ -218,10 +230,10 @@
         return jax.ShapeDtypeStruct(((NF * self.rows + 2) * SUB, LANES), f32)
 
     def faces(self):
-        x = jax.ShapeDtypeStruct((NF, self.pad, SUB, LANES), f32)
+        x = jax.ShapeDtypeStruct((2, NF, self.pad, SUB, LANES), f32)
         y = jax.ShapeDtypeStruct((NF, self.edge // self.fit, SUB, LANES), f32)
         z = jax.ShapeDtypeStruct((NF, self.rows, LANES), f32)
-        return [x, x, y, y, z, z]
+        return [x, y, y, z, z]
 
 
 def send_slab(shape, prim, y_lo, y_hi, z_lo, z_hi, slab):
@@ -248,53 +260,46 @@
         z_hi[f, to, :] = prim[shape.across(f, slab, SUB - 1), :]
 
 
-def send_x(shape, prim, x_lo, x_hi):
+def send_x(shape, prim, faces, low=True, high=True):
     for f in FIELDS:
         for i in range(shape.pad):
-            x_lo[f, i] = prim[shape.at(f, i), :]
-            x_hi[f, i] = prim[shape.at(f, shape.rows - shape.pad + i), :]
-
-
-def assemble_kernel(tags, state, *refs, pieces, slabs, slots, moves, occ, shape, first):
-    given = refs[: 3 * len(pieces)]
-    rest = refs[len(given) + (0 if first else 7) :]
-    field, prim, y_lo, y_hi, z_lo, z_hi, other = rest[:7]
-    held = rest[7]
+            if high:
+                faces[0, f, i] = prim[shape.at(f, shape.rows - shape.pad + i), :]
+            if low:
+                faces[1, f, i] = prim[shape.at(f, i), :]
+
+
+def assemble_kernel(tags, state, *refs, held, slabs, slots, moves, occ, shape, first):
+    given = len(held)
+    arrived = group_levels(refs[:given], held)
+    outs = refs[given + (0 if first else 7) :]
+    field, prim, y_lo, y_hi, z_lo, z_hi, x_faces = outs[:7]
+    blocks = outs[-1]
     units = NF * shape.slabs
-    begin_unit, end_unit = slabs[0] * NF, slabs[1] * NF
     for b in range(occ):
         tag = tags[2 * moves + b]
-        for number, (begin, end) in enumerate(pieces):
-            sources = given[3 * number : 3 * number + 3]
-            for unit in range(max(begin, begin_unit), min(end, end_unit)):
-                at = (b * units + unit) * SUB
-                held[at : at + SUB, :] = pick(
-                    tag, unit, unit - begin, state, sources, slots, shape.rows, moves
-                )
+        for unit in range(slabs[0] * NF, slabs[1] * NF):
+            at = (b * units + unit) * SUB
+            blocks[at : at + SUB, :] = pick(tag, unit, state, arrived, slots, shape.rows, moves)
     for slab in range(*slabs):
         for i in range(SUB):
             row = slab * SUB + i
             cons = [
-                held[pl.ds((slab * NF + f) * SUB + i, occ, stride=units * SUB), :] for f in FIELDS
+                blocks[pl.ds((slab * NF + f) * SUB + i, occ, stride=units * SUB), :] for f in FIELDS
             ]
             for f, (c, w) in enumerate(zip(cons, primitives(cons))):
                 field[shape.at(f, row), :] = c
                 prim[shape.at(f, row), :] = w
         send_slab(shape, prim, y_lo, y_hi, z_lo, z_hi, slab)
     if first:
+        canvas = outs[7]
 
         def clear(i, carry):
-            other[pl.ds(pl.multiple_of(i * SUB, SUB), SUB), :] = jnp.zeros((SUB, LANES), f32)
+            canvas[pl.ds(pl.multiple_of(i * SUB, SUB), SUB), :] = jnp.zeros((SUB, LANES), f32)
             return carry
 
-        lax.fori_loop(0, other.shape[0] // SUB, clear, 0, unroll=16)
-        for f in FIELDS:
-            for i in range(shape.pad):
-                rest[8][f, i] = prim[shape.at(f, i), :]
-    else:
-        for f in FIELDS:
-            for i in range(shape.pad):
-                rest[8][f, i] = prim[shape.at(f, shape.rows - shape.pad + i), :]
+        lax.fori_loop(0, canvas.shape[0] // SUB, clear, 0, unroll=16)
+    send_x(shape, prim, x_faces, low=first, high=not first)
 
 
 def sweep_z_kernel(prim, z_lo, z_hi, z_prev, z_next, total, flux_z, right_z, left, right, flux, *, shape):
@@ -378,12 +383,12 @@
     lax.fori_loop(0, shape.slabs, differences, 0)
 
 
-def sweep_x_kernel(prim, x_prev, x_next, sofar, total, wide, *, shape):
+def sweep_x_kernel(prim, x_faces, sofar, total, wide, *, shape):
     rows, halves, pad = shape.rows, shape.halves, shape.pad
     for f in FIELDS:
         for i in range(pad):
-            wide[f, i] = x_prev[f, i]
-            wide[f, pad + rows + i] = x_next[f, i]
+            wide[f, i] = x_faces[0, f, i]
+            wide[f, pad + rows + i] = x_faces[1, f, i]
 
         def copy(r, carry, f=f):
             wide[f, pad + r] = prim[shape.at(f, r), :]
@@ -414,7 +419,7 @@
         lax.fori_loop(0, shape.edge, body, (flux, keep), unroll=4)
 
 
-def sweep_y(prim, y_lo, y_hi, y_prev, y_next, sofar, ghost_prim, ghost_flux, left, right, flux,
+def sweep_y(prim, y_lo, y_hi, y_prev, y_next, sofar, ghost_prim, ghost_flux, left, right, flux, turned,
             shape, finish, after_slab):
     edge, halves, fit, width = shape.edge, shape.halves, shape.fit, shape.width
     lane = lane_of()
@@ -473,7 +478,9 @@
             rights = []
             for f in FIELDS:
                 mine = [right[shape.at(f, base + h), :] for h in range(halves)]
-                rights.append(up(mine, lane_roll(ghost_flux[f, q], turn)))
+                ghost = lane_roll(ghost_flux[f, q], turn)
+                turned[shape.at(f, base), :] = ghost
+                rights.append(up(mine, ghost))
             for h in range(halves):
                 lefts = [left[shape.at(f, base + h), :] for f in FIELDS]
                 result = twice_flux(lefts, [rights[f][h] for f in FIELDS], 1)
@@ -486,7 +493,7 @@
             total = [[None] * NF for _ in range(halves)]
             for f in FIELDS:
                 mine = [flux[shape.at(f, base + h), :] for h in range(halves)]
-                under = down(mine, lane_roll(ghost_flux[f, q], turn))
+                under = down(mine, turned[shape.at(f, base), :])
                 for h in range(halves):
                     total[h][f] = sofar[shape.at(f, base + h), :] + (mine[h] - under[h])
             for h in range(halves):
@@ -500,7 +507,7 @@
 
 
 def sweep_y_one_kernel(field, prim, y_lo, y_hi, y_prev, y_next, sofar, *refs, shape):
-    one, one_prim, x_lo, x_hi, out_y_lo, out_y_hi, z_lo, z_hi = refs[:8]
+    one, one_prim, x_faces, out_y_lo, out_y_hi, z_lo, z_hi = refs[:7]
 
     def finish(row, total):
         cons = [field[shape.at(f, row), :] - (0.5 * time_step) * total[f] for f in FIELDS]
@@ -511,13 +518,13 @@
     def after_slab(q):
         send_slab(shape, one_prim, out_y_lo, out_y_hi, z_lo, z_hi, q)
 
-    sweep_y(prim, y_lo, y_hi, y_prev, y_next, sofar, *refs[8:], shape, finish, after_slab)
-    send_x(shape, one_prim, x_lo, x_hi)
+    sweep_y(prim, y_lo, y_hi, y_prev, y_next, sofar, *refs[7:], shape, finish, after_slab)
+    send_x(shape, one_prim, x_faces)
 
 
 def sweep_y_two_kernel(own, field, one, prim, y_lo, y_hi, y_prev, y_next, sofar, zeros, out,
                        canvas, *refs, shape, occ, groups):
-    scratch, (result, sems) = refs[:5], refs[5:]
+    scratch, (result, sems) = refs[:6], refs[6:]
     rows = shape.rows
     span = SUB * SUB
 
@@ -564,8 +571,9 @@
     rows = cells // LANES
     groups = slots // SUB
     shape = Shape(rows, edge)
-    pieces = split_units(NF * shape.slabs)
-    count = len(pieces)
+    units = NF * shape.slabs
+    pieces = split_units(units, (2, 4, 6, 5, 3))
+    firsts = split_units(units, (2, 4, 6, 8))
 
     bit_z = size_z.bit_length() - 2
     bit_y = bit_z + size_y.bit_length() - 1
@@ -588,16 +596,16 @@
     own = lax.dynamic_slice(owner_slot, (device * occ,), (occ,))
     sizes = dict(slots=slots, moves=moves)
 
-    def message(p):
-        begin, end = pieces[p]
+    def message(piece):
+        begin, end = piece
         return jax.ShapeDtypeStruct((moves, (end - begin) * SUB, LANES), f32)
 
     state_rows = NF * groups * rows * SUB
-    head = pieces[0]
-    sent = [None] * count
+    head = firsts[0]
+    sent = [None] * len(firsts)
     sent[0] = pl.pallas_call(
         functools.partial(first_kernel, piece=head, rows=rows, **sizes),
-        out_shape=message(0),
+        out_shape=message(head),
         in_specs=[whole(HBM)] * 2,
         out_specs=whole(VMEM),
         scratch_shapes=[
@@ -609,50 +617,59 @@
         name="pack_first",
     )(send_there, rows_of_state)
     rows_of_state, tags, *sent[1:] = pl.pallas_call(
-        functools.partial(load_kernel, pieces=pieces[1:], rows=rows, occ=occ, **sizes),
+        functools.partial(load_kernel, pieces=firsts[1:], rows=rows, occ=occ, **sizes),
         out_shape=[
             jax.ShapeDtypeStruct((state_rows, LANES), f32),
             jax.ShapeDtypeStruct((2 * moves + occ,), jnp.int32),
         ]
-        + [message(p) for p in range(1, count)],
+        + [message(piece) for piece in firsts[1:]],
         in_specs=[whole(SMEM)] * 3 + [whole(HBM)],
-        out_specs=[whole(VMEM), whole(SMEM)] + [whole(VMEM)] * (count - 1),
-        scratch_shapes=[SMEM((slots + SUB,), jnp.int32), pltpu.SemaphoreType.DMA],
+        out_specs=[whole(VMEM), whole(SMEM)] + [whole(VMEM)] * len(firsts[1:]),
+        scratch_shapes=[SMEM((slots + SUB,), jnp.int32), pltpu.SemaphoreType.DMA((NF,))],
         compiler_params=params(),
         name="load_state",
     )(send_slots, recv_slots, own, rows_of_state)
 
-    got = [[None] * count for _ in range(3)]
+    cuts = (firsts, pieces, pieces)
+    got = [[None] * len(cut) for cut in cuts]
+
+    def holding(levels, begin, end):
+        found = [
+            ((level, piece), got[level][p])
+            for level in levels
+            for p, piece in enumerate(cuts[level])
+            if piece[0] < end and piece[1] > begin
+        ]
+        return found
 
     def make(wanted, through):
-        arrays, plan, shapes = [], [], []
+        found = {}
         for level, p in wanted:
-            which = []
-            for earlier in range(level):
-                which.append(len(arrays))
-                arrays.append(got[earlier][p])
-            plan.append((level, *pieces[p], tuple(which)))
-            shapes.append(message(p))
-        given, passed, made = len(arrays), len(through), len(wanted)
+            for key, value in holding(range(level), *pieces[p]):
+                found[key] = value
+        plan = tuple((level, pieces[p]) for level, p in wanted)
+        given, passed, made = len(found), len(through), len(wanted)
         outs = pl.pallas_call(
             functools.partial(
-                pick_kernel, plan=tuple(plan), given=given, passed=passed, rows=rows, **sizes
+                pick_kernel, plan=plan, held=tuple(found), passed=passed, rows=rows, **sizes
             ),
-            out_shape=shapes + [jax.ShapeDtypeStruct(t.shape, f32) for t in through],
+            out_shape=[message(piece) for _, piece in plan]
+            + [jax.ShapeDtypeStruct(t.shape, f32) for t in through],
             in_specs=[whole(SMEM)] + [whole(VMEM)] * (1 + given) + [whole(pl.ANY)] * passed,
             out_specs=[whole(VMEM)] * made + [whole(pl.ANY)] * passed,
             input_output_aliases={2 + given + i: made + i for i in range(passed)},
             compiler_params=params(),
+            cost_estimate=cost(10**9, 10**9),
             name="pick_" + "_".join("%d%d" % w for w in wanted),
-        )(tags, rows_of_state, *arrays, *through)
+        )(tags, rows_of_state, *found.values(), *through)
         return outs[:made], outs[made:]
 
     steps = [
         ([(1, 0)], [2], []),
         ([(1, 1), (2, 0)], [3], []),
-        ([(1, 2)], [4], []),
-        ([(1, 3), (2, 1)], [], [0]),
-        ([(1, 4), (2, 2)], [], []),
+        ([(1, 2)], [], []),
+        ([(1, 3), (1, 4), (2, 1)], [], [0]),
+        ([(2, 2)], [], []),
         ([(2, 3)], [], [1]),
         ([(2, 4)], [], [2]),
     ]
@@ -661,61 +678,53 @@
     for wanted, leaving, awaited in steps:
         through = [sent[p] for p in leaving] + [got[2][p] for p in awaited]
         made, passed = make(wanted, through)
-        for (level, p), value in zip(wanted, made):
-            got[level][p] = swapped(value, level)
         for p, value in zip(leaving, passed):
             got[0][p] = swapped(value, 0)
+        for (level, p), value in reversed(list(zip(wanted, made))):
+            got[level][p] = swapped(value, level)
         for p, value in zip(awaited, passed[len(leaving) :]):
             got[2][p] = value
 
     grid = shape.grid()
-    face_x, _, face_y, _, face_z, _ = shape.faces()
-    part = [grid, grid, face_y, face_y, face_z, face_z]
+    face_x, face_y, _, face_z, _ = shape.faces()
+    part = [grid, grid, face_y, face_y, face_z, face_z, face_x]
     canvas = jax.ShapeDtypeStruct((state_rows, LANES), f32)
     full = pieces[-1][0] // NF
 
     def assemble(slabs, before):
         first = not before
-        use = [p for p in range(count) if pieces[p][0] < slabs[1] * NF and pieces[p][1] > slabs[0] * NF]
-        sources = [got[level][p] for p in use for level in range(3)]
-        shapes = part + [canvas if first else face_x, face_x]
-        fixed = 2 + len(sources)
-
-        def kernel(tags, state, *refs):
-            lead = refs[: len(sources) + len(before)]
-            outs = refs[len(lead) : len(lead) + 8]
-            assemble_kernel(
-                tags, state, *lead, *outs[:7], refs[-1], outs[7],
-                pieces=[pieces[p] for p in use], slabs=slabs, occ=occ, shape=shape, first=first,
-                **sizes,
-            )
-
+        found = dict(holding(range(3), slabs[0] * NF, slabs[1] * NF))
+        shapes = part + [canvas] * first
+        fixed = 2 + len(found)
         return pl.pallas_call(
-            kernel,
+            functools.partial(
+                assemble_kernel, held=tuple(found), slabs=slabs, occ=occ, shape=shape,
+                first=first, **sizes,
+            ),
             out_shape=shapes,
-            in_specs=[whole(SMEM)] + [whole(VMEM)] * (1 + len(sources)) + [whole(VMEM)] * len(before),
+            in_specs=[whole(SMEM)] + [whole(VMEM)] * (1 + len(found) + len(before)),
             out_specs=[whole(VMEM)] * len(shapes),
             scratch_shapes=[VMEM((occ * NF * rows, LANES), f32)],
             input_output_aliases={fixed + i: i for i in range(len(before))},
             compiler_params=params(),
             name="assemble_%d" % slabs[0],
-        )(tags, rows_of_state, *sources, *before)
-
-    *made, blank, x_lo = assemble((0, full), [])
-    *made, x_lo, x_hi = assemble((full, shape.slabs), [*made, x_lo])
-    made = made[:2] + [x_lo, x_hi] + made[2:]
+        )(tags, rows_of_state, *found.values(), *before)
+
+    *made, blank = assemble((0, full), [])
+    *made, x_faces = assemble((full, shape.slabs), made)
+    made = made[:2] + [x_faces] + made[2:]
 
     def ring(value, axis, step):
         size = lax.axis_size(axis)
         return lax.ppermute(value, axis, [(i, (i + step) % size) for i in range(size)])
 
-    def flux_sums(prim, x_lo, x_hi, y_lo, y_hi, z_lo, z_hi):
+    def flux_sums(prim, x_faces, y_lo, y_hi, z_lo, z_hi):
+        if size_x == 2:
+            x_faces = ring(x_faces, "gx", 1)
+        else:
+            x_faces = jnp.stack([ring(x_faces[0], "gx", 1), ring(x_faces[1], "gx", -1)])
         y_prev, y_next = ring(y_hi, "gy", 1), ring(y_lo, "gy", -1)
         z_prev, z_next = ring(z_hi, "gz", 1), ring(z_lo, "gz", -1)
-        if size_x == 2:
-            x_prev, x_next = ring(jnp.stack([x_hi, x_lo]), "gx", 1)
-        else:
-            x_prev, x_next = ring(x_hi, "gx", 1), ring(x_lo, "gx", -1)
         ghost = VMEM((NF, rows, LANES), f32)
         work = [VMEM(grid.shape, f32)] * 3
         total = pl.pallas_call(
@@ -730,17 +739,17 @@
         total = pl.pallas_call(
             functools.partial(sweep_x_kernel, shape=shape),
             out_shape=grid,
-            in_specs=[whole(VMEM)] * 4,
+            in_specs=[whole(VMEM)] * 3,
             out_specs=whole(VMEM),
             scratch_shapes=[VMEM((NF, rows + 2 * shape.pad, SUB, LANES), f32)],
-            input_output_aliases={3: 0},
+            input_output_aliases={2: 0},
             compiler_params=params(),
             name="sweep_x",
-        )(prim, x_prev, x_next, total)
+        )(prim, x_faces, total)
         return y_lo, y_hi, y_prev, y_next, total
 
     produced = [grid, grid] + shape.faces()
-    scratch = [VMEM(face_y.shape, f32)] * 2 + [VMEM(grid.shape, f32)] * 3
+    scratch = [VMEM(face_y.shape, f32)] * 2 + [VMEM(grid.shape, f32)] * 4
     field, prim = made[0], made[1]
     sums = flux_sums(prim, *made[2:])
     made = pl.pallas_call(

time: 81.4 us -> 78.7 us (0.967)
  waiting for transfers between devices: 26.4 us -> 23.9 us
    ppermute x15 -> x14, waiting for transfers between devices: 21.8 us -> 18.6 us  [swapped(): return lax.ppermute(value, AXES, pairs)]
    ppermute x10, starting transfers between devices: 7.27 us -> 9.97 us  [ring(): lax.ppermute(value, axis, [(i, (i + step) % size) for i in range(size)])]
    ppermute x15 -> x14, starting transfers between devices: 22.2 us -> 19.6 us  [swapped(): return lax.ppermute(value, AXES, pairs)]
  transfers between devices with their start and end apart: 25 -> 24, of which waited for: 12 -> 11; matrix products, arithmetic and copies ran while one was open for 0% -> 0% of each run, Pallas kernels for 19% -> 20%
where the time goes in v2:
time: 78.7 us; the launch traced here: 78.5 us
  starting transfers between devices  29.6 us (38%)
  Pallas kernels  24.8 us (32%)
  waiting for transfers between devices  23.9 us (30%)
    ppermute x14, starting transfers between devices, swapped(): return lax.ppermute(value, AXES, pairs)  19.6 us
    ppermute x14, waiting for transfers between devices, swapped(): return lax.ppermute(value, AXES, pairs)  18.6 us
    ppermute x10, starting transfers between devices, ring(): lax.ppermute(value, axis, [(i, (i + step) % size) for i in range(size)])  9.97 us
    ppermute x10, waiting for transfers between devices, ring(): lax.ppermute(value, axis, [(i, (i + step) % size) for i in range(size)])  5.26 us
    pallas_call x2, Pallas kernels, flux_sums(): pl.pallas_call(functools.partial(sweep_z_kernel, shape=shape), out_shape=...  4.76 us
    pallas_call x1, Pallas kernels, shards(): pl.pallas_call(functools.partial(sweep_y_two_kernel, shape=shape, occ=occ...  4.6 us
    pallas_call x7, Pallas kernels, make(): pl.pallas_call(functools.partial(pick_kernel, plan=plan, held=tuple(found...  4.6 us
    pallas_call x1, Pallas kernels, shards(): pl.pallas_call(functools.partial(load_kernel, pieces=firsts[1:], rows=row...  2.93 us
  transfers between devices with their start and end apart: 24, of which 11 were waited for; matrix products, arithmetic and copies ran while one was open for 0% of the time, Pallas kernels for 20%

profile of v2, /device:TPU:0, one launch (start us, length us, event | category | flops | bytes accessed | tf_op | source)
XLA Modules:
  0.0 78.5 jit_solution(18010658542339629110)
XLA Ops:
  0.0 1.0 %pack_first.1 = f32[8,16,128]{2,1,0:T(8,128)S(1)} custom-call(s32[3,1,8]{2,1,0:T(1,128)} %send_hbm.1, f32[5120,128]{1,0:T(8,128)} %bitcast.10), custom_call_target="tpu_custom_call" | custom-call | tf_op jit(solution)/shard_map/pack_first/pallas_call | solution.py:606
  1.0 3.0 %collective-permute-start.1 = (f32[8,16,128]{2,1,0:T(8,128)S(1)}, f32[8,16,128]{2,1,0:T(8,128)S(1)}, u32[]{:S(2)}, u32[]{:S(2)}) collective-permute-start(f32[8,16,128]{2,1,0:T(8,128)S(1)} %pack_first.1), channel_id=1, source_target_pairs={{0,16},{1,17},{2,18},{3,19},{4,20},{5,21},{6,22},{7,23},{8,24},{9,... | collective-permute-start | bytes 196616 | tf_op jit(solution)/shard_map/ppermute | solution.py:586
  4.1 0.1 dynamic_slice.3.own
  4.1 2.9 %load_state.1 = (f32[5120,128]{1,0:T(8,128)S(1)}, s32[24]{0:T(128)S(1)}, f32[8,32,128]{2,1,0:T(8,128)S(1)}, f32[8,48,128]{2,1,0:T(8,128)S(1)}, f32[8,64,128]{2,1,0:T(8,128)S(1)}) custom-call(s32[3,1,8]{2,1,0:T(1,128)S(1)} %copy-done, s32[3,1,8]{2,1,0:T(1,128)S(1)} %copy-done.1, s32[8]{0:T(128)S(1)} %dynamic_slice.3.own, f32[5120,128]{1,0:T(8,128)} %bitcast.11), custom_call_target="tpu_custom_call" | custom-call | tf_op jit(solution)/shard_map/load_state/pallas_call | solution.py:619
  7.1 0.1 collective-permute-start
  7.2 0.0 collective-permute-done.1.refs_0_.refs_1_
  7.2 0.6 pick_10.1
  7.8 3.1 %collective-permute-start.2 = (f32[8,16,128]{2,1,0:T(8,128)S(1)}, f32[8,16,128]{2,1,0:T(8,128)S(1)}, u32[]{:S(2)}, u32[]{:S(2)}) collective-permute-start(f32[8,16,128]{2,1,0:T(8,128)S(1)} %get-tuple-element.50), channel_id=1, source_target_pairs={{0,8},{1,9},{2,10},{3,11},{4,12},{5,13},{6,14},{7,15},{8,0},{9,1},... | collective-permute-start | bytes 196616 | tf_op jit(solution)/shard_map/ppermute | solution.py:586
  10.9 1.5 %collective-permute-start.10 = (f32[8,48,128]{2,1,0:T(8,128)S(1)}, f32[8,48,128]{2,1,0:T(8,128)S(1)}, u32[]{:S(2)}, u32[]{:S(2)}) collective-permute-start(f32[8,48,128]{2,1,0:T(8,128)S(1)} %get-tuple-element.59), channel_id=1, source_target_pairs={{0,16},{1,17},{2,18},{3,19},{4,20},{5,21},{6,22},{7,23},{8,24},{9,... | collective-permute-start | bytes 589832 | tf_op jit(solution)/shard_map/ppermute | solution.py:586
  12.5 0.0 collective-permute-done.refs_0_.refs_1_
  12.5 1.1 %collective-permute-done.2.refs_2_.refs_4_ = f32[8,16,128]{2,1,0:T(8,128)S(1)} collective-permute-done((f32[8,16,128]{2,1,0:T(8,128)S(1)}, f32[8,16,128]{2,1,0:T(8,128)S(1)}, u32[]{:S(2)}, u32[]{:S(2)}) %collective-permute-start.2) | collective-permute-done | bytes 65568 | tf_op jit(solution)/shard_map/ppermute | solution.py:586
  13.5 0.7 pick_11_20.1
  14.3 1.6 %collective-permute-start.3 = (f32[8,64,128]{2,1,0:T(8,128)S(1)}, f32[8,64,128]{2,1,0:T(8,128)S(1)}, u32[]{:S(2)}, u32[]{:S(2)}) collective-permute-start(f32[8,64,128]{2,1,0:T(8,128)S(1)} %get-tuple-element.52), channel_id=1, source_target_pairs={{0,16},{1,17},{2,18},{3,19},{4,20},{5,21},{6,22},{7,23},{8,24},{9,... | collective-permute-start | bytes 786440 | tf_op jit(solution)/shard_map/ppermute | solution.py:586
  15.8 2.6 %collective-permute-start.4 = (f32[8,32,128]{2,1,0:T(8,128)S(1)}, f32[8,32,128]{2,1,0:T(8,128)S(1)}, u32[]{:S(2)}, u32[]{:S(2)}) collective-permute-start(f32[8,32,128]{2,1,0:T(8,128)S(1)} %get-tuple-element.53), channel_id=1, source_target_pairs={{0,8},{1,9},{2,10},{3,11},{4,12},{5,13},{6,14},{7,15},{8,0},{9,1},... | collective-permute-start | bytes 393224 | tf_op jit(solution)/shard_map/ppermute | solution.py:586
  18.5 0.0 collective-permute-done.10.refs_0_.refs_2_
  18.5 0.6 pick_12.1
  19.1 1.6 %collective-permute-start.11 = (f32[8,48,128]{2,1,0:T(8,128)S(1)}, f32[8,48,128]{2,1,0:T(8,128)S(1)}, u32[]{:S(2)}, u32[]{:S(2)}) collective-permute-start(f32[8,48,128]{2,1,0:T(8,128)S(1)} %pick_12.1), channel_id=1, source_target_pairs={{0,8},{1,9},{2,10},{3,11},{4,12},{5,13},{6,14},{7,15},{8,0},{9,1},... | collective-permute-start | bytes 589832 | tf_op jit(solution)/shard_map/ppermute | solution.py:586
  20.8 1.5 %collective-permute-start.5 = (f32[8,16,128]{2,1,0:T(8,128)S(1)}, f32[8,16,128]{2,1,0:T(8,128)S(1)}, u32[]{:S(2)}, u32[]{:S(2)}) collective-permute-start(f32[8,16,128]{2,1,0:T(8,128)S(1)} %get-tuple-element.54), channel_id=1, source_target_pairs={{0,2},{1,3},{2,0},{3,1},{4,6},{5,7},{6,4},{7,5},{8,10},{9,11},{10,... | collective-permute-start | bytes 196616 | tf_op jit(solution)/shard_map/ppermute | solution.py:586
  22.3 3.1 %collective-permute-done.5.refs_3_ = f32[8,16,128]{2,1,0:T(8,128)S(1)} collective-permute-done((f32[8,16,128]{2,1,0:T(8,128)S(1)}, f32[8,16,128]{2,1,0:T(8,128)S(1)}, u32[]{:S(2)}, u32[]{:S(2)}) %collective-permute-start.5) | collective-permute-done | bytes 65568 | tf_op jit(solution)/shard_map/ppermute | solution.py:586
  25.4 3.3 %collective-permute-done.4.refs_2_.refs_5_ = f32[8,32,128]{2,1,0:T(8,128)S(1)} collective-permute-done((f32[8,32,128]{2,1,0:T(8,128)S(1)}, f32[8,32,128]{2,1,0:T(8,128)S(1)}, u32[]{:S(2)}, u32[]{:S(2)}) %collective-permute-start.4) | collective-permute-done | bytes 131104 | tf_op jit(solution)/shard_map/ppermute | solution.py:586
  28.7 0.0 collective-permute-done.3.refs_0_.refs_3_
  28.7 0.7 pick_13_14_21.1
  29.5 1.6 %collective-permute-start.8 = (f32[8,32,128]{2,1,0:T(8,128)S(1)}, f32[8,32,128]{2,1,0:T(8,128)S(1)}, u32[]{:S(2)}, u32[]{:S(2)}) collective-permute-start(f32[8,32,128]{2,1,0:T(8,128)S(1)} %get-tuple-element.57), channel_id=1, source_target_pairs={{0,2},{1,3},{2,0},{3,1},{4,6},{5,7},{6,4},{7,5},{8,10},{9,11},{10,... | collective-permute-start | bytes 393224 | tf_op jit(solution)/shard_map/ppermute | solution.py:586
  31.0 0.0 collective-permute-start.6
  31.0 1.9 %collective-permute-done.11.refs_1_.refs_6_ = f32[8,48,128]{2,1,0:T(8,128)S(1)} collective-permute-done((f32[8,48,128]{2,1,0:T(8,128)S(1)}, f32[8,48,128]{2,1,0:T(8,128)S(1)}, u32[]{:S(2)}, u32[]{:S(2)}) %collective-permute-start.11) | collective-permute-done | bytes 196640 | tf_op jit(solution)/shard_map/ppermute | solution.py:586
  32.9 0.6 pick_22.1
  33.6 1.6 %collective-permute-start.12 = (f32[8,48,128]{2,1,0:T(8,128)S(1)}, f32[8,48,128]{2,1,0:T(8,128)S(1)}, u32[]{:S(2)}, u32[]{:S(2)}) collective-permute-start(f32[8,48,128]{2,1,0:T(8,128)S(1)} %pick_22.1), channel_id=1, source_target_pairs={{0,2},{1,3},{2,0},{3,1},{4,6},{5,7},{6,4},{7,5},{8,10},{9,11},{10,... | collective-permute-start | bytes 589832 | tf_op jit(solution)/shard_map/ppermute | solution.py:586
  35.1 0.0 collective-permute-start.7
  35.2 0.4 collective-permute-done.8.refs_2_
  35.6 5.3 %collective-permute-done.6.refs_1_.refs_7_ = f32[8,40,128]{2,1,0:T(8,128)S(1)} collective-permute-done((f32[8,40,128]{2,1,0:T(8,128)S(1)}, f32[8,40,128]{2,1,0:T(8,128)S(1)}, u32[]{:S(2)}, u32[]{:S(2)}) %collective-permute-start.6) | collective-permute-done | bytes 163872 | tf_op jit(solution)/shard_map/ppermute | solution.py:586
  40.9 0.6 pick_23.1
  41.5 0.6 collective-permute-start.9
  42.1 0.9 %collective-permute-done.7.refs_1_.refs_2_ = f32[8,24,128]{2,1,0:T(8,128)S(1)} collective-permute-done((f32[8,24,128]{2,1,0:T(8,128)S(1)}, f32[8,24,128]{2,1,0:T(8,128)S(1)}, u32[]{:S(2)}, u32[]{:S(2)}) %collective-permute-start.7) | collective-permute-done | bytes 98336 | tf_op jit(solution)/shard_map/ppermute | solution.py:586
  43.0 0.0 collective-permute-done.12.refs_2_
  43.0 0.6 pick_24.1
  43.6 0.7 collective-permute-start.13
  44.4 2.6 %collective-permute-done.9.refs_11_.refs_3_ = f32[8,40,128]{2,1,0:T(8,128)S(1)} collective-permute-done((f32[8,40,128]{2,1,0:T(8,128)S(1)}, f32[8,40,128]{2,1,0:T(8,128)S(1)}, u32[]{:S(2)}, u32[]{:S(2)}) %collective-permute-start.9) | collective-permute-done | bytes 163872 | tf_op jit(solution)/shard_map/ppermute | solution.py:586
  46.9 1.5 %assemble_0.1 = (f32[1296,128]{1,0:T(8,128)S(1)}, f32[1296,128]{1,0:T(8,128)S(1)}, f32[5,4,8,128]{3,2,1,0:T(8,128)S(1)}, f32[5,4,8,128]{3,2,1,0:T(8,128)S(1)}, f...) custom-call(s32[24]{0:T(128)S(1)} %get-tuple-element.46.tags, ...), custom_call_target="tpu_custom_call" | custom-call | tf_op jit(solution)/shard_map/assemble_0/pallas_call | solution.py:699
  48.5 0.0 collective-permute-done.13.refs_4_
  48.5 0.9 %assemble_3.1 = (f32[1296,128]{1,0:T(8,128)S(1)}, f32[1296,128]{1,0:T(8,128)S(1)}, f32[5,4,8,128]{3,2,1,0:T(8,128)S(1)}, f32[5,4,8,128]{3,2,1,0:T(8,128)S(1)}, f...) custom-call(s32[24]{0:T(128)S(1)} %get-tuple-element.46.tags, ...), custom_call_target="tpu_custom_call", output_to_operand_aliasing={{0}: (7, {}), {1}: (8, {}), {2}: (9, {}), {3}: (10, {}), {4... | custom-call | tf_op jit(solution)/shard_map/assemble_3/pallas_call | solution.py:699
  49.4 0.3 collective-permute-start.16
  49.7 0.0 collective-permute-start.18
  49.7 0.5 collective-permute-start.17
  50.2 5.1 %collective-permute-start.15 = (f32[5,4,8,128]{3,2,1,0:T(8,128)S(1)}, f32[5,4,8,128]{3,2,1,0:T(8,128)S(1)}, u32[]{:S(2)}, u32[]{:S(2)}) collective-permute-start(f32[5,4,8,128]{3,2,1,0:T(8,128)S(1)} %get-tuple-element.73.y_lo), channel_id=1, source_target_pairs={{0,12},{4,0},{8,4},{12,8},{1,13},{5,1},{9,5},{13,9},{2,14},{6,2},{... | collective-permute-start | bytes 245768 | tf_op jit(solution)/shard_map/ppermute | solution.py:719
  55.3 0.0 collective-permute-start.14
  55.3 0.0 collective-permute-done.18.z_next
  55.3 0.0 collective-permute-done.17.z_prev
  55.3 2.4 %sweep_z.2.sofar = f32[1296,128]{1,0:T(8,128)S(1)} custom-call(f32[1296,128]{1,0:T(8,128)S(1)} %get-tuple-element.72.prim, f32[5,32,128]{2,1,0:T(8,128)S(1)} %get-tuple-element.76.z_lo, f32[5,32,128]{2,1,0:T(8,128)S(1)} %get-tuple-element.77.z_hi, f32[5,32,128]{2,1,0:T(8,128)S(1)} %collective-permute-done.17.z_prev, ...), custom_call_target="tpu_custom_call" | custom-call | tf_op jit(solution)/shard_map/sweep_z/pallas_call | solution.py:730
  57.7 0.0 collective-permute-done.16.x_faces
  57.7 1.0 %sweep_x.2.sofar = f32[1296,128]{1,0:T(8,128)S(1)} custom-call(f32[1296,128]{1,0:T(8,128)S(1)} %get-tuple-element.72.prim, f32[2,5,4,8,128]{4,3,2,1,0:T(8,128)S(1)} %collective-permute-done.16.x_faces, f32[1296,128]{1,0:T(8,128)S(1)} %sweep_z.2.sofar), custom_call_target="tpu_custom_call", output_to_operand_aliasing={{}: (2, {})} | custom-call | tf_op jit(solution)/shard_map/sweep_x/pallas_call | solution.py:739
  58.7 3.0 %collective-permute-done.14.y_prev = f32[5,4,8,128]{3,2,1,0:T(8,128)S(1)} collective-permute-done((f32[5,4,8,128]{3,2,1,0:T(8,128)S(1)}, f32[5,4,8,128]{3,2,1,0:T(8,128)S(1)}, u32[]{:S(2)}, u32[]{:S(2)}) %collective-permute-start.14) | collective-permute-done | bytes 81952 | tf_op jit(solution)/shard_map/ppermute | solution.py:719
  61.7 2.5 %sweep_y_one.1 = (f32[1296,128]{1,0:T(8,128)S(1)}, f32[1296,128]{1,0:T(8,128)S(1)}, f32[2,5,4,8,128]{4,3,2,1,0:T(8,128)S(1)}, f32[5,4,8,128]{3,2,1,0:T(8,128)S(1...) custom-call(f32[1296,128]{1,0:T(8,128)S(1)} %get-tuple-element.71.field, ...), custom_call_target="tpu_custom_call" | custom-call | tf_op jit(solution)/shard_map/sweep_y_one/pallas_call | solution.py:755
  64.2 1.5 %collective-permute-start.21 = (f32[2,5,4,8,128]{4,3,2,1,0:T(8,128)S(1)}, f32[2,5,4,8,128]{4,3,2,1,0:T(8,128)S(1)}, u32[]{:S(2)}, u32[]{:S(2)}) collective-permute-start(f32[2,5,4,8,128]{4,3,2,1,0:T(8,128)S(1)} %get-tuple-element.82), channel_id=1, source_target_pairs={{0,16},{16,0},{1,17},{17,1},{2,18},{18,2},{3,19},{19,3},{4,20},{20... | collective-permute-start | bytes 491528 | tf_op jit(solution)/shard_map/ppermute | solution.py:719
  65.7 0.0 collective-permute-start.23
  65.7 0.5 collective-permute-start.22
  66.2 0.7 collective-permute-start.20
  66.9 1.3 %collective-permute-start.19 = (f32[5,4,8,128]{3,2,1,0:T(8,128)S(1)}, f32[5,4,8,128]{3,2,1,0:T(8,128)S(1)}, u32[]{:S(2)}, u32[]{:S(2)}) collective-permute-start(f32[5,4,8,128]{3,2,1,0:T(8,128)S(1)} %get-tuple-element.81.y_hi), channel_id=1, source_target_pairs={{0,4},{4,8},{8,12},{12,0},{1,5},{5,9},{9,13},{13,1},{2,6},{6,10},{... | collective-permute-start | bytes 245768 | tf_op jit(solution)/shard_map/ppermute | solution.py:719
  68.3 0.0 collective-permute-done.23.z_next
  68.3 1.8 %collective-permute-done.22.z_prev = f32[5,32,128]{2,1,0:T(8,128)S(1)} collective-permute-done((f32[5,32,128]{2,1,0:T(8,128)S(1)}, f32[5,32,128]{2,1,0:T(8,128)S(1)}, u32[]{:S(2)}, u32[]{:S(2)}) %collective-permute-start.22) | collective-permute-done | bytes 81952 | tf_op jit(solution)/shard_map/ppermute | solution.py:719
  70.1 2.4 %sweep_z.3.sofar = f32[1296,128]{1,0:T(8,128)S(1)} custom-call(f32[1296,128]{1,0:T(8,128)S(1)} %get-tuple-element.79.prim, f32[5,32,128]{2,1,0:T(8,128)S(1)} %get-tuple-element.83.z_lo, f32[5,32,128]{2,1,0:T(8,128)S(1)} %get-tuple-element.84.z_hi, f32[5,32,128]{2,1,0:T(8,128)S(1)} %collective-permute-done.22.z_prev, ...), custom_call_target="tpu_custom_call" | custom-call | tf_op jit(solution)/shard_map/sweep_z/pallas_call | solution.py:730
  72.5 1.0 %sweep_x.3.sofar = f32[1296,128]{1,0:T(8,128)S(1)} custom-call(f32[1296,128]{1,0:T(8,128)S(1)} %get-tuple-element.79.prim, f32[2,5,4,8,128]{4,3,2,1,0:T(8,128)S(1)} %collective-permute-done.21.x_faces, f32[1296,128]{1,0:T(8,128)S(1)} %sweep_z.3.sofar), custom_call_target="tpu_custom_call", output_to_operand_aliasing={{}: (2, {})} | custom-call | tf_op jit(solution)/shard_map/sweep_x/pallas_call | solution.py:739
  73.5 0.0 collective-permute-done.20.y_next
  73.5 0.4 collective-permute-done.19.y_prev
  73.9 4.6 %sweep_y_two.1 = (f32[5120,128]{1,0:T(8,128)}, f32[5120,128]{1,0:T(8,128)S(1)}) custom-call(s32[8]{0:T(128)S(1)} %dynamic_slice.3.own, f32[1296,128]{1,0:T(8,128)S(1)} %get-tuple-element.71.field, f32[1296,128]{1,0:T(8,128)S(1)} %get-tuple-element.78.one, f32[1296,128]{1,0:T(8,128)S(1)} %get-tuple-element.79.prim, ...), custom_call_target="tpu_custom_call", output_to_operand_aliasing={{1}: (9, {})} | custom-call | tf_op jit(solution)/shard_map/sweep_y_two/pallas_call | solution.py:766
  (8 shorter events, 0.0 us)
Async XLA Ops:
  0.0 4.1 %copy-start = (s32[3,1,8]{2,1,0:T(1,128)S(1)}, s32[3,1,8]{2,1,0:T(1,128)}, u32[]{:S(2)}) copy-start(s32[3,1,8]{2,1,0:T(1,128)} %send_hbm.1) | copy-start | bytes 292
  0.0 4.1 %copy-start.2 = (s32[256]{0:T(256)S(1)}, s32[256]{0:T(256)}, u32[]{:S(2)}) copy-start(s32[256]{0:T(256)} %param.7) | copy-start | bytes 3076
  0.0 4.1 %copy-start.1 = (s32[3,1,8]{2,1,0:T(1,128)S(1)}, s32[3,1,8]{2,1,0:T(1,128)}, u32[]{:S(2)}) copy-start(s32[3,1,8]{2,1,0:T(1,128)} %recv.1) | copy-start | bytes 292
  1.0 6.2 %collective-permute-start.1 = (f32[8,16,128]{2,1,0:T(8,128)S(1)}, f32[8,16,128]{2,1,0:T(8,128)S(1)}, u32[]{:S(2)}, u32[]{:S(2)}) collective-permute-start(f32[8,16,128]{2,1,0:T(8,128)S(1)} %pack_first.1), channel_id=1, source_target_pairs={{0,16},{1,17},{2,18},{3,19},{4,20},{5,21},{6,22},{7,23},{8,24},{9,... | collective-permute-start | bytes 196616 | tf_op jit(solution)/shard_map/ppermute | solution.py:586
  7.1 5.4 %collective-permute-start = (f32[8,32,128]{2,1,0:T(8,128)S(1)}, f32[8,32,128]{2,1,0:T(8,128)S(1)}, u32[]{:S(2)}, u32[]{:S(2)}) collective-permute-start(f32[8,32,128]{2,1,0:T(8,128)S(1)} %get-tuple-element.48), channel_id=1, source_target_pairs={{0,16},{1,17},{2,18},{3,19},{4,20},{5,21},{6,22},{7,23},{8,24},{9,... | collective-permute-start | bytes 393224 | tf_op jit(solution)/shard_map/ppermute | solution.py:586
  7.8 5.7 %collective-permute-start.2 = (f32[8,16,128]{2,1,0:T(8,128)S(1)}, f32[8,16,128]{2,1,0:T(8,128)S(1)}, u32[]{:S(2)}, u32[]{:S(2)}) collective-permute-start(f32[8,16,128]{2,1,0:T(8,128)S(1)} %get-tuple-element.50), channel_id=1, source_target_pairs={{0,8},{1,9},{2,10},{3,11},{4,12},{5,13},{6,14},{7,15},{8,0},{9,1},... | collective-permute-start | bytes 196616 | tf_op jit(solution)/shard_map/ppermute | solution.py:586
  10.9 7.6 %collective-permute-start.10 = (f32[8,48,128]{2,1,0:T(8,128)S(1)}, f32[8,48,128]{2,1,0:T(8,128)S(1)}, u32[]{:S(2)}, u32[]{:S(2)}) collective-permute-start(f32[8,48,128]{2,1,0:T(8,128)S(1)} %get-tuple-element.59), channel_id=1, source_target_pairs={{0,16},{1,17},{2,18},{3,19},{4,20},{5,21},{6,22},{7,23},{8,24},{9,... | collective-permute-start | bytes 589832 | tf_op jit(solution)/shard_map/ppermute | solution.py:586
  14.3 14.5 %collective-permute-start.3 = (f32[8,64,128]{2,1,0:T(8,128)S(1)}, f32[8,64,128]{2,1,0:T(8,128)S(1)}, u32[]{:S(2)}, u32[]{:S(2)}) collective-permute-start(f32[8,64,128]{2,1,0:T(8,128)S(1)} %get-tuple-element.52), channel_id=1, source_target_pairs={{0,16},{1,17},{2,18},{3,19},{4,20},{5,21},{6,22},{7,23},{8,24},{9,... | collective-permute-start | bytes 786440 | tf_op jit(solution)/shard_map/ppermute | solution.py:586
  15.8 12.9 %collective-permute-start.4 = (f32[8,32,128]{2,1,0:T(8,128)S(1)}, f32[8,32,128]{2,1,0:T(8,128)S(1)}, u32[]{:S(2)}, u32[]{:S(2)}) collective-permute-start(f32[8,32,128]{2,1,0:T(8,128)S(1)} %get-tuple-element.53), channel_id=1, source_target_pairs={{0,8},{1,9},{2,10},{3,11},{4,12},{5,13},{6,14},{7,15},{8,0},{9,1},... | collective-permute-start | bytes 393224 | tf_op jit(solution)/shard_map/ppermute | solution.py:586
  19.1 13.8 %collective-permute-start.11 = (f32[8,48,128]{2,1,0:T(8,128)S(1)}, f32[8,48,128]{2,1,0:T(8,128)S(1)}, u32[]{:S(2)}, u32[]{:S(2)}) collective-permute-start(f32[8,48,128]{2,1,0:T(8,128)S(1)} %pick_12.1), channel_id=1, source_target_pairs={{0,8},{1,9},{2,10},{3,11},{4,12},{5,13},{6,14},{7,15},{8,0},{9,1},... | collective-permute-start | bytes 589832 | tf_op jit(solution)/shard_map/ppermute | solution.py:586
  20.8 4.6 %collective-permute-start.5 = (f32[8,16,128]{2,1,0:T(8,128)S(1)}, f32[8,16,128]{2,1,0:T(8,128)S(1)}, u32[]{:S(2)}, u32[]{:S(2)}) collective-permute-start(f32[8,16,128]{2,1,0:T(8,128)S(1)} %get-tuple-element.54), channel_id=1, source_target_pairs={{0,2},{1,3},{2,0},{3,1},{4,6},{5,7},{6,4},{7,5},{8,10},{9,11},{10,... | collective-permute-start | bytes 196616 | tf_op jit(solution)/shard_map/ppermute | solution.py:586
  29.5 6.1 %collective-permute-start.8 = (f32[8,32,128]{2,1,0:T(8,128)S(1)}, f32[8,32,128]{2,1,0:T(8,128)S(1)}, u32[]{:S(2)}, u32[]{:S(2)}) collective-permute-start(f32[8,32,128]{2,1,0:T(8,128)S(1)} %get-tuple-element.57), channel_id=1, source_target_pairs={{0,2},{1,3},{2,0},{3,1},{4,6},{5,7},{6,4},{7,5},{8,10},{9,11},{10,... | collective-permute-start | bytes 393224 | tf_op jit(solution)/shard_map/ppermute | solution.py:586
  31.0 9.9 %collective-permute-start.6 = (f32[8,40,128]{2,1,0:T(8,128)S(1)}, f32[8,40,128]{2,1,0:T(8,128)S(1)}, u32[]{:S(2)}, u32[]{:S(2)}) collective-permute-start(f32[8,40,128]{2,1,0:T(8,128)S(1)} %get-tuple-element.55), channel_id=1, source_target_pairs={{0,8},{1,9},{2,10},{3,11},{4,12},{5,13},{6,14},{7,15},{8,0},{9,1},... | collective-permute-start | bytes 491528 | tf_op jit(solution)/shard_map/ppermute | solution.py:586
  33.6 9.4 %collective-permute-start.12 = (f32[8,48,128]{2,1,0:T(8,128)S(1)}, f32[8,48,128]{2,1,0:T(8,128)S(1)}, u32[]{:S(2)}, u32[]{:S(2)}) collective-permute-start(f32[8,48,128]{2,1,0:T(8,128)S(1)} %pick_22.1), channel_id=1, source_target_pairs={{0,2},{1,3},{2,0},{3,1},{4,6},{5,7},{6,4},{7,5},{8,10},{9,11},{10,... | collective-permute-start | bytes 589832 | tf_op jit(solution)/shard_map/ppermute | solution.py:586
  35.1 7.8 %collective-permute-start.7 = (f32[8,24,128]{2,1,0:T(8,128)S(1)}, f32[8,24,128]{2,1,0:T(8,128)S(1)}, u32[]{:S(2)}, u32[]{:S(2)}) collective-permute-start(f32[8,24,128]{2,1,0:T(8,128)S(1)} %get-tuple-element.56), channel_id=1, source_target_pairs={{0,8},{1,9},{2,10},{3,11},{4,12},{5,13},{6,14},{7,15},{8,0},{9,1},... | collective-permute-start | bytes 294920 | tf_op jit(solution)/shard_map/ppermute | solution.py:586
  41.5 5.4 %collective-permute-start.9 = (f32[8,40,128]{2,1,0:T(8,128)S(1)}, f32[8,40,128]{2,1,0:T(8,128)S(1)}, u32[]{:S(2)}, u32[]{:S(2)}) collective-permute-start(f32[8,40,128]{2,1,0:T(8,128)S(1)} %get-tuple-element.58), channel_id=1, source_target_pairs={{0,2},{1,3},{2,0},{3,1},{4,6},{5,7},{6,4},{7,5},{8,10},{9,11},{10,... | collective-permute-start | bytes 491528 | tf_op jit(solution)/shard_map/ppermute | solution.py:586
  43.6 4.8 %collective-permute-start.13 = (f32[8,24,128]{2,1,0:T(8,128)S(1)}, f32[8,24,128]{2,1,0:T(8,128)S(1)}, u32[]{:S(2)}, u32[]{:S(2)}) collective-permute-start(f32[8,24,128]{2,1,0:T(8,128)S(1)} %get-tuple-element.60), channel_id=1, source_target_pairs={{0,2},{1,3},{2,0},{3,1},{4,6},{5,7},{6,4},{7,5},{8,10},{9,11},{10,... | collective-permute-start | bytes 294920 | tf_op jit(solution)/shard_map/ppermute | solution.py:586
  49.4 8.3 %collective-permute-start.16 = (f32[2,5,4,8,128]{4,3,2,1,0:T(8,128)S(1)}, f32[2,5,4,8,128]{4,3,2,1,0:T(8,128)S(1)}, u32[]{:S(2)}, u32[]{:S(2)}) collective-permute-start(f32[2,5,4,8,128]{4,3,2,1,0:T(8,128)S(1)} %get-tuple-element.75), channel_id=1, source_target_pairs={{0,16},{16,0},{1,17},{17,1},{2,18},{18,2},{3,19},{19,3},{4,20},{20... | collective-permute-start | bytes 491528 | tf_op jit(solution)/shard_map/ppermute | solution.py:719
  49.7 5.6 %collective-permute-start.18 = (f32[5,32,128]{2,1,0:T(8,128)S(1)}, f32[5,32,128]{2,1,0:T(8,128)S(1)}, u32[]{:S(2)}, u32[]{:S(2)}) collective-permute-start(f32[5,32,128]{2,1,0:T(8,128)S(1)} %get-tuple-element.76.z_lo), channel_id=1, source_target_pairs={{0,3},{1,0},{2,1},{3,2},{4,7},{5,4},{6,5},{7,6},{8,11},{9,8},{10,9... | collective-permute-start | bytes 245768 | tf_op jit(solution)/shard_map/ppermute | solution.py:719
  49.7 5.6 %collective-permute-start.17 = (f32[5,32,128]{2,1,0:T(8,128)S(1)}, f32[5,32,128]{2,1,0:T(8,128)S(1)}, u32[]{:S(2)}, u32[]{:S(2)}) collective-permute-start(f32[5,32,128]{2,1,0:T(8,128)S(1)} %get-tuple-element.77.z_hi), channel_id=1, source_target_pairs={{0,1},{1,2},{2,3},{3,0},{4,5},{5,6},{6,7},{7,4},{8,9},{9,10},{10,1... | collective-permute-start | bytes 245768 | tf_op jit(solution)/shard_map/ppermute | solution.py:719
  50.2 8.5 %collective-permute-start.15 = (f32[5,4,8,128]{3,2,1,0:T(8,128)S(1)}, f32[5,4,8,128]{3,2,1,0:T(8,128)S(1)}, u32[]{:S(2)}, u32[]{:S(2)}) collective-permute-start(f32[5,4,8,128]{3,2,1,0:T(8,128)S(1)} %get-tuple-element.73.y_lo), channel_id=1, source_target_pairs={{0,12},{4,0},{8,4},{12,8},{1,13},{5,1},{9,5},{13,9},{2,14},{6,2},{... | collective-permute-start | bytes 245768 | tf_op jit(solution)/shard_map/ppermute | solution.py:719
  55.3 6.4 %collective-permute-start.14 = (f32[5,4,8,128]{3,2,1,0:T(8,128)S(1)}, f32[5,4,8,128]{3,2,1,0:T(8,128)S(1)}, u32[]{:S(2)}, u32[]{:S(2)}) collective-permute-start(f32[5,4,8,128]{3,2,1,0:T(8,128)S(1)} %get-tuple-element.74.y_hi), channel_id=1, source_target_pairs={{0,4},{4,8},{8,12},{12,0},{1,5},{5,9},{9,13},{13,1},{2,6},{6,10},{... | collective-permute-start | bytes 245768 | tf_op jit(solution)/shard_map/ppermute | solution.py:719
  64.2 8.3 %collective-permute-start.21 = (f32[2,5,4,8,128]{4,3,2,1,0:T(8,128)S(1)}, f32[2,5,4,8,128]{4,3,2,1,0:T(8,128)S(1)}, u32[]{:S(2)}, u32[]{:S(2)}) collective-permute-start(f32[2,5,4,8,128]{4,3,2,1,0:T(8,128)S(1)} %get-tuple-element.82), channel_id=1, source_target_pairs={{0,16},{16,0},{1,17},{17,1},{2,18},{18,2},{3,19},{19,3},{4,20},{20... | collective-permute-start | bytes 491528 | tf_op jit(solution)/shard_map/ppermute | solution.py:719
  65.7 2.5 %collective-permute-start.23 = (f32[5,32,128]{2,1,0:T(8,128)S(1)}, f32[5,32,128]{2,1,0:T(8,128)S(1)}, u32[]{:S(2)}, u32[]{:S(2)}) collective-permute-start(f32[5,32,128]{2,1,0:T(8,128)S(1)} %get-tuple-element.83.z_lo), channel_id=1, source_target_pairs={{0,3},{1,0},{2,1},{3,2},{4,7},{5,4},{6,5},{7,6},{8,11},{9,8},{10,9... | collective-permute-start | bytes 245768 | tf_op jit(solution)/shard_map/ppermute | solution.py:719
  65.7 4.4 %collective-permute-start.22 = (f32[5,32,128]{2,1,0:T(8,128)S(1)}, f32[5,32,128]{2,1,0:T(8,128)S(1)}, u32[]{:S(2)}, u32[]{:S(2)}) collective-permute-start(f32[5,32,128]{2,1,0:T(8,128)S(1)} %get-tuple-element.84.z_hi), channel_id=1, source_target_pairs={{0,1},{1,2},{2,3},{3,0},{4,5},{5,6},{6,7},{7,4},{8,9},{9,10},{10,1... | collective-permute-start | bytes 245768 | tf_op jit(solution)/shard_map/ppermute | solution.py:719
  66.2 7.3 %collective-permute-start.20 = (f32[5,4,8,128]{3,2,1,0:T(8,128)S(1)}, f32[5,4,8,128]{3,2,1,0:T(8,128)S(1)}, u32[]{:S(2)}, u32[]{:S(2)}) collective-permute-start(f32[5,4,8,128]{3,2,1,0:T(8,128)S(1)} %get-tuple-element.80.y_lo), channel_id=1, source_target_pairs={{0,12},{4,0},{8,4},{12,8},{1,13},{5,1},{9,5},{13,9},{2,14},{6,2},{... | collective-permute-start | bytes 245768 | tf_op jit(solution)/shard_map/ppermute | solution.py:719
  66.9 6.9 %collective-permute-start.19 = (f32[5,4,8,128]{3,2,1,0:T(8,128)S(1)}, f32[5,4,8,128]{3,2,1,0:T(8,128)S(1)}, u32[]{:S(2)}, u32[]{:S(2)}) collective-permute-start(f32[5,4,8,128]{3,2,1,0:T(8,128)S(1)} %get-tuple-element.81.y_hi), channel_id=1, source_target_pairs={{0,4},{4,8},{8,12},{12,0},{1,5},{5,9},{9,13},{13,1},{2,6},{6,10},{... | collective-permute-start | bytes 245768 | tf_op jit(solution)/shard_map/ppermute | solution.py:719

commit v3 on v2

--- a/solution.py
+++ b/solution.py
@@ -87,19 +87,9 @@
             ]
 
 
-def load_kernel(send, recv, own, state_hbm, *refs, pieces, slots, rows, moves, occ):
-    state, tags = refs[:2]
-    outs = refs[2 : 2 + len(pieces)]
-    where, sems = refs[2 + len(pieces) :]
-    span = slots * rows
-    copies = [
-        pltpu.make_async_copy(
-            state_hbm.at[pl.ds(f * span, span), :], state.at[pl.ds(f * span, span), :], sems.at[f]
-        )
-        for f in FIELDS
-    ]
-    for c in copies:
-        c.start()
+def rest_kernel(send, recv, own, state, tags, token, *refs, pieces, slots, rows, moves, occ):
+    outs, where = refs[:-1], refs[-1]
+    token[...] = jnp.zeros_like(token)
     for slot in range(slots):
         where[slot] = slot
     for level in range(3):
@@ -111,15 +101,12 @@
             where[recv[level, 0, k]] = slots + level * moves + k
     for b in range(occ):
         tags[2 * moves + b] = where[own[b]]
-    for f in FIELDS:
-        copies[f].wait()
-        for k in range(moves):
-            slot = jnp.minimum(send[0, 0, k], slots - 1)
-            for (begin, end), out in zip(pieces, outs):
-                for unit in range(begin, end):
-                    if unit % NF == f:
-                        at = (unit - begin) * SUB
-                        out[k, at : at + SUB, :] = from_state(state, slot, unit, slots, rows)
+    for k in range(moves):
+        slot = jnp.minimum(send[0, 0, k], slots - 1)
+        for (begin, end), out in zip(pieces, outs):
+            for unit in range(begin, end):
+                at = (unit - begin) * SUB
+                out[k, at : at + SUB, :] = from_state(state, slot, unit, slots, rows)
 
 
 def group_levels(refs, held):
@@ -295,10 +282,11 @@
         canvas = outs[7]
 
         def clear(i, carry):
-            canvas[pl.ds(pl.multiple_of(i * SUB, SUB), SUB), :] = jnp.zeros((SUB, LANES), f32)
+            for c in range(canvas.shape[0]):
+                canvas[c, pl.ds(pl.multiple_of(i * SUB, SUB), SUB), :] = jnp.zeros((SUB, LANES), f32)
             return carry
 
-        lax.fori_loop(0, canvas.shape[0] // SUB, clear, 0, unroll=16)
+        lax.fori_loop(0, canvas.shape[1] // SUB, clear, 0)
     send_x(shape, prim, x_faces, low=first, high=not first)
 
 
@@ -536,30 +524,20 @@
 
     def copy(part):
         begin = part * span if isinstance(part, int) else pl.multiple_of(part * span, span)
-        return [
-            pltpu.make_async_copy(
-                canvas.at[pl.ds(i * rows * SUB + begin, span), :],
-                out.at[pl.ds(i * rows * SUB + begin, span), :],
-                sems.at[part, i],
-            )
-            for i in range(NF * groups)
-        ]
+        at = pl.ds(begin, span)
+        return pltpu.make_async_copy(canvas.at[:, at, :], out.at[:, at, :], sems.at[part])
 
     def after_slab(q):
         for b in range(occ):
             slot = own[b]
-            base = (slot // SUB) * (rows * SUB) + lax.rem(slot, SUB) + q * span
+            to = pl.ds(q * span + lax.rem(slot, SUB), SUB, stride=SUB)
             for f in FIELDS:
-                canvas[pl.ds(base + f * groups * rows * SUB, SUB, stride=SUB), :] = result[
-                    shape.across(f, q, b), :
-                ]
-        for c in copy(q):
-            c.start()
+                canvas[f * groups + slot // SUB, to, :] = result[shape.across(f, q, b), :]
+        copy(q).start()
 
     sweep_y(prim, y_lo, y_hi, y_prev, y_next, sofar, *scratch, shape, finish, after_slab)
     for part in range(shape.slabs):
-        for c in copy(part):
-            c.wait()
+        copy(part).wait()
 
 
 def shards(state, send_slots, recv_slots, owner_slot):
@@ -572,8 +550,8 @@
     groups = slots // SUB
     shape = Shape(rows, edge)
     units = NF * shape.slabs
-    pieces = split_units(units, (2, 4, 6, 5, 3))
-    firsts = split_units(units, (2, 4, 6, 8))
+    pieces = split_units(units, (4, 5, 5, 4, 2))
+    firsts = split_units(units, (4, 5, 5, 6))
 
     bit_z = size_z.bit_length() - 2
     bit_y = bit_z + size_y.bit_length() - 1
@@ -590,7 +568,7 @@
         .transpose(2, 0, 3, 1, 4)
         .reshape(NF * groups * rows * SUB, LANES)
     )
-    rows_of_state = pltpu.with_memory_space_constraint(rows_of_state, HBM)
+    state_there = pltpu.with_memory_space_constraint(rows_of_state, HBM)
     send_there = pltpu.with_memory_space_constraint(send_slots, HBM)
     device = lax.axis_index(AXES)
     own = lax.dynamic_slice(owner_slot, (device * occ,), (occ,))
@@ -600,7 +578,6 @@
         begin, end = piece
         return jax.ShapeDtypeStruct((moves, (end - begin) * SUB, LANES), f32)
 
-    state_rows = NF * groups * rows * SUB
     head = firsts[0]
     sent = [None] * len(firsts)
     sent[0] = pl.pallas_call(
@@ -615,19 +592,19 @@
         ],
         compiler_params=params(),
         name="pack_first",
-    )(send_there, rows_of_state)
-    rows_of_state, tags, *sent[1:] = pl.pallas_call(
-        functools.partial(load_kernel, pieces=firsts[1:], rows=rows, occ=occ, **sizes),
+    )(send_there, state_there)
+    tags, token, *sent[1:] = pl.pallas_call(
+        functools.partial(rest_kernel, pieces=firsts[1:], rows=rows, occ=occ, **sizes),
         out_shape=[
-            jax.ShapeDtypeStruct((state_rows, LANES), f32),
             jax.ShapeDtypeStruct((2 * moves + occ,), jnp.int32),
+            jax.ShapeDtypeStruct((SUB, LANES), f32),
         ]
         + [message(piece) for piece in firsts[1:]],
-        in_specs=[whole(SMEM)] * 3 + [whole(HBM)],
-        out_specs=[whole(VMEM), whole(SMEM)] + [whole(VMEM)] * len(firsts[1:]),
-        scratch_shapes=[SMEM((slots + SUB,), jnp.int32), pltpu.SemaphoreType.DMA((NF,))],
+        in_specs=[whole(SMEM)] * 3 + [whole(VMEM)],
+        out_specs=[whole(SMEM)] + [whole(VMEM)] * len(firsts),
+        scratch_shapes=[SMEM((slots + SUB,), jnp.int32)],
         compiler_params=params(),
-        name="load_state",
+        name="pack_rest",
     )(send_slots, recv_slots, own, rows_of_state)
 
     cuts = (firsts, pieces, pieces)
@@ -666,18 +643,18 @@
 
     steps = [
         ([(1, 0)], [2], []),
-        ([(1, 1), (2, 0)], [3], []),
-        ([(1, 2)], [], []),
-        ([(1, 3), (1, 4), (2, 1)], [], [0]),
-        ([(2, 2)], [], []),
+        ([(1, 1)], [3], []),
+        ([(1, 2), (2, 0)], [], []),
+        ([(1, 3), (2, 1)], [], []),
+        ([(1, 4), (2, 2)], [], [0]),
         ([(2, 3)], [], [1]),
         ([(2, 4)], [], [2]),
     ]
     got[0][0] = swapped(sent[0], 0)
     got[0][1] = swapped(sent[1], 0)
     for wanted, leaving, awaited in steps:
-        through = [sent[p] for p in leaving] + [got[2][p] for p in awaited]
-        made, passed = make(wanted, through)
+        through = [token] + [sent[p] for p in leaving] + [got[2][p] for p in awaited]
+        made, (token, *passed) = make(wanted, through)
         for p, value in zip(leaving, passed):
             got[0][p] = swapped(value, 0)
         for (level, p), value in reversed(list(zip(wanted, made))):
@@ -688,7 +665,7 @@
     grid = shape.grid()
     face_x, face_y, _, face_z, _ = shape.faces()
     part = [grid, grid, face_y, face_y, face_z, face_z, face_x]
-    canvas = jax.ShapeDtypeStruct((state_rows, LANES), f32)
+    canvas = jax.ShapeDtypeStruct((NF * groups, rows * SUB, LANES), f32)
     full = pieces[-1][0] // NF
 
     def assemble(slabs, before):
@@ -771,7 +748,7 @@
         scratch_shapes=scratch
         + [
             VMEM(grid.shape, f32),
-            pltpu.SemaphoreType.DMA((shape.slabs, NF * groups)),
+            pltpu.SemaphoreType.DMA((shape.slabs,)),
         ],
         input_output_aliases={9: 1},
         compiler_params=params(),

time: 78.7 us -> 78.2 us (level)
  Pallas kernels: 24.8 us -> 22.9 us
  starting transfers between devices: 29.6 us -> 30.8 us
    pallas_call x1, Pallas kernels: 2.93 us -> 1.39 us  [shards(): pl.pallas_call(functools.partial(rest_kernel, pieces=firsts[1:], rows=row...]
    ppermute x10, starting transfers between devices: 9.97 us -> 11.5 us  [ring(): lax.ppermute(value, axis, [(i, (i + step) % size) for i in range(size)])]
  transfers between devices with their start and end apart: 24 -> 24, of which waited for: 11 -> 11; matrix products, arithmetic and copies ran while one was open for 0% -> 0% of each run, Pallas kernels for 20% -> 18%
where the time goes in v3:
time: 78.2 us; the launch traced here: 78 us
  starting transfers between devices  30.8 us (39%)
  waiting for transfers between devices  24.1 us (31%)
  Pallas kernels  22.9 us (29%)
    ppermute x14, starting transfers between devices, swapped(): return lax.ppermute(value, AXES, pairs)  19.3 us
    ppermute x14, waiting for transfers between devices, swapped(): return lax.ppermute(value, AXES, pairs)  18.7 us
    ppermute x10, starting transfers between devices, ring(): lax.ppermute(value, axis, [(i, (i + step) % size) for i in range(size)])  11.5 us
    ppermute x10, waiting for transfers between devices, ring(): lax.ppermute(value, axis, [(i, (i + step) % size) for i in range(size)])  5.39 us
    pallas_call x2, Pallas kernels, flux_sums(): pl.pallas_call(functools.partial(sweep_z_kernel, shape=shape), out_shape=...  4.76 us
    pallas_call x7, Pallas kernels, make(): pl.pallas_call(functools.partial(pick_kernel, plan=plan, held=tuple(found...  4.67 us
    pallas_call x1, Pallas kernels, shards(): pl.pallas_call(functools.partial(sweep_y_two_kernel, shape=shape, occ=occ...  3.95 us
    pallas_call x1, Pallas kernels, shards(): pl.pallas_call(functools.partial(sweep_y_one_kernel, shape=shape), out_sh...  2.46 us
  transfers between devices with their start and end apart: 24, of which 11 were waited for; matrix products, arithmetic and copies ran while one was open for 0% of the time, Pallas kernels for 18%

profile of v3, /device:TPU:0, one launch (start us, length us, event | category | flops | bytes accessed | tf_op | source)
XLA Modules:
  0.0 78.0 jit_solution(575142507332768610)
XLA Ops:
  0.0 1.3 %pack_first.1 = f32[8,32,128]{2,1,0:T(8,128)S(1)} custom-call(s32[3,1,8]{2,1,0:T(1,128)} %send_hbm.1, f32[5120,128]{1,0:T(8,128)} %bitcast.10), custom_call_target="tpu_custom_call" | custom-call | tf_op jit(solution)/shard_map/pack_first/pallas_call | solution.py:583
  1.4 3.0 %collective-permute-start.1 = (f32[8,32,128]{2,1,0:T(8,128)S(1)}, f32[8,32,128]{2,1,0:T(8,128)S(1)}, u32[]{:S(2)}, u32[]{:S(2)}) collective-permute-start(f32[8,32,128]{2,1,0:T(8,128)S(1)} %pack_first.1), channel_id=1, source_target_pairs={{0,16},{1,17},{2,18},{3,19},{4,20},{5,21},{6,22},{7,23},{8,24},{9,... | collective-permute-start | bytes 393224 | tf_op jit(solution)/shard_map/ppermute | solution.py:564
  4.4 0.1 dynamic_slice.3.own
  4.5 1.4 %pack_rest.1 = (s32[24]{0:T(128)S(1)}, f32[8,128]{1,0:T(8,128)S(1)}, f32[8,40,128]{2,1,0:T(8,128)S(1)}, f32[8,40,128]{2,1,0:T(8,128)S(1)}, f32[8,48,128]{2,1,0:T(8,128)S(1)}) custom-call(s32[3,1,8]{2,1,0:T(1,128)S(1)} %copy-done.1, s32[3,1,8]{2,1,0:T(1,128)S(1)} %copy-done.2, s32[8]{0:T(128)S(1)} %dynamic_slice.3.own, f32[5120,128]{1,0:T(8,128)S(1)} %bitcast.11), custom_call_target="tpu_custom_call" | custom-call | tf_op jit(solution)/shard_map/pack_rest/pallas_call | solution.py:596
  5.9 0.6 collective-permute-start
  6.5 1.5 %collective-permute-done.1.refs_0_.refs_1_ = f32[8,32,128]{2,1,0:T(8,128)S(1)} collective-permute-done((f32[8,32,128]{2,1,0:T(8,128)S(1)}, f32[8,32,128]{2,1,0:T(8,128)S(1)}, u32[]{:S(2)}, u32[]{:S(2)}) %collective-permute-start.1) | collective-permute-done | bytes 131104 | tf_op jit(solution)/shard_map/ppermute | solution.py:564
  7.9 0.6 pick_10.1
  8.5 2.5 %collective-permute-start.4 = (f32[8,40,128]{2,1,0:T(8,128)S(1)}, f32[8,40,128]{2,1,0:T(8,128)S(1)}, u32[]{:S(2)}, u32[]{:S(2)}) collective-permute-start(f32[8,40,128]{2,1,0:T(8,128)S(1)} %get-tuple-element.62), channel_id=1, source_target_pairs={{0,16},{1,17},{2,18},{3,19},{4,20},{5,21},{6,22},{7,23},{8,24},{9,... | collective-permute-start | bytes 491528 | tf_op jit(solution)/shard_map/ppermute | solution.py:564
  11.1 2.6 %collective-permute-start.5 = (f32[8,32,128]{2,1,0:T(8,128)S(1)}, f32[8,32,128]{2,1,0:T(8,128)S(1)}, u32[]{:S(2)}, u32[]{:S(2)}) collective-permute-start(f32[8,32,128]{2,1,0:T(8,128)S(1)} %get-tuple-element.63), channel_id=1, source_target_pairs={{0,8},{1,9},{2,10},{3,11},{4,12},{5,13},{6,14},{7,15},{8,0},{9,1},... | collective-permute-start | bytes 393224 | tf_op jit(solution)/shard_map/ppermute | solution.py:564
  13.7 0.0 collective-permute-done.refs_0_.refs_1_
  13.7 0.6 pick_11.1
  14.3 0.3 collective-permute-start.2
  14.6 2.6 %collective-permute-start.3 = (f32[8,40,128]{2,1,0:T(8,128)S(1)}, f32[8,40,128]{2,1,0:T(8,128)S(1)}, u32[]{:S(2)}, u32[]{:S(2)}) collective-permute-start(f32[8,40,128]{2,1,0:T(8,128)S(1)} %get-tuple-element.61), channel_id=1, source_target_pairs={{0,8},{1,9},{2,10},{3,11},{4,12},{5,13},{6,14},{7,15},{8,0},{9,1},... | collective-permute-start | bytes 491528 | tf_op jit(solution)/shard_map/ppermute | solution.py:564
  17.2 7.0 %collective-permute-done.5.refs_2_.refs_4_ = f32[8,32,128]{2,1,0:T(8,128)S(1)} collective-permute-done((f32[8,32,128]{2,1,0:T(8,128)S(1)}, f32[8,32,128]{2,1,0:T(8,128)S(1)}, u32[]{:S(2)}, u32[]{:S(2)}) %collective-permute-start.5) | collective-permute-done | bytes 131104 | tf_op jit(solution)/shard_map/ppermute | solution.py:564
  24.2 0.0 collective-permute-done.4.refs_0_.refs_1_.refs_2_
  24.2 0.7 pick_12_20.1
  24.9 0.1 collective-permute-start.7
  25.0 1.6 %collective-permute-start.8 = (f32[8,32,128]{2,1,0:T(8,128)S(1)}, f32[8,32,128]{2,1,0:T(8,128)S(1)}, u32[]{:S(2)}, u32[]{:S(2)}) collective-permute-start(f32[8,32,128]{2,1,0:T(8,128)S(1)} %get-tuple-element.69), channel_id=1, source_target_pairs={{0,2},{1,3},{2,0},{3,1},{4,6},{5,7},{6,4},{7,5},{8,10},{9,11},{10,... | collective-permute-start | bytes 393224 | tf_op jit(solution)/shard_map/ppermute | solution.py:564
  26.6 1.1 %collective-permute-done.3.refs_2_.refs_5_ = f32[8,40,128]{2,1,0:T(8,128)S(1)} collective-permute-done((f32[8,40,128]{2,1,0:T(8,128)S(1)}, f32[8,40,128]{2,1,0:T(8,128)S(1)}, u32[]{:S(2)}, u32[]{:S(2)}) %collective-permute-start.3) | collective-permute-done | bytes 163872 | tf_op jit(solution)/shard_map/ppermute | solution.py:564
  27.7 0.0 collective-permute-done.2.refs_0_.refs_3_
  27.7 0.7 pick_13_21.1
  28.4 1.6 %collective-permute-start.10 = (f32[8,40,128]{2,1,0:T(8,128)S(1)}, f32[8,40,128]{2,1,0:T(8,128)S(1)}, u32[]{:S(2)}, u32[]{:S(2)}) collective-permute-start(f32[8,40,128]{2,1,0:T(8,128)S(1)} %get-tuple-element.72), channel_id=1, source_target_pairs={{0,2},{1,3},{2,0},{3,1},{4,6},{5,7},{6,4},{7,5},{8,10},{9,11},{10,... | collective-permute-start | bytes 491528 | tf_op jit(solution)/shard_map/ppermute | solution.py:564
  30.0 0.7 collective-permute-start.6
  30.7 0.0 collective-permute-done.8.refs_4_
  30.7 3.9 %collective-permute-done.7.refs_2_.refs_6_ = f32[8,40,128]{2,1,0:T(8,128)S(1)} collective-permute-done((f32[8,40,128]{2,1,0:T(8,128)S(1)}, f32[8,40,128]{2,1,0:T(8,128)S(1)}, u32[]{:S(2)}, u32[]{:S(2)}) %collective-permute-start.7) | collective-permute-done | bytes 163872 | tf_op jit(solution)/shard_map/ppermute | solution.py:564
  34.6 0.7 pick_14_22.1
  35.4 1.6 %collective-permute-start.12 = (f32[8,40,128]{2,1,0:T(8,128)S(1)}, f32[8,40,128]{2,1,0:T(8,128)S(1)}, u32[]{:S(2)}, u32[]{:S(2)}) collective-permute-start(f32[8,40,128]{2,1,0:T(8,128)S(1)} %get-tuple-element.75), channel_id=1, source_target_pairs={{0,2},{1,3},{2,0},{3,1},{4,6},{5,7},{6,4},{7,5},{8,10},{9,11},{10,... | collective-permute-start | bytes 491528 | tf_op jit(solution)/shard_map/ppermute | solution.py:564
  36.9 0.0 collective-permute-start.9
  36.9 0.5 collective-permute-done.6.refs_1_.refs_7_
  37.5 0.0 collective-permute-done.10.refs_3_
  37.5 0.6 pick_23.1
  38.1 1.6 %collective-permute-start.11 = (f32[8,32,128]{2,1,0:T(8,128)S(1)}, f32[8,32,128]{2,1,0:T(8,128)S(1)}, u32[]{:S(2)}, u32[]{:S(2)}) collective-permute-start(f32[8,32,128]{2,1,0:T(8,128)S(1)} %get-tuple-element.73), channel_id=1, source_target_pairs={{0,2},{1,3},{2,0},{3,1},{4,6},{5,7},{6,4},{7,5},{8,10},{9,11},{10,... | collective-permute-start | bytes 393224 | tf_op jit(solution)/shard_map/ppermute | solution.py:564
  39.7 2.4 %collective-permute-done.9.refs_1_.refs_2_ = f32[8,16,128]{2,1,0:T(8,128)S(1)} collective-permute-done((f32[8,16,128]{2,1,0:T(8,128)S(1)}, f32[8,16,128]{2,1,0:T(8,128)S(1)}, u32[]{:S(2)}, u32[]{:S(2)}) %collective-permute-start.9) | collective-permute-done | bytes 65568 | tf_op jit(solution)/shard_map/ppermute | solution.py:564
  42.1 0.0 collective-permute-done.12.refs_3_
  42.1 0.6 pick_24.1
  42.7 0.6 collective-permute-start.13
  43.3 0.9 %collective-permute-done.11.refs_11_.refs_3_ = f32[8,32,128]{2,1,0:T(8,128)S(1)} collective-permute-done((f32[8,32,128]{2,1,0:T(8,128)S(1)}, f32[8,32,128]{2,1,0:T(8,128)S(1)}, u32[]{:S(2)}, u32[]{:S(2)}) %collective-permute-start.11) | collective-permute-done | bytes 131104 | tf_op jit(solution)/shard_map/ppermute | solution.py:564
  44.3 1.5 %assemble_0.1 = (f32[1296,128]{1,0:T(8,128)S(1)}, f32[1296,128]{1,0:T(8,128)S(1)}, f32[5,4,8,128]{3,2,1,0:T(8,128)S(1)}, f32[5,4,8,128]{3,2,1,0:T(8,128)S(1)}, f...) custom-call(s32[24]{0:T(128)S(1)} %get-tuple-element.54.tags, ...), custom_call_target="tpu_custom_call" | custom-call | tf_op jit(solution)/shard_map/assemble_0/pallas_call | solution.py:676
  45.8 1.3 %collective-permute-done.13.refs_4_ = f32[8,16,128]{2,1,0:T(8,128)S(1)} collective-permute-done((f32[8,16,128]{2,1,0:T(8,128)S(1)}, f32[8,16,128]{2,1,0:T(8,128)S(1)}, u32[]{:S(2)}, u32[]{:S(2)}) %collective-permute-start.13) | collective-permute-done | bytes 65568 | tf_op jit(solution)/shard_map/ppermute | solution.py:564
  47.1 0.8 %assemble_3.1 = (f32[1296,128]{1,0:T(8,128)S(1)}, f32[1296,128]{1,0:T(8,128)S(1)}, f32[5,4,8,128]{3,2,1,0:T(8,128)S(1)}, f32[5,4,8,128]{3,2,1,0:T(8,128)S(1)}, f...) custom-call(s32[24]{0:T(128)S(1)} %get-tuple-element.54.tags, ...), custom_call_target="tpu_custom_call", output_to_operand_aliasing={{0}: (7, {}), {1}: (8, {}), {2}: (9, {}), {3}: (10, {}), {4... | custom-call | tf_op jit(solution)/shard_map/assemble_3/pallas_call | solution.py:676
  47.9 0.1 collective-permute-start.16
  48.0 0.1 collective-permute-start.18
  48.0 0.5 collective-permute-start.17
  48.5 7.0 %collective-permute-start.15 = (f32[5,4,8,128]{3,2,1,0:T(8,128)S(1)}, f32[5,4,8,128]{3,2,1,0:T(8,128)S(1)}, u32[]{:S(2)}, u32[]{:S(2)}) collective-permute-start(f32[5,4,8,128]{3,2,1,0:T(8,128)S(1)} %get-tuple-element.89.y_lo), channel_id=1, source_target_pairs={{0,12},{4,0},{8,4},{12,8},{1,13},{5,1},{9,5},{13,9},{2,14},{6,2},{... | collective-permute-start | bytes 245768 | tf_op jit(solution)/shard_map/ppermute | solution.py:696
  55.6 0.0 collective-permute-start.14
  55.6 0.0 collective-permute-done.18.z_next
  55.6 0.0 collective-permute-done.17.z_prev
  55.6 2.4 %sweep_z.2.sofar = f32[1296,128]{1,0:T(8,128)S(1)} custom-call(f32[1296,128]{1,0:T(8,128)S(1)} %get-tuple-element.88.prim, f32[5,32,128]{2,1,0:T(8,128)S(1)} %get-tuple-element.92.z_lo, f32[5,32,128]{2,1,0:T(8,128)S(1)} %get-tuple-element.93.z_hi, f32[5,32,128]{2,1,0:T(8,128)S(1)} %collective-permute-done.17.z_prev, ...), custom_call_target="tpu_custom_call" | custom-call | tf_op jit(solution)/shard_map/sweep_z/pallas_call | solution.py:707
  58.0 0.0 collective-permute-done.16.x_faces
  58.0 1.0 %sweep_x.2.sofar = f32[1296,128]{1,0:T(8,128)S(1)} custom-call(f32[1296,128]{1,0:T(8,128)S(1)} %get-tuple-element.88.prim, f32[2,5,4,8,128]{4,3,2,1,0:T(8,128)S(1)} %collective-permute-done.16.x_faces, f32[1296,128]{1,0:T(8,128)S(1)} %sweep_z.2.sofar), custom_call_target="tpu_custom_call", output_to_operand_aliasing={{}: (2, {})} | custom-call | tf_op jit(solution)/shard_map/sweep_x/pallas_call | solution.py:716
  59.0 0.0 collective-permute-done.15.y_next
  59.0 3.2 %collective-permute-done.14.y_prev = f32[5,4,8,128]{3,2,1,0:T(8,128)S(1)} collective-permute-done((f32[5,4,8,128]{3,2,1,0:T(8,128)S(1)}, f32[5,4,8,128]{3,2,1,0:T(8,128)S(1)}, u32[]{:S(2)}, u32[]{:S(2)}) %collective-permute-start.14) | collective-permute-done | bytes 81952 | tf_op jit(solution)/shard_map/ppermute | solution.py:696
  62.2 2.5 %sweep_y_one.1 = (f32[1296,128]{1,0:T(8,128)S(1)}, f32[1296,128]{1,0:T(8,128)S(1)}, f32[2,5,4,8,128]{4,3,2,1,0:T(8,128)S(1)}, f32[5,4,8,128]{3,2,1,0:T(8,128)S(1...) custom-call(f32[1296,128]{1,0:T(8,128)S(1)} %get-tuple-element.87.field, ...), custom_call_target="tpu_custom_call" | custom-call | tf_op jit(solution)/shard_map/sweep_y_one/pallas_call | solution.py:732
  64.6 1.3 %collective-permute-start.21 = (f32[2,5,4,8,128]{4,3,2,1,0:T(8,128)S(1)}, f32[2,5,4,8,128]{4,3,2,1,0:T(8,128)S(1)}, u32[]{:S(2)}, u32[]{:S(2)}) collective-permute-start(f32[2,5,4,8,128]{4,3,2,1,0:T(8,128)S(1)} %get-tuple-element.98), channel_id=1, source_target_pairs={{0,16},{16,0},{1,17},{17,1},{2,18},{18,2},{3,19},{19,3},{4,20},{20... | collective-permute-start | bytes 491528 | tf_op jit(solution)/shard_map/ppermute | solution.py:696
  65.9 0.5 collective-permute-start.22
  66.4 0.7 collective-permute-start.20
  67.2 1.3 %collective-permute-start.19 = (f32[5,4,8,128]{3,2,1,0:T(8,128)S(1)}, f32[5,4,8,128]{3,2,1,0:T(8,128)S(1)}, u32[]{:S(2)}, u32[]{:S(2)}) collective-permute-start(f32[5,4,8,128]{3,2,1,0:T(8,128)S(1)} %get-tuple-element.97.y_hi), channel_id=1, source_target_pairs={{0,4},{4,8},{8,12},{12,0},{1,5},{5,9},{9,13},{13,1},{2,6},{6,10},{... | collective-permute-start | bytes 245768 | tf_op jit(solution)/shard_map/ppermute | solution.py:696
  68.5 0.0 collective-permute-done.23.z_next
  68.5 1.9 %collective-permute-done.22.z_prev = f32[5,32,128]{2,1,0:T(8,128)S(1)} collective-permute-done((f32[5,32,128]{2,1,0:T(8,128)S(1)}, f32[5,32,128]{2,1,0:T(8,128)S(1)}, u32[]{:S(2)}, u32[]{:S(2)}) %collective-permute-start.22) | collective-permute-done | bytes 81952 | tf_op jit(solution)/shard_map/ppermute | solution.py:696
  70.4 2.4 %sweep_z.3.sofar = f32[1296,128]{1,0:T(8,128)S(1)} custom-call(f32[1296,128]{1,0:T(8,128)S(1)} %get-tuple-element.95.prim, f32[5,32,128]{2,1,0:T(8,128)S(1)} %get-tuple-element.99.z_lo, f32[5,32,128]{2,1,0:T(8,128)S(1)} %get-tuple-element.100.z_hi, f32[5,32,128]{2,1,0:T(8,128)S(1)} %collective-permute-done.22.z_prev, ...), custom_call_target="tpu_custom_call" | custom-call | tf_op jit(solution)/shard_map/sweep_z/pallas_call | solution.py:707
  72.8 0.0 collective-permute-done.21.x_faces
  72.8 1.0 %sweep_x.3.sofar = f32[1296,128]{1,0:T(8,128)S(1)} custom-call(f32[1296,128]{1,0:T(8,128)S(1)} %get-tuple-element.95.prim, f32[2,5,4,8,128]{4,3,2,1,0:T(8,128)S(1)} %collective-permute-done.21.x_faces, f32[1296,128]{1,0:T(8,128)S(1)} %sweep_z.3.sofar), custom_call_target="tpu_custom_call", output_to_operand_aliasing={{}: (2, {})} | custom-call | tf_op jit(solution)/shard_map/sweep_x/pallas_call | solution.py:716
  73.8 0.3 collective-permute-done.19.y_prev
  74.1 4.0 %sweep_y_two.1 = (f32[20,256,128]{2,1,0:T(8,128)}, f32[20,256,128]{2,1,0:T(8,128)S(1)}) custom-call(s32[8]{0:T(128)S(1)} %dynamic_slice.3.own, f32[1296,128]{1,0:T(8,128)S(1)} %get-tuple-element.87.field, f32[1296,128]{1,0:T(8,128)S(1)} %get-tuple-element.94.one, f32[1296,128]{1,0:T(8,128)S(1)} %get-tuple-element.95.prim, ...), custom_call_target="tpu_custom_call", output_to_operand_aliasing={{1}: (9, {})} | custom-call | tf_op jit(solution)/shard_map/sweep_y_two/pallas_call | solution.py:743
  (10 shorter events, 0.0 us)
Async XLA Ops:
  0.0 4.5 %copy-start.1 = (s32[3,1,8]{2,1,0:T(1,128)S(1)}, s32[3,1,8]{2,1,0:T(1,128)}, u32[]{:S(2)}) copy-start(s32[3,1,8]{2,1,0:T(1,128)} %send_hbm.1) | copy-start | bytes 292
  0.0 4.5 %copy-start = (f32[32,5,4096]{2,0,1:T(8,128)S(1)}, f32[32,5,4096]{2,0,1:T(8,128)}, u32[]{:S(2)}) copy-start(f32[32,5,4096]{2,0,1:T(8,128)} %param.4) | copy-start | bytes 7864324
  0.0 4.4 %copy-start.3 = (s32[256]{0:T(256)S(1)}, s32[256]{0:T(256)}, u32[]{:S(2)}) copy-start(s32[256]{0:T(256)} %param.7) | copy-start | bytes 3076
  0.0 4.5 %copy-start.2 = (s32[3,1,8]{2,1,0:T(1,128)S(1)}, s32[3,1,8]{2,1,0:T(1,128)}, u32[]{:S(2)}) copy-start(s32[3,1,8]{2,1,0:T(1,128)} %recv.1) | copy-start | bytes 292
  1.4 6.6 %collective-permute-start.1 = (f32[8,32,128]{2,1,0:T(8,128)S(1)}, f32[8,32,128]{2,1,0:T(8,128)S(1)}, u32[]{:S(2)}, u32[]{:S(2)}) collective-permute-start(f32[8,32,128]{2,1,0:T(8,128)S(1)} %pack_first.1), channel_id=1, source_target_pairs={{0,16},{1,17},{2,18},{3,19},{4,20},{5,21},{6,22},{7,23},{8,24},{9,... | collective-permute-start | bytes 393224 | tf_op jit(solution)/shard_map/ppermute | solution.py:564
  5.9 7.8 %collective-permute-start = (f32[8,40,128]{2,1,0:T(8,128)S(1)}, f32[8,40,128]{2,1,0:T(8,128)S(1)}, u32[]{:S(2)}, u32[]{:S(2)}) collective-permute-start(f32[8,40,128]{2,1,0:T(8,128)S(1)} %get-tuple-element.55), channel_id=1, source_target_pairs={{0,16},{1,17},{2,18},{3,19},{4,20},{5,21},{6,22},{7,23},{8,24},{9,... | collective-permute-start | bytes 491528 | tf_op jit(solution)/shard_map/ppermute | solution.py:564
  8.5 15.7 %collective-permute-start.4 = (f32[8,40,128]{2,1,0:T(8,128)S(1)}, f32[8,40,128]{2,1,0:T(8,128)S(1)}, u32[]{:S(2)}, u32[]{:S(2)}) collective-permute-start(f32[8,40,128]{2,1,0:T(8,128)S(1)} %get-tuple-element.62), channel_id=1, source_target_pairs={{0,16},{1,17},{2,18},{3,19},{4,20},{5,21},{6,22},{7,23},{8,24},{9,... | collective-permute-start | bytes 491528 | tf_op jit(solution)/shard_map/ppermute | solution.py:564
  11.1 13.1 %collective-permute-start.5 = (f32[8,32,128]{2,1,0:T(8,128)S(1)}, f32[8,32,128]{2,1,0:T(8,128)S(1)}, u32[]{:S(2)}, u32[]{:S(2)}) collective-permute-start(f32[8,32,128]{2,1,0:T(8,128)S(1)} %get-tuple-element.63), channel_id=1, source_target_pairs={{0,8},{1,9},{2,10},{3,11},{4,12},{5,13},{6,14},{7,15},{8,0},{9,1},... | collective-permute-start | bytes 393224 | tf_op jit(solution)/shard_map/ppermute | solution.py:564
  14.3 13.4 %collective-permute-start.2 = (f32[8,48,128]{2,1,0:T(8,128)S(1)}, f32[8,48,128]{2,1,0:T(8,128)S(1)}, u32[]{:S(2)}, u32[]{:S(2)}) collective-permute-start(f32[8,48,128]{2,1,0:T(8,128)S(1)} %get-tuple-element.60), channel_id=1, source_target_pairs={{0,16},{1,17},{2,18},{3,19},{4,20},{5,21},{6,22},{7,23},{8,24},{9,... | collective-permute-start | bytes 589832 | tf_op jit(solution)/shard_map/ppermute | solution.py:564
  14.6 13.1 %collective-permute-start.3 = (f32[8,40,128]{2,1,0:T(8,128)S(1)}, f32[8,40,128]{2,1,0:T(8,128)S(1)}, u32[]{:S(2)}, u32[]{:S(2)}) collective-permute-start(f32[8,40,128]{2,1,0:T(8,128)S(1)} %get-tuple-element.61), channel_id=1, source_target_pairs={{0,8},{1,9},{2,10},{3,11},{4,12},{5,13},{6,14},{7,15},{8,0},{9,1},... | collective-permute-start | bytes 491528 | tf_op jit(solution)/shard_map/ppermute | solution.py:564
  24.9 9.7 %collective-permute-start.7 = (f32[8,40,128]{2,1,0:T(8,128)S(1)}, f32[8,40,128]{2,1,0:T(8,128)S(1)}, u32[]{:S(2)}, u32[]{:S(2)}) collective-permute-start(f32[8,40,128]{2,1,0:T(8,128)S(1)} %get-tuple-element.67), channel_id=1, source_target_pairs={{0,8},{1,9},{2,10},{3,11},{4,12},{5,13},{6,14},{7,15},{8,0},{9,1},... | collective-permute-start | bytes 491528 | tf_op jit(solution)/shard_map/ppermute | solution.py:564
  25.0 5.7 %collective-permute-start.8 = (f32[8,32,128]{2,1,0:T(8,128)S(1)}, f32[8,32,128]{2,1,0:T(8,128)S(1)}, u32[]{:S(2)}, u32[]{:S(2)}) collective-permute-start(f32[8,32,128]{2,1,0:T(8,128)S(1)} %get-tuple-element.69), channel_id=1, source_target_pairs={{0,2},{1,3},{2,0},{3,1},{4,6},{5,7},{6,4},{7,5},{8,10},{9,11},{10,... | collective-permute-start | bytes 393224 | tf_op jit(solution)/shard_map/ppermute | solution.py:564
  28.4 9.0 %collective-permute-start.10 = (f32[8,40,128]{2,1,0:T(8,128)S(1)}, f32[8,40,128]{2,1,0:T(8,128)S(1)}, u32[]{:S(2)}, u32[]{:S(2)}) collective-permute-start(f32[8,40,128]{2,1,0:T(8,128)S(1)} %get-tuple-element.72), channel_id=1, source_target_pairs={{0,2},{1,3},{2,0},{3,1},{4,6},{5,7},{6,4},{7,5},{8,10},{9,11},{10,... | collective-permute-start | bytes 491528 | tf_op jit(solution)/shard_map/ppermute | solution.py:564
  30.0 7.5 %collective-permute-start.6 = (f32[8,32,128]{2,1,0:T(8,128)S(1)}, f32[8,32,128]{2,1,0:T(8,128)S(1)}, u32[]{:S(2)}, u32[]{:S(2)}) collective-permute-start(f32[8,32,128]{2,1,0:T(8,128)S(1)} %get-tuple-element.66), channel_id=1, source_target_pairs={{0,8},{1,9},{2,10},{3,11},{4,12},{5,13},{6,14},{7,15},{8,0},{9,1},... | collective-permute-start | bytes 393224 | tf_op jit(solution)/shard_map/ppermute | solution.py:564
  35.4 6.7 %collective-permute-start.12 = (f32[8,40,128]{2,1,0:T(8,128)S(1)}, f32[8,40,128]{2,1,0:T(8,128)S(1)}, u32[]{:S(2)}, u32[]{:S(2)}) collective-permute-start(f32[8,40,128]{2,1,0:T(8,128)S(1)} %get-tuple-element.75), channel_id=1, source_target_pairs={{0,2},{1,3},{2,0},{3,1},{4,6},{5,7},{6,4},{7,5},{8,10},{9,11},{10,... | collective-permute-start | bytes 491528 | tf_op jit(solution)/shard_map/ppermute | solution.py:564
  36.9 5.2 %collective-permute-start.9 = (f32[8,16,128]{2,1,0:T(8,128)S(1)}, f32[8,16,128]{2,1,0:T(8,128)S(1)}, u32[]{:S(2)}, u32[]{:S(2)}) collective-permute-start(f32[8,16,128]{2,1,0:T(8,128)S(1)} %get-tuple-element.70), channel_id=1, source_target_pairs={{0,8},{1,9},{2,10},{3,11},{4,12},{5,13},{6,14},{7,15},{8,0},{9,1},... | collective-permute-start | bytes 196616 | tf_op jit(solution)/shard_map/ppermute | solution.py:564
  38.1 6.2 %collective-permute-start.11 = (f32[8,32,128]{2,1,0:T(8,128)S(1)}, f32[8,32,128]{2,1,0:T(8,128)S(1)}, u32[]{:S(2)}, u32[]{:S(2)}) collective-permute-start(f32[8,32,128]{2,1,0:T(8,128)S(1)} %get-tuple-element.73), channel_id=1, source_target_pairs={{0,2},{1,3},{2,0},{3,1},{4,6},{5,7},{6,4},{7,5},{8,10},{9,11},{10,... | collective-permute-start | bytes 393224 | tf_op jit(solution)/shard_map/ppermute | solution.py:564
  42.7 4.3 %collective-permute-start.13 = (f32[8,16,128]{2,1,0:T(8,128)S(1)}, f32[8,16,128]{2,1,0:T(8,128)S(1)}, u32[]{:S(2)}, u32[]{:S(2)}) collective-permute-start(f32[8,16,128]{2,1,0:T(8,128)S(1)} %get-tuple-element.76), channel_id=1, source_target_pairs={{0,2},{1,3},{2,0},{3,1},{4,6},{5,7},{6,4},{7,5},{8,10},{9,11},{10,... | collective-permute-start | bytes 196616 | tf_op jit(solution)/shard_map/ppermute | solution.py:564
  47.9 10.1 %collective-permute-start.16 = (f32[2,5,4,8,128]{4,3,2,1,0:T(8,128)S(1)}, f32[2,5,4,8,128]{4,3,2,1,0:T(8,128)S(1)}, u32[]{:S(2)}, u32[]{:S(2)}) collective-permute-start(f32[2,5,4,8,128]{4,3,2,1,0:T(8,128)S(1)} %get-tuple-element.91), channel_id=1, source_target_pairs={{0,16},{16,0},{1,17},{17,1},{2,18},{18,2},{3,19},{19,3},{4,20},{20... | collective-permute-start | bytes 491528 | tf_op jit(solution)/shard_map/ppermute | solution.py:696
  48.0 7.6 %collective-permute-start.18 = (f32[5,32,128]{2,1,0:T(8,128)S(1)}, f32[5,32,128]{2,1,0:T(8,128)S(1)}, u32[]{:S(2)}, u32[]{:S(2)}) collective-permute-start(f32[5,32,128]{2,1,0:T(8,128)S(1)} %get-tuple-element.92.z_lo), channel_id=1, source_target_pairs={{0,3},{1,0},{2,1},{3,2},{4,7},{5,4},{6,5},{7,6},{8,11},{9,8},{10,9... | collective-permute-start | bytes 245768 | tf_op jit(solution)/shard_map/ppermute | solution.py:696
  48.0 7.5 %collective-permute-start.17 = (f32[5,32,128]{2,1,0:T(8,128)S(1)}, f32[5,32,128]{2,1,0:T(8,128)S(1)}, u32[]{:S(2)}, u32[]{:S(2)}) collective-permute-start(f32[5,32,128]{2,1,0:T(8,128)S(1)} %get-tuple-element.93.z_hi), channel_id=1, source_target_pairs={{0,1},{1,2},{2,3},{3,0},{4,5},{5,6},{6,7},{7,4},{8,9},{9,10},{10,1... | collective-permute-start | bytes 245768 | tf_op jit(solution)/shard_map/ppermute | solution.py:696
  48.5 10.4 %collective-permute-start.15 = (f32[5,4,8,128]{3,2,1,0:T(8,128)S(1)}, f32[5,4,8,128]{3,2,1,0:T(8,128)S(1)}, u32[]{:S(2)}, u32[]{:S(2)}) collective-permute-start(f32[5,4,8,128]{3,2,1,0:T(8,128)S(1)} %get-tuple-element.89.y_lo), channel_id=1, source_target_pairs={{0,12},{4,0},{8,4},{12,8},{1,13},{5,1},{9,5},{13,9},{2,14},{6,2},{... | collective-permute-start | bytes 245768 | tf_op jit(solution)/shard_map/ppermute | solution.py:696
  55.6 6.6 %collective-permute-start.14 = (f32[5,4,8,128]{3,2,1,0:T(8,128)S(1)}, f32[5,4,8,128]{3,2,1,0:T(8,128)S(1)}, u32[]{:S(2)}, u32[]{:S(2)}) collective-permute-start(f32[5,4,8,128]{3,2,1,0:T(8,128)S(1)} %get-tuple-element.90.y_hi), channel_id=1, source_target_pairs={{0,4},{4,8},{8,12},{12,0},{1,5},{5,9},{9,13},{13,1},{2,6},{6,10},{... | collective-permute-start | bytes 245768 | tf_op jit(solution)/shard_map/ppermute | solution.py:696
  64.6 8.1 %collective-permute-start.21 = (f32[2,5,4,8,128]{4,3,2,1,0:T(8,128)S(1)}, f32[2,5,4,8,128]{4,3,2,1,0:T(8,128)S(1)}, u32[]{:S(2)}, u32[]{:S(2)}) collective-permute-start(f32[2,5,4,8,128]{4,3,2,1,0:T(8,128)S(1)} %get-tuple-element.98), channel_id=1, source_target_pairs={{0,16},{16,0},{1,17},{17,1},{2,18},{18,2},{3,19},{19,3},{4,20},{20... | collective-permute-start | bytes 491528 | tf_op jit(solution)/shard_map/ppermute | solution.py:696
  65.9 2.5 %collective-permute-start.23 = (f32[5,32,128]{2,1,0:T(8,128)S(1)}, f32[5,32,128]{2,1,0:T(8,128)S(1)}, u32[]{:S(2)}, u32[]{:S(2)}) collective-permute-start(f32[5,32,128]{2,1,0:T(8,128)S(1)} %get-tuple-element.99.z_lo), channel_id=1, source_target_pairs={{0,3},{1,0},{2,1},{3,2},{4,7},{5,4},{6,5},{7,6},{8,11},{9,8},{10,9... | collective-permute-start | bytes 245768 | tf_op jit(solution)/shard_map/ppermute | solution.py:696
  65.9 4.4 %collective-permute-start.22 = (f32[5,32,128]{2,1,0:T(8,128)S(1)}, f32[5,32,128]{2,1,0:T(8,128)S(1)}, u32[]{:S(2)}, u32[]{:S(2)}) collective-permute-start(f32[5,32,128]{2,1,0:T(8,128)S(1)} %get-tuple-element.100.z_hi), channel_id=1, source_target_pairs={{0,1},{1,2},{2,3},{3,0},{4,5},{5,6},{6,7},{7,4},{8,9},{9,10},{10,1... | collective-permute-start | bytes 245768 | tf_op jit(solution)/shard_map/ppermute | solution.py:696
  66.4 7.3 %collective-permute-start.20 = (f32[5,4,8,128]{3,2,1,0:T(8,128)S(1)}, f32[5,4,8,128]{3,2,1,0:T(8,128)S(1)}, u32[]{:S(2)}, u32[]{:S(2)}) collective-permute-start(f32[5,4,8,128]{3,2,1,0:T(8,128)S(1)} %get-tuple-element.96.y_lo), channel_id=1, source_target_pairs={{0,12},{4,0},{8,4},{12,8},{1,13},{5,1},{9,5},{13,9},{2,14},{6,2},{... | collective-permute-start | bytes 245768 | tf_op jit(solution)/shard_map/ppermute | solution.py:696
  67.2 6.9 %collective-permute-start.19 = (f32[5,4,8,128]{3,2,1,0:T(8,128)S(1)}, f32[5,4,8,128]{3,2,1,0:T(8,128)S(1)}, u32[]{:S(2)}, u32[]{:S(2)}) collective-permute-start(f32[5,4,8,128]{3,2,1,0:T(8,128)S(1)} %get-tuple-element.97.y_hi), channel_id=1, source_target_pairs={{0,4},{4,8},{8,12},{12,0},{1,5},{5,9},{9,13},{13,1},{2,6},{6,10},{... | collective-permute-start | bytes 245768 | tf_op jit(solution)/shard_map/ppermute | solution.py:696

commit v4 on v3

--- a/solution.py
+++ b/solution.py
@@ -204,23 +204,27 @@
         self.pad = 2 * self.halves
 
     def at(self, f, row):
-        start = SUB + (f * self.rows + row) * SUB
+        start = (f * self.rows + row) * SUB
         return pl.ds(start if isinstance(start, int) else pl.multiple_of(start, SUB), SUB)
 
     def across(self, f, slab, sub):
-        return pl.ds(SUB + (f * self.rows + slab * SUB) * SUB + sub, SUB, stride=SUB)
-
-    def beside(self, f, row, step):
-        return pl.ds(SUB + (f * self.rows + row) * SUB + step, SUB)
+        return pl.ds((f * self.rows + slab * SUB) * SUB + sub, SUB, stride=SUB)
 
     def grid(self):
-        return jax.ShapeDtypeStruct(((NF * self.rows + 2) * SUB, LANES), f32)
+        return jax.ShapeDtypeStruct((NF * self.rows * SUB, LANES), f32)
 
     def faces(self):
         x = jax.ShapeDtypeStruct((2, NF, self.pad, SUB, LANES), f32)
         y = jax.ShapeDtypeStruct((NF, self.edge // self.fit, SUB, LANES), f32)
         z = jax.ShapeDtypeStruct((NF, self.rows, LANES), f32)
         return [x, y, y, z, z]
+
+
+def in_turn(count, *phases):
+    for step in range(count + len(phases) - 1):
+        for late, phase in enumerate(phases):
+            if 0 <= step - late < count:
+                phase(step - late)
 
 
 def send_slab(shape, prim, y_lo, y_hi, z_lo, z_hi, slab):
@@ -293,8 +297,8 @@
 def sweep_z_kernel(prim, z_lo, z_hi, z_prev, z_next, total, flux_z, right_z, left, right, flux, *, shape):
     edge, rows = shape.edge, shape.rows
 
-    def ghost(a, carry):
-        at = pl.ds(pl.multiple_of(a * SUB, SUB), SUB)
+    def ghost(a):
+        at = pl.ds(a * SUB, SUB)
         low = [z_lo[f, at, :] for f in FIELDS]
         high = [z_hi[f, at, :] for f in FIELDS]
         prev = [z_prev[f, at, :] for f in FIELDS]
@@ -311,9 +315,7 @@
         for f in FIELDS:
             flux_z[f, at, :] = lane_roll(fluxes[f], edge - 1)
             right_z[f, at, :] = over[f]
-        return carry
-
-    lax.fori_loop(0, shape.slabs, ghost, 0)
+
     lane = lane_of()
     z_of = lax.rem(lane, edge)
     sub = sub_of()
@@ -325,50 +327,39 @@
     def insert(ref, f, row):
         return jnp.broadcast_to(ref[f, pl.ds(row, 1), :], (SUB, LANES))
 
-    def up(ref, value, f, row, ghosts):
-        across = ref[shape.beside(f, row, 1), :]
-        across = jnp.where(last_sub, insert(ghosts, f, row), across)
+    def up(value, f, row, ghosts):
+        across = jnp.where(last_sub, insert(ghosts, f, row), pltpu.roll(value, SUB - 1, 0))
         return jnp.take_along_axis(jnp.where(first_z, across, value), higher, axis=1)
 
-    def down(ref, value, f, row, ghosts):
-        across = ref[shape.beside(f, row, -1), :]
-        across = jnp.where(first_sub, insert(ghosts, f, row), across)
+    def down(value, f, row, ghosts):
+        across = jnp.where(first_sub, insert(ghosts, f, row), pltpu.roll(value, 1, 0))
         return jnp.take_along_axis(jnp.where(last_z, across, value), lower, axis=1)
 
-    def slopes(slab, carry):
-        for i in range(SUB):
-            row = slab * SUB + i
+    def slopes(slab):
+        ghost(slab)
+        for row in range(slab * SUB, (slab + 1) * SUB):
             for f in FIELDS:
                 at = shape.at(f, row)
                 mine = prim[at, :]
-                shift = half_minmod(
-                    mine - down(prim, mine, f, row, z_prev), up(prim, mine, f, row, z_next) - mine
-                )
+                shift = half_minmod(mine - down(mine, f, row, z_prev), up(mine, f, row, z_next) - mine)
                 left[at, :] = mine + shift
                 right[at, :] = mine - shift
-        return carry
-
-    def fluxes(slab, carry):
-        for i in range(SUB):
-            row = slab * SUB + i
+
+    def fluxes(slab):
+        for row in range(slab * SUB, (slab + 1) * SUB):
             lefts = [left[shape.at(f, row), :] for f in FIELDS]
-            rights = [up(right, right[shape.at(f, row), :], f, row, right_z) for f in FIELDS]
+            rights = [up(right[shape.at(f, row), :], f, row, right_z) for f in FIELDS]
             for f, value in enumerate(twice_flux(lefts, rights, 2)):
                 flux[shape.at(f, row), :] = value
-        return carry
-
-    def differences(slab, carry):
-        for i in range(SUB):
-            row = slab * SUB + i
+
+    def differences(slab):
+        for row in range(slab * SUB, (slab + 1) * SUB):
             for f in FIELDS:
                 at = shape.at(f, row)
                 mine = flux[at, :]
-                total[at, :] = mine - down(flux, mine, f, row, flux_z)
-        return carry
-
-    lax.fori_loop(0, shape.slabs, slopes, 0)
-    lax.fori_loop(0, shape.slabs, fluxes, 0)
-    lax.fori_loop(0, shape.slabs, differences, 0)
+                total[at, :] = mine - down(mine, f, row, flux_z)
+
+    in_turn(shape.slabs, slopes, fluxes, differences)
 
 
 def sweep_x_kernel(prim, x_faces, sofar, total, wide, *, shape):
@@ -413,7 +404,7 @@
     lane = lane_of()
     upper = lax.rem(lane, width) >= edge
 
-    def ghost(q, carry):
+    def prepare(q):
         low = [y_lo[f, q] for f in FIELDS]
         high = [y_hi[f, q] for f in FIELDS]
         below = [y_prev[f, q] for f in FIELDS]
@@ -429,9 +420,7 @@
         for f in FIELDS:
             ghost_prim[f, q] = jnp.where(upper, below[f], after[f])
             ghost_flux[f, q] = jnp.where(upper, fluxes[f], over[f])
-        return carry
-
-    lax.fori_loop(0, edge // fit, ghost, 0)
+
     top_lanes = lane >= LANES - edge
     low_lanes = lane < edge
 
@@ -449,7 +438,8 @@
         for k in range(fit):
             yield -(width * k + edge), (q * fit + k) * halves
 
-    def slopes(q, carry):
+    def slopes(q):
+        prepare(q)
         for turn, base in each(q):
             for f in FIELDS:
                 mine = [prim[shape.at(f, base + h), :] for h in range(halves)]
@@ -459,9 +449,8 @@
                     shift = half_minmod(mine[h] - under[h], over[h] - mine[h])
                     left[shape.at(f, base + h), :] = mine[h] + shift
                     right[shape.at(f, base + h), :] = mine[h] - shift
-        return carry
-
-    def fluxes(q, carry):
+
+    def fluxes(q):
         for turn, base in each(q):
             rights = []
             for f in FIELDS:
@@ -474,9 +463,8 @@
                 result = twice_flux(lefts, [rights[f][h] for f in FIELDS], 1)
                 for f in FIELDS:
                     flux[shape.at(f, base + h), :] = result[f]
-        return carry
-
-    def differences(q, carry):
+
+    def differences(q):
         for turn, base in each(q):
             total = [[None] * NF for _ in range(halves)]
             for f in FIELDS:
@@ -486,12 +474,8 @@
                     total[h][f] = sofar[shape.at(f, base + h), :] + (mine[h] - under[h])
             for h in range(halves):
                 finish(base + h, total[h])
-        after_slab(q)
-        return carry
-
-    lax.fori_loop(0, edge // fit, slopes, 0)
-    lax.fori_loop(0, edge // fit, fluxes, 0)
-    lax.fori_loop(0, edge // fit, differences, 0)
+
+    in_turn(edge // fit, slopes, fluxes, differences, after_slab)
 
 
 def sweep_y_one_kernel(field, prim, y_lo, y_hi, y_prev, y_next, sofar, *refs, shape):
@@ -550,8 +534,8 @@
     groups = slots // SUB
     shape = Shape(rows, edge)
     units = NF * shape.slabs
-    pieces = split_units(units, (4, 5, 5, 4, 2))
-    firsts = split_units(units, (4, 5, 5, 6))
+    pieces = split_units(units, (3, 5, 4, 3, 3, 2))
+    firsts = split_units(units, (3, 5, 7, 5))
 
     bit_z = size_z.bit_length() - 2
     bit_y = bit_z + size_y.bit_length() - 1
@@ -647,8 +631,9 @@
         ([(1, 2), (2, 0)], [], []),
         ([(1, 3), (2, 1)], [], []),
         ([(1, 4), (2, 2)], [], [0]),
-        ([(2, 3)], [], [1]),
+        ([(1, 5), (2, 3)], [], [1]),
         ([(2, 4)], [], [2]),
+        ([(2, 5)], [], [3]),
     ]
     got[0][0] = swapped(sent[0], 0)
     got[0][1] = swapped(sent[1], 0)
@@ -666,7 +651,7 @@
     face_x, face_y, _, face_z, _ = shape.faces()
     part = [grid, grid, face_y, face_y, face_z, face_z, face_x]
     canvas = jax.ShapeDtypeStruct((NF * groups, rows * SUB, LANES), f32)
-    full = pieces[-1][0] // NF
+    full = pieces[-2][0] // NF
 
     def assemble(slabs, before):
         first = not before

time: 78.2 us -> 74.7 us (0.955)
  waiting for transfers between devices: 24.1 us -> 20.8 us
  Pallas kernels: 22.9 us -> 19.6 us
  starting transfers between devices: 30.8 us -> 33.9 us
    ppermute x14 -> x16, waiting for transfers between devices: 18.7 us -> 14.5 us  [swapped(): return lax.ppermute(value, AXES, pairs)]
    ppermute x14 -> x16, starting transfers between devices: 19.3 us -> 22.9 us  [swapped(): return lax.ppermute(value, AXES, pairs)]
    pallas_call x2, Pallas kernels: 4.76 us -> 3.08 us  [flux_sums(): pl.pallas_call(functools.partial(sweep_z_kernel, shape=shape), out_shape=...]
    pallas_call x1, Pallas kernels: 2.46 us -> 1.27 us  [shards(): pl.pallas_call(functools.partial(sweep_y_one_kernel, shape=shape), out_sh...]
    pallas_call x1, Pallas kernels: 3.95 us -> 2.92 us  [shards(): pl.pallas_call(functools.partial(sweep_y_two_kernel, shape=shape, occ=occ...]
    ppermute x10, waiting for transfers between devices: 5.39 us -> 6.33 us  [ring(): lax.ppermute(value, axis, [(i, (i + step) % size) for i in range(size)])]
    pallas_call x7 -> x8, Pallas kernels: 4.67 us -> 5.37 us  [make(): pl.pallas_call(functools.partial(pick_kernel, plan=plan, held=tuple(found...]
  transfers between devices with their start and end apart: 24 -> 26, of which waited for: 11 -> 13; matrix products, arithmetic and copies ran while one was open for 0% -> 0% of each run, Pallas kernels for 18% -> 18%
where the time goes in v4:
time: 74.7 us; the launch traced here: 74.6 us
  starting transfers between devices  33.9 us (45%)
  waiting for transfers between devices  20.8 us (28%)
  Pallas kernels  19.6 us (26%)
    ppermute x16, starting transfers between devices, swapped(): return lax.ppermute(value, AXES, pairs)  22.9 us
    ppermute x16, waiting for transfers between devices, swapped(): return lax.ppermute(value, AXES, pairs)  14.5 us
    ppermute x10, starting transfers between devices, ring(): lax.ppermute(value, axis, [(i, (i + step) % size) for i in range(size)])  11 us
    ppermute x10, waiting for transfers between devices, ring(): lax.ppermute(value, axis, [(i, (i + step) % size) for i in range(size)])  6.33 us
    pallas_call x8, Pallas kernels, make(): pl.pallas_call(functools.partial(pick_kernel, plan=plan, held=tuple(found...  5.37 us
    pallas_call x2, Pallas kernels, flux_sums(): pl.pallas_call(functools.partial(sweep_z_kernel, shape=shape), out_shape=...  3.08 us
    pallas_call x1, Pallas kernels, shards(): pl.pallas_call(functools.partial(sweep_y_two_kernel, shape=shape, occ=occ...  2.92 us
    pallas_call x2, Pallas kernels, assemble(): pl.pallas_call(functools.partial(assemble_kernel, held=tuple(found), slab...  2.36 us
  transfers between devices with their start and end apart: 26, of which 13 were waited for; matrix products, arithmetic and copies ran while one was open for 0% of the time, Pallas kernels for 18%

profile of v4, /device:TPU:0, one launch (start us, length us, event | category | flops | bytes accessed | tf_op | source)
XLA Modules:
  0.0 74.6 jit_solution(12012622880939517904)
XLA Ops:
  0.0 1.2 %pack_first.1 = f32[8,24,128]{2,1,0:T(8,128)S(1)} custom-call(s32[3,1,8]{2,1,0:T(1,128)} %send_hbm.1, f32[5120,128]{1,0:T(8,128)} %bitcast.10), custom_call_target="tpu_custom_call" | custom-call | tf_op jit(solution)/shard_map/pack_first/pallas_call | solution.py:567
  1.3 3.0 %collective-permute-start.1 = (f32[8,24,128]{2,1,0:T(8,128)S(1)}, f32[8,24,128]{2,1,0:T(8,128)S(1)}, u32[]{:S(2)}, u32[]{:S(2)}) collective-permute-start(f32[8,24,128]{2,1,0:T(8,128)S(1)} %pack_first.1), channel_id=1, source_target_pairs={{0,16},{1,17},{2,18},{3,19},{4,20},{5,21},{6,22},{7,23},{8,24},{9,... | collective-permute-start | bytes 294920 | tf_op jit(solution)/shard_map/ppermute | solution.py:548
  4.3 0.1 dynamic_slice.3.own
  4.4 1.4 %pack_rest.1 = (s32[24]{0:T(128)S(1)}, f32[8,128]{1,0:T(8,128)S(1)}, f32[8,40,128]{2,1,0:T(8,128)S(1)}, f32[8,56,128]{2,1,0:T(8,128)S(1)}, f32[8,40,128]{2,1,0:T(8,128)S(1)}) custom-call(s32[3,1,8]{2,1,0:T(1,128)S(1)} %copy-done.1, s32[3,1,8]{2,1,0:T(1,128)S(1)} %copy-done.2, s32[8]{0:T(128)S(1)} %dynamic_slice.3.own, f32[5120,128]{1,0:T(8,128)S(1)} %bitcast.11), custom_call_target="tpu_custom_call" | custom-call | tf_op jit(solution)/shard_map/pack_rest/pallas_call | solution.py:580
  5.8 0.6 collective-permute-start
  6.4 0.7 collective-permute-done.1.refs_0_.refs_1_
  7.1 0.6 pick_10.1
  7.7 2.0 %collective-permute-start.3 = (f32[8,56,128]{2,1,0:T(8,128)S(1)}, f32[8,56,128]{2,1,0:T(8,128)S(1)}, u32[]{:S(2)}, u32[]{:S(2)}) collective-permute-start(f32[8,56,128]{2,1,0:T(8,128)S(1)} %get-tuple-element.65), channel_id=1, source_target_pairs={{0,16},{1,17},{2,18},{3,19},{4,20},{5,21},{6,22},{7,23},{8,24},{9,... | collective-permute-start | bytes 688136 | tf_op jit(solution)/shard_map/ppermute | solution.py:548
  9.7 2.6 %collective-permute-start.4 = (f32[8,24,128]{2,1,0:T(8,128)S(1)}, f32[8,24,128]{2,1,0:T(8,128)S(1)}, u32[]{:S(2)}, u32[]{:S(2)}) collective-permute-start(f32[8,24,128]{2,1,0:T(8,128)S(1)} %get-tuple-element.66), channel_id=1, source_target_pairs={{0,8},{1,9},{2,10},{3,11},{4,12},{5,13},{6,14},{7,15},{8,0},{9,1},... | collective-permute-start | bytes 294920 | tf_op jit(solution)/shard_map/ppermute | solution.py:548
  12.3 0.7 collective-permute-done.refs_0_.refs_1_
  13.0 0.6 pick_11.1
  13.6 2.7 %collective-permute-start.6 = (f32[8,40,128]{2,1,0:T(8,128)S(1)}, f32[8,40,128]{2,1,0:T(8,128)S(1)}, u32[]{:S(2)}, u32[]{:S(2)}) collective-permute-start(f32[8,40,128]{2,1,0:T(8,128)S(1)} %get-tuple-element.69), channel_id=1, source_target_pairs={{0,8},{1,9},{2,10},{3,11},{4,12},{5,13},{6,14},{7,15},{8,0},{9,1},... | collective-permute-start | bytes 491528 | tf_op jit(solution)/shard_map/ppermute | solution.py:548
  16.3 0.5 collective-permute-start.2
  16.8 2.0 %collective-permute-done.4.refs_2_.refs_3_ = f32[8,24,128]{2,1,0:T(8,128)S(1)} collective-permute-done((f32[8,24,128]{2,1,0:T(8,128)S(1)}, f32[8,24,128]{2,1,0:T(8,128)S(1)}, u32[]{:S(2)}, u32[]{:S(2)}) %collective-permute-start.4) | collective-permute-done | bytes 98336 | tf_op jit(solution)/shard_map/ppermute | solution.py:548
  18.8 0.0 collective-permute-done.3.refs_0_.refs_1_.refs_2_
  18.8 0.7 pick_12_20.1
  19.5 1.7 %collective-permute-start.5 = (f32[8,32,128]{2,1,0:T(8,128)S(1)}, f32[8,32,128]{2,1,0:T(8,128)S(1)}, u32[]{:S(2)}, u32[]{:S(2)}) collective-permute-start(f32[8,32,128]{2,1,0:T(8,128)S(1)} %get-tuple-element.68), channel_id=1, source_target_pairs={{0,8},{1,9},{2,10},{3,11},{4,12},{5,13},{6,14},{7,15},{8,0},{9,1},... | collective-permute-start | bytes 393224 | tf_op jit(solution)/shard_map/ppermute | solution.py:548
  21.3 1.5 %collective-permute-start.7 = (f32[8,24,128]{2,1,0:T(8,128)S(1)}, f32[8,24,128]{2,1,0:T(8,128)S(1)}, u32[]{:S(2)}, u32[]{:S(2)}) collective-permute-start(f32[8,24,128]{2,1,0:T(8,128)S(1)} %get-tuple-element.72), channel_id=1, source_target_pairs={{0,2},{1,3},{2,0},{3,1},{4,6},{5,7},{6,4},{7,5},{8,10},{9,11},{10,... | collective-permute-start | bytes 294920 | tf_op jit(solution)/shard_map/ppermute | solution.py:548
  22.8 2.7 %collective-permute-done.6.refs_2_.refs_4_ = f32[8,40,128]{2,1,0:T(8,128)S(1)} collective-permute-done((f32[8,40,128]{2,1,0:T(8,128)S(1)}, f32[8,40,128]{2,1,0:T(8,128)S(1)}, u32[]{:S(2)}, u32[]{:S(2)}) %collective-permute-start.6) | collective-permute-done | bytes 163872 | tf_op jit(solution)/shard_map/ppermute | solution.py:548
  25.5 0.7 pick_13_21.1
  26.2 1.6 %collective-permute-start.10 = (f32[8,40,128]{2,1,0:T(8,128)S(1)}, f32[8,40,128]{2,1,0:T(8,128)S(1)}, u32[]{:S(2)}, u32[]{:S(2)}) collective-permute-start(f32[8,40,128]{2,1,0:T(8,128)S(1)} %get-tuple-element.76), channel_id=1, source_target_pairs={{0,2},{1,3},{2,0},{3,1},{4,6},{5,7},{6,4},{7,5},{8,10},{9,11},{10,... | collective-permute-start | bytes 491528 | tf_op jit(solution)/shard_map/ppermute | solution.py:548
  27.8 0.0 collective-permute-start.9
  27.8 0.0 collective-permute-done.5.refs_2_.refs_5_
  27.8 0.7 pick_14_22.1
  28.5 1.3 %collective-permute-start.12 = (f32[8,32,128]{2,1,0:T(8,128)S(1)}, f32[8,32,128]{2,1,0:T(8,128)S(1)}, u32[]{:S(2)}, u32[]{:S(2)}) collective-permute-start(f32[8,32,128]{2,1,0:T(8,128)S(1)} %get-tuple-element.79), channel_id=1, source_target_pairs={{0,2},{1,3},{2,0},{3,1},{4,6},{5,7},{6,4},{7,5},{8,10},{9,11},{10,... | collective-permute-start | bytes 393224 | tf_op jit(solution)/shard_map/ppermute | solution.py:548
  29.8 2.2 %collective-permute-start.8 = (f32[8,24,128]{2,1,0:T(8,128)S(1)}, f32[8,24,128]{2,1,0:T(8,128)S(1)}, u32[]{:S(2)}, u32[]{:S(2)}) collective-permute-start(f32[8,24,128]{2,1,0:T(8,128)S(1)} %get-tuple-element.73), channel_id=1, source_target_pairs={{0,8},{1,9},{2,10},{3,11},{4,12},{5,13},{6,14},{7,15},{8,0},{9,1},... | collective-permute-start | bytes 294920 | tf_op jit(solution)/shard_map/ppermute | solution.py:548
  32.0 2.6 %collective-permute-done.9.refs_2_.refs_6_ = f32[8,24,128]{2,1,0:T(8,128)S(1)} collective-permute-done((f32[8,24,128]{2,1,0:T(8,128)S(1)}, f32[8,24,128]{2,1,0:T(8,128)S(1)}, u32[]{:S(2)}, u32[]{:S(2)}) %collective-permute-start.9) | collective-permute-done | bytes 98336 | tf_op jit(solution)/shard_map/ppermute | solution.py:548
  34.7 0.0 collective-permute-done.10.refs_4_
  34.7 0.7 pick_15_23.1
  35.4 0.6 collective-permute-start.14
  36.0 1.9 %collective-permute-done.8.refs_1_ = f32[8,24,128]{2,1,0:T(8,128)S(1)} collective-permute-done((f32[8,24,128]{2,1,0:T(8,128)S(1)}, f32[8,24,128]{2,1,0:T(8,128)S(1)}, u32[]{:S(2)}, u32[]{:S(2)}) %collective-permute-start.8) | collective-permute-done | bytes 98336 | tf_op jit(solution)/shard_map/ppermute | solution.py:548
  37.9 0.0 collective-permute-done.12.refs_3_
  37.9 0.6 pick_24.1
  38.5 1.1 %collective-permute-start.13 = (f32[8,24,128]{2,1,0:T(8,128)S(1)}, f32[8,24,128]{2,1,0:T(8,128)S(1)}, u32[]{:S(2)}, u32[]{:S(2)}) collective-permute-start(f32[8,24,128]{2,1,0:T(8,128)S(1)} %get-tuple-element.80), channel_id=1, source_target_pairs={{0,2},{1,3},{2,0},{3,1},{4,6},{5,7},{6,4},{7,5},{8,10},{9,11},{10,... | collective-permute-start | bytes 294920 | tf_op jit(solution)/shard_map/ppermute | solution.py:548
  39.6 2.6 %collective-permute-done.11.refs_1_.refs_2_ = f32[8,16,128]{2,1,0:T(8,128)S(1)} collective-permute-done((f32[8,16,128]{2,1,0:T(8,128)S(1)}, f32[8,16,128]{2,1,0:T(8,128)S(1)}, u32[]{:S(2)}, u32[]{:S(2)}) %collective-permute-start.11) | collective-permute-done | bytes 65568 | tf_op jit(solution)/shard_map/ppermute | solution.py:548
  42.2 0.0 collective-permute-done.14.refs_3_
  42.2 0.6 pick_25.1
  42.8 1.6 %collective-permute-start.15 = (f32[8,16,128]{2,1,0:T(8,128)S(1)}, f32[8,16,128]{2,1,0:T(8,128)S(1)}, u32[]{:S(2)}, u32[]{:S(2)}) collective-permute-start(f32[8,16,128]{2,1,0:T(8,128)S(1)} %get-tuple-element.83), channel_id=1, source_target_pairs={{0,2},{1,3},{2,0},{3,1},{4,6},{5,7},{6,4},{7,5},{8,10},{9,11},{10,... | collective-permute-start | bytes 196616 | tf_op jit(solution)/shard_map/ppermute | solution.py:548
  44.4 1.5 %assemble_0.1 = (f32[1280,128]{1,0:T(8,128)S(1)}, f32[1280,128]{1,0:T(8,128)S(1)}, f32[5,4,8,128]{3,2,1,0:T(8,128)S(1)}, f32[5,4,8,128]{3,2,1,0:T(8,128)S(1)}, f...) custom-call(s32[24]{0:T(128)S(1)} %get-tuple-element.58.tags, ...), custom_call_target="tpu_custom_call" | custom-call | tf_op jit(solution)/shard_map/assemble_0/pallas_call | solution.py:661
  45.9 1.2 %collective-permute-done.15.refs_4_ = f32[8,16,128]{2,1,0:T(8,128)S(1)} collective-permute-done((f32[8,16,128]{2,1,0:T(8,128)S(1)}, f32[8,16,128]{2,1,0:T(8,128)S(1)}, u32[]{:S(2)}, u32[]{:S(2)}) %collective-permute-start.15) | collective-permute-done | bytes 65568 | tf_op jit(solution)/shard_map/ppermute | solution.py:548
  47.1 0.0 collective-permute-done.13.refs_3_
  47.1 0.8 %assemble_3.1 = (f32[1280,128]{1,0:T(8,128)S(1)}, f32[1280,128]{1,0:T(8,128)S(1)}, f32[5,4,8,128]{3,2,1,0:T(8,128)S(1)}, f32[5,4,8,128]{3,2,1,0:T(8,128)S(1)}, f...) custom-call(s32[24]{0:T(128)S(1)} %get-tuple-element.58.tags, ...), custom_call_target="tpu_custom_call", output_to_operand_aliasing={{0}: (7, {}), {1}: (8, {}), {2}: (9, {}), {3}: (10, {}), {4... | custom-call | tf_op jit(solution)/shard_map/assemble_3/pallas_call | solution.py:661
  48.0 0.5 collective-permute-start.18
  48.5 0.0 collective-permute-start.20
  48.5 0.5 collective-permute-start.19
  49.0 5.9 %collective-permute-start.17 = (f32[5,4,8,128]{3,2,1,0:T(8,128)S(1)}, f32[5,4,8,128]{3,2,1,0:T(8,128)S(1)}, u32[]{:S(2)}, u32[]{:S(2)}) collective-permute-start(f32[5,4,8,128]{3,2,1,0:T(8,128)S(1)} %get-tuple-element.97.y_lo), channel_id=1, source_target_pairs={{0,12},{4,0},{8,4},{12,8},{1,13},{5,1},{9,5},{13,9},{2,14},{6,2},{... | collective-permute-start | bytes 245768 | tf_op jit(solution)/shard_map/ppermute | solution.py:681
  54.9 0.0 collective-permute-start.16
  54.9 1.5 %sweep_z.2.sofar = f32[1280,128]{1,0:T(8,128)S(1)} custom-call(f32[1280,128]{1,0:T(8,128)S(1)} %get-tuple-element.96.prim, f32[5,32,128]{2,1,0:T(8,128)S(1)} %get-tuple-element.100.z_lo, f32[5,32,128]{2,1,0:T(8,128)S(1)} %get-tuple-element.101.z_hi, f32[5,32,128]{2,1,0:T(8,128)S(1)} %collective-permute-done.19.z_prev, ...), custom_call_target="tpu_custom_call" | custom-call | tf_op jit(solution)/shard_map/sweep_z/pallas_call | solution.py:692
  56.5 0.0 collective-permute-done.18.x_faces
  56.5 1.0 %sweep_x.2.sofar = f32[1280,128]{1,0:T(8,128)S(1)} custom-call(f32[1280,128]{1,0:T(8,128)S(1)} %get-tuple-element.96.prim, f32[2,5,4,8,128]{4,3,2,1,0:T(8,128)S(1)} %collective-permute-done.18.x_faces, f32[1280,128]{1,0:T(8,128)S(1)} %sweep_z.2.sofar), custom_call_target="tpu_custom_call", output_to_operand_aliasing={{}: (2, {})} | custom-call | tf_op jit(solution)/shard_map/sweep_x/pallas_call | solution.py:701
  57.5 0.3 collective-permute-done.17.y_next
  57.8 3.7 %collective-permute-done.16.y_prev = f32[5,4,8,128]{3,2,1,0:T(8,128)S(1)} collective-permute-done((f32[5,4,8,128]{3,2,1,0:T(8,128)S(1)}, f32[5,4,8,128]{3,2,1,0:T(8,128)S(1)}, u32[]{:S(2)}, u32[]{:S(2)}) %collective-permute-start.16) | collective-permute-done | bytes 81952 | tf_op jit(solution)/shard_map/ppermute | solution.py:681
  61.5 1.3 %sweep_y_one.1 = (f32[1280,128]{1,0:T(8,128)S(1)}, f32[1280,128]{1,0:T(8,128)S(1)}, f32[2,5,4,8,128]{4,3,2,1,0:T(8,128)S(1)}, f32[5,4,8,128]{3,2,1,0:T(8,128)S(1...) custom-call(f32[1280,128]{1,0:T(8,128)S(1)} %get-tuple-element.95.field, ...), custom_call_target="tpu_custom_call" | custom-call | tf_op jit(solution)/shard_map/sweep_y_one/pallas_call | solution.py:717
  62.8 1.3 %collective-permute-start.23 = (f32[2,5,4,8,128]{4,3,2,1,0:T(8,128)S(1)}, f32[2,5,4,8,128]{4,3,2,1,0:T(8,128)S(1)}, u32[]{:S(2)}, u32[]{:S(2)}) collective-permute-start(f32[2,5,4,8,128]{4,3,2,1,0:T(8,128)S(1)} %get-tuple-element.106), channel_id=1, source_target_pairs={{0,16},{16,0},{1,17},{17,1},{2,18},{18,2},{3,19},{19,3},{4,20},{20... | collective-permute-start | bytes 491528 | tf_op jit(solution)/shard_map/ppermute | solution.py:681
  64.1 0.7 collective-permute-start.25
  64.8 0.6 collective-permute-start.22
  65.4 1.4 %collective-permute-start.21 = (f32[5,4,8,128]{3,2,1,0:T(8,128)S(1)}, f32[5,4,8,128]{3,2,1,0:T(8,128)S(1)}, u32[]{:S(2)}, u32[]{:S(2)}) collective-permute-start(f32[5,4,8,128]{3,2,1,0:T(8,128)S(1)} %get-tuple-element.105.y_hi), channel_id=1, source_target_pairs={{0,4},{4,8},{8,12},{12,0},{1,5},{5,9},{9,13},{13,1},{2,6},{6,10},{... | collective-permute-start | bytes 245768 | tf_op jit(solution)/shard_map/ppermute | solution.py:681
  66.8 0.8 %collective-permute-done.25.z_next = f32[5,32,128]{2,1,0:T(8,128)S(1)} collective-permute-done((f32[5,32,128]{2,1,0:T(8,128)S(1)}, f32[5,32,128]{2,1,0:T(8,128)S(1)}, u32[]{:S(2)}, u32[]{:S(2)}) %collective-permute-start.25) | collective-permute-done | bytes 81952 | tf_op jit(solution)/shard_map/ppermute | solution.py:681
  67.6 1.0 %collective-permute-done.24.z_prev = f32[5,32,128]{2,1,0:T(8,128)S(1)} collective-permute-done((f32[5,32,128]{2,1,0:T(8,128)S(1)}, f32[5,32,128]{2,1,0:T(8,128)S(1)}, u32[]{:S(2)}, u32[]{:S(2)}) %collective-permute-start.24) | collective-permute-done | bytes 81952 | tf_op jit(solution)/shard_map/ppermute | solution.py:681
  68.7 1.5 %sweep_z.3.sofar = f32[1280,128]{1,0:T(8,128)S(1)} custom-call(f32[1280,128]{1,0:T(8,128)S(1)} %get-tuple-element.103.prim, f32[5,32,128]{2,1,0:T(8,128)S(1)} %get-tuple-element.107.z_lo, f32[5,32,128]{2,1,0:T(8,128)S(1)} %get-tuple-element.108.z_hi, f32[5,32,128]{2,1,0:T(8,128)S(1)} %collective-permute-done.24.z_prev, ...), custom_call_target="tpu_custom_call" | custom-call | tf_op jit(solution)/shard_map/sweep_z/pallas_call | solution.py:692
  70.2 0.0 collective-permute-done.23.x_faces
  70.2 1.0 %sweep_x.3.sofar = f32[1280,128]{1,0:T(8,128)S(1)} custom-call(f32[1280,128]{1,0:T(8,128)S(1)} %get-tuple-element.103.prim, f32[2,5,4,8,128]{4,3,2,1,0:T(8,128)S(1)} %collective-permute-done.23.x_faces, f32[1280,128]{1,0:T(8,128)S(1)} %sweep_z.3.sofar), custom_call_target="tpu_custom_call", output_to_operand_aliasing={{}: (2, {})} | custom-call | tf_op jit(solution)/shard_map/sweep_x/pallas_call | solution.py:701
  71.2 0.4 collective-permute-done.21.y_prev
  71.7 2.9 %sweep_y_two.1 = (f32[20,256,128]{2,1,0:T(8,128)}, f32[20,256,128]{2,1,0:T(8,128)S(1)}) custom-call(s32[8]{0:T(128)S(1)} %dynamic_slice.3.own, f32[1280,128]{1,0:T(8,128)S(1)} %get-tuple-element.95.field, f32[1280,128]{1,0:T(8,128)S(1)} %get-tuple-element.102.one, f32[1280,128]{1,0:T(8,128)S(1)} %get-tuple-element.103.prim, ...), custom_call_target="tpu_custom_call", output_to_operand_aliasing={{1}: (9, {})} | custom-call | tf_op jit(solution)/shard_map/sweep_y_two/pallas_call | solution.py:728
  (15 shorter events, 0.0 us)
Async XLA Ops:
  0.0 4.4 %copy-start.1 = (s32[3,1,8]{2,1,0:T(1,128)S(1)}, s32[3,1,8]{2,1,0:T(1,128)}, u32[]{:S(2)}) copy-start(s32[3,1,8]{2,1,0:T(1,128)} %send_hbm.1) | copy-start | bytes 292
  0.0 4.4 %copy-start = (f32[32,5,4096]{2,0,1:T(8,128)S(1)}, f32[32,5,4096]{2,0,1:T(8,128)}, u32[]{:S(2)}) copy-start(f32[32,5,4096]{2,0,1:T(8,128)} %param.4) | copy-start | bytes 7864324
  0.0 4.3 %copy-start.3 = (s32[256]{0:T(256)S(1)}, s32[256]{0:T(256)}, u32[]{:S(2)}) copy-start(s32[256]{0:T(256)} %param.7) | copy-start | bytes 3076
  0.0 4.4 %copy-start.2 = (s32[3,1,8]{2,1,0:T(1,128)S(1)}, s32[3,1,8]{2,1,0:T(1,128)}, u32[]{:S(2)}) copy-start(s32[3,1,8]{2,1,0:T(1,128)} %recv.1) | copy-start | bytes 292
  1.3 5.8 %collective-permute-start.1 = (f32[8,24,128]{2,1,0:T(8,128)S(1)}, f32[8,24,128]{2,1,0:T(8,128)S(1)}, u32[]{:S(2)}, u32[]{:S(2)}) collective-permute-start(f32[8,24,128]{2,1,0:T(8,128)S(1)} %pack_first.1), channel_id=1, source_target_pairs={{0,16},{1,17},{2,18},{3,19},{4,20},{5,21},{6,22},{7,23},{8,24},{9,... | collective-permute-start | bytes 294920 | tf_op jit(solution)/shard_map/ppermute | solution.py:548
  5.8 7.2 %collective-permute-start = (f32[8,40,128]{2,1,0:T(8,128)S(1)}, f32[8,40,128]{2,1,0:T(8,128)S(1)}, u32[]{:S(2)}, u32[]{:S(2)}) collective-permute-start(f32[8,40,128]{2,1,0:T(8,128)S(1)} %get-tuple-element.59), channel_id=1, source_target_pairs={{0,16},{1,17},{2,18},{3,19},{4,20},{5,21},{6,22},{7,23},{8,24},{9,... | collective-permute-start | bytes 491528 | tf_op jit(solution)/shard_map/ppermute | solution.py:548
  7.7 11.1 %collective-permute-start.3 = (f32[8,56,128]{2,1,0:T(8,128)S(1)}, f32[8,56,128]{2,1,0:T(8,128)S(1)}, u32[]{:S(2)}, u32[]{:S(2)}) collective-permute-start(f32[8,56,128]{2,1,0:T(8,128)S(1)} %get-tuple-element.65), channel_id=1, source_target_pairs={{0,16},{1,17},{2,18},{3,19},{4,20},{5,21},{6,22},{7,23},{8,24},{9,... | collective-permute-start | bytes 688136 | tf_op jit(solution)/shard_map/ppermute | solution.py:548
  9.7 9.1 %collective-permute-start.4 = (f32[8,24,128]{2,1,0:T(8,128)S(1)}, f32[8,24,128]{2,1,0:T(8,128)S(1)}, u32[]{:S(2)}, u32[]{:S(2)}) collective-permute-start(f32[8,24,128]{2,1,0:T(8,128)S(1)} %get-tuple-element.66), channel_id=1, source_target_pairs={{0,8},{1,9},{2,10},{3,11},{4,12},{5,13},{6,14},{7,15},{8,0},{9,1},... | collective-permute-start | bytes 294920 | tf_op jit(solution)/shard_map/ppermute | solution.py:548
  13.6 11.9 %collective-permute-start.6 = (f32[8,40,128]{2,1,0:T(8,128)S(1)}, f32[8,40,128]{2,1,0:T(8,128)S(1)}, u32[]{:S(2)}, u32[]{:S(2)}) collective-permute-start(f32[8,40,128]{2,1,0:T(8,128)S(1)} %get-tuple-element.69), channel_id=1, source_target_pairs={{0,8},{1,9},{2,10},{3,11},{4,12},{5,13},{6,14},{7,15},{8,0},{9,1},... | collective-permute-start | bytes 491528 | tf_op jit(solution)/shard_map/ppermute | solution.py:548
  16.3 11.5 %collective-permute-start.2 = (f32[8,40,128]{2,1,0:T(8,128)S(1)}, f32[8,40,128]{2,1,0:T(8,128)S(1)}, u32[]{:S(2)}, u32[]{:S(2)}) collective-permute-start(f32[8,40,128]{2,1,0:T(8,128)S(1)} %get-tuple-element.64), channel_id=1, source_target_pairs={{0,16},{1,17},{2,18},{3,19},{4,20},{5,21},{6,22},{7,23},{8,24},{9,... | collective-permute-start | bytes 491528 | tf_op jit(solution)/shard_map/ppermute | solution.py:548
  19.5 8.2 %collective-permute-start.5 = (f32[8,32,128]{2,1,0:T(8,128)S(1)}, f32[8,32,128]{2,1,0:T(8,128)S(1)}, u32[]{:S(2)}, u32[]{:S(2)}) collective-permute-start(f32[8,32,128]{2,1,0:T(8,128)S(1)} %get-tuple-element.68), channel_id=1, source_target_pairs={{0,8},{1,9},{2,10},{3,11},{4,12},{5,13},{6,14},{7,15},{8,0},{9,1},... | collective-permute-start | bytes 393224 | tf_op jit(solution)/shard_map/ppermute | solution.py:548
  21.3 6.5 %collective-permute-start.7 = (f32[8,24,128]{2,1,0:T(8,128)S(1)}, f32[8,24,128]{2,1,0:T(8,128)S(1)}, u32[]{:S(2)}, u32[]{:S(2)}) collective-permute-start(f32[8,24,128]{2,1,0:T(8,128)S(1)} %get-tuple-element.72), channel_id=1, source_target_pairs={{0,2},{1,3},{2,0},{3,1},{4,6},{5,7},{6,4},{7,5},{8,10},{9,11},{10,... | collective-permute-start | bytes 294920 | tf_op jit(solution)/shard_map/ppermute | solution.py:548
  26.2 8.5 %collective-permute-start.10 = (f32[8,40,128]{2,1,0:T(8,128)S(1)}, f32[8,40,128]{2,1,0:T(8,128)S(1)}, u32[]{:S(2)}, u32[]{:S(2)}) collective-permute-start(f32[8,40,128]{2,1,0:T(8,128)S(1)} %get-tuple-element.76), channel_id=1, source_target_pairs={{0,2},{1,3},{2,0},{3,1},{4,6},{5,7},{6,4},{7,5},{8,10},{9,11},{10,... | collective-permute-start | bytes 491528 | tf_op jit(solution)/shard_map/ppermute | solution.py:548
  27.8 6.9 %collective-permute-start.9 = (f32[8,24,128]{2,1,0:T(8,128)S(1)}, f32[8,24,128]{2,1,0:T(8,128)S(1)}, u32[]{:S(2)}, u32[]{:S(2)}) collective-permute-start(f32[8,24,128]{2,1,0:T(8,128)S(1)} %get-tuple-element.74), channel_id=1, source_target_pairs={{0,8},{1,9},{2,10},{3,11},{4,12},{5,13},{6,14},{7,15},{8,0},{9,1},... | collective-permute-start | bytes 294920 | tf_op jit(solution)/shard_map/ppermute | solution.py:548
  28.5 9.4 %collective-permute-start.12 = (f32[8,32,128]{2,1,0:T(8,128)S(1)}, f32[8,32,128]{2,1,0:T(8,128)S(1)}, u32[]{:S(2)}, u32[]{:S(2)}) collective-permute-start(f32[8,32,128]{2,1,0:T(8,128)S(1)} %get-tuple-element.79), channel_id=1, source_target_pairs={{0,2},{1,3},{2,0},{3,1},{4,6},{5,7},{6,4},{7,5},{8,10},{9,11},{10,... | collective-permute-start | bytes 393224 | tf_op jit(solution)/shard_map/ppermute | solution.py:548
  29.8 8.1 %collective-permute-start.8 = (f32[8,24,128]{2,1,0:T(8,128)S(1)}, f32[8,24,128]{2,1,0:T(8,128)S(1)}, u32[]{:S(2)}, u32[]{:S(2)}) collective-permute-start(f32[8,24,128]{2,1,0:T(8,128)S(1)} %get-tuple-element.73), channel_id=1, source_target_pairs={{0,8},{1,9},{2,10},{3,11},{4,12},{5,13},{6,14},{7,15},{8,0},{9,1},... | collective-permute-start | bytes 294920 | tf_op jit(solution)/shard_map/ppermute | solution.py:548
  35.4 6.8 %collective-permute-start.14 = (f32[8,24,128]{2,1,0:T(8,128)S(1)}, f32[8,24,128]{2,1,0:T(8,128)S(1)}, u32[]{:S(2)}, u32[]{:S(2)}) collective-permute-start(f32[8,24,128]{2,1,0:T(8,128)S(1)} %get-tuple-element.82), channel_id=1, source_target_pairs={{0,2},{1,3},{2,0},{3,1},{4,6},{5,7},{6,4},{7,5},{8,10},{9,11},{10,... | collective-permute-start | bytes 294920 | tf_op jit(solution)/shard_map/ppermute | solution.py:548
  36.0 6.2 %collective-permute-start.11 = (f32[8,16,128]{2,1,0:T(8,128)S(1)}, f32[8,16,128]{2,1,0:T(8,128)S(1)}, u32[]{:S(2)}, u32[]{:S(2)}) collective-permute-start(f32[8,16,128]{2,1,0:T(8,128)S(1)} %get-tuple-element.77), channel_id=1, source_target_pairs={{0,8},{1,9},{2,10},{3,11},{4,12},{5,13},{6,14},{7,15},{8,0},{9,1},... | collective-permute-start | bytes 196616 | tf_op jit(solution)/shard_map/ppermute | solution.py:548
  38.5 8.6 %collective-permute-start.13 = (f32[8,24,128]{2,1,0:T(8,128)S(1)}, f32[8,24,128]{2,1,0:T(8,128)S(1)}, u32[]{:S(2)}, u32[]{:S(2)}) collective-permute-start(f32[8,24,128]{2,1,0:T(8,128)S(1)} %get-tuple-element.80), channel_id=1, source_target_pairs={{0,2},{1,3},{2,0},{3,1},{4,6},{5,7},{6,4},{7,5},{8,10},{9,11},{10,... | collective-permute-start | bytes 294920 | tf_op jit(solution)/shard_map/ppermute | solution.py:548
  42.8 4.3 %collective-permute-start.15 = (f32[8,16,128]{2,1,0:T(8,128)S(1)}, f32[8,16,128]{2,1,0:T(8,128)S(1)}, u32[]{:S(2)}, u32[]{:S(2)}) collective-permute-start(f32[8,16,128]{2,1,0:T(8,128)S(1)} %get-tuple-element.83), channel_id=1, source_target_pairs={{0,2},{1,3},{2,0},{3,1},{4,6},{5,7},{6,4},{7,5},{8,10},{9,11},{10,... | collective-permute-start | bytes 196616 | tf_op jit(solution)/shard_map/ppermute | solution.py:548
  48.0 8.5 %collective-permute-start.18 = (f32[2,5,4,8,128]{4,3,2,1,0:T(8,128)S(1)}, f32[2,5,4,8,128]{4,3,2,1,0:T(8,128)S(1)}, u32[]{:S(2)}, u32[]{:S(2)}) collective-permute-start(f32[2,5,4,8,128]{4,3,2,1,0:T(8,128)S(1)} %get-tuple-element.99), channel_id=1, source_target_pairs={{0,16},{16,0},{1,17},{17,1},{2,18},{18,2},{3,19},{19,3},{4,20},{20... | collective-permute-start | bytes 491528 | tf_op jit(solution)/shard_map/ppermute | solution.py:681
  48.5 6.4 %collective-permute-start.20 = (f32[5,32,128]{2,1,0:T(8,128)S(1)}, f32[5,32,128]{2,1,0:T(8,128)S(1)}, u32[]{:S(2)}, u32[]{:S(2)}) collective-permute-start(f32[5,32,128]{2,1,0:T(8,128)S(1)} %get-tuple-element.100.z_lo), channel_id=1, source_target_pairs={{0,3},{1,0},{2,1},{3,2},{4,7},{5,4},{6,5},{7,6},{8,11},{9,8},{10,9... | collective-permute-start | bytes 245768 | tf_op jit(solution)/shard_map/ppermute | solution.py:681
  48.5 6.4 %collective-permute-start.19 = (f32[5,32,128]{2,1,0:T(8,128)S(1)}, f32[5,32,128]{2,1,0:T(8,128)S(1)}, u32[]{:S(2)}, u32[]{:S(2)}) collective-permute-start(f32[5,32,128]{2,1,0:T(8,128)S(1)} %get-tuple-element.101.z_hi), channel_id=1, source_target_pairs={{0,1},{1,2},{2,3},{3,0},{4,5},{5,6},{6,7},{7,4},{8,9},{9,10},{10,1... | collective-permute-start | bytes 245768 | tf_op jit(solution)/shard_map/ppermute | solution.py:681
  49.0 8.8 %collective-permute-start.17 = (f32[5,4,8,128]{3,2,1,0:T(8,128)S(1)}, f32[5,4,8,128]{3,2,1,0:T(8,128)S(1)}, u32[]{:S(2)}, u32[]{:S(2)}) collective-permute-start(f32[5,4,8,128]{3,2,1,0:T(8,128)S(1)} %get-tuple-element.97.y_lo), channel_id=1, source_target_pairs={{0,12},{4,0},{8,4},{12,8},{1,13},{5,1},{9,5},{13,9},{2,14},{6,2},{... | collective-permute-start | bytes 245768 | tf_op jit(solution)/shard_map/ppermute | solution.py:681
  54.9 6.6 %collective-permute-start.16 = (f32[5,4,8,128]{3,2,1,0:T(8,128)S(1)}, f32[5,4,8,128]{3,2,1,0:T(8,128)S(1)}, u32[]{:S(2)}, u32[]{:S(2)}) collective-permute-start(f32[5,4,8,128]{3,2,1,0:T(8,128)S(1)} %get-tuple-element.98.y_hi), channel_id=1, source_target_pairs={{0,4},{4,8},{8,12},{12,0},{1,5},{5,9},{9,13},{13,1},{2,6},{6,10},{... | collective-permute-start | bytes 245768 | tf_op jit(solution)/shard_map/ppermute | solution.py:681
  62.8 7.4 %collective-permute-start.23 = (f32[2,5,4,8,128]{4,3,2,1,0:T(8,128)S(1)}, f32[2,5,4,8,128]{4,3,2,1,0:T(8,128)S(1)}, u32[]{:S(2)}, u32[]{:S(2)}) collective-permute-start(f32[2,5,4,8,128]{4,3,2,1,0:T(8,128)S(1)} %get-tuple-element.106), channel_id=1, source_target_pairs={{0,16},{16,0},{1,17},{17,1},{2,18},{18,2},{3,19},{19,3},{4,20},{20... | collective-permute-start | bytes 491528 | tf_op jit(solution)/shard_map/ppermute | solution.py:681
  64.1 3.5 %collective-permute-start.25 = (f32[5,32,128]{2,1,0:T(8,128)S(1)}, f32[5,32,128]{2,1,0:T(8,128)S(1)}, u32[]{:S(2)}, u32[]{:S(2)}) collective-permute-start(f32[5,32,128]{2,1,0:T(8,128)S(1)} %get-tuple-element.107.z_lo), channel_id=1, source_target_pairs={{0,3},{1,0},{2,1},{3,2},{4,7},{5,4},{6,5},{7,6},{8,11},{9,8},{10,9... | collective-permute-start | bytes 245768 | tf_op jit(solution)/shard_map/ppermute | solution.py:681
  64.8 3.9 %collective-permute-start.24 = (f32[5,32,128]{2,1,0:T(8,128)S(1)}, f32[5,32,128]{2,1,0:T(8,128)S(1)}, u32[]{:S(2)}, u32[]{:S(2)}) collective-permute-start(f32[5,32,128]{2,1,0:T(8,128)S(1)} %get-tuple-element.108.z_hi), channel_id=1, source_target_pairs={{0,1},{1,2},{2,3},{3,0},{4,5},{5,6},{6,7},{7,4},{8,9},{9,10},{10,1... | collective-permute-start | bytes 245768 | tf_op jit(solution)/shard_map/ppermute | solution.py:681
  64.8 6.4 %collective-permute-start.22 = (f32[5,4,8,128]{3,2,1,0:T(8,128)S(1)}, f32[5,4,8,128]{3,2,1,0:T(8,128)S(1)}, u32[]{:S(2)}, u32[]{:S(2)}) collective-permute-start(f32[5,4,8,128]{3,2,1,0:T(8,128)S(1)} %get-tuple-element.104.y_lo), channel_id=1, source_target_pairs={{0,12},{4,0},{8,4},{12,8},{1,13},{5,1},{9,5},{13,9},{2,14},{6,2},{... | collective-permute-start | bytes 245768 | tf_op jit(solution)/shard_map/ppermute | solution.py:681
  65.4 6.2 %collective-permute-start.21 = (f32[5,4,8,128]{3,2,1,0:T(8,128)S(1)}, f32[5,4,8,128]{3,2,1,0:T(8,128)S(1)}, u32[]{:S(2)}, u32[]{:S(2)}) collective-permute-start(f32[5,4,8,128]{3,2,1,0:T(8,128)S(1)} %get-tuple-element.105.y_hi), channel_id=1, source_target_pairs={{0,4},{4,8},{8,12},{12,0},{1,5},{5,9},{9,13},{13,1},{2,6},{6,10},{... | collective-permute-start | bytes 245768 | tf_op jit(solution)/shard_map/ppermute | solution.py:681

commit v5 on v4

--- a/solution.py
+++ b/solution.py
@@ -216,7 +216,7 @@
     def faces(self):
         x = jax.ShapeDtypeStruct((2, NF, self.pad, SUB, LANES), f32)
         y = jax.ShapeDtypeStruct((NF, self.edge // self.fit, SUB, LANES), f32)
-        z = jax.ShapeDtypeStruct((NF, self.rows, LANES), f32)
+        z = jax.ShapeDtypeStruct((NF, SUB, LANES), f32)
         return [x, y, y, z, z]
 
 
@@ -244,11 +244,14 @@
                 hi = jnp.where(mine, above, hi)
         y_lo[f, slab] = lo
         y_hi[f, slab] = hi
-        to = pl.ds(slab * SUB, SUB) if isinstance(slab, int) else pl.ds(
-            pl.multiple_of(slab * SUB, SUB), SUB
-        )
-        z_lo[f, to, :] = prim[shape.across(f, slab, 0), :]
-        z_hi[f, to, :] = prim[shape.across(f, slab, SUB - 1), :]
+        below = lane_roll(prim[shape.across(f, slab, 0), :], 2 * slab)
+        above = lane_roll(prim[shape.across(f, slab, SUB - 1), :], 2 * slab + 2 - shape.edge)
+        if slab:
+            mine = lax.rem(lane, shape.edge) >= 2 * slab
+            below = jnp.where(mine, below, z_lo[f])
+            above = jnp.where(mine, above, z_hi[f])
+        z_lo[f] = below
+        z_hi[f] = above
 
 
 def send_x(shape, prim, faces, low=True, high=True):
@@ -294,15 +297,18 @@
     send_x(shape, prim, x_faces, low=first, high=not first)
 
 
-def sweep_z_kernel(prim, z_lo, z_hi, z_prev, z_next, total, flux_z, right_z, left, right, flux, *, shape):
+def sweep_z_kernel(prim, z_prev, z_next, total, prev_z, next_z, flux_z, right_z, left, right, flux, *, shape):
     edge, rows = shape.edge, shape.rows
 
     def ghost(a):
         at = pl.ds(a * SUB, SUB)
-        low = [z_lo[f, at, :] for f in FIELDS]
-        high = [z_hi[f, at, :] for f in FIELDS]
-        prev = [z_prev[f, at, :] for f in FIELDS]
-        after = [z_next[f, at, :] for f in FIELDS]
+        low = [prim[shape.across(f, a, 0), :] for f in FIELDS]
+        high = [prim[shape.across(f, a, SUB - 1), :] for f in FIELDS]
+        prev = [lane_roll(z_prev[f], edge - 2 - 2 * a) for f in FIELDS]
+        after = [lane_roll(z_next[f], -2 * a) for f in FIELDS]
+        for f in FIELDS:
+            prev_z[f, at, :] = prev[f]
+            next_z[f, at, :] = after[f]
         below = [lane_roll(v, -(edge - 1)) for v in prev]
         before = [lane_roll(v, -(edge - 2)) for v in prev]
         second = [lane_roll(v, -1) for v in low]
@@ -341,7 +347,7 @@
             for f in FIELDS:
                 at = shape.at(f, row)
                 mine = prim[at, :]
-                shift = half_minmod(mine - down(mine, f, row, z_prev), up(mine, f, row, z_next) - mine)
+                shift = half_minmod(mine - down(mine, f, row, prev_z), up(mine, f, row, next_z) - mine)
                 left[at, :] = mine + shift
                 right[at, :] = mine - shift
 
@@ -362,40 +368,31 @@
     in_turn(shape.slabs, slopes, fluxes, differences)
 
 
-def sweep_x_kernel(prim, x_faces, sofar, total, wide, *, shape):
-    rows, halves, pad = shape.rows, shape.halves, shape.pad
-    for f in FIELDS:
-        for i in range(pad):
-            wide[f, i] = x_faces[0, f, i]
-            wide[f, pad + rows + i] = x_faces[1, f, i]
-
-        def copy(r, carry, f=f):
-            wide[f, pad + r] = prim[shape.at(f, r), :]
-            return carry
-
-        lax.fori_loop(0, rows, copy, 0, unroll=8)
+def sweep_x_kernel(prim, x_faces, sofar, total, *, shape):
+    halves, edge = shape.halves, shape.edge
+
+    def cells(x, h):
+        if x < 0:
+            return [x_faces[0, f, (x + 2) * halves + h] for f in FIELDS]
+        if x >= edge:
+            return [x_faces[1, f, (x - edge) * halves + h] for f in FIELDS]
+        return [prim[shape.at(f, x * halves + h), :] for f in FIELDS]
 
     for h in range(halves):
-        cells = [[wide[f, i * halves + h] for f in FIELDS] for i in range(4)]
-        left = plus(cells[1], half_slopes(*cells[0:3]))
-        shift = half_slopes(*cells[1:4])
-        flux = twice_flux(left, minus(cells[2], shift), 0)
-        keep = plus(cells[2], shift)
-
-        def body(x, carry, h=h):
-            below, left = carry
-            here, one, two = (
-                [wide[f, pad + (x + i) * halves + h] for f in FIELDS] for i in range(3)
-            )
-            shift = half_slopes(here, one, two)
-            flux = twice_flux(left, minus(one, shift), 0)
-            row = x * halves + h
-            for f in FIELDS:
-                at = shape.at(f, row)
-                total[at, :] = sofar[at, :] + (flux[f] - below[f])
-            return flux, plus(one, shift)
-
-        lax.fori_loop(0, shape.edge, body, (flux, keep), unroll=4)
+        left = below = None
+        ahead = [cells(x, h) for x in (-2, -1, 0)]
+        for x in range(-1, edge + 1):
+            shift = half_slopes(*ahead)
+            if left is not None:
+                flux = twice_flux(left, minus(ahead[1], shift), 0)
+                if below is not None:
+                    for f in FIELDS:
+                        at = shape.at(f, (x - 1) * halves + h)
+                        total[at, :] = sofar[at, :] + (flux[f] - below[f])
+                below = flux
+            left = plus(ahead[1], shift)
+            if x < edge:
+                ahead = ahead[1:] + [cells(x + 2, h)]
 
 
 def sweep_y(prim, y_lo, y_hi, y_prev, y_next, sofar, ghost_prim, ghost_flux, left, right, flux, turned,
@@ -534,7 +531,7 @@
     groups = slots // SUB
     shape = Shape(rows, edge)
     units = NF * shape.slabs
-    pieces = split_units(units, (3, 5, 4, 3, 3, 2))
+    pieces = split_units(units, (3, 5, 7, 5))
     firsts = split_units(units, (3, 5, 7, 5))
 
     bit_z = size_z.bit_length() - 2
@@ -630,10 +627,8 @@
         ([(1, 1)], [3], []),
         ([(1, 2), (2, 0)], [], []),
         ([(1, 3), (2, 1)], [], []),
-        ([(1, 4), (2, 2)], [], [0]),
-        ([(1, 5), (2, 3)], [], [1]),
-        ([(2, 4)], [], [2]),
-        ([(2, 5)], [], [3]),
+        ([(2, 2)], [], [0]),
+        ([(2, 3)], [], [1]),
     ]
     got[0][0] = swapped(sent[0], 0)
     got[0][1] = swapped(sent[1], 0)
@@ -651,7 +646,7 @@
     face_x, face_y, _, face_z, _ = shape.faces()
     part = [grid, grid, face_y, face_y, face_z, face_z, face_x]
     canvas = jax.ShapeDtypeStruct((NF * groups, rows * SUB, LANES), f32)
-    full = pieces[-2][0] // NF
+    full = pieces[-1][0] // NF
 
     def assemble(slabs, before):
         first = not before
@@ -692,20 +687,21 @@
         total = pl.pallas_call(
             functools.partial(sweep_z_kernel, shape=shape),
             out_shape=grid,
-            in_specs=[whole(VMEM)] * 5,
+            in_specs=[whole(VMEM)] * 3,
             out_specs=whole(VMEM),
-            scratch_shapes=[ghost] * 2 + work,
+            scratch_shapes=[ghost] * 4 + work,
             compiler_params=params(),
+            cost_estimate=cost(1, 1),
             name="sweep_z",
-        )(prim, z_lo, z_hi, z_prev, z_next)
+        )(prim, z_prev, z_next)
         total = pl.pallas_call(
             functools.partial(sweep_x_kernel, shape=shape),
             out_shape=grid,
             in_specs=[whole(VMEM)] * 3,
             out_specs=whole(VMEM),
-            scratch_shapes=[VMEM((NF, rows + 2 * shape.pad, SUB, LANES), f32)],
             input_output_aliases={2: 0},
             compiler_params=params(),
+            cost_estimate=cost(1, 1),
             name="sweep_x",
         )(prim, x_faces, total)
         return y_lo, y_hi, y_prev, y_next, total

time: 74.7 us -> 75.1 us (level)
  starting transfers between devices: 33.9 us -> 35.7 us
  Pallas kernels: 19.6 us -> 18 us
    ppermute x10, starting transfers between devices: 11 us -> 15.5 us  [ring(): lax.ppermute(value, axis, [(i, (i + step) % size) for i in range(size)])]
    ppermute x16 -> x12, starting transfers between devices: 22.9 us -> 20.3 us  [swapped(): return lax.ppermute(value, AXES, pairs)]
    ppermute x16 -> x12, waiting for transfers between devices: 14.5 us -> 16 us  [swapped(): return lax.ppermute(value, AXES, pairs)]
    pallas_call x8 -> x6, Pallas kernels: 5.37 us -> 3.97 us  [make(): pl.pallas_call(functools.partial(pick_kernel, plan=plan, held=tuple(found...]
    ppermute x10, waiting for transfers between devices: 6.33 us -> 5.08 us  [ring(): lax.ppermute(value, axis, [(i, (i + step) % size) for i in range(size)])]
    pallas_call x2, Pallas kernels: 1.98 us -> 1.16 us  [flux_sums(): pl.pallas_call(functools.partial(sweep_x_kernel, shape=shape), out_shape=...]
  transfers between devices with their start and end apart: 26 -> 22, of which waited for: 13 -> 12; matrix products, arithmetic and copies ran while one was open for 0% -> 0% of each run, Pallas kernels for 18% -> 16%
where the time goes in v5:
time: 75.1 us; the launch traced here: 75 us
  starting transfers between devices  35.7 us (48%)
  waiting for transfers between devices  21 us (28%)
  Pallas kernels  18 us (24%)
    ppermute x12, starting transfers between devices, swapped(): return lax.ppermute(value, AXES, pairs)  20.3 us
    ppermute x12, waiting for transfers between devices, swapped(): return lax.ppermute(value, AXES, pairs)  16 us
    ppermute x10, starting transfers between devices, ring(): lax.ppermute(value, axis, [(i, (i + step) % size) for i in range(size)])  15.5 us
    ppermute x10, waiting for transfers between devices, ring(): lax.ppermute(value, axis, [(i, (i + step) % size) for i in range(size)])  5.08 us
    pallas_call x6, Pallas kernels, make(): pl.pallas_call(functools.partial(pick_kernel, plan=plan, held=tuple(found...  3.97 us
    pallas_call x2, Pallas kernels, flux_sums(): pl.pallas_call(functools.partial(sweep_z_kernel, shape=shape), out_shape=...  3.5 us
    pallas_call x1, Pallas kernels, shards(): pl.pallas_call(functools.partial(sweep_y_two_kernel, shape=shape, occ=occ...  2.92 us
    pallas_call x2, Pallas kernels, assemble(): pl.pallas_call(functools.partial(assemble_kernel, held=tuple(found), slab...  2.49 us
  transfers between devices with their start and end apart: 22, of which 12 were waited for; matrix products, arithmetic and copies ran while one was open for 0% of the time, Pallas kernels for 16%

profile of v5, /device:TPU:0, one launch (start us, length us, event | category | flops | bytes accessed | tf_op | source)
XLA Modules:
  0.0 75.0 jit_solution(8204110246372968375)
XLA Ops:
  0.0 1.2 %pack_first.1 = f32[8,24,128]{2,1,0:T(8,128)S(1)} custom-call(s32[3,1,8]{2,1,0:T(1,128)} %send_hbm.1, f32[5120,128]{1,0:T(8,128)} %bitcast.10), custom_call_target="tpu_custom_call" | custom-call | tf_op jit(solution)/shard_map/pack_first/pallas_call | solution.py:564
  1.3 3.0 %collective-permute-start.1 = (f32[8,24,128]{2,1,0:T(8,128)S(1)}, f32[8,24,128]{2,1,0:T(8,128)S(1)}, u32[]{:S(2)}, u32[]{:S(2)}) collective-permute-start(f32[8,24,128]{2,1,0:T(8,128)S(1)} %pack_first.1), channel_id=1, source_target_pairs={{0,16},{1,17},{2,18},{3,19},{4,20},{5,21},{6,22},{7,23},{8,24},{9,... | collective-permute-start | bytes 294920 | tf_op jit(solution)/shard_map/ppermute | solution.py:545
  4.3 0.0 copy-done.3
  4.3 0.1 dynamic_slice.3.own
  4.4 0.0 copy-done.1
  4.4 0.0 copy-done.2
  4.4 1.4 %pack_rest.1 = (s32[24]{0:T(128)S(1)}, f32[8,128]{1,0:T(8,128)S(1)}, f32[8,40,128]{2,1,0:T(8,128)S(1)}, f32[8,56,128]{2,1,0:T(8,128)S(1)}, f32[8,40,128]{2,1,0:T(8,128)S(1)}) custom-call(s32[3,1,8]{2,1,0:T(1,128)S(1)} %copy-done.1, s32[3,1,8]{2,1,0:T(1,128)S(1)} %copy-done.2, s32[8]{0:T(128)S(1)} %dynamic_slice.3.own, f32[5120,128]{1,0:T(8,128)S(1)} %bitcast.11), custom_call_target="tpu_custom_call" | custom-call | tf_op jit(solution)/shard_map/pack_rest/pallas_call | solution.py:577
  5.8 0.6 collective-permute-start
  6.4 0.7 collective-permute-done.1.refs_0_.refs_1_
  7.1 0.6 pick_10.1
  7.7 2.0 %collective-permute-start.4 = (f32[8,56,128]{2,1,0:T(8,128)S(1)}, f32[8,56,128]{2,1,0:T(8,128)S(1)}, u32[]{:S(2)}, u32[]{:S(2)}) collective-permute-start(f32[8,56,128]{2,1,0:T(8,128)S(1)} %get-tuple-element.58), channel_id=1, source_target_pairs={{0,16},{1,17},{2,18},{3,19},{4,20},{5,21},{6,22},{7,23},{8,24},{9,... | collective-permute-start | bytes 688136 | tf_op jit(solution)/shard_map/ppermute | solution.py:545
  9.7 2.6 %collective-permute-start.5 = (f32[8,24,128]{2,1,0:T(8,128)S(1)}, f32[8,24,128]{2,1,0:T(8,128)S(1)}, u32[]{:S(2)}, u32[]{:S(2)}) collective-permute-start(f32[8,24,128]{2,1,0:T(8,128)S(1)} %get-tuple-element.59), channel_id=1, source_target_pairs={{0,8},{1,9},{2,10},{3,11},{4,12},{5,13},{6,14},{7,15},{8,0},{9,1},... | collective-permute-start | bytes 294920 | tf_op jit(solution)/shard_map/ppermute | solution.py:545
  12.3 0.7 collective-permute-done.refs_0_.refs_1_
  13.0 0.6 pick_11.1
  13.6 0.6 collective-permute-start.2
  14.2 2.6 %collective-permute-start.3 = (f32[8,40,128]{2,1,0:T(8,128)S(1)}, f32[8,40,128]{2,1,0:T(8,128)S(1)}, u32[]{:S(2)}, u32[]{:S(2)}) collective-permute-start(f32[8,40,128]{2,1,0:T(8,128)S(1)} %get-tuple-element.57), channel_id=1, source_target_pairs={{0,8},{1,9},{2,10},{3,11},{4,12},{5,13},{6,14},{7,15},{8,0},{9,1},... | collective-permute-start | bytes 491528 | tf_op jit(solution)/shard_map/ppermute | solution.py:545
  16.8 0.0 collective-permute-done.5.refs_2_.refs_3_
  16.8 1.1 %collective-permute-done.4.refs_0_.refs_2_ = f32[8,56,128]{2,1,0:T(8,128)S(1)} collective-permute-done((f32[8,56,128]{2,1,0:T(8,128)S(1)}, f32[8,56,128]{2,1,0:T(8,128)S(1)}, u32[]{:S(2)}, u32[]{:S(2)}) %collective-permute-start.4) | collective-permute-done | bytes 229408 | tf_op jit(solution)/shard_map/ppermute | solution.py:545
  17.9 0.7 pick_12_20.1
  18.6 2.7 %collective-permute-start.7 = (f32[8,56,128]{2,1,0:T(8,128)S(1)}, f32[8,56,128]{2,1,0:T(8,128)S(1)}, u32[]{:S(2)}, u32[]{:S(2)}) collective-permute-start(f32[8,56,128]{2,1,0:T(8,128)S(1)} %get-tuple-element.63), channel_id=1, source_target_pairs={{0,8},{1,9},{2,10},{3,11},{4,12},{5,13},{6,14},{7,15},{8,0},{9,1},... | collective-permute-start | bytes 688136 | tf_op jit(solution)/shard_map/ppermute | solution.py:545
  21.3 1.5 %collective-permute-start.8 = (f32[8,24,128]{2,1,0:T(8,128)S(1)}, f32[8,24,128]{2,1,0:T(8,128)S(1)}, u32[]{:S(2)}, u32[]{:S(2)}) collective-permute-start(f32[8,24,128]{2,1,0:T(8,128)S(1)} %get-tuple-element.65), channel_id=1, source_target_pairs={{0,2},{1,3},{2,0},{3,1},{4,6},{5,7},{6,4},{7,5},{8,10},{9,11},{10,... | collective-permute-start | bytes 294920 | tf_op jit(solution)/shard_map/ppermute | solution.py:545
  22.8 0.0 collective-permute-done.2.refs_0_
  22.8 3.7 %collective-permute-done.3.refs_2_.refs_4_ = f32[8,40,128]{2,1,0:T(8,128)S(1)} collective-permute-done((f32[8,40,128]{2,1,0:T(8,128)S(1)}, f32[8,40,128]{2,1,0:T(8,128)S(1)}, u32[]{:S(2)}, u32[]{:S(2)}) %collective-permute-start.3) | collective-permute-done | bytes 163872 | tf_op jit(solution)/shard_map/ppermute | solution.py:545
  26.4 0.7 pick_13_21.1
  27.2 0.1 collective-permute-start.6
  27.2 1.6 %collective-permute-start.9 = (f32[8,40,128]{2,1,0:T(8,128)S(1)}, f32[8,40,128]{2,1,0:T(8,128)S(1)}, u32[]{:S(2)}, u32[]{:S(2)}) collective-permute-start(f32[8,40,128]{2,1,0:T(8,128)S(1)} %get-tuple-element.67), channel_id=1, source_target_pairs={{0,2},{1,3},{2,0},{3,1},{4,6},{5,7},{6,4},{7,5},{8,10},{9,11},{10,... | collective-permute-start | bytes 491528 | tf_op jit(solution)/shard_map/ppermute | solution.py:545
  28.8 0.0 collective-permute-done.8.refs_3_
  28.8 5.0 %collective-permute-done.7.refs_1_.refs_5_ = f32[8,56,128]{2,1,0:T(8,128)S(1)} collective-permute-done((f32[8,56,128]{2,1,0:T(8,128)S(1)}, f32[8,56,128]{2,1,0:T(8,128)S(1)}, u32[]{:S(2)}, u32[]{:S(2)}) %collective-permute-start.7) | collective-permute-done | bytes 229408 | tf_op jit(solution)/shard_map/ppermute | solution.py:545
  33.8 0.6 pick_22.1
  34.5 1.6 %collective-permute-start.11 = (f32[8,56,128]{2,1,0:T(8,128)S(1)}, f32[8,56,128]{2,1,0:T(8,128)S(1)}, u32[]{:S(2)}, u32[]{:S(2)}) collective-permute-start(f32[8,56,128]{2,1,0:T(8,128)S(1)} %get-tuple-element.71), channel_id=1, source_target_pairs={{0,2},{1,3},{2,0},{3,1},{4,6},{5,7},{6,4},{7,5},{8,10},{9,11},{10,... | collective-permute-start | bytes 688136 | tf_op jit(solution)/shard_map/ppermute | solution.py:545
  36.0 2.4 %collective-permute-done.6.refs_1_ = f32[8,40,128]{2,1,0:T(8,128)S(1)} collective-permute-done((f32[8,40,128]{2,1,0:T(8,128)S(1)}, f32[8,40,128]{2,1,0:T(8,128)S(1)}, u32[]{:S(2)}, u32[]{:S(2)}) %collective-permute-start.6) | collective-permute-done | bytes 163872 | tf_op jit(solution)/shard_map/ppermute | solution.py:545
  38.4 0.0 collective-permute-done.9.refs_3_
  38.4 0.6 pick_23.1
  39.0 1.6 %collective-permute-start.10 = (f32[8,40,128]{2,1,0:T(8,128)S(1)}, f32[8,40,128]{2,1,0:T(8,128)S(1)}, u32[]{:S(2)}, u32[]{:S(2)}) collective-permute-start(f32[8,40,128]{2,1,0:T(8,128)S(1)} %get-tuple-element.68), channel_id=1, source_target_pairs={{0,2},{1,3},{2,0},{3,1},{4,6},{5,7},{6,4},{7,5},{8,10},{9,11},{10,... | collective-permute-start | bytes 491528 | tf_op jit(solution)/shard_map/ppermute | solution.py:545
  40.6 0.2 collective-permute-done.11.refs_8_
  40.8 1.6 %assemble_0.1 = (f32[1280,128]{1,0:T(8,128)S(1)}, f32[1280,128]{1,0:T(8,128)S(1)}, f32[5,4,8,128]{3,2,1,0:T(8,128)S(1)}, f32[5,4,8,128]{3,2,1,0:T(8,128)S(1)}, f...) custom-call(s32[24]{0:T(128)S(1)} %get-tuple-element.50.tags, ...), custom_call_target="tpu_custom_call" | custom-call | tf_op jit(solution)/shard_map/assemble_0/pallas_call | solution.py:656
  42.4 2.2 %collective-permute-done.10.refs_2_ = f32[8,40,128]{2,1,0:T(8,128)S(1)} collective-permute-done((f32[8,40,128]{2,1,0:T(8,128)S(1)}, f32[8,40,128]{2,1,0:T(8,128)S(1)}, u32[]{:S(2)}, u32[]{:S(2)}) %collective-permute-start.10) | collective-permute-done | bytes 163872 | tf_op jit(solution)/shard_map/ppermute | solution.py:545
  44.6 0.9 %assemble_3.1 = (f32[1280,128]{1,0:T(8,128)S(1)}, f32[1280,128]{1,0:T(8,128)S(1)}, f32[5,4,8,128]{3,2,1,0:T(8,128)S(1)}, f32[5,4,8,128]{3,2,1,0:T(8,128)S(1)}, f...) custom-call(s32[24]{0:T(128)S(1)} %get-tuple-element.50.tags, ...), custom_call_target="tpu_custom_call", output_to_operand_aliasing={{0}: (5, {}), {1}: (6, {}), {2}: (7, {}), {3}: (8, {}), {4}... | custom-call | tf_op jit(solution)/shard_map/assemble_3/pallas_call | solution.py:656
  45.5 2.0 %collective-permute-start.14 = (f32[2,5,4,8,128]{4,3,2,1,0:T(8,128)S(1)}, f32[2,5,4,8,128]{4,3,2,1,0:T(8,128)S(1)}, u32[]{:S(2)}, u32[]{:S(2)}) collective-permute-start(f32[2,5,4,8,128]{4,3,2,1,0:T(8,128)S(1)} %get-tuple-element.83), channel_id=1, source_target_pairs={{0,16},{16,0},{1,17},{17,1},{2,18},{18,2},{3,19},{19,3},{4,20},{20... | collective-permute-start | bytes 491528 | tf_op jit(solution)/shard_map/ppermute | solution.py:676
  47.5 5.2 %collective-permute-start.13 = (f32[5,4,8,128]{3,2,1,0:T(8,128)S(1)}, f32[5,4,8,128]{3,2,1,0:T(8,128)S(1)}, u32[]{:S(2)}, u32[]{:S(2)}) collective-permute-start(f32[5,4,8,128]{3,2,1,0:T(8,128)S(1)} %get-tuple-element.81.y_lo), channel_id=1, source_target_pairs={{0,12},{4,0},{8,4},{12,8},{1,13},{5,1},{9,5},{13,9},{2,14},{6,2},{... | collective-permute-start | bytes 245768 | tf_op jit(solution)/shard_map/ppermute | solution.py:676
  52.7 0.0 collective-permute-start.12
  52.7 0.0 collective-permute-start.15
  52.7 1.7 %collective-permute-start.16 = (f32[5,8,128]{2,1,0:T(8,128)S(1)}, f32[5,8,128]{2,1,0:T(8,128)S(1)}, u32[]{:S(2)}, u32[]{:S(2)}) collective-permute-start(f32[5,8,128]{2,1,0:T(8,128)S(1)} %get-tuple-element.85), channel_id=1, source_target_pairs={{0,3},{1,0},{2,1},{3,2},{4,7},{5,4},{6,5},{7,6},{8,11},{9,8},{10,9... | collective-permute-start | bytes 61448 | tf_op jit(solution)/shard_map/ppermute | solution.py:676
  54.4 1.5 %collective-permute-done.15.z_prev = f32[5,8,128]{2,1,0:T(8,128)S(1)} collective-permute-done((f32[5,8,128]{2,1,0:T(8,128)S(1)}, f32[5,8,128]{2,1,0:T(8,128)S(1)}, u32[]{:S(2)}, u32[]{:S(2)}) %collective-permute-start.15) | collective-permute-done | bytes 20512 | tf_op jit(solution)/shard_map/ppermute | solution.py:676
  55.9 0.0 collective-permute-done.16.z_next
  55.9 1.8 %sweep_z.2.sofar = f32[1280,128]{1,0:T(8,128)S(1)} custom-call(f32[1280,128]{1,0:T(8,128)S(1)} %get-tuple-element.80.prim, f32[5,8,128]{2,1,0:T(8,128)S(1)} %collective-permute-done.15.z_prev, f32[5,8,128]{2,1,0:T(8,128)S(1)} %collective-permute-done.16.z_next), custom_call_target="tpu_custom_call" | custom-call | flops 1 | bytes 1 | tf_op jit(solution)/shard_map/sweep_z/pallas_call | solution.py:687
  57.7 0.0 collective-permute-done.14.x_faces
  57.7 0.6 sweep_x.2.sofar
  58.2 0.0 collective-permute-done.13.y_next
  58.3 0.6 collective-permute-done.12.y_prev
  58.9 1.3 %sweep_y_one.1 = (f32[1280,128]{1,0:T(8,128)S(1)}, f32[1280,128]{1,0:T(8,128)S(1)}, f32[2,5,4,8,128]{4,3,2,1,0:T(8,128)S(1)}, f32[5,4,8,128]{3,2,1,0:T(8,128)S(1...) custom-call(f32[1280,128]{1,0:T(8,128)S(1)} %get-tuple-element.79.field, ...), custom_call_target="tpu_custom_call" | custom-call | tf_op jit(solution)/shard_map/sweep_y_one/pallas_call | solution.py:713
  60.2 1.6 %collective-permute-start.19 = (f32[2,5,4,8,128]{4,3,2,1,0:T(8,128)S(1)}, f32[2,5,4,8,128]{4,3,2,1,0:T(8,128)S(1)}, u32[]{:S(2)}, u32[]{:S(2)}) collective-permute-start(f32[2,5,4,8,128]{4,3,2,1,0:T(8,128)S(1)} %get-tuple-element.90), channel_id=1, source_target_pairs={{0,16},{16,0},{1,17},{17,1},{2,18},{18,2},{3,19},{19,3},{4,20},{20... | collective-permute-start | bytes 491528 | tf_op jit(solution)/shard_map/ppermute | solution.py:676
  61.8 3.2 %collective-permute-start.18 = (f32[5,4,8,128]{3,2,1,0:T(8,128)S(1)}, f32[5,4,8,128]{3,2,1,0:T(8,128)S(1)}, u32[]{:S(2)}, u32[]{:S(2)}) collective-permute-start(f32[5,4,8,128]{3,2,1,0:T(8,128)S(1)} %get-tuple-element.88.y_lo), channel_id=1, source_target_pairs={{0,12},{4,0},{8,4},{12,8},{1,13},{5,1},{9,5},{13,9},{2,14},{6,2},{... | collective-permute-start | bytes 245768 | tf_op jit(solution)/shard_map/ppermute | solution.py:676
  65.0 0.0 collective-permute-start.17
  65.0 1.0 %collective-permute-start.20 = (f32[5,8,128]{2,1,0:T(8,128)S(1)}, f32[5,8,128]{2,1,0:T(8,128)S(1)}, u32[]{:S(2)}, u32[]{:S(2)}) collective-permute-start(f32[5,8,128]{2,1,0:T(8,128)S(1)} %get-tuple-element.91), channel_id=1, source_target_pairs={{0,1},{1,2},{2,3},{3,0},{4,5},{5,6},{6,7},{7,4},{8,9},{9,10},{10,1... | collective-permute-start | bytes 61448 | tf_op jit(solution)/shard_map/ppermute | solution.py:676
  66.1 0.7 collective-permute-start.21
  66.8 1.5 %collective-permute-done.20.z_prev = f32[5,8,128]{2,1,0:T(8,128)S(1)} collective-permute-done((f32[5,8,128]{2,1,0:T(8,128)S(1)}, f32[5,8,128]{2,1,0:T(8,128)S(1)}, u32[]{:S(2)}, u32[]{:S(2)}) %collective-permute-start.20) | collective-permute-done | bytes 20512 | tf_op jit(solution)/shard_map/ppermute | solution.py:676
  68.2 0.0 collective-permute-done.21.z_next
  68.3 1.7 %sweep_z.3.sofar = f32[1280,128]{1,0:T(8,128)S(1)} custom-call(f32[1280,128]{1,0:T(8,128)S(1)} %get-tuple-element.87.prim, f32[5,8,128]{2,1,0:T(8,128)S(1)} %collective-permute-done.20.z_prev, f32[5,8,128]{2,1,0:T(8,128)S(1)} %collective-permute-done.21.z_next), custom_call_target="tpu_custom_call" | custom-call | flops 1 | bytes 1 | tf_op jit(solution)/shard_map/sweep_z/pallas_call | solution.py:687
  70.0 0.0 collective-permute-done.19.x_faces
  70.0 0.6 sweep_x.3.sofar
  70.6 0.0 collective-permute-done.18.y_next
  70.6 1.5 %collective-permute-done.17.y_prev = f32[5,4,8,128]{3,2,1,0:T(8,128)S(1)} collective-permute-done((f32[5,4,8,128]{3,2,1,0:T(8,128)S(1)}, f32[5,4,8,128]{3,2,1,0:T(8,128)S(1)}, u32[]{:S(2)}, u32[]{:S(2)}) %collective-permute-start.17) | collective-permute-done | bytes 81952 | tf_op jit(solution)/shard_map/ppermute | solution.py:676
  72.1 2.9 %sweep_y_two.1 = (f32[20,256,128]{2,1,0:T(8,128)}, f32[20,256,128]{2,1,0:T(8,128)S(1)}) custom-call(s32[8]{0:T(128)S(1)} %dynamic_slice.3.own, f32[1280,128]{1,0:T(8,128)S(1)} %get-tuple-element.79.field, f32[1280,128]{1,0:T(8,128)S(1)} %get-tuple-element.86.one, f32[1280,128]{1,0:T(8,128)S(1)} %get-tuple-element.87.prim, ...), custom_call_target="tpu_custom_call", output_to_operand_aliasing={{1}: (9, {})} | custom-call | tf_op jit(solution)/shard_map/sweep_y_two/pallas_call | solution.py:724
  (5 shorter events, 0.0 us)
Async XLA Ops:
  0.0 4.4 %copy-start.1 = (s32[3,1,8]{2,1,0:T(1,128)S(1)}, s32[3,1,8]{2,1,0:T(1,128)}, u32[]{:S(2)}) copy-start(s32[3,1,8]{2,1,0:T(1,128)} %send_hbm.1) | copy-start | bytes 292
  0.0 4.4 %copy-start = (f32[32,5,4096]{2,0,1:T(8,128)S(1)}, f32[32,5,4096]{2,0,1:T(8,128)}, u32[]{:S(2)}) copy-start(f32[32,5,4096]{2,0,1:T(8,128)} %param.4) | copy-start | bytes 7864324
  0.0 4.3 %copy-start.3 = (s32[256]{0:T(256)S(1)}, s32[256]{0:T(256)}, u32[]{:S(2)}) copy-start(s32[256]{0:T(256)} %param.7) | copy-start | bytes 3076
  0.0 4.4 %copy-start.2 = (s32[3,1,8]{2,1,0:T(1,128)S(1)}, s32[3,1,8]{2,1,0:T(1,128)}, u32[]{:S(2)}) copy-start(s32[3,1,8]{2,1,0:T(1,128)} %recv.1) | copy-start | bytes 292
  1.3 5.8 %collective-permute-start.1 = (f32[8,24,128]{2,1,0:T(8,128)S(1)}, f32[8,24,128]{2,1,0:T(8,128)S(1)}, u32[]{:S(2)}, u32[]{:S(2)}) collective-permute-start(f32[8,24,128]{2,1,0:T(8,128)S(1)} %pack_first.1), channel_id=1, source_target_pairs={{0,16},{1,17},{2,18},{3,19},{4,20},{5,21},{6,22},{7,23},{8,24},{9,... | collective-permute-start | bytes 294920 | tf_op jit(solution)/shard_map/ppermute | solution.py:545
  5.8 7.2 %collective-permute-start = (f32[8,40,128]{2,1,0:T(8,128)S(1)}, f32[8,40,128]{2,1,0:T(8,128)S(1)}, u32[]{:S(2)}, u32[]{:S(2)}) collective-permute-start(f32[8,40,128]{2,1,0:T(8,128)S(1)} %get-tuple-element.51), channel_id=1, source_target_pairs={{0,16},{1,17},{2,18},{3,19},{4,20},{5,21},{6,22},{7,23},{8,24},{9,... | collective-permute-start | bytes 491528 | tf_op jit(solution)/shard_map/ppermute | solution.py:545
  7.7 10.2 %collective-permute-start.4 = (f32[8,56,128]{2,1,0:T(8,128)S(1)}, f32[8,56,128]{2,1,0:T(8,128)S(1)}, u32[]{:S(2)}, u32[]{:S(2)}) collective-permute-start(f32[8,56,128]{2,1,0:T(8,128)S(1)} %get-tuple-element.58), channel_id=1, source_target_pairs={{0,16},{1,17},{2,18},{3,19},{4,20},{5,21},{6,22},{7,23},{8,24},{9,... | collective-permute-start | bytes 688136 | tf_op jit(solution)/shard_map/ppermute | solution.py:545
  9.7 7.1 %collective-permute-start.5 = (f32[8,24,128]{2,1,0:T(8,128)S(1)}, f32[8,24,128]{2,1,0:T(8,128)S(1)}, u32[]{:S(2)}, u32[]{:S(2)}) collective-permute-start(f32[8,24,128]{2,1,0:T(8,128)S(1)} %get-tuple-element.59), channel_id=1, source_target_pairs={{0,8},{1,9},{2,10},{3,11},{4,12},{5,13},{6,14},{7,15},{8,0},{9,1},... | collective-permute-start | bytes 294920 | tf_op jit(solution)/shard_map/ppermute | solution.py:545
  13.6 9.2 %collective-permute-start.2 = (f32[8,40,128]{2,1,0:T(8,128)S(1)}, f32[8,40,128]{2,1,0:T(8,128)S(1)}, u32[]{:S(2)}, u32[]{:S(2)}) collective-permute-start(f32[8,40,128]{2,1,0:T(8,128)S(1)} %get-tuple-element.56), channel_id=1, source_target_pairs={{0,16},{1,17},{2,18},{3,19},{4,20},{5,21},{6,22},{7,23},{8,24},{9,... | collective-permute-start | bytes 491528 | tf_op jit(solution)/shard_map/ppermute | solution.py:545
  14.2 12.3 %collective-permute-start.3 = (f32[8,40,128]{2,1,0:T(8,128)S(1)}, f32[8,40,128]{2,1,0:T(8,128)S(1)}, u32[]{:S(2)}, u32[]{:S(2)}) collective-permute-start(f32[8,40,128]{2,1,0:T(8,128)S(1)} %get-tuple-element.57), channel_id=1, source_target_pairs={{0,8},{1,9},{2,10},{3,11},{4,12},{5,13},{6,14},{7,15},{8,0},{9,1},... | collective-permute-start | bytes 491528 | tf_op jit(solution)/shard_map/ppermute | solution.py:545
  18.6 15.2 %collective-permute-start.7 = (f32[8,56,128]{2,1,0:T(8,128)S(1)}, f32[8,56,128]{2,1,0:T(8,128)S(1)}, u32[]{:S(2)}, u32[]{:S(2)}) collective-permute-start(f32[8,56,128]{2,1,0:T(8,128)S(1)} %get-tuple-element.63), channel_id=1, source_target_pairs={{0,8},{1,9},{2,10},{3,11},{4,12},{5,13},{6,14},{7,15},{8,0},{9,1},... | collective-permute-start | bytes 688136 | tf_op jit(solution)/shard_map/ppermute | solution.py:545
  21.3 7.5 %collective-permute-start.8 = (f32[8,24,128]{2,1,0:T(8,128)S(1)}, f32[8,24,128]{2,1,0:T(8,128)S(1)}, u32[]{:S(2)}, u32[]{:S(2)}) collective-permute-start(f32[8,24,128]{2,1,0:T(8,128)S(1)} %get-tuple-element.65), channel_id=1, source_target_pairs={{0,2},{1,3},{2,0},{3,1},{4,6},{5,7},{6,4},{7,5},{8,10},{9,11},{10,... | collective-permute-start | bytes 294920 | tf_op jit(solution)/shard_map/ppermute | solution.py:545
  27.2 11.2 %collective-permute-start.6 = (f32[8,40,128]{2,1,0:T(8,128)S(1)}, f32[8,40,128]{2,1,0:T(8,128)S(1)}, u32[]{:S(2)}, u32[]{:S(2)}) collective-permute-start(f32[8,40,128]{2,1,0:T(8,128)S(1)} %get-tuple-element.62), channel_id=1, source_target_pairs={{0,8},{1,9},{2,10},{3,11},{4,12},{5,13},{6,14},{7,15},{8,0},{9,1},... | collective-permute-start | bytes 491528 | tf_op jit(solution)/shard_map/ppermute | solution.py:545
  27.2 11.1 %collective-permute-start.9 = (f32[8,40,128]{2,1,0:T(8,128)S(1)}, f32[8,40,128]{2,1,0:T(8,128)S(1)}, u32[]{:S(2)}, u32[]{:S(2)}) collective-permute-start(f32[8,40,128]{2,1,0:T(8,128)S(1)} %get-tuple-element.67), channel_id=1, source_target_pairs={{0,2},{1,3},{2,0},{3,1},{4,6},{5,7},{6,4},{7,5},{8,10},{9,11},{10,... | collective-permute-start | bytes 491528 | tf_op jit(solution)/shard_map/ppermute | solution.py:545
  34.5 6.3 %collective-permute-start.11 = (f32[8,56,128]{2,1,0:T(8,128)S(1)}, f32[8,56,128]{2,1,0:T(8,128)S(1)}, u32[]{:S(2)}, u32[]{:S(2)}) collective-permute-start(f32[8,56,128]{2,1,0:T(8,128)S(1)} %get-tuple-element.71), channel_id=1, source_target_pairs={{0,2},{1,3},{2,0},{3,1},{4,6},{5,7},{6,4},{7,5},{8,10},{9,11},{10,... | collective-permute-start | bytes 688136 | tf_op jit(solution)/shard_map/ppermute | solution.py:545
  39.0 5.6 %collective-permute-start.10 = (f32[8,40,128]{2,1,0:T(8,128)S(1)}, f32[8,40,128]{2,1,0:T(8,128)S(1)}, u32[]{:S(2)}, u32[]{:S(2)}) collective-permute-start(f32[8,40,128]{2,1,0:T(8,128)S(1)} %get-tuple-element.68), channel_id=1, source_target_pairs={{0,2},{1,3},{2,0},{3,1},{4,6},{5,7},{6,4},{7,5},{8,10},{9,11},{10,... | collective-permute-start | bytes 491528 | tf_op jit(solution)/shard_map/ppermute | solution.py:545
  45.5 12.2 %collective-permute-start.14 = (f32[2,5,4,8,128]{4,3,2,1,0:T(8,128)S(1)}, f32[2,5,4,8,128]{4,3,2,1,0:T(8,128)S(1)}, u32[]{:S(2)}, u32[]{:S(2)}) collective-permute-start(f32[2,5,4,8,128]{4,3,2,1,0:T(8,128)S(1)} %get-tuple-element.83), channel_id=1, source_target_pairs={{0,16},{16,0},{1,17},{17,1},{2,18},{18,2},{3,19},{19,3},{4,20},{20... | collective-permute-start | bytes 491528 | tf_op jit(solution)/shard_map/ppermute | solution.py:676
  47.5 10.8 %collective-permute-start.13 = (f32[5,4,8,128]{3,2,1,0:T(8,128)S(1)}, f32[5,4,8,128]{3,2,1,0:T(8,128)S(1)}, u32[]{:S(2)}, u32[]{:S(2)}) collective-permute-start(f32[5,4,8,128]{3,2,1,0:T(8,128)S(1)} %get-tuple-element.81.y_lo), channel_id=1, source_target_pairs={{0,12},{4,0},{8,4},{12,8},{1,13},{5,1},{9,5},{13,9},{2,14},{6,2},{... | collective-permute-start | bytes 245768 | tf_op jit(solution)/shard_map/ppermute | solution.py:676
  52.7 6.2 %collective-permute-start.12 = (f32[5,4,8,128]{3,2,1,0:T(8,128)S(1)}, f32[5,4,8,128]{3,2,1,0:T(8,128)S(1)}, u32[]{:S(2)}, u32[]{:S(2)}) collective-permute-start(f32[5,4,8,128]{3,2,1,0:T(8,128)S(1)} %get-tuple-element.82.y_hi), channel_id=1, source_target_pairs={{0,4},{4,8},{8,12},{12,0},{1,5},{5,9},{9,13},{13,1},{2,6},{6,10},{... | collective-permute-start | bytes 245768 | tf_op jit(solution)/shard_map/ppermute | solution.py:676
  52.7 3.2 %collective-permute-start.15 = (f32[5,8,128]{2,1,0:T(8,128)S(1)}, f32[5,8,128]{2,1,0:T(8,128)S(1)}, u32[]{:S(2)}, u32[]{:S(2)}) collective-permute-start(f32[5,8,128]{2,1,0:T(8,128)S(1)} %get-tuple-element.84), channel_id=1, source_target_pairs={{0,1},{1,2},{2,3},{3,0},{4,5},{5,6},{6,7},{7,4},{8,9},{9,10},{10,1... | collective-permute-start | bytes 61448 | tf_op jit(solution)/shard_map/ppermute | solution.py:676
  52.7 3.2 %collective-permute-start.16 = (f32[5,8,128]{2,1,0:T(8,128)S(1)}, f32[5,8,128]{2,1,0:T(8,128)S(1)}, u32[]{:S(2)}, u32[]{:S(2)}) collective-permute-start(f32[5,8,128]{2,1,0:T(8,128)S(1)} %get-tuple-element.85), channel_id=1, source_target_pairs={{0,3},{1,0},{2,1},{3,2},{4,7},{5,4},{6,5},{7,6},{8,11},{9,8},{10,9... | collective-permute-start | bytes 61448 | tf_op jit(solution)/shard_map/ppermute | solution.py:676
  60.2 9.8 %collective-permute-start.19 = (f32[2,5,4,8,128]{4,3,2,1,0:T(8,128)S(1)}, f32[2,5,4,8,128]{4,3,2,1,0:T(8,128)S(1)}, u32[]{:S(2)}, u32[]{:S(2)}) collective-permute-start(f32[2,5,4,8,128]{4,3,2,1,0:T(8,128)S(1)} %get-tuple-element.90), channel_id=1, source_target_pairs={{0,16},{16,0},{1,17},{17,1},{2,18},{18,2},{3,19},{19,3},{4,20},{20... | collective-permute-start | bytes 491528 | tf_op jit(solution)/shard_map/ppermute | solution.py:676
  61.8 8.8 %collective-permute-start.18 = (f32[5,4,8,128]{3,2,1,0:T(8,128)S(1)}, f32[5,4,8,128]{3,2,1,0:T(8,128)S(1)}, u32[]{:S(2)}, u32[]{:S(2)}) collective-permute-start(f32[5,4,8,128]{3,2,1,0:T(8,128)S(1)} %get-tuple-element.88.y_lo), channel_id=1, source_target_pairs={{0,12},{4,0},{8,4},{12,8},{1,13},{5,1},{9,5},{13,9},{2,14},{6,2},{... | collective-permute-start | bytes 245768 | tf_op jit(solution)/shard_map/ppermute | solution.py:676
  65.0 7.1 %collective-permute-start.17 = (f32[5,4,8,128]{3,2,1,0:T(8,128)S(1)}, f32[5,4,8,128]{3,2,1,0:T(8,128)S(1)}, u32[]{:S(2)}, u32[]{:S(2)}) collective-permute-start(f32[5,4,8,128]{3,2,1,0:T(8,128)S(1)} %get-tuple-element.89.y_hi), channel_id=1, source_target_pairs={{0,4},{4,8},{8,12},{12,0},{1,5},{5,9},{9,13},{13,1},{2,6},{6,10},{... | collective-permute-start | bytes 245768 | tf_op jit(solution)/shard_map/ppermute | solution.py:676
  65.0 3.2 %collective-permute-start.20 = (f32[5,8,128]{2,1,0:T(8,128)S(1)}, f32[5,8,128]{2,1,0:T(8,128)S(1)}, u32[]{:S(2)}, u32[]{:S(2)}) collective-permute-start(f32[5,8,128]{2,1,0:T(8,128)S(1)} %get-tuple-element.91), channel_id=1, source_target_pairs={{0,1},{1,2},{2,3},{3,0},{4,5},{5,6},{6,7},{7,4},{8,9},{9,10},{10,1... | collective-permute-start | bytes 61448 | tf_op jit(solution)/shard_map/ppermute | solution.py:676
  66.1 2.2 %collective-permute-start.21 = (f32[5,8,128]{2,1,0:T(8,128)S(1)}, f32[5,8,128]{2,1,0:T(8,128)S(1)}, u32[]{:S(2)}, u32[]{:S(2)}) collective-permute-start(f32[5,8,128]{2,1,0:T(8,128)S(1)} %get-tuple-element.92), channel_id=1, source_target_pairs={{0,3},{1,0},{2,1},{3,2},{4,7},{5,4},{6,5},{7,6},{8,11},{9,8},{10,9... | collective-permute-start | bytes 61448 | tf_op jit(solution)/shard_map/ppermute | solution.py:676

commit v6 on v5

--- a/solution.py
+++ b/solution.py
@@ -216,7 +216,7 @@
     def faces(self):
         x = jax.ShapeDtypeStruct((2, NF, self.pad, SUB, LANES), f32)
         y = jax.ShapeDtypeStruct((NF, self.edge // self.fit, SUB, LANES), f32)
-        z = jax.ShapeDtypeStruct((NF, SUB, LANES), f32)
+        z = jax.ShapeDtypeStruct((NF, self.rows, LANES), f32)
         return [x, y, y, z, z]
 
 
@@ -244,14 +244,11 @@
                 hi = jnp.where(mine, above, hi)
         y_lo[f, slab] = lo
         y_hi[f, slab] = hi
-        below = lane_roll(prim[shape.across(f, slab, 0), :], 2 * slab)
-        above = lane_roll(prim[shape.across(f, slab, SUB - 1), :], 2 * slab + 2 - shape.edge)
-        if slab:
-            mine = lax.rem(lane, shape.edge) >= 2 * slab
-            below = jnp.where(mine, below, z_lo[f])
-            above = jnp.where(mine, above, z_hi[f])
-        z_lo[f] = below
-        z_hi[f] = above
+        to = pl.ds(slab * SUB, SUB) if isinstance(slab, int) else pl.ds(
+            pl.multiple_of(slab * SUB, SUB), SUB
+        )
+        z_lo[f, to, :] = prim[shape.across(f, slab, 0), :]
+        z_hi[f, to, :] = prim[shape.across(f, slab, SUB - 1), :]
 
 
 def send_x(shape, prim, faces, low=True, high=True):
@@ -297,18 +294,15 @@
     send_x(shape, prim, x_faces, low=first, high=not first)
 
 
-def sweep_z_kernel(prim, z_prev, z_next, total, prev_z, next_z, flux_z, right_z, left, right, flux, *, shape):
+def sweep_z_kernel(prim, z_lo, z_hi, z_prev, z_next, total, flux_z, right_z, left, right, flux, *, shape):
     edge, rows = shape.edge, shape.rows
 
     def ghost(a):
         at = pl.ds(a * SUB, SUB)
-        low = [prim[shape.across(f, a, 0), :] for f in FIELDS]
-        high = [prim[shape.across(f, a, SUB - 1), :] for f in FIELDS]
-        prev = [lane_roll(z_prev[f], edge - 2 - 2 * a) for f in FIELDS]
-        after = [lane_roll(z_next[f], -2 * a) for f in FIELDS]
-        for f in FIELDS:
-            prev_z[f, at, :] = prev[f]
-            next_z[f, at, :] = after[f]
+        low = [z_lo[f, at, :] for f in FIELDS]
+        high = [z_hi[f, at, :] for f in FIELDS]
+        prev = [z_prev[f, at, :] for f in FIELDS]
+        after = [z_next[f, at, :] for f in FIELDS]
         below = [lane_roll(v, -(edge - 1)) for v in prev]
         before = [lane_roll(v, -(edge - 2)) for v in prev]
         second = [lane_roll(v, -1) for v in low]
@@ -347,7 +341,7 @@
             for f in FIELDS:
                 at = shape.at(f, row)
                 mine = prim[at, :]
-                shift = half_minmod(mine - down(mine, f, row, prev_z), up(mine, f, row, next_z) - mine)
+                shift = half_minmod(mine - down(mine, f, row, z_prev), up(mine, f, row, z_next) - mine)
                 left[at, :] = mine + shift
                 right[at, :] = mine - shift
 
@@ -531,7 +525,7 @@
     groups = slots // SUB
     shape = Shape(rows, edge)
     units = NF * shape.slabs
-    pieces = split_units(units, (3, 5, 7, 5))
+    pieces = split_units(units, (3, 5, 5, 4, 3))
     firsts = split_units(units, (3, 5, 7, 5))
 
     bit_z = size_z.bit_length() - 2
@@ -627,8 +621,9 @@
         ([(1, 1)], [3], []),
         ([(1, 2), (2, 0)], [], []),
         ([(1, 3), (2, 1)], [], []),
-        ([(2, 2)], [], [0]),
+        ([(1, 4), (2, 2)], [], [0]),
         ([(2, 3)], [], [1]),
+        ([(2, 4)], [], [2]),
     ]
     got[0][0] = swapped(sent[0], 0)
     got[0][1] = swapped(sent[1], 0)
@@ -687,13 +682,12 @@
         total = pl.pallas_call(
             functools.partial(sweep_z_kernel, shape=shape),
             out_shape=grid,
-            in_specs=[whole(VMEM)] * 3,
+            in_specs=[whole(VMEM)] * 5,
             out_specs=whole(VMEM),
-            scratch_shapes=[ghost] * 4 + work,
+            scratch_shapes=[ghost] * 2 + work,
             compiler_params=params(),
-            cost_estimate=cost(1, 1),
             name="sweep_z",
-        )(prim, z_prev, z_next)
+        )(prim, z_lo, z_hi, z_prev, z_next)
         total = pl.pallas_call(
             functools.partial(sweep_x_kernel, shape=shape),
             out_shape=grid,
@@ -701,7 +695,6 @@
             out_specs=whole(VMEM),
             input_output_aliases={2: 0},
             compiler_params=params(),
-            cost_estimate=cost(1, 1),
             name="sweep_x",
         )(prim, x_faces, total)
         return y_lo, y_hi, y_prev, y_next, total

time: 75.1 us -> 75.1 us (level)
    ppermute x12 -> x14, waiting for transfers between devices: 16 us -> 13.3 us  [swapped(): return lax.ppermute(value, AXES, pairs)]
    ppermute x10, waiting for transfers between devices: 5.08 us -> 7.62 us  [ring(): lax.ppermute(value, axis, [(i, (i + step) % size) for i in range(size)])]
    ppermute x10, starting transfers between devices: 15.5 us -> 13.9 us  [ring(): lax.ppermute(value, axis, [(i, (i + step) % size) for i in range(size)])]
    ppermute x12 -> x14, starting transfers between devices: 20.3 us -> 21.8 us  [swapped(): return lax.ppermute(value, AXES, pairs)]
    pallas_call x6 -> x7, Pallas kernels: 3.97 us -> 4.67 us  [make(): pl.pallas_call(functools.partial(pick_kernel, plan=plan, held=tuple(found...]
  transfers between devices with their start and end apart: 22 -> 24, of which waited for: 12 -> 13; matrix products, arithmetic and copies ran while one was open for 0% -> 0% of each run, Pallas kernels for 16% -> 16%
where the time goes in v6:
time: 75.1 us; the launch traced here: 74.9 us
  starting transfers between devices  35.6 us (47%)
  waiting for transfers between devices  20.9 us (28%)
  Pallas kernels  18.1 us (24%)
    ppermute x14, starting transfers between devices, swapped(): return lax.ppermute(value, AXES, pairs)  21.8 us
    ppermute x10, starting transfers between devices, ring(): lax.ppermute(value, axis, [(i, (i + step) % size) for i in range(size)])  13.9 us
    ppermute x14, waiting for transfers between devices, swapped(): return lax.ppermute(value, AXES, pairs)  13.3 us
    ppermute x10, waiting for transfers between devices, ring(): lax.ppermute(value, axis, [(i, (i + step) % size) for i in range(size)])  7.62 us
    pallas_call x7, Pallas kernels, make(): pl.pallas_call(functools.partial(pick_kernel, plan=plan, held=tuple(found...  4.67 us
    pallas_call x2, Pallas kernels, flux_sums(): pl.pallas_call(functools.partial(sweep_z_kernel, shape=shape), out_shape=...  3.08 us
    pallas_call x1, Pallas kernels, shards(): pl.pallas_call(functools.partial(sweep_y_two_kernel, shape=shape, occ=occ...  2.92 us
    pallas_call x2, Pallas kernels, assemble(): pl.pallas_call(functools.partial(assemble_kernel, held=tuple(found), slab...  2.38 us
  transfers between devices with their start and end apart: 24, of which 13 were waited for; matrix products, arithmetic and copies ran while one was open for 0% of the time, Pallas kernels for 16%

profile of v6, /device:TPU:0, one launch (start us, length us, event | category | flops | bytes accessed | tf_op | source)
XLA Modules:
  0.0 74.9 jit_solution(8530257003433703850)
XLA Ops:
  0.0 1.2 %pack_first.1 = f32[8,24,128]{2,1,0:T(8,128)S(1)} custom-call(s32[3,1,8]{2,1,0:T(1,128)} %send_hbm.1, f32[5120,128]{1,0:T(8,128)} %bitcast.10), custom_call_target="tpu_custom_call" | custom-call | tf_op jit(solution)/shard_map/pack_first/pallas_call | solution.py:558
  1.3 3.0 %collective-permute-start.1 = (f32[8,24,128]{2,1,0:T(8,128)S(1)}, f32[8,24,128]{2,1,0:T(8,128)S(1)}, u32[]{:S(2)}, u32[]{:S(2)}) collective-permute-start(f32[8,24,128]{2,1,0:T(8,128)S(1)} %pack_first.1), channel_id=1, source_target_pairs={{0,16},{1,17},{2,18},{3,19},{4,20},{5,21},{6,22},{7,23},{8,24},{9,... | collective-permute-start | bytes 294920 | tf_op jit(solution)/shard_map/ppermute | solution.py:539
  4.3 0.1 dynamic_slice.3.own
  4.4 1.4 %pack_rest.1 = (s32[24]{0:T(128)S(1)}, f32[8,128]{1,0:T(8,128)S(1)}, f32[8,40,128]{2,1,0:T(8,128)S(1)}, f32[8,56,128]{2,1,0:T(8,128)S(1)}, f32[8,40,128]{2,1,0:T(8,128)S(1)}) custom-call(s32[3,1,8]{2,1,0:T(1,128)S(1)} %copy-done.1, s32[3,1,8]{2,1,0:T(1,128)S(1)} %copy-done.2, s32[8]{0:T(128)S(1)} %dynamic_slice.3.own, f32[5120,128]{1,0:T(8,128)S(1)} %bitcast.11), custom_call_target="tpu_custom_call" | custom-call | tf_op jit(solution)/shard_map/pack_rest/pallas_call | solution.py:571
  5.8 0.6 collective-permute-start
  6.4 0.7 collective-permute-done.1.refs_0_.refs_1_
  7.1 0.6 pick_10.1
  7.7 2.0 %collective-permute-start.3 = (f32[8,56,128]{2,1,0:T(8,128)S(1)}, f32[8,56,128]{2,1,0:T(8,128)S(1)}, u32[]{:S(2)}, u32[]{:S(2)}) collective-permute-start(f32[8,56,128]{2,1,0:T(8,128)S(1)} %get-tuple-element.61), channel_id=1, source_target_pairs={{0,16},{1,17},{2,18},{3,19},{4,20},{5,21},{6,22},{7,23},{8,24},{9,... | collective-permute-start | bytes 688136 | tf_op jit(solution)/shard_map/ppermute | solution.py:539
  9.7 2.6 %collective-permute-start.5 = (f32[8,24,128]{2,1,0:T(8,128)S(1)}, f32[8,24,128]{2,1,0:T(8,128)S(1)}, u32[]{:S(2)}, u32[]{:S(2)}) collective-permute-start(f32[8,24,128]{2,1,0:T(8,128)S(1)} %get-tuple-element.63), channel_id=1, source_target_pairs={{0,8},{1,9},{2,10},{3,11},{4,12},{5,13},{6,14},{7,15},{8,0},{9,1},... | collective-permute-start | bytes 294920 | tf_op jit(solution)/shard_map/ppermute | solution.py:539
  12.3 0.7 collective-permute-done.refs_0_.refs_2_.refs_1_
  13.0 0.6 pick_11.1
  13.6 0.6 collective-permute-start.2
  14.2 2.6 %collective-permute-start.4 = (f32[8,40,128]{2,1,0:T(8,128)S(1)}, f32[8,40,128]{2,1,0:T(8,128)S(1)}, u32[]{:S(2)}, u32[]{:S(2)}) collective-permute-start(f32[8,40,128]{2,1,0:T(8,128)S(1)} %get-tuple-element.62), channel_id=1, source_target_pairs={{0,8},{1,9},{2,10},{3,11},{4,12},{5,13},{6,14},{7,15},{8,0},{9,1},... | collective-permute-start | bytes 491528 | tf_op jit(solution)/shard_map/ppermute | solution.py:539
  16.8 0.0 collective-permute-done.5.refs_2_.refs_3_
  16.8 1.1 %collective-permute-done.3.refs_0_.refs_1_.refs_2_ = f32[8,56,128]{2,1,0:T(8,128)S(1)} collective-permute-done((f32[8,56,128]{2,1,0:T(8,128)S(1)}, f32[8,56,128]{2,1,0:T(8,128)S(1)}, u32[]{:S(2)}, u32[]{:S(2)}) %collective-permute-start.3) | collective-permute-done | bytes 229408 | tf_op jit(solution)/shard_map/ppermute | solution.py:539
  17.9 0.7 pick_12_20.1
  18.6 2.7 %collective-permute-start.7 = (f32[8,40,128]{2,1,0:T(8,128)S(1)}, f32[8,40,128]{2,1,0:T(8,128)S(1)}, u32[]{:S(2)}, u32[]{:S(2)}) collective-permute-start(f32[8,40,128]{2,1,0:T(8,128)S(1)} %get-tuple-element.67), channel_id=1, source_target_pairs={{0,8},{1,9},{2,10},{3,11},{4,12},{5,13},{6,14},{7,15},{8,0},{9,1},... | collective-permute-start | bytes 491528 | tf_op jit(solution)/shard_map/ppermute | solution.py:539
  21.3 1.5 %collective-permute-start.8 = (f32[8,24,128]{2,1,0:T(8,128)S(1)}, f32[8,24,128]{2,1,0:T(8,128)S(1)}, u32[]{:S(2)}, u32[]{:S(2)}) collective-permute-start(f32[8,24,128]{2,1,0:T(8,128)S(1)} %get-tuple-element.69), channel_id=1, source_target_pairs={{0,2},{1,3},{2,0},{3,1},{4,6},{5,7},{6,4},{7,5},{8,10},{9,11},{10,... | collective-permute-start | bytes 294920 | tf_op jit(solution)/shard_map/ppermute | solution.py:539
  22.8 0.0 collective-permute-done.2.refs_1_.refs_0_
  22.8 3.0 %collective-permute-done.4.refs_3_.refs_4_ = f32[8,40,128]{2,1,0:T(8,128)S(1)} collective-permute-done((f32[8,40,128]{2,1,0:T(8,128)S(1)}, f32[8,40,128]{2,1,0:T(8,128)S(1)}, u32[]{:S(2)}, u32[]{:S(2)}) %collective-permute-start.4) | collective-permute-done | bytes 163872 | tf_op jit(solution)/shard_map/ppermute | solution.py:539
  25.7 0.7 pick_13_21.1
  26.5 0.1 collective-permute-start.6
  26.5 1.6 %collective-permute-start.10 = (f32[8,40,128]{2,1,0:T(8,128)S(1)}, f32[8,40,128]{2,1,0:T(8,128)S(1)}, u32[]{:S(2)}, u32[]{:S(2)}) collective-permute-start(f32[8,40,128]{2,1,0:T(8,128)S(1)} %get-tuple-element.72), channel_id=1, source_target_pairs={{0,2},{1,3},{2,0},{3,1},{4,6},{5,7},{6,4},{7,5},{8,10},{9,11},{10,... | collective-permute-start | bytes 491528 | tf_op jit(solution)/shard_map/ppermute | solution.py:539
  28.1 0.0 collective-permute-done.8.refs_4_
  28.1 2.4 %collective-permute-done.7.refs_2_.refs_5_ = f32[8,40,128]{2,1,0:T(8,128)S(1)} collective-permute-done((f32[8,40,128]{2,1,0:T(8,128)S(1)}, f32[8,40,128]{2,1,0:T(8,128)S(1)}, u32[]{:S(2)}, u32[]{:S(2)}) %collective-permute-start.7) | collective-permute-done | bytes 163872 | tf_op jit(solution)/shard_map/ppermute | solution.py:539
  30.5 0.7 pick_14_22.1
  31.2 1.6 %collective-permute-start.12 = (f32[8,40,128]{2,1,0:T(8,128)S(1)}, f32[8,40,128]{2,1,0:T(8,128)S(1)}, u32[]{:S(2)}, u32[]{:S(2)}) collective-permute-start(f32[8,40,128]{2,1,0:T(8,128)S(1)} %get-tuple-element.75), channel_id=1, source_target_pairs={{0,2},{1,3},{2,0},{3,1},{4,6},{5,7},{6,4},{7,5},{8,10},{9,11},{10,... | collective-permute-start | bytes 491528 | tf_op jit(solution)/shard_map/ppermute | solution.py:539
  32.7 0.0 collective-permute-start.9
  32.7 2.5 %collective-permute-done.6.refs_2_.refs_6_.refs_1_ = f32[8,32,128]{2,1,0:T(8,128)S(1)} collective-permute-done((f32[8,32,128]{2,1,0:T(8,128)S(1)}, f32[8,32,128]{2,1,0:T(8,128)S(1)}, u32[]{:S(2)}, u32[]{:S(2)}) %collective-permute-start.6) | collective-permute-done | bytes 131104 | tf_op jit(solution)/shard_map/ppermute | solution.py:539
  35.3 0.0 collective-permute-done.10.refs_4_
  35.3 0.6 pick_23.1
  35.9 1.6 %collective-permute-start.11 = (f32[8,32,128]{2,1,0:T(8,128)S(1)}, f32[8,32,128]{2,1,0:T(8,128)S(1)}, u32[]{:S(2)}, u32[]{:S(2)}) collective-permute-start(f32[8,32,128]{2,1,0:T(8,128)S(1)} %get-tuple-element.73), channel_id=1, source_target_pairs={{0,2},{1,3},{2,0},{3,1},{4,6},{5,7},{6,4},{7,5},{8,10},{9,11},{10,... | collective-permute-start | bytes 393224 | tf_op jit(solution)/shard_map/ppermute | solution.py:539
  37.5 1.3 %collective-permute-done.9.refs_1_.refs_2_ = f32[8,24,128]{2,1,0:T(8,128)S(1)} collective-permute-done((f32[8,24,128]{2,1,0:T(8,128)S(1)}, f32[8,24,128]{2,1,0:T(8,128)S(1)}, u32[]{:S(2)}, u32[]{:S(2)}) %collective-permute-start.9) | collective-permute-done | bytes 98336 | tf_op jit(solution)/shard_map/ppermute | solution.py:539
  38.8 0.0 collective-permute-done.12.refs_3_
  38.8 0.6 pick_24.1
  39.4 1.5 %collective-permute-start.13 = (f32[8,24,128]{2,1,0:T(8,128)S(1)}, f32[8,24,128]{2,1,0:T(8,128)S(1)}, u32[]{:S(2)}, u32[]{:S(2)}) collective-permute-start(f32[8,24,128]{2,1,0:T(8,128)S(1)} %get-tuple-element.76), channel_id=1, source_target_pairs={{0,2},{1,3},{2,0},{3,1},{4,6},{5,7},{6,4},{7,5},{8,10},{9,11},{10,... | collective-permute-start | bytes 294920 | tf_op jit(solution)/shard_map/ppermute | solution.py:539
  40.9 0.7 collective-permute-done.11.refs_10_.refs_3_
  41.6 1.5 %assemble_0.1 = (f32[1280,128]{1,0:T(8,128)S(1)}, f32[1280,128]{1,0:T(8,128)S(1)}, f32[5,4,8,128]{3,2,1,0:T(8,128)S(1)}, f32[5,4,8,128]{3,2,1,0:T(8,128)S(1)}, f...) custom-call(s32[24]{0:T(128)S(1)} %get-tuple-element.54.tags, ...), custom_call_target="tpu_custom_call" | custom-call | tf_op jit(solution)/shard_map/assemble_0/pallas_call | solution.py:651
  43.1 1.0 %collective-permute-done.13.refs_4_ = f32[8,24,128]{2,1,0:T(8,128)S(1)} collective-permute-done((f32[8,24,128]{2,1,0:T(8,128)S(1)}, f32[8,24,128]{2,1,0:T(8,128)S(1)}, u32[]{:S(2)}, u32[]{:S(2)}) %collective-permute-start.13) | collective-permute-done | bytes 98336 | tf_op jit(solution)/shard_map/ppermute | solution.py:539
  44.1 0.9 %assemble_3.1 = (f32[1280,128]{1,0:T(8,128)S(1)}, f32[1280,128]{1,0:T(8,128)S(1)}, f32[5,4,8,128]{3,2,1,0:T(8,128)S(1)}, f32[5,4,8,128]{3,2,1,0:T(8,128)S(1)}, f...) custom-call(s32[24]{0:T(128)S(1)} %get-tuple-element.54.tags, ...), custom_call_target="tpu_custom_call", output_to_operand_aliasing={{0}: (7, {}), {1}: (8, {}), {2}: (9, {}), {3}: (10, {}), {4... | custom-call | tf_op jit(solution)/shard_map/assemble_3/pallas_call | solution.py:651
  45.0 3.7 %collective-permute-start.16 = (f32[2,5,4,8,128]{4,3,2,1,0:T(8,128)S(1)}, f32[2,5,4,8,128]{4,3,2,1,0:T(8,128)S(1)}, u32[]{:S(2)}, u32[]{:S(2)}) collective-permute-start(f32[2,5,4,8,128]{4,3,2,1,0:T(8,128)S(1)} %get-tuple-element.91), channel_id=1, source_target_pairs={{0,16},{16,0},{1,17},{17,1},{2,18},{18,2},{3,19},{19,3},{4,20},{20... | collective-permute-start | bytes 491528 | tf_op jit(solution)/shard_map/ppermute | solution.py:671
  48.6 0.5 collective-permute-start.17
  49.1 5.2 %collective-permute-start.15 = (f32[5,4,8,128]{3,2,1,0:T(8,128)S(1)}, f32[5,4,8,128]{3,2,1,0:T(8,128)S(1)}, u32[]{:S(2)}, u32[]{:S(2)}) collective-permute-start(f32[5,4,8,128]{3,2,1,0:T(8,128)S(1)} %get-tuple-element.89.y_lo), channel_id=1, source_target_pairs={{0,12},{4,0},{8,4},{12,8},{1,13},{5,1},{9,5},{13,9},{2,14},{6,2},{... | collective-permute-start | bytes 245768 | tf_op jit(solution)/shard_map/ppermute | solution.py:671
  54.3 0.0 collective-permute-start.14
  54.3 0.0 collective-permute-done.18.z_next
  54.3 0.0 collective-permute-done.17.z_prev
  54.3 1.5 %sweep_z.2.sofar = f32[1280,128]{1,0:T(8,128)S(1)} custom-call(f32[1280,128]{1,0:T(8,128)S(1)} %get-tuple-element.88.prim, f32[5,32,128]{2,1,0:T(8,128)S(1)} %get-tuple-element.92.z_lo, f32[5,32,128]{2,1,0:T(8,128)S(1)} %get-tuple-element.93.z_hi, f32[5,32,128]{2,1,0:T(8,128)S(1)} %collective-permute-done.17.z_prev, ...), custom_call_target="tpu_custom_call" | custom-call | tf_op jit(solution)/shard_map/sweep_z/pallas_call | solution.py:682
  55.9 0.6 sweep_x.2.sofar
  56.5 0.7 collective-permute-done.15.y_next
  57.2 4.0 %collective-permute-done.14.y_prev = f32[5,4,8,128]{3,2,1,0:T(8,128)S(1)} collective-permute-done((f32[5,4,8,128]{3,2,1,0:T(8,128)S(1)}, f32[5,4,8,128]{3,2,1,0:T(8,128)S(1)}, u32[]{:S(2)}, u32[]{:S(2)}) %collective-permute-start.14) | collective-permute-done | bytes 81952 | tf_op jit(solution)/shard_map/ppermute | solution.py:671
  61.2 1.3 %sweep_y_one.1 = (f32[1280,128]{1,0:T(8,128)S(1)}, f32[1280,128]{1,0:T(8,128)S(1)}, f32[2,5,4,8,128]{4,3,2,1,0:T(8,128)S(1)}, f32[5,4,8,128]{3,2,1,0:T(8,128)S(1...) custom-call(f32[1280,128]{1,0:T(8,128)S(1)} %get-tuple-element.87.field, ...), custom_call_target="tpu_custom_call" | custom-call | tf_op jit(solution)/shard_map/sweep_y_one/pallas_call | solution.py:706
  62.5 2.0 %collective-permute-start.21 = (f32[2,5,4,8,128]{4,3,2,1,0:T(8,128)S(1)}, f32[2,5,4,8,128]{4,3,2,1,0:T(8,128)S(1)}, u32[]{:S(2)}, u32[]{:S(2)}) collective-permute-start(f32[2,5,4,8,128]{4,3,2,1,0:T(8,128)S(1)} %get-tuple-element.98), channel_id=1, source_target_pairs={{0,16},{16,0},{1,17},{17,1},{2,18},{18,2},{3,19},{19,3},{4,20},{20... | collective-permute-start | bytes 491528 | tf_op jit(solution)/shard_map/ppermute | solution.py:671
  64.4 0.0 collective-permute-start.23
  64.4 0.5 collective-permute-start.22
  64.9 0.1 collective-permute-start.20
  65.1 1.9 %collective-permute-start.19 = (f32[5,4,8,128]{3,2,1,0:T(8,128)S(1)}, f32[5,4,8,128]{3,2,1,0:T(8,128)S(1)}, u32[]{:S(2)}, u32[]{:S(2)}) collective-permute-start(f32[5,4,8,128]{3,2,1,0:T(8,128)S(1)} %get-tuple-element.97.y_hi), channel_id=1, source_target_pairs={{0,4},{4,8},{8,12},{12,0},{1,5},{5,9},{9,13},{13,1},{2,6},{6,10},{... | collective-permute-start | bytes 245768 | tf_op jit(solution)/shard_map/ppermute | solution.py:671
  67.0 0.0 collective-permute-done.23.z_next
  67.0 2.0 %collective-permute-done.22.z_prev = f32[5,32,128]{2,1,0:T(8,128)S(1)} collective-permute-done((f32[5,32,128]{2,1,0:T(8,128)S(1)}, f32[5,32,128]{2,1,0:T(8,128)S(1)}, u32[]{:S(2)}, u32[]{:S(2)}) %collective-permute-start.22) | collective-permute-done | bytes 81952 | tf_op jit(solution)/shard_map/ppermute | solution.py:671
  69.0 1.5 %sweep_z.3.sofar = f32[1280,128]{1,0:T(8,128)S(1)} custom-call(f32[1280,128]{1,0:T(8,128)S(1)} %get-tuple-element.95.prim, f32[5,32,128]{2,1,0:T(8,128)S(1)} %get-tuple-element.99.z_lo, f32[5,32,128]{2,1,0:T(8,128)S(1)} %get-tuple-element.100.z_hi, f32[5,32,128]{2,1,0:T(8,128)S(1)} %collective-permute-done.22.z_prev, ...), custom_call_target="tpu_custom_call" | custom-call | tf_op jit(solution)/shard_map/sweep_z/pallas_call | solution.py:682
  70.5 0.0 collective-permute-done.21.x_faces
  70.5 0.6 sweep_x.3.sofar
  71.1 0.0 collective-permute-done.20.y_next
  71.1 0.9 %collective-permute-done.19.y_prev = f32[5,4,8,128]{3,2,1,0:T(8,128)S(1)} collective-permute-done((f32[5,4,8,128]{3,2,1,0:T(8,128)S(1)}, f32[5,4,8,128]{3,2,1,0:T(8,128)S(1)}, u32[]{:S(2)}, u32[]{:S(2)}) %collective-permute-start.19) | collective-permute-done | bytes 81952 | tf_op jit(solution)/shard_map/ppermute | solution.py:671
  72.0 2.9 %sweep_y_two.1 = (f32[20,256,128]{2,1,0:T(8,128)}, f32[20,256,128]{2,1,0:T(8,128)S(1)}) custom-call(s32[8]{0:T(128)S(1)} %dynamic_slice.3.own, f32[1280,128]{1,0:T(8,128)S(1)} %get-tuple-element.87.field, f32[1280,128]{1,0:T(8,128)S(1)} %get-tuple-element.94.one, f32[1280,128]{1,0:T(8,128)S(1)} %get-tuple-element.95.prim, ...), custom_call_target="tpu_custom_call", output_to_operand_aliasing={{1}: (9, {})} | custom-call | tf_op jit(solution)/shard_map/sweep_y_two/pallas_call | solution.py:717
  (10 shorter events, 0.0 us)
Async XLA Ops:
  0.0 4.4 %copy-start.1 = (s32[3,1,8]{2,1,0:T(1,128)S(1)}, s32[3,1,8]{2,1,0:T(1,128)}, u32[]{:S(2)}) copy-start(s32[3,1,8]{2,1,0:T(1,128)} %send_hbm.1) | copy-start | bytes 292
  0.0 4.4 %copy-start = (f32[32,5,4096]{2,0,1:T(8,128)S(1)}, f32[32,5,4096]{2,0,1:T(8,128)}, u32[]{:S(2)}) copy-start(f32[32,5,4096]{2,0,1:T(8,128)} %param.4) | copy-start | bytes 7864324
  0.0 4.3 %copy-start.3 = (s32[256]{0:T(256)S(1)}, s32[256]{0:T(256)}, u32[]{:S(2)}) copy-start(s32[256]{0:T(256)} %param.7) | copy-start | bytes 3076
  0.0 4.4 %copy-start.2 = (s32[3,1,8]{2,1,0:T(1,128)S(1)}, s32[3,1,8]{2,1,0:T(1,128)}, u32[]{:S(2)}) copy-start(s32[3,1,8]{2,1,0:T(1,128)} %recv.1) | copy-start | bytes 292
  1.3 5.8 %collective-permute-start.1 = (f32[8,24,128]{2,1,0:T(8,128)S(1)}, f32[8,24,128]{2,1,0:T(8,128)S(1)}, u32[]{:S(2)}, u32[]{:S(2)}) collective-permute-start(f32[8,24,128]{2,1,0:T(8,128)S(1)} %pack_first.1), channel_id=1, source_target_pairs={{0,16},{1,17},{2,18},{3,19},{4,20},{5,21},{6,22},{7,23},{8,24},{9,... | collective-permute-start | bytes 294920 | tf_op jit(solution)/shard_map/ppermute | solution.py:539
  5.8 7.2 %collective-permute-start = (f32[8,40,128]{2,1,0:T(8,128)S(1)}, f32[8,40,128]{2,1,0:T(8,128)S(1)}, u32[]{:S(2)}, u32[]{:S(2)}) collective-permute-start(f32[8,40,128]{2,1,0:T(8,128)S(1)} %get-tuple-element.55), channel_id=1, source_target_pairs={{0,16},{1,17},{2,18},{3,19},{4,20},{5,21},{6,22},{7,23},{8,24},{9,... | collective-permute-start | bytes 491528 | tf_op jit(solution)/shard_map/ppermute | solution.py:539
  7.7 10.2 %collective-permute-start.3 = (f32[8,56,128]{2,1,0:T(8,128)S(1)}, f32[8,56,128]{2,1,0:T(8,128)S(1)}, u32[]{:S(2)}, u32[]{:S(2)}) collective-permute-start(f32[8,56,128]{2,1,0:T(8,128)S(1)} %get-tuple-element.61), channel_id=1, source_target_pairs={{0,16},{1,17},{2,18},{3,19},{4,20},{5,21},{6,22},{7,23},{8,24},{9,... | collective-permute-start | bytes 688136 | tf_op jit(solution)/shard_map/ppermute | solution.py:539
  9.7 7.1 %collective-permute-start.5 = (f32[8,24,128]{2,1,0:T(8,128)S(1)}, f32[8,24,128]{2,1,0:T(8,128)S(1)}, u32[]{:S(2)}, u32[]{:S(2)}) collective-permute-start(f32[8,24,128]{2,1,0:T(8,128)S(1)} %get-tuple-element.63), channel_id=1, source_target_pairs={{0,8},{1,9},{2,10},{3,11},{4,12},{5,13},{6,14},{7,15},{8,0},{9,1},... | collective-permute-start | bytes 294920 | tf_op jit(solution)/shard_map/ppermute | solution.py:539
  13.6 9.2 %collective-permute-start.2 = (f32[8,40,128]{2,1,0:T(8,128)S(1)}, f32[8,40,128]{2,1,0:T(8,128)S(1)}, u32[]{:S(2)}, u32[]{:S(2)}) collective-permute-start(f32[8,40,128]{2,1,0:T(8,128)S(1)} %get-tuple-element.60), channel_id=1, source_target_pairs={{0,16},{1,17},{2,18},{3,19},{4,20},{5,21},{6,22},{7,23},{8,24},{9,... | collective-permute-start | bytes 491528 | tf_op jit(solution)/shard_map/ppermute | solution.py:539
  14.2 11.5 %collective-permute-start.4 = (f32[8,40,128]{2,1,0:T(8,128)S(1)}, f32[8,40,128]{2,1,0:T(8,128)S(1)}, u32[]{:S(2)}, u32[]{:S(2)}) collective-permute-start(f32[8,40,128]{2,1,0:T(8,128)S(1)} %get-tuple-element.62), channel_id=1, source_target_pairs={{0,8},{1,9},{2,10},{3,11},{4,12},{5,13},{6,14},{7,15},{8,0},{9,1},... | collective-permute-start | bytes 491528 | tf_op jit(solution)/shard_map/ppermute | solution.py:539
  18.6 11.8 %collective-permute-start.7 = (f32[8,40,128]{2,1,0:T(8,128)S(1)}, f32[8,40,128]{2,1,0:T(8,128)S(1)}, u32[]{:S(2)}, u32[]{:S(2)}) collective-permute-start(f32[8,40,128]{2,1,0:T(8,128)S(1)} %get-tuple-element.67), channel_id=1, source_target_pairs={{0,8},{1,9},{2,10},{3,11},{4,12},{5,13},{6,14},{7,15},{8,0},{9,1},... | collective-permute-start | bytes 491528 | tf_op jit(solution)/shard_map/ppermute | solution.py:539
  21.3 6.8 %collective-permute-start.8 = (f32[8,24,128]{2,1,0:T(8,128)S(1)}, f32[8,24,128]{2,1,0:T(8,128)S(1)}, u32[]{:S(2)}, u32[]{:S(2)}) collective-permute-start(f32[8,24,128]{2,1,0:T(8,128)S(1)} %get-tuple-element.69), channel_id=1, source_target_pairs={{0,2},{1,3},{2,0},{3,1},{4,6},{5,7},{6,4},{7,5},{8,10},{9,11},{10,... | collective-permute-start | bytes 294920 | tf_op jit(solution)/shard_map/ppermute | solution.py:539
  26.5 8.8 %collective-permute-start.6 = (f32[8,32,128]{2,1,0:T(8,128)S(1)}, f32[8,32,128]{2,1,0:T(8,128)S(1)}, u32[]{:S(2)}, u32[]{:S(2)}) collective-permute-start(f32[8,32,128]{2,1,0:T(8,128)S(1)} %get-tuple-element.66), channel_id=1, source_target_pairs={{0,8},{1,9},{2,10},{3,11},{4,12},{5,13},{6,14},{7,15},{8,0},{9,1},... | collective-permute-start | bytes 393224 | tf_op jit(solution)/shard_map/ppermute | solution.py:539
  26.5 8.7 %collective-permute-start.10 = (f32[8,40,128]{2,1,0:T(8,128)S(1)}, f32[8,40,128]{2,1,0:T(8,128)S(1)}, u32[]{:S(2)}, u32[]{:S(2)}) collective-permute-start(f32[8,40,128]{2,1,0:T(8,128)S(1)} %get-tuple-element.72), channel_id=1, source_target_pairs={{0,2},{1,3},{2,0},{3,1},{4,6},{5,7},{6,4},{7,5},{8,10},{9,11},{10,... | collective-permute-start | bytes 491528 | tf_op jit(solution)/shard_map/ppermute | solution.py:539
  31.2 7.6 %collective-permute-start.12 = (f32[8,40,128]{2,1,0:T(8,128)S(1)}, f32[8,40,128]{2,1,0:T(8,128)S(1)}, u32[]{:S(2)}, u32[]{:S(2)}) collective-permute-start(f32[8,40,128]{2,1,0:T(8,128)S(1)} %get-tuple-element.75), channel_id=1, source_target_pairs={{0,2},{1,3},{2,0},{3,1},{4,6},{5,7},{6,4},{7,5},{8,10},{9,11},{10,... | collective-permute-start | bytes 491528 | tf_op jit(solution)/shard_map/ppermute | solution.py:539
  32.7 6.0 %collective-permute-start.9 = (f32[8,24,128]{2,1,0:T(8,128)S(1)}, f32[8,24,128]{2,1,0:T(8,128)S(1)}, u32[]{:S(2)}, u32[]{:S(2)}) collective-permute-start(f32[8,24,128]{2,1,0:T(8,128)S(1)} %get-tuple-element.70), channel_id=1, source_target_pairs={{0,8},{1,9},{2,10},{3,11},{4,12},{5,13},{6,14},{7,15},{8,0},{9,1},... | collective-permute-start | bytes 294920 | tf_op jit(solution)/shard_map/ppermute | solution.py:539
  35.9 5.7 %collective-permute-start.11 = (f32[8,32,128]{2,1,0:T(8,128)S(1)}, f32[8,32,128]{2,1,0:T(8,128)S(1)}, u32[]{:S(2)}, u32[]{:S(2)}) collective-permute-start(f32[8,32,128]{2,1,0:T(8,128)S(1)} %get-tuple-element.73), channel_id=1, source_target_pairs={{0,2},{1,3},{2,0},{3,1},{4,6},{5,7},{6,4},{7,5},{8,10},{9,11},{10,... | collective-permute-start | bytes 393224 | tf_op jit(solution)/shard_map/ppermute | solution.py:539
  39.4 4.7 %collective-permute-start.13 = (f32[8,24,128]{2,1,0:T(8,128)S(1)}, f32[8,24,128]{2,1,0:T(8,128)S(1)}, u32[]{:S(2)}, u32[]{:S(2)}) collective-permute-start(f32[8,24,128]{2,1,0:T(8,128)S(1)} %get-tuple-element.76), channel_id=1, source_target_pairs={{0,2},{1,3},{2,0},{3,1},{4,6},{5,7},{6,4},{7,5},{8,10},{9,11},{10,... | collective-permute-start | bytes 294920 | tf_op jit(solution)/shard_map/ppermute | solution.py:539
  45.0 10.9 %collective-permute-start.16 = (f32[2,5,4,8,128]{4,3,2,1,0:T(8,128)S(1)}, f32[2,5,4,8,128]{4,3,2,1,0:T(8,128)S(1)}, u32[]{:S(2)}, u32[]{:S(2)}) collective-permute-start(f32[2,5,4,8,128]{4,3,2,1,0:T(8,128)S(1)} %get-tuple-element.91), channel_id=1, source_target_pairs={{0,16},{16,0},{1,17},{17,1},{2,18},{18,2},{3,19},{19,3},{4,20},{20... | collective-permute-start | bytes 491528 | tf_op jit(solution)/shard_map/ppermute | solution.py:671
  48.6 5.7 %collective-permute-start.18 = (f32[5,32,128]{2,1,0:T(8,128)S(1)}, f32[5,32,128]{2,1,0:T(8,128)S(1)}, u32[]{:S(2)}, u32[]{:S(2)}) collective-permute-start(f32[5,32,128]{2,1,0:T(8,128)S(1)} %get-tuple-element.92.z_lo), channel_id=1, source_target_pairs={{0,3},{1,0},{2,1},{3,2},{4,7},{5,4},{6,5},{7,6},{8,11},{9,8},{10,9... | collective-permute-start | bytes 245768 | tf_op jit(solution)/shard_map/ppermute | solution.py:671
  48.6 5.7 %collective-permute-start.17 = (f32[5,32,128]{2,1,0:T(8,128)S(1)}, f32[5,32,128]{2,1,0:T(8,128)S(1)}, u32[]{:S(2)}, u32[]{:S(2)}) collective-permute-start(f32[5,32,128]{2,1,0:T(8,128)S(1)} %get-tuple-element.93.z_hi), channel_id=1, source_target_pairs={{0,1},{1,2},{2,3},{3,0},{4,5},{5,6},{6,7},{7,4},{8,9},{9,10},{10,1... | collective-permute-start | bytes 245768 | tf_op jit(solution)/shard_map/ppermute | solution.py:671
  49.1 8.0 %collective-permute-start.15 = (f32[5,4,8,128]{3,2,1,0:T(8,128)S(1)}, f32[5,4,8,128]{3,2,1,0:T(8,128)S(1)}, u32[]{:S(2)}, u32[]{:S(2)}) collective-permute-start(f32[5,4,8,128]{3,2,1,0:T(8,128)S(1)} %get-tuple-element.89.y_lo), channel_id=1, source_target_pairs={{0,12},{4,0},{8,4},{12,8},{1,13},{5,1},{9,5},{13,9},{2,14},{6,2},{... | collective-permute-start | bytes 245768 | tf_op jit(solution)/shard_map/ppermute | solution.py:671
  54.3 6.8 %collective-permute-start.14 = (f32[5,4,8,128]{3,2,1,0:T(8,128)S(1)}, f32[5,4,8,128]{3,2,1,0:T(8,128)S(1)}, u32[]{:S(2)}, u32[]{:S(2)}) collective-permute-start(f32[5,4,8,128]{3,2,1,0:T(8,128)S(1)} %get-tuple-element.90.y_hi), channel_id=1, source_target_pairs={{0,4},{4,8},{8,12},{12,0},{1,5},{5,9},{9,13},{13,1},{2,6},{6,10},{... | collective-permute-start | bytes 245768 | tf_op jit(solution)/shard_map/ppermute | solution.py:671
  62.5 8.1 %collective-permute-start.21 = (f32[2,5,4,8,128]{4,3,2,1,0:T(8,128)S(1)}, f32[2,5,4,8,128]{4,3,2,1,0:T(8,128)S(1)}, u32[]{:S(2)}, u32[]{:S(2)}) collective-permute-start(f32[2,5,4,8,128]{4,3,2,1,0:T(8,128)S(1)} %get-tuple-element.98), channel_id=1, source_target_pairs={{0,16},{16,0},{1,17},{17,1},{2,18},{18,2},{3,19},{19,3},{4,20},{20... | collective-permute-start | bytes 491528 | tf_op jit(solution)/shard_map/ppermute | solution.py:671
  64.4 2.5 %collective-permute-start.23 = (f32[5,32,128]{2,1,0:T(8,128)S(1)}, f32[5,32,128]{2,1,0:T(8,128)S(1)}, u32[]{:S(2)}, u32[]{:S(2)}) collective-permute-start(f32[5,32,128]{2,1,0:T(8,128)S(1)} %get-tuple-element.99.z_lo), channel_id=1, source_target_pairs={{0,3},{1,0},{2,1},{3,2},{4,7},{5,4},{6,5},{7,6},{8,11},{9,8},{10,9... | collective-permute-start | bytes 245768 | tf_op jit(solution)/shard_map/ppermute | solution.py:671
  64.4 4.5 %collective-permute-start.22 = (f32[5,32,128]{2,1,0:T(8,128)S(1)}, f32[5,32,128]{2,1,0:T(8,128)S(1)}, u32[]{:S(2)}, u32[]{:S(2)}) collective-permute-start(f32[5,32,128]{2,1,0:T(8,128)S(1)} %get-tuple-element.100.z_hi), channel_id=1, source_target_pairs={{0,1},{1,2},{2,3},{3,0},{4,5},{5,6},{6,7},{7,4},{8,9},{9,10},{10,1... | collective-permute-start | bytes 245768 | tf_op jit(solution)/shard_map/ppermute | solution.py:671
  64.9 6.2 %collective-permute-start.20 = (f32[5,4,8,128]{3,2,1,0:T(8,128)S(1)}, f32[5,4,8,128]{3,2,1,0:T(8,128)S(1)}, u32[]{:S(2)}, u32[]{:S(2)}) collective-permute-start(f32[5,4,8,128]{3,2,1,0:T(8,128)S(1)} %get-tuple-element.96.y_lo), channel_id=1, source_target_pairs={{0,12},{4,0},{8,4},{12,8},{1,13},{5,1},{9,5},{13,9},{2,14},{6,2},{... | collective-permute-start | bytes 245768 | tf_op jit(solution)/shard_map/ppermute | solution.py:671
  65.1 7.0 %collective-permute-start.19 = (f32[5,4,8,128]{3,2,1,0:T(8,128)S(1)}, f32[5,4,8,128]{3,2,1,0:T(8,128)S(1)}, u32[]{:S(2)}, u32[]{:S(2)}) collective-permute-start(f32[5,4,8,128]{3,2,1,0:T(8,128)S(1)} %get-tuple-element.97.y_hi), channel_id=1, source_target_pairs={{0,4},{4,8},{8,12},{12,0},{1,5},{5,9},{9,13},{13,1},{2,6},{6,10},{... | collective-permute-start | bytes 245768 | tf_op jit(solution)/shard_map/ppermute | solution.py:671

commit v7 on v6

--- a/solution.py
+++ b/solution.py
@@ -227,9 +227,14 @@
                 phase(step - late)
 
 
-def send_slab(shape, prim, y_lo, y_hi, z_lo, z_hi, slab):
+def odd_y():
+    return lax.rem(lax.axis_index("gy"), 2) == 1
+
+
+def send_slab(shape, prim, y_one, y_two, z_lo, z_hi, slab):
     lane = lane_of()
     halves = shape.halves
+    odd = odd_y()
     for f in FIELDS:
         lo = hi = None
         for k in range(shape.fit):
@@ -242,8 +247,8 @@
                 mine = lane >= shape.width * k
                 lo = jnp.where(mine, below, lo)
                 hi = jnp.where(mine, above, hi)
-        y_lo[f, slab] = lo
-        y_hi[f, slab] = hi
+        y_one[f, slab] = jnp.where(odd, lo, hi)
+        y_two[f, slab] = jnp.where(odd, hi, lo)
         to = pl.ds(slab * SUB, SUB) if isinstance(slab, int) else pl.ds(
             pl.multiple_of(slab * SUB, SUB), SUB
         )
@@ -264,7 +269,7 @@
     given = len(held)
     arrived = group_levels(refs[:given], held)
     outs = refs[given + (0 if first else 7) :]
-    field, prim, y_lo, y_hi, z_lo, z_hi, x_faces = outs[:7]
+    field, prim, y_one, y_two, z_lo, z_hi, x_faces = outs[:7]
     blocks = outs[-1]
     units = NF * shape.slabs
     for b in range(occ):
@@ -281,7 +286,7 @@
             for f, (c, w) in enumerate(zip(cons, primitives(cons))):
                 field[shape.at(f, row), :] = c
                 prim[shape.at(f, row), :] = w
-        send_slab(shape, prim, y_lo, y_hi, z_lo, z_hi, slab)
+        send_slab(shape, prim, y_one, y_two, z_lo, z_hi, slab)
     if first:
         canvas = outs[7]
 
@@ -389,17 +394,18 @@
                 ahead = ahead[1:] + [cells(x + 2, h)]
 
 
-def sweep_y(prim, y_lo, y_hi, y_prev, y_next, sofar, ghost_prim, ghost_flux, left, right, flux, turned,
+def sweep_y(prim, y_one, y_two, got_one, got_two, sofar, ghost_prim, ghost_flux, left, right, flux, turned,
             shape, finish, after_slab):
     edge, halves, fit, width = shape.edge, shape.halves, shape.fit, shape.width
     lane = lane_of()
     upper = lax.rem(lane, width) >= edge
+    odd = odd_y()
 
     def prepare(q):
-        low = [y_lo[f, q] for f in FIELDS]
-        high = [y_hi[f, q] for f in FIELDS]
-        below = [y_prev[f, q] for f in FIELDS]
-        after = [y_next[f, q] for f in FIELDS]
+        low = [jnp.where(odd, y_one[f, q], y_two[f, q]) for f in FIELDS]
+        high = [jnp.where(odd, y_two[f, q], y_one[f, q]) for f in FIELDS]
+        below = [jnp.where(odd, got_one[f, q], got_two[f, q]) for f in FIELDS]
+        after = [jnp.where(odd, got_two[f, q], got_one[f, q]) for f in FIELDS]
         before = [lane_roll(v, edge) for v in below]
         first = [lane_roll(v, edge) for v in low]
         lefts = plus(below, half_slopes(before, below, first))
@@ -469,8 +475,8 @@
     in_turn(edge // fit, slopes, fluxes, differences, after_slab)
 
 
-def sweep_y_one_kernel(field, prim, y_lo, y_hi, y_prev, y_next, sofar, *refs, shape):
-    one, one_prim, x_faces, out_y_lo, out_y_hi, z_lo, z_hi = refs[:7]
+def sweep_y_one_kernel(field, prim, y_one, y_two, got_one, got_two, sofar, *refs, shape):
+    one, one_prim, x_faces, out_y_one, out_y_two, z_lo, z_hi = refs[:7]
 
     def finish(row, total):
         cons = [field[shape.at(f, row), :] - (0.5 * time_step) * total[f] for f in FIELDS]
@@ -479,15 +485,17 @@
             one_prim[shape.at(f, row), :] = w
 
     def after_slab(q):
-        send_slab(shape, one_prim, out_y_lo, out_y_hi, z_lo, z_hi, q)
-
-    sweep_y(prim, y_lo, y_hi, y_prev, y_next, sofar, *refs[7:], shape, finish, after_slab)
+        send_slab(shape, one_prim, out_y_one, out_y_two, z_lo, z_hi, q)
+
+    sweep_y(prim, y_one, y_two, got_one, got_two, sofar, *refs[7:], shape, finish, after_slab)
     send_x(shape, one_prim, x_faces)
 
 
-def sweep_y_two_kernel(own, field, one, prim, y_lo, y_hi, y_prev, y_next, sofar, zeros, out,
+def sweep_y_two_kernel(own_there, field, one, prim, y_one, y_two, got_one, got_two, sofar, zeros, out,
                        canvas, *refs, shape, occ, groups):
-    scratch, (result, sems) = refs[:6], refs[6:]
+    scratch, (result, sems, own, own_sem) = refs[:6], refs[6:]
+    slots = pltpu.make_async_copy(own_there, own, own_sem)
+    slots.start()
     rows = shape.rows
     span = SUB * SUB
 
@@ -503,6 +511,8 @@
         return pltpu.make_async_copy(canvas.at[:, at, :], out.at[:, at, :], sems.at[part])
 
     def after_slab(q):
+        if q == 0:
+            slots.wait()
         for b in range(occ):
             slot = own[b]
             to = pl.ds(q * span + lax.rem(slot, SUB), SUB, stride=SUB)
@@ -510,7 +520,7 @@
                 canvas[f * groups + slot // SUB, to, :] = result[shape.across(f, q, b), :]
         copy(q).start()
 
-    sweep_y(prim, y_lo, y_hi, y_prev, y_next, sofar, *scratch, shape, finish, after_slab)
+    sweep_y(prim, y_one, y_two, got_one, got_two, sofar, *scratch, shape, finish, after_slab)
     for part in range(shape.slabs):
         copy(part).wait()
 
@@ -525,8 +535,8 @@
     groups = slots // SUB
     shape = Shape(rows, edge)
     units = NF * shape.slabs
-    pieces = split_units(units, (3, 5, 5, 4, 3))
-    firsts = split_units(units, (3, 5, 7, 5))
+    cuts = [split_units(units, shares) for shares in ((3, 5, 7, 5), (3, 5, 5, 4, 3), (8, 5, 4, 3))]
+    firsts, final = cuts[0], cuts[2]
 
     bit_z = size_z.bit_length() - 2
     bit_y = bit_z + size_y.bit_length() - 1
@@ -582,7 +592,6 @@
         name="pack_rest",
     )(send_slots, recv_slots, own, rows_of_state)
 
-    cuts = (firsts, pieces, pieces)
     got = [[None] * len(cut) for cut in cuts]
 
     def holding(levels, begin, end):
@@ -597,9 +606,9 @@
     def make(wanted, through):
         found = {}
         for level, p in wanted:
-            for key, value in holding(range(level), *pieces[p]):
+            for key, value in holding(range(level), *cuts[level][p]):
                 found[key] = value
-        plan = tuple((level, pieces[p]) for level, p in wanted)
+        plan = tuple((level, cuts[level][p]) for level, p in wanted)
         given, passed, made = len(found), len(through), len(wanted)
         outs = pl.pallas_call(
             functools.partial(
@@ -619,29 +628,29 @@
     steps = [
         ([(1, 0)], [2], []),
         ([(1, 1)], [3], []),
-        ([(1, 2), (2, 0)], [], []),
-        ([(1, 3), (2, 1)], [], []),
-        ([(1, 4), (2, 2)], [], [0]),
-        ([(2, 3)], [], [1]),
-        ([(2, 4)], [], [2]),
+        ([(1, 2)], [], [(1, 0)]),
+        ([(1, 3), (2, 0)], [], []),
+        ([(1, 4), (2, 1)], [], []),
+        ([(2, 2)], [], [(2, 0)]),
+        ([(2, 3)], [], [(2, 1)]),
     ]
     got[0][0] = swapped(sent[0], 0)
     got[0][1] = swapped(sent[1], 0)
     for wanted, leaving, awaited in steps:
-        through = [token] + [sent[p] for p in leaving] + [got[2][p] for p in awaited]
+        through = [token] + [sent[p] for p in leaving] + [got[level][p] for level, p in awaited]
         made, (token, *passed) = make(wanted, through)
         for p, value in zip(leaving, passed):
             got[0][p] = swapped(value, 0)
         for (level, p), value in reversed(list(zip(wanted, made))):
             got[level][p] = swapped(value, level)
-        for p, value in zip(awaited, passed[len(leaving) :]):
-            got[2][p] = value
+        for (level, p), value in zip(awaited, passed[len(leaving) :]):
+            got[level][p] = value
 
     grid = shape.grid()
     face_x, face_y, _, face_z, _ = shape.faces()
     part = [grid, grid, face_y, face_y, face_z, face_z, face_x]
     canvas = jax.ShapeDtypeStruct((NF * groups, rows * SUB, LANES), f32)
-    full = pieces[-1][0] // NF
+    full = final[-1][0] // NF
 
     def assemble(slabs, before):
         first = not before
@@ -670,12 +679,17 @@
         size = lax.axis_size(axis)
         return lax.ppermute(value, axis, [(i, (i + step) % size) for i in range(size)])
 
-    def flux_sums(prim, x_faces, y_lo, y_hi, z_lo, z_hi):
+    def beside(value, axis, shift):
+        size = lax.axis_size(axis)
+        pairs = [(i, ((i + shift) ^ 1) - shift) for i in range(size)]
+        return lax.ppermute(value, axis, [(i, j % size) for i, j in pairs])
+
+    def flux_sums(prim, x_faces, y_one, y_two, z_lo, z_hi):
         if size_x == 2:
             x_faces = ring(x_faces, "gx", 1)
         else:
             x_faces = jnp.stack([ring(x_faces[0], "gx", 1), ring(x_faces[1], "gx", -1)])
-        y_prev, y_next = ring(y_hi, "gy", 1), ring(y_lo, "gy", -1)
+        got_one, got_two = beside(y_one, "gy", 0), beside(y_two, "gy", 1)
         z_prev, z_next = ring(z_hi, "gz", 1), ring(z_lo, "gz", -1)
         ghost = VMEM((NF, rows, LANES), f32)
         work = [VMEM(grid.shape, f32)] * 3
@@ -697,7 +711,7 @@
             compiler_params=params(),
             name="sweep_x",
         )(prim, x_faces, total)
-        return y_lo, y_hi, y_prev, y_next, total
+        return y_one, y_two, got_one, got_two, total
 
     produced = [grid, grid] + shape.faces()
     scratch = [VMEM(face_y.shape, f32)] * 2 + [VMEM(grid.shape, f32)] * 4
@@ -717,17 +731,19 @@
     out, _ = pl.pallas_call(
         functools.partial(sweep_y_two_kernel, shape=shape, occ=occ, groups=groups),
         out_shape=[canvas, canvas],
-        in_specs=[whole(SMEM)] + [whole(VMEM)] * 9,
+        in_specs=[whole(HBM)] + [whole(VMEM)] * 9,
         out_specs=[whole(HBM), whole(VMEM)],
         scratch_shapes=scratch
         + [
             VMEM(grid.shape, f32),
             pltpu.SemaphoreType.DMA((shape.slabs,)),
+            SMEM((occ,), jnp.int32),
+            pltpu.SemaphoreType.DMA,
         ],
         input_output_aliases={9: 1},
         compiler_params=params(),
         name="sweep_y_two",
-    )(own, field, one, one_prim, *sums, blank)
+    )(pltpu.with_memory_space_constraint(own, HBM), field, one, one_prim, *sums, blank)
     return (
         out.reshape(NF, groups, rows, SUB, LANES)
         .transpose(1, 3, 0, 2, 4)

time: 75.1 us -> 74.8 us (level)
  starting transfers between devices: 35.6 us -> 31.9 us
  waiting for transfers between devices: 20.9 us -> 24.6 us
    ppermute x10 -> x6, starting transfers between devices: 13.9 us -> 5.26 us  [ring(): lax.ppermute(value, axis, [(i, (i + step) % size) for i in range(size)])]
    ppermute x0 -> x4, starting transfers between devices: none -> 8.55 us  [beside(): return lax.ppermute(value, axis, [(i, j % size) for i, j in pairs])]
    ppermute x10 -> x6, waiting for transfers between devices: 7.62 us -> 0.21 us  [ring(): lax.ppermute(value, axis, [(i, (i + step) % size) for i in range(size)])]
    ppermute x14 -> x13, waiting for transfers between devices: 13.3 us -> 19 us  [swapped(): return lax.ppermute(value, AXES, pairs)]
    ppermute x0 -> x4, waiting for transfers between devices: none -> 5.38 us  [beside(): return lax.ppermute(value, axis, [(i, j % size) for i, j in pairs])]
    ppermute x14 -> x13, starting transfers between devices: 21.8 us -> 18.1 us  [swapped(): return lax.ppermute(value, AXES, pairs)]
  transfers between devices with their start and end apart: 24 -> 23, of which waited for: 13 -> 12; matrix products, arithmetic and copies ran while one was open for 0% -> 0% of each run, Pallas kernels for 16% -> 16%
where the time goes in v7:
time: 74.8 us; the launch traced here: 74.6 us
  starting transfers between devices  31.9 us (43%)
  waiting for transfers between devices  24.6 us (33%)
  Pallas kernels  17.8 us (24%)
    ppermute x13, waiting for transfers between devices, swapped(): return lax.ppermute(value, AXES, pairs)  19 us
    ppermute x13, starting transfers between devices, swapped(): return lax.ppermute(value, AXES, pairs)  18.1 us
    ppermute x4, starting transfers between devices, beside(): return lax.ppermute(value, axis, [(i, j % size) for i, j in pairs])  8.55 us
    ppermute x4, waiting for transfers between devices, beside(): return lax.ppermute(value, axis, [(i, j % size) for i, j in pairs])  5.38 us
    ppermute x6, starting transfers between devices, ring(): lax.ppermute(value, axis, [(i, (i + step) % size) for i in range(size)])  5.26 us
    pallas_call x7, Pallas kernels, make(): pl.pallas_call(functools.partial(pick_kernel, plan=plan, held=tuple(found...  4.6 us
    pallas_call x2, Pallas kernels, flux_sums(): pl.pallas_call(functools.partial(sweep_z_kernel, shape=shape), out_shape=...  3.04 us
    pallas_call x1, Pallas kernels, shards(): pl.pallas_call(functools.partial(sweep_y_two_kernel, shape=shape, occ=occ...  2.69 us
  transfers between devices with their start and end apart: 23, of which 12 were waited for; matrix products, arithmetic and copies ran while one was open for 0% of the time, Pallas kernels for 16%

profile of v7, /device:TPU:0, one launch (start us, length us, event | category | flops | bytes accessed | tf_op | source)
XLA Modules:
  0.0 74.6 jit_solution(17639664567283166313)
XLA Ops:
  0.0 1.2 %pack_first.1 = f32[8,24,128]{2,1,0:T(8,128)S(1)} custom-call(s32[3,1,8]{2,1,0:T(1,128)} %send_hbm.1, f32[5120,128]{1,0:T(8,128)} %bitcast.10), custom_call_target="tpu_custom_call" | custom-call | tf_op jit(solution)/shard_map/pack_first/pallas_call | solution.py:568
  1.3 3.0 %collective-permute-start.1 = (f32[8,24,128]{2,1,0:T(8,128)S(1)}, f32[8,24,128]{2,1,0:T(8,128)S(1)}, u32[]{:S(2)}, u32[]{:S(2)}) collective-permute-start(f32[8,24,128]{2,1,0:T(8,128)S(1)} %pack_first.1), channel_id=1, source_target_pairs={{0,16},{1,17},{2,18},{3,19},{4,20},{5,21},{6,22},{7,23},{8,24},{9,... | collective-permute-start | bytes 294920 | tf_op jit(solution)/shard_map/ppermute | solution.py:549
  4.3 0.1 dynamic_slice.3.own.own_there
  4.4 1.4 %pack_rest.1 = (s32[24]{0:T(128)S(1)}, f32[8,128]{1,0:T(8,128)S(1)}, f32[8,40,128]{2,1,0:T(8,128)S(1)}, f32[8,56,128]{2,1,0:T(8,128)S(1)}, f32[8,40,128]{2,1,0:T(8,128)S(1)}) custom-call(s32[3,1,8]{2,1,0:T(1,128)S(1)} %copy-done.1, s32[3,1,8]{2,1,0:T(1,128)S(1)} %copy-done.3, s32[8]{0:T(128)S(1)} %dynamic_slice.3.own.own_there, f32[5120,128]{1,0:T(8,128)S(1)} %bitcast.11), custom_call_target="tpu_custom_call" | custom-call | tf_op jit(solution)/shard_map/pack_rest/pallas_call | solution.py:581
  5.8 0.6 collective-permute-start
  6.4 0.7 collective-permute-done.1.refs_0_.refs_2_
  7.1 0.6 pick_10.1
  7.7 2.0 %collective-permute-start.3 = (f32[8,56,128]{2,1,0:T(8,128)S(1)}, f32[8,56,128]{2,1,0:T(8,128)S(1)}, u32[]{:S(2)}, u32[]{:S(2)}) collective-permute-start(f32[8,56,128]{2,1,0:T(8,128)S(1)} %get-tuple-element.60), channel_id=1, source_target_pairs={{0,16},{1,17},{2,18},{3,19},{4,20},{5,21},{6,22},{7,23},{8,24},{9,... | collective-permute-start | bytes 688136 | tf_op jit(solution)/shard_map/ppermute | solution.py:549
  9.7 2.6 %collective-permute-start.4 = (f32[8,24,128]{2,1,0:T(8,128)S(1)}, f32[8,24,128]{2,1,0:T(8,128)S(1)}, u32[]{:S(2)}, u32[]{:S(2)}) collective-permute-start(f32[8,24,128]{2,1,0:T(8,128)S(1)} %get-tuple-element.62), channel_id=1, source_target_pairs={{0,8},{1,9},{2,10},{3,11},{4,12},{5,13},{6,14},{7,15},{8,0},{9,1},... | collective-permute-start | bytes 294920 | tf_op jit(solution)/shard_map/ppermute | solution.py:549
  12.3 0.7 collective-permute-done.refs_0_.refs_3_.refs_1_
  13.0 0.6 pick_11.1
  13.6 0.6 collective-permute-start.2
  14.2 2.6 %collective-permute-start.5 = (f32[8,40,128]{2,1,0:T(8,128)S(1)}, f32[8,40,128]{2,1,0:T(8,128)S(1)}, u32[]{:S(2)}, u32[]{:S(2)}) collective-permute-start(f32[8,40,128]{2,1,0:T(8,128)S(1)} %get-tuple-element.64), channel_id=1, source_target_pairs={{0,8},{1,9},{2,10},{3,11},{4,12},{5,13},{6,14},{7,15},{8,0},{9,1},... | collective-permute-start | bytes 491528 | tf_op jit(solution)/shard_map/ppermute | solution.py:549
  16.8 0.0 collective-permute-done.4.refs_2_
  16.8 1.1 %collective-permute-done.3.refs_0_.refs_1_.refs_2_ = f32[8,56,128]{2,1,0:T(8,128)S(1)} collective-permute-done((f32[8,56,128]{2,1,0:T(8,128)S(1)}, f32[8,56,128]{2,1,0:T(8,128)S(1)}, u32[]{:S(2)}, u32[]{:S(2)}) %collective-permute-start.3) | collective-permute-done | bytes 229408 | tf_op jit(solution)/shard_map/ppermute | solution.py:549
  17.9 0.6 pick_12.1
  18.5 2.7 %collective-permute-start.7 = (f32[8,40,128]{2,1,0:T(8,128)S(1)}, f32[8,40,128]{2,1,0:T(8,128)S(1)}, u32[]{:S(2)}, u32[]{:S(2)}) collective-permute-start(f32[8,40,128]{2,1,0:T(8,128)S(1)} %get-tuple-element.67), channel_id=1, source_target_pairs={{0,8},{1,9},{2,10},{3,11},{4,12},{5,13},{6,14},{7,15},{8,0},{9,1},... | collective-permute-start | bytes 491528 | tf_op jit(solution)/shard_map/ppermute | solution.py:549
  21.2 0.0 collective-permute-done.2.refs_1_.refs_0_
  21.2 4.5 %collective-permute-done.5.refs_5_.refs_4_ = f32[8,40,128]{2,1,0:T(8,128)S(1)} collective-permute-done((f32[8,40,128]{2,1,0:T(8,128)S(1)}, f32[8,40,128]{2,1,0:T(8,128)S(1)}, u32[]{:S(2)}, u32[]{:S(2)}) %collective-permute-start.5) | collective-permute-done | bytes 163872 | tf_op jit(solution)/shard_map/ppermute | solution.py:549
  25.7 0.7 pick_13_20.1
  26.5 1.6 %collective-permute-start.9 = (f32[8,64,128]{2,1,0:T(8,128)S(1)}, f32[8,64,128]{2,1,0:T(8,128)S(1)}, u32[]{:S(2)}, u32[]{:S(2)}) collective-permute-start(f32[8,64,128]{2,1,0:T(8,128)S(1)} %get-tuple-element.71), channel_id=1, source_target_pairs={{0,2},{1,3},{2,0},{3,1},{4,6},{5,7},{6,4},{7,5},{8,10},{9,11},{10,... | collective-permute-start | bytes 786440 | tf_op jit(solution)/shard_map/ppermute | solution.py:549
  28.0 0.0 collective-permute-start.6
  28.0 2.5 %collective-permute-done.7.refs_2_.refs_5_ = f32[8,40,128]{2,1,0:T(8,128)S(1)} collective-permute-done((f32[8,40,128]{2,1,0:T(8,128)S(1)}, f32[8,40,128]{2,1,0:T(8,128)S(1)}, u32[]{:S(2)}, u32[]{:S(2)}) %collective-permute-start.7) | collective-permute-done | bytes 163872 | tf_op jit(solution)/shard_map/ppermute | solution.py:549
  30.5 0.7 pick_14_21.1
  31.3 1.6 %collective-permute-start.11 = (f32[8,40,128]{2,1,0:T(8,128)S(1)}, f32[8,40,128]{2,1,0:T(8,128)S(1)}, u32[]{:S(2)}, u32[]{:S(2)}) collective-permute-start(f32[8,40,128]{2,1,0:T(8,128)S(1)} %get-tuple-element.74), channel_id=1, source_target_pairs={{0,2},{1,3},{2,0},{3,1},{4,6},{5,7},{6,4},{7,5},{8,10},{9,11},{10,... | collective-permute-start | bytes 491528 | tf_op jit(solution)/shard_map/ppermute | solution.py:549
  32.8 0.0 collective-permute-start.8
  32.8 3.4 %collective-permute-done.6.refs_2_.refs_6_.refs_1_ = f32[8,32,128]{2,1,0:T(8,128)S(1)} collective-permute-done((f32[8,32,128]{2,1,0:T(8,128)S(1)}, f32[8,32,128]{2,1,0:T(8,128)S(1)}, u32[]{:S(2)}, u32[]{:S(2)}) %collective-permute-start.6) | collective-permute-done | bytes 131104 | tf_op jit(solution)/shard_map/ppermute | solution.py:549
  36.2 0.0 collective-permute-done.9.refs_4_
  36.2 0.6 pick_22.1
  36.9 0.9 %collective-permute-start.10 = (f32[8,32,128]{2,1,0:T(8,128)S(1)}, f32[8,32,128]{2,1,0:T(8,128)S(1)}, u32[]{:S(2)}, u32[]{:S(2)}) collective-permute-start(f32[8,32,128]{2,1,0:T(8,128)S(1)} %get-tuple-element.72), channel_id=1, source_target_pairs={{0,2},{1,3},{2,0},{3,1},{4,6},{5,7},{6,4},{7,5},{8,10},{9,11},{10,... | collective-permute-start | bytes 393224 | tf_op jit(solution)/shard_map/ppermute | solution.py:549
  37.8 3.0 %collective-permute-done.8.refs_1_.refs_2_ = f32[8,24,128]{2,1,0:T(8,128)S(1)} collective-permute-done((f32[8,24,128]{2,1,0:T(8,128)S(1)}, f32[8,24,128]{2,1,0:T(8,128)S(1)}, u32[]{:S(2)}, u32[]{:S(2)}) %collective-permute-start.8) | collective-permute-done | bytes 98336 | tf_op jit(solution)/shard_map/ppermute | solution.py:549
  40.8 0.0 collective-permute-done.11.refs_3_
  40.8 0.6 pick_23.1
  41.4 0.1 collective-permute-start.12
  41.5 0.4 collective-permute-done.10.refs_9_.refs_3_
  41.9 1.5 %assemble_0.1 = (f32[1280,128]{1,0:T(8,128)S(1)}, f32[1280,128]{1,0:T(8,128)S(1)}, f32[5,4,8,128]{3,2,1,0:T(8,128)S(1)}, f32[5,4,8,128]{3,2,1,0:T(8,128)S(1)}, f...) custom-call(s32[24]{0:T(128)S(1)} %get-tuple-element.53.tags, ...), custom_call_target="tpu_custom_call" | custom-call | tf_op jit(solution)/shard_map/assemble_0/pallas_call | solution.py:660
  43.5 2.7 %collective-permute-done.12.refs_4_ = f32[8,24,128]{2,1,0:T(8,128)S(1)} collective-permute-done((f32[8,24,128]{2,1,0:T(8,128)S(1)}, f32[8,24,128]{2,1,0:T(8,128)S(1)}, u32[]{:S(2)}, u32[]{:S(2)}) %collective-permute-start.12) | collective-permute-done | bytes 98336 | tf_op jit(solution)/shard_map/ppermute | solution.py:549
  46.1 0.9 %assemble_3.1 = (f32[1280,128]{1,0:T(8,128)S(1)}, f32[1280,128]{1,0:T(8,128)S(1)}, f32[5,4,8,128]{3,2,1,0:T(8,128)S(1)}, f32[5,4,8,128]{3,2,1,0:T(8,128)S(1)}, f...) custom-call(s32[24]{0:T(128)S(1)} %get-tuple-element.53.tags, ...), custom_call_target="tpu_custom_call", output_to_operand_aliasing={{0}: (7, {}), {1}: (8, {}), {2}: (9, {}), {3}: (10, {}), {4... | custom-call | tf_op jit(solution)/shard_map/assemble_3/pallas_call | solution.py:660
  47.0 2.4 %collective-permute-start.15 = (f32[2,5,4,8,128]{4,3,2,1,0:T(8,128)S(1)}, f32[2,5,4,8,128]{4,3,2,1,0:T(8,128)S(1)}, u32[]{:S(2)}, u32[]{:S(2)}) collective-permute-start(f32[2,5,4,8,128]{4,3,2,1,0:T(8,128)S(1)} %get-tuple-element.89), channel_id=1, source_target_pairs={{0,16},{16,0},{1,17},{17,1},{2,18},{18,2},{3,19},{19,3},{4,20},{20... | collective-permute-start | bytes 491528 | tf_op jit(solution)/shard_map/ppermute | solution.py:680
  49.3 0.0 collective-permute-start.17
  49.3 0.5 collective-permute-start.16
  49.8 2.1 %collective-permute-start.13 = (f32[5,4,8,128]{3,2,1,0:T(8,128)S(1)}, f32[5,4,8,128]{3,2,1,0:T(8,128)S(1)}, u32[]{:S(2)}, u32[]{:S(2)}) collective-permute-start(f32[5,4,8,128]{3,2,1,0:T(8,128)S(1)} %get-tuple-element.87.y_one), channel_id=1, source_target_pairs={{0,4},{4,0},{8,12},{12,8},{1,5},{5,1},{9,13},{13,9},{2,6},{6,2},{1... | collective-permute-start | bytes 245768 | tf_op jit(solution)/shard_map/ppermute | solution.py:685
  52.0 2.4 %collective-permute-start.14 = (f32[5,4,8,128]{3,2,1,0:T(8,128)S(1)}, f32[5,4,8,128]{3,2,1,0:T(8,128)S(1)}, u32[]{:S(2)}, u32[]{:S(2)}) collective-permute-start(f32[5,4,8,128]{3,2,1,0:T(8,128)S(1)} %get-tuple-element.88.y_two), channel_id=1, source_target_pairs={{0,12},{4,8},{8,4},{12,0},{1,13},{5,9},{9,5},{13,1},{2,14},{6,10},... | collective-permute-start | bytes 245768 | tf_op jit(solution)/shard_map/ppermute | solution.py:685
  54.4 0.0 collective-permute-done.17.z_next
  54.4 0.0 collective-permute-done.16.z_prev
  54.4 1.5 %sweep_z.2.sofar = f32[1280,128]{1,0:T(8,128)S(1)} custom-call(f32[1280,128]{1,0:T(8,128)S(1)} %get-tuple-element.86.prim, f32[5,32,128]{2,1,0:T(8,128)S(1)} %get-tuple-element.90.z_lo, f32[5,32,128]{2,1,0:T(8,128)S(1)} %get-tuple-element.91.z_hi, f32[5,32,128]{2,1,0:T(8,128)S(1)} %collective-permute-done.16.z_prev, ...), custom_call_target="tpu_custom_call" | custom-call | tf_op jit(solution)/shard_map/sweep_z/pallas_call | solution.py:696
  55.9 0.0 collective-permute-done.15.x_faces
  55.9 0.6 sweep_x.2.sofar
  56.5 0.0 collective-permute-done.13.got_one
  56.5 2.7 %collective-permute-done.14.got_two = f32[5,4,8,128]{3,2,1,0:T(8,128)S(1)} collective-permute-done((f32[5,4,8,128]{3,2,1,0:T(8,128)S(1)}, f32[5,4,8,128]{3,2,1,0:T(8,128)S(1)}, u32[]{:S(2)}, u32[]{:S(2)}) %collective-permute-start.14) | collective-permute-done | bytes 81952 | tf_op jit(solution)/shard_map/ppermute | solution.py:685
  59.2 1.3 %sweep_y_one.1 = (f32[1280,128]{1,0:T(8,128)S(1)}, f32[1280,128]{1,0:T(8,128)S(1)}, f32[2,5,4,8,128]{4,3,2,1,0:T(8,128)S(1)}, f32[5,4,8,128]{3,2,1,0:T(8,128)S(1...) custom-call(f32[1280,128]{1,0:T(8,128)S(1)} %get-tuple-element.85.field, ...), custom_call_target="tpu_custom_call" | custom-call | tf_op jit(solution)/shard_map/sweep_y_one/pallas_call | solution.py:720
  60.5 1.9 %collective-permute-start.20 = (f32[2,5,4,8,128]{4,3,2,1,0:T(8,128)S(1)}, f32[2,5,4,8,128]{4,3,2,1,0:T(8,128)S(1)}, u32[]{:S(2)}, u32[]{:S(2)}) collective-permute-start(f32[2,5,4,8,128]{4,3,2,1,0:T(8,128)S(1)} %get-tuple-element.96), channel_id=1, source_target_pairs={{0,16},{16,0},{1,17},{17,1},{2,18},{18,2},{3,19},{19,3},{4,20},{20... | collective-permute-start | bytes 491528 | tf_op jit(solution)/shard_map/ppermute | solution.py:680
  62.4 0.1 collective-permute-start.22
  62.5 0.4 collective-permute-start.21
  62.9 1.2 %collective-permute-start.18 = (f32[5,4,8,128]{3,2,1,0:T(8,128)S(1)}, f32[5,4,8,128]{3,2,1,0:T(8,128)S(1)}, u32[]{:S(2)}, u32[]{:S(2)}) collective-permute-start(f32[5,4,8,128]{3,2,1,0:T(8,128)S(1)} %get-tuple-element.94.y_one), channel_id=1, source_target_pairs={{0,4},{4,0},{8,12},{12,8},{1,5},{5,1},{9,13},{13,9},{2,6},{6,2},{1... | collective-permute-start | bytes 245768 | tf_op jit(solution)/shard_map/ppermute | solution.py:685
  64.1 2.8 %collective-permute-start.19 = (f32[5,4,8,128]{3,2,1,0:T(8,128)S(1)}, f32[5,4,8,128]{3,2,1,0:T(8,128)S(1)}, u32[]{:S(2)}, u32[]{:S(2)}) collective-permute-start(f32[5,4,8,128]{3,2,1,0:T(8,128)S(1)} %get-tuple-element.95.y_two), channel_id=1, source_target_pairs={{0,12},{4,8},{8,4},{12,0},{1,13},{5,9},{9,5},{13,1},{2,14},{6,10},... | collective-permute-start | bytes 245768 | tf_op jit(solution)/shard_map/ppermute | solution.py:685
  67.0 0.0 collective-permute-done.22.z_next
  67.0 0.2 collective-permute-done.21.z_prev
  67.2 1.5 %sweep_z.3.sofar = f32[1280,128]{1,0:T(8,128)S(1)} custom-call(f32[1280,128]{1,0:T(8,128)S(1)} %get-tuple-element.93.prim, f32[5,32,128]{2,1,0:T(8,128)S(1)} %get-tuple-element.97.z_lo, f32[5,32,128]{2,1,0:T(8,128)S(1)} %get-tuple-element.98.z_hi, f32[5,32,128]{2,1,0:T(8,128)S(1)} %collective-permute-done.21.z_prev, ...), custom_call_target="tpu_custom_call" | custom-call | tf_op jit(solution)/shard_map/sweep_z/pallas_call | solution.py:696
  68.7 0.0 collective-permute-done.20.x_faces
  68.7 0.6 sweep_x.3.sofar
  69.3 0.0 collective-permute-done.18.got_one
  69.3 2.7 %collective-permute-done.19.got_two = f32[5,4,8,128]{3,2,1,0:T(8,128)S(1)} collective-permute-done((f32[5,4,8,128]{3,2,1,0:T(8,128)S(1)}, f32[5,4,8,128]{3,2,1,0:T(8,128)S(1)}, u32[]{:S(2)}, u32[]{:S(2)}) %collective-permute-start.19) | collective-permute-done | bytes 81952 | tf_op jit(solution)/shard_map/ppermute | solution.py:685
  71.9 2.7 %sweep_y_two.1 = (f32[20,256,128]{2,1,0:T(8,128)}, f32[20,256,128]{2,1,0:T(8,128)S(1)}) custom-call(s32[8]{0:T(128)} %copy-done.2, f32[1280,128]{1,0:T(8,128)S(1)} %get-tuple-element.85.field, f32[1280,128]{1,0:T(8,128)S(1)} %get-tuple-element.92.one, f32[1280,128]{1,0:T(8,128)S(1)} %get-tuple-element.93.prim, ...), custom_call_target="tpu_custom_call", output_to_operand_aliasing={{1}: (9, {})} | custom-call | tf_op jit(solution)/shard_map/sweep_y_two/pallas_call | solution.py:731
  (10 shorter events, 0.0 us)
Async XLA Ops:
  0.0 4.4 %copy-start.1 = (s32[3,1,8]{2,1,0:T(1,128)S(1)}, s32[3,1,8]{2,1,0:T(1,128)}, u32[]{:S(2)}) copy-start(s32[3,1,8]{2,1,0:T(1,128)} %send_hbm.1) | copy-start | bytes 292
  0.0 4.4 %copy-start = (f32[32,5,4096]{2,0,1:T(8,128)S(1)}, f32[32,5,4096]{2,0,1:T(8,128)}, u32[]{:S(2)}) copy-start(f32[32,5,4096]{2,0,1:T(8,128)} %param.4) | copy-start | bytes 7864324
  0.0 4.3 %copy-start.4 = (s32[256]{0:T(256)S(1)}, s32[256]{0:T(256)}, u32[]{:S(2)}) copy-start(s32[256]{0:T(256)} %param.7) | copy-start | bytes 3076
  0.0 4.4 %copy-start.3 = (s32[3,1,8]{2,1,0:T(1,128)S(1)}, s32[3,1,8]{2,1,0:T(1,128)}, u32[]{:S(2)}) copy-start(s32[3,1,8]{2,1,0:T(1,128)} %recv.1) | copy-start | bytes 292
  1.3 5.8 %collective-permute-start.1 = (f32[8,24,128]{2,1,0:T(8,128)S(1)}, f32[8,24,128]{2,1,0:T(8,128)S(1)}, u32[]{:S(2)}, u32[]{:S(2)}) collective-permute-start(f32[8,24,128]{2,1,0:T(8,128)S(1)} %pack_first.1), channel_id=1, source_target_pairs={{0,16},{1,17},{2,18},{3,19},{4,20},{5,21},{6,22},{7,23},{8,24},{9,... | collective-permute-start | bytes 294920 | tf_op jit(solution)/shard_map/ppermute | solution.py:549
  4.4 3.3 %copy-start.2 = (s32[8]{0:T(128)}, s32[8]{0:T(128)S(1)}, u32[]{:S(2)}) copy-start(s32[8]{0:T(128)S(1)} %dynamic_slice.3.own.own_there) | copy-start | bytes 100
  5.8 7.2 %collective-permute-start = (f32[8,40,128]{2,1,0:T(8,128)S(1)}, f32[8,40,128]{2,1,0:T(8,128)S(1)}, u32[]{:S(2)}, u32[]{:S(2)}) collective-permute-start(f32[8,40,128]{2,1,0:T(8,128)S(1)} %get-tuple-element.54), channel_id=1, source_target_pairs={{0,16},{1,17},{2,18},{3,19},{4,20},{5,21},{6,22},{7,23},{8,24},{9,... | collective-permute-start | bytes 491528 | tf_op jit(solution)/shard_map/ppermute | solution.py:549
  7.7 10.2 %collective-permute-start.3 = (f32[8,56,128]{2,1,0:T(8,128)S(1)}, f32[8,56,128]{2,1,0:T(8,128)S(1)}, u32[]{:S(2)}, u32[]{:S(2)}) collective-permute-start(f32[8,56,128]{2,1,0:T(8,128)S(1)} %get-tuple-element.60), channel_id=1, source_target_pairs={{0,16},{1,17},{2,18},{3,19},{4,20},{5,21},{6,22},{7,23},{8,24},{9,... | collective-permute-start | bytes 688136 | tf_op jit(solution)/shard_map/ppermute | solution.py:549
  9.7 7.1 %collective-permute-start.4 = (f32[8,24,128]{2,1,0:T(8,128)S(1)}, f32[8,24,128]{2,1,0:T(8,128)S(1)}, u32[]{:S(2)}, u32[]{:S(2)}) collective-permute-start(f32[8,24,128]{2,1,0:T(8,128)S(1)} %get-tuple-element.62), channel_id=1, source_target_pairs={{0,8},{1,9},{2,10},{3,11},{4,12},{5,13},{6,14},{7,15},{8,0},{9,1},... | collective-permute-start | bytes 294920 | tf_op jit(solution)/shard_map/ppermute | solution.py:549
  13.6 7.6 %collective-permute-start.2 = (f32[8,40,128]{2,1,0:T(8,128)S(1)}, f32[8,40,128]{2,1,0:T(8,128)S(1)}, u32[]{:S(2)}, u32[]{:S(2)}) collective-permute-start(f32[8,40,128]{2,1,0:T(8,128)S(1)} %get-tuple-element.59), channel_id=1, source_target_pairs={{0,16},{1,17},{2,18},{3,19},{4,20},{5,21},{6,22},{7,23},{8,24},{9,... | collective-permute-start | bytes 491528 | tf_op jit(solution)/shard_map/ppermute | solution.py:549
  14.2 11.5 %collective-permute-start.5 = (f32[8,40,128]{2,1,0:T(8,128)S(1)}, f32[8,40,128]{2,1,0:T(8,128)S(1)}, u32[]{:S(2)}, u32[]{:S(2)}) collective-permute-start(f32[8,40,128]{2,1,0:T(8,128)S(1)} %get-tuple-element.64), channel_id=1, source_target_pairs={{0,8},{1,9},{2,10},{3,11},{4,12},{5,13},{6,14},{7,15},{8,0},{9,1},... | collective-permute-start | bytes 491528 | tf_op jit(solution)/shard_map/ppermute | solution.py:549
  18.5 12.0 %collective-permute-start.7 = (f32[8,40,128]{2,1,0:T(8,128)S(1)}, f32[8,40,128]{2,1,0:T(8,128)S(1)}, u32[]{:S(2)}, u32[]{:S(2)}) collective-permute-start(f32[8,40,128]{2,1,0:T(8,128)S(1)} %get-tuple-element.67), channel_id=1, source_target_pairs={{0,8},{1,9},{2,10},{3,11},{4,12},{5,13},{6,14},{7,15},{8,0},{9,1},... | collective-permute-start | bytes 491528 | tf_op jit(solution)/shard_map/ppermute | solution.py:549
  26.5 9.8 %collective-permute-start.9 = (f32[8,64,128]{2,1,0:T(8,128)S(1)}, f32[8,64,128]{2,1,0:T(8,128)S(1)}, u32[]{:S(2)}, u32[]{:S(2)}) collective-permute-start(f32[8,64,128]{2,1,0:T(8,128)S(1)} %get-tuple-element.71), channel_id=1, source_target_pairs={{0,2},{1,3},{2,0},{3,1},{4,6},{5,7},{6,4},{7,5},{8,10},{9,11},{10,... | collective-permute-start | bytes 786440 | tf_op jit(solution)/shard_map/ppermute | solution.py:549
  28.0 8.2 %collective-permute-start.6 = (f32[8,32,128]{2,1,0:T(8,128)S(1)}, f32[8,32,128]{2,1,0:T(8,128)S(1)}, u32[]{:S(2)}, u32[]{:S(2)}) collective-permute-start(f32[8,32,128]{2,1,0:T(8,128)S(1)} %get-tuple-element.66), channel_id=1, source_target_pairs={{0,8},{1,9},{2,10},{3,11},{4,12},{5,13},{6,14},{7,15},{8,0},{9,1},... | collective-permute-start | bytes 393224 | tf_op jit(solution)/shard_map/ppermute | solution.py:549
  31.3 9.5 %collective-permute-start.11 = (f32[8,40,128]{2,1,0:T(8,128)S(1)}, f32[8,40,128]{2,1,0:T(8,128)S(1)}, u32[]{:S(2)}, u32[]{:S(2)}) collective-permute-start(f32[8,40,128]{2,1,0:T(8,128)S(1)} %get-tuple-element.74), channel_id=1, source_target_pairs={{0,2},{1,3},{2,0},{3,1},{4,6},{5,7},{6,4},{7,5},{8,10},{9,11},{10,... | collective-permute-start | bytes 491528 | tf_op jit(solution)/shard_map/ppermute | solution.py:549
  32.8 8.0 %collective-permute-start.8 = (f32[8,24,128]{2,1,0:T(8,128)S(1)}, f32[8,24,128]{2,1,0:T(8,128)S(1)}, u32[]{:S(2)}, u32[]{:S(2)}) collective-permute-start(f32[8,24,128]{2,1,0:T(8,128)S(1)} %get-tuple-element.69), channel_id=1, source_target_pairs={{0,8},{1,9},{2,10},{3,11},{4,12},{5,13},{6,14},{7,15},{8,0},{9,1},... | collective-permute-start | bytes 294920 | tf_op jit(solution)/shard_map/ppermute | solution.py:549
  36.9 5.0 %collective-permute-start.10 = (f32[8,32,128]{2,1,0:T(8,128)S(1)}, f32[8,32,128]{2,1,0:T(8,128)S(1)}, u32[]{:S(2)}, u32[]{:S(2)}) collective-permute-start(f32[8,32,128]{2,1,0:T(8,128)S(1)} %get-tuple-element.72), channel_id=1, source_target_pairs={{0,2},{1,3},{2,0},{3,1},{4,6},{5,7},{6,4},{7,5},{8,10},{9,11},{10,... | collective-permute-start | bytes 393224 | tf_op jit(solution)/shard_map/ppermute | solution.py:549
  41.4 4.7 %collective-permute-start.12 = (f32[8,24,128]{2,1,0:T(8,128)S(1)}, f32[8,24,128]{2,1,0:T(8,128)S(1)}, u32[]{:S(2)}, u32[]{:S(2)}) collective-permute-start(f32[8,24,128]{2,1,0:T(8,128)S(1)} %get-tuple-element.75), channel_id=1, source_target_pairs={{0,2},{1,3},{2,0},{3,1},{4,6},{5,7},{6,4},{7,5},{8,10},{9,11},{10,... | collective-permute-start | bytes 294920 | tf_op jit(solution)/shard_map/ppermute | solution.py:549
  47.0 8.9 %collective-permute-start.15 = (f32[2,5,4,8,128]{4,3,2,1,0:T(8,128)S(1)}, f32[2,5,4,8,128]{4,3,2,1,0:T(8,128)S(1)}, u32[]{:S(2)}, u32[]{:S(2)}) collective-permute-start(f32[2,5,4,8,128]{4,3,2,1,0:T(8,128)S(1)} %get-tuple-element.89), channel_id=1, source_target_pairs={{0,16},{16,0},{1,17},{17,1},{2,18},{18,2},{3,19},{19,3},{4,20},{20... | collective-permute-start | bytes 491528 | tf_op jit(solution)/shard_map/ppermute | solution.py:680
  49.3 5.0 %collective-permute-start.17 = (f32[5,32,128]{2,1,0:T(8,128)S(1)}, f32[5,32,128]{2,1,0:T(8,128)S(1)}, u32[]{:S(2)}, u32[]{:S(2)}) collective-permute-start(f32[5,32,128]{2,1,0:T(8,128)S(1)} %get-tuple-element.90.z_lo), channel_id=1, source_target_pairs={{0,3},{1,0},{2,1},{3,2},{4,7},{5,4},{6,5},{7,6},{8,11},{9,8},{10,9... | collective-permute-start | bytes 245768 | tf_op jit(solution)/shard_map/ppermute | solution.py:680
  49.3 5.0 %collective-permute-start.16 = (f32[5,32,128]{2,1,0:T(8,128)S(1)}, f32[5,32,128]{2,1,0:T(8,128)S(1)}, u32[]{:S(2)}, u32[]{:S(2)}) collective-permute-start(f32[5,32,128]{2,1,0:T(8,128)S(1)} %get-tuple-element.91.z_hi), channel_id=1, source_target_pairs={{0,1},{1,2},{2,3},{3,0},{4,5},{5,6},{6,7},{7,4},{8,9},{9,10},{10,1... | collective-permute-start | bytes 245768 | tf_op jit(solution)/shard_map/ppermute | solution.py:680
  49.8 6.7 %collective-permute-start.13 = (f32[5,4,8,128]{3,2,1,0:T(8,128)S(1)}, f32[5,4,8,128]{3,2,1,0:T(8,128)S(1)}, u32[]{:S(2)}, u32[]{:S(2)}) collective-permute-start(f32[5,4,8,128]{3,2,1,0:T(8,128)S(1)} %get-tuple-element.87.y_one), channel_id=1, source_target_pairs={{0,4},{4,0},{8,12},{12,8},{1,5},{5,1},{9,13},{13,9},{2,6},{6,2},{1... | collective-permute-start | bytes 245768 | tf_op jit(solution)/shard_map/ppermute | solution.py:685
  52.0 7.2 %collective-permute-start.14 = (f32[5,4,8,128]{3,2,1,0:T(8,128)S(1)}, f32[5,4,8,128]{3,2,1,0:T(8,128)S(1)}, u32[]{:S(2)}, u32[]{:S(2)}) collective-permute-start(f32[5,4,8,128]{3,2,1,0:T(8,128)S(1)} %get-tuple-element.88.y_two), channel_id=1, source_target_pairs={{0,12},{4,8},{8,4},{12,0},{1,13},{5,9},{9,5},{13,1},{2,14},{6,10},... | collective-permute-start | bytes 245768 | tf_op jit(solution)/shard_map/ppermute | solution.py:685
  60.5 8.1 %collective-permute-start.20 = (f32[2,5,4,8,128]{4,3,2,1,0:T(8,128)S(1)}, f32[2,5,4,8,128]{4,3,2,1,0:T(8,128)S(1)}, u32[]{:S(2)}, u32[]{:S(2)}) collective-permute-start(f32[2,5,4,8,128]{4,3,2,1,0:T(8,128)S(1)} %get-tuple-element.96), channel_id=1, source_target_pairs={{0,16},{16,0},{1,17},{17,1},{2,18},{18,2},{3,19},{19,3},{4,20},{20... | collective-permute-start | bytes 491528 | tf_op jit(solution)/shard_map/ppermute | solution.py:680
  62.4 4.6 %collective-permute-start.22 = (f32[5,32,128]{2,1,0:T(8,128)S(1)}, f32[5,32,128]{2,1,0:T(8,128)S(1)}, u32[]{:S(2)}, u32[]{:S(2)}) collective-permute-start(f32[5,32,128]{2,1,0:T(8,128)S(1)} %get-tuple-element.97.z_lo), channel_id=1, source_target_pairs={{0,3},{1,0},{2,1},{3,2},{4,7},{5,4},{6,5},{7,6},{8,11},{9,8},{10,9... | collective-permute-start | bytes 245768 | tf_op jit(solution)/shard_map/ppermute | solution.py:680
  62.5 4.6 %collective-permute-start.21 = (f32[5,32,128]{2,1,0:T(8,128)S(1)}, f32[5,32,128]{2,1,0:T(8,128)S(1)}, u32[]{:S(2)}, u32[]{:S(2)}) collective-permute-start(f32[5,32,128]{2,1,0:T(8,128)S(1)} %get-tuple-element.98.z_hi), channel_id=1, source_target_pairs={{0,1},{1,2},{2,3},{3,0},{4,5},{5,6},{6,7},{7,4},{8,9},{9,10},{10,1... | collective-permute-start | bytes 245768 | tf_op jit(solution)/shard_map/ppermute | solution.py:680
  62.9 6.3 %collective-permute-start.18 = (f32[5,4,8,128]{3,2,1,0:T(8,128)S(1)}, f32[5,4,8,128]{3,2,1,0:T(8,128)S(1)}, u32[]{:S(2)}, u32[]{:S(2)}) collective-permute-start(f32[5,4,8,128]{3,2,1,0:T(8,128)S(1)} %get-tuple-element.94.y_one), channel_id=1, source_target_pairs={{0,4},{4,0},{8,12},{12,8},{1,5},{5,1},{9,13},{13,9},{2,6},{6,2},{1... | collective-permute-start | bytes 245768 | tf_op jit(solution)/shard_map/ppermute | solution.py:685
  64.1 7.8 %collective-permute-start.19 = (f32[5,4,8,128]{3,2,1,0:T(8,128)S(1)}, f32[5,4,8,128]{3,2,1,0:T(8,128)S(1)}, u32[]{:S(2)}, u32[]{:S(2)}) collective-permute-start(f32[5,4,8,128]{3,2,1,0:T(8,128)S(1)} %get-tuple-element.95.y_two), channel_id=1, source_target_pairs={{0,12},{4,8},{8,4},{12,0},{1,13},{5,9},{9,5},{13,1},{2,14},{6,10},... | collective-permute-start | bytes 245768 | tf_op jit(solution)/shard_map/ppermute | solution.py:685

commit v8 on v7

--- a/solution.py
+++ b/solution.py
@@ -247,8 +247,8 @@
                 mine = lane >= shape.width * k
                 lo = jnp.where(mine, below, lo)
                 hi = jnp.where(mine, above, hi)
-        y_one[f, slab] = jnp.where(odd, lo, hi)
-        y_two[f, slab] = jnp.where(odd, hi, lo)
+        y_one[f, slab] = jnp.where(odd, hi, lo)
+        y_two[f, slab] = jnp.where(odd, lo, hi)
         to = pl.ds(slab * SUB, SUB) if isinstance(slab, int) else pl.ds(
             pl.multiple_of(slab * SUB, SUB), SUB
         )
@@ -402,10 +402,10 @@
     odd = odd_y()
 
     def prepare(q):
-        low = [jnp.where(odd, y_one[f, q], y_two[f, q]) for f in FIELDS]
-        high = [jnp.where(odd, y_two[f, q], y_one[f, q]) for f in FIELDS]
-        below = [jnp.where(odd, got_one[f, q], got_two[f, q]) for f in FIELDS]
-        after = [jnp.where(odd, got_two[f, q], got_one[f, q]) for f in FIELDS]
+        low = [jnp.where(odd, y_two[f, q], y_one[f, q]) for f in FIELDS]
+        high = [jnp.where(odd, y_one[f, q], y_two[f, q]) for f in FIELDS]
+        below = [jnp.where(odd, got_two[f, q], got_one[f, q]) for f in FIELDS]
+        after = [jnp.where(odd, got_one[f, q], got_two[f, q]) for f in FIELDS]
         before = [lane_roll(v, edge) for v in below]
         first = [lane_roll(v, edge) for v in low]
         lefts = plus(below, half_slopes(before, below, first))
@@ -689,7 +689,7 @@
             x_faces = ring(x_faces, "gx", 1)
         else:
             x_faces = jnp.stack([ring(x_faces[0], "gx", 1), ring(x_faces[1], "gx", -1)])
-        got_one, got_two = beside(y_one, "gy", 0), beside(y_two, "gy", 1)
+        got_one, got_two = beside(y_one, "gy", 1), beside(y_two, "gy", 0)
         z_prev, z_next = ring(z_hi, "gz", 1), ring(z_lo, "gz", -1)
         ghost = VMEM((NF, rows, LANES), f32)
         work = [VMEM(grid.shape, f32)] * 3

time: 74.8 us -> 74.9 us (level)
  waiting for transfers between devices: 24.6 us -> 27 us
  starting transfers between devices: 31.9 us -> 29.7 us
    ppermute x4, starting transfers between devices: 8.55 us -> 6.29 us  [beside(): return lax.ppermute(value, axis, [(i, j % size) for i, j in pairs])]
    ppermute x6, waiting for transfers between devices: 0.21 us -> 2.39 us  [ring(): lax.ppermute(value, axis, [(i, (i + step) % size) for i in range(size)])]
  transfers between devices with their start and end apart: 23 -> 23, of which waited for: 12 -> 14; matrix products, arithmetic and copies ran while one was open for 0% -> 0% of each run, Pallas kernels for 16% -> 16%
where the time goes in v8:
time: 74.9 us; the launch traced here: 74.7 us
  starting transfers between devices  29.7 us (40%)
  waiting for transfers between devices  27 us (36%)
  Pallas kernels  17.8 us (24%)
    ppermute x13, waiting for transfers between devices, swapped(): return lax.ppermute(value, AXES, pairs)  19 us
    ppermute x13, starting transfers between devices, swapped(): return lax.ppermute(value, AXES, pairs)  18.1 us
    ppermute x4, starting transfers between devices, beside(): return lax.ppermute(value, axis, [(i, j % size) for i, j in pairs])  6.29 us
    ppermute x4, waiting for transfers between devices, beside(): return lax.ppermute(value, axis, [(i, j % size) for i, j in pairs])  5.55 us
    ppermute x6, starting transfers between devices, ring(): lax.ppermute(value, axis, [(i, (i + step) % size) for i in range(size)])  5.28 us
    pallas_call x7, Pallas kernels, make(): pl.pallas_call(functools.partial(pick_kernel, plan=plan, held=tuple(found...  4.6 us
    pallas_call x2, Pallas kernels, flux_sums(): pl.pallas_call(functools.partial(sweep_z_kernel, shape=shape), out_shape=...  3.04 us
    pallas_call x1, Pallas kernels, shards(): pl.pallas_call(functools.partial(sweep_y_two_kernel, shape=shape, occ=occ...  2.69 us
  transfers between devices with their start and end apart: 23, of which 14 were waited for; matrix products, arithmetic and copies ran while one was open for 0% of the time, Pallas kernels for 16%

profile of v8, /device:TPU:0, one launch (start us, length us, event | category | flops | bytes accessed | tf_op | source)
XLA Modules:
  0.0 74.7 jit_solution(1970177991435828861)
XLA Ops:
  0.0 1.2 %pack_first.1 = f32[8,24,128]{2,1,0:T(8,128)S(1)} custom-call(s32[3,1,8]{2,1,0:T(1,128)} %send_hbm.1, f32[5120,128]{1,0:T(8,128)} %bitcast.10), custom_call_target="tpu_custom_call" | custom-call | tf_op jit(solution)/shard_map/pack_first/pallas_call | solution.py:568
  1.3 3.0 %collective-permute-start.1 = (f32[8,24,128]{2,1,0:T(8,128)S(1)}, f32[8,24,128]{2,1,0:T(8,128)S(1)}, u32[]{:S(2)}, u32[]{:S(2)}) collective-permute-start(f32[8,24,128]{2,1,0:T(8,128)S(1)} %pack_first.1), channel_id=1, source_target_pairs={{0,16},{1,17},{2,18},{3,19},{4,20},{5,21},{6,22},{7,23},{8,24},{9,... | collective-permute-start | bytes 294920 | tf_op jit(solution)/shard_map/ppermute | solution.py:549
  4.3 0.1 dynamic_slice.3.own.own_there
  4.4 1.4 %pack_rest.1 = (s32[24]{0:T(128)S(1)}, f32[8,128]{1,0:T(8,128)S(1)}, f32[8,40,128]{2,1,0:T(8,128)S(1)}, f32[8,56,128]{2,1,0:T(8,128)S(1)}, f32[8,40,128]{2,1,0:T(8,128)S(1)}) custom-call(s32[3,1,8]{2,1,0:T(1,128)S(1)} %copy-done.1, s32[3,1,8]{2,1,0:T(1,128)S(1)} %copy-done.3, s32[8]{0:T(128)S(1)} %dynamic_slice.3.own.own_there, f32[5120,128]{1,0:T(8,128)S(1)} %bitcast.11), custom_call_target="tpu_custom_call" | custom-call | tf_op jit(solution)/shard_map/pack_rest/pallas_call | solution.py:581
  5.8 0.6 collective-permute-start
  6.4 0.7 collective-permute-done.1.refs_0_.refs_2_
  7.1 0.6 pick_10.1
  7.7 2.0 %collective-permute-start.3 = (f32[8,56,128]{2,1,0:T(8,128)S(1)}, f32[8,56,128]{2,1,0:T(8,128)S(1)}, u32[]{:S(2)}, u32[]{:S(2)}) collective-permute-start(f32[8,56,128]{2,1,0:T(8,128)S(1)} %get-tuple-element.60), channel_id=1, source_target_pairs={{0,16},{1,17},{2,18},{3,19},{4,20},{5,21},{6,22},{7,23},{8,24},{9,... | collective-permute-start | bytes 688136 | tf_op jit(solution)/shard_map/ppermute | solution.py:549
  9.7 2.6 %collective-permute-start.4 = (f32[8,24,128]{2,1,0:T(8,128)S(1)}, f32[8,24,128]{2,1,0:T(8,128)S(1)}, u32[]{:S(2)}, u32[]{:S(2)}) collective-permute-start(f32[8,24,128]{2,1,0:T(8,128)S(1)} %get-tuple-element.62), channel_id=1, source_target_pairs={{0,8},{1,9},{2,10},{3,11},{4,12},{5,13},{6,14},{7,15},{8,0},{9,1},... | collective-permute-start | bytes 294920 | tf_op jit(solution)/shard_map/ppermute | solution.py:549
  12.3 0.7 collective-permute-done.refs_0_.refs_3_.refs_1_
  13.0 0.6 pick_11.1
  13.6 0.6 collective-permute-start.2
  14.2 2.6 %collective-permute-start.5 = (f32[8,40,128]{2,1,0:T(8,128)S(1)}, f32[8,40,128]{2,1,0:T(8,128)S(1)}, u32[]{:S(2)}, u32[]{:S(2)}) collective-permute-start(f32[8,40,128]{2,1,0:T(8,128)S(1)} %get-tuple-element.64), channel_id=1, source_target_pairs={{0,8},{1,9},{2,10},{3,11},{4,12},{5,13},{6,14},{7,15},{8,0},{9,1},... | collective-permute-start | bytes 491528 | tf_op jit(solution)/shard_map/ppermute | solution.py:549
  16.8 0.0 collective-permute-done.4.refs_2_
  16.8 1.1 %collective-permute-done.3.refs_0_.refs_1_.refs_2_ = f32[8,56,128]{2,1,0:T(8,128)S(1)} collective-permute-done((f32[8,56,128]{2,1,0:T(8,128)S(1)}, f32[8,56,128]{2,1,0:T(8,128)S(1)}, u32[]{:S(2)}, u32[]{:S(2)}) %collective-permute-start.3) | collective-permute-done | bytes 229408 | tf_op jit(solution)/shard_map/ppermute | solution.py:549
  17.9 0.6 pick_12.1
  18.5 2.7 %collective-permute-start.7 = (f32[8,40,128]{2,1,0:T(8,128)S(1)}, f32[8,40,128]{2,1,0:T(8,128)S(1)}, u32[]{:S(2)}, u32[]{:S(2)}) collective-permute-start(f32[8,40,128]{2,1,0:T(8,128)S(1)} %get-tuple-element.67), channel_id=1, source_target_pairs={{0,8},{1,9},{2,10},{3,11},{4,12},{5,13},{6,14},{7,15},{8,0},{9,1},... | collective-permute-start | bytes 491528 | tf_op jit(solution)/shard_map/ppermute | solution.py:549
  21.2 0.0 collective-permute-done.2.refs_1_.refs_0_
  21.2 4.5 %collective-permute-done.5.refs_5_.refs_4_ = f32[8,40,128]{2,1,0:T(8,128)S(1)} collective-permute-done((f32[8,40,128]{2,1,0:T(8,128)S(1)}, f32[8,40,128]{2,1,0:T(8,128)S(1)}, u32[]{:S(2)}, u32[]{:S(2)}) %collective-permute-start.5) | collective-permute-done | bytes 163872 | tf_op jit(solution)/shard_map/ppermute | solution.py:549
  25.7 0.7 pick_13_20.1
  26.5 1.6 %collective-permute-start.9 = (f32[8,64,128]{2,1,0:T(8,128)S(1)}, f32[8,64,128]{2,1,0:T(8,128)S(1)}, u32[]{:S(2)}, u32[]{:S(2)}) collective-permute-start(f32[8,64,128]{2,1,0:T(8,128)S(1)} %get-tuple-element.71), channel_id=1, source_target_pairs={{0,2},{1,3},{2,0},{3,1},{4,6},{5,7},{6,4},{7,5},{8,10},{9,11},{10,... | collective-permute-start | bytes 786440 | tf_op jit(solution)/shard_map/ppermute | solution.py:549
  28.0 0.0 collective-permute-start.6
  28.0 2.5 %collective-permute-done.7.refs_2_.refs_5_ = f32[8,40,128]{2,1,0:T(8,128)S(1)} collective-permute-done((f32[8,40,128]{2,1,0:T(8,128)S(1)}, f32[8,40,128]{2,1,0:T(8,128)S(1)}, u32[]{:S(2)}, u32[]{:S(2)}) %collective-permute-start.7) | collective-permute-done | bytes 163872 | tf_op jit(solution)/shard_map/ppermute | solution.py:549
  30.5 0.7 pick_14_21.1
  31.3 1.6 %collective-permute-start.11 = (f32[8,40,128]{2,1,0:T(8,128)S(1)}, f32[8,40,128]{2,1,0:T(8,128)S(1)}, u32[]{:S(2)}, u32[]{:S(2)}) collective-permute-start(f32[8,40,128]{2,1,0:T(8,128)S(1)} %get-tuple-element.74), channel_id=1, source_target_pairs={{0,2},{1,3},{2,0},{3,1},{4,6},{5,7},{6,4},{7,5},{8,10},{9,11},{10,... | collective-permute-start | bytes 491528 | tf_op jit(solution)/shard_map/ppermute | solution.py:549
  32.8 0.0 collective-permute-start.8
  32.8 3.4 %collective-permute-done.6.refs_2_.refs_6_.refs_1_ = f32[8,32,128]{2,1,0:T(8,128)S(1)} collective-permute-done((f32[8,32,128]{2,1,0:T(8,128)S(1)}, f32[8,32,128]{2,1,0:T(8,128)S(1)}, u32[]{:S(2)}, u32[]{:S(2)}) %collective-permute-start.6) | collective-permute-done | bytes 131104 | tf_op jit(solution)/shard_map/ppermute | solution.py:549
  36.2 0.0 collective-permute-done.9.refs_4_
  36.2 0.6 pick_22.1
  36.9 0.9 %collective-permute-start.10 = (f32[8,32,128]{2,1,0:T(8,128)S(1)}, f32[8,32,128]{2,1,0:T(8,128)S(1)}, u32[]{:S(2)}, u32[]{:S(2)}) collective-permute-start(f32[8,32,128]{2,1,0:T(8,128)S(1)} %get-tuple-element.72), channel_id=1, source_target_pairs={{0,2},{1,3},{2,0},{3,1},{4,6},{5,7},{6,4},{7,5},{8,10},{9,11},{10,... | collective-permute-start | bytes 393224 | tf_op jit(solution)/shard_map/ppermute | solution.py:549
  37.8 3.0 %collective-permute-done.8.refs_1_.refs_2_ = f32[8,24,128]{2,1,0:T(8,128)S(1)} collective-permute-done((f32[8,24,128]{2,1,0:T(8,128)S(1)}, f32[8,24,128]{2,1,0:T(8,128)S(1)}, u32[]{:S(2)}, u32[]{:S(2)}) %collective-permute-start.8) | collective-permute-done | bytes 98336 | tf_op jit(solution)/shard_map/ppermute | solution.py:549
  40.8 0.0 collective-permute-done.11.refs_3_
  40.8 0.6 pick_23.1
  41.4 0.1 collective-permute-start.12
  41.5 0.4 collective-permute-done.10.refs_9_.refs_3_
  41.9 1.5 %assemble_0.1 = (f32[1280,128]{1,0:T(8,128)S(1)}, f32[1280,128]{1,0:T(8,128)S(1)}, f32[5,4,8,128]{3,2,1,0:T(8,128)S(1)}, f32[5,4,8,128]{3,2,1,0:T(8,128)S(1)}, f...) custom-call(s32[24]{0:T(128)S(1)} %get-tuple-element.53.tags, ...), custom_call_target="tpu_custom_call" | custom-call | tf_op jit(solution)/shard_map/assemble_0/pallas_call | solution.py:660
  43.5 2.7 %collective-permute-done.12.refs_4_ = f32[8,24,128]{2,1,0:T(8,128)S(1)} collective-permute-done((f32[8,24,128]{2,1,0:T(8,128)S(1)}, f32[8,24,128]{2,1,0:T(8,128)S(1)}, u32[]{:S(2)}, u32[]{:S(2)}) %collective-permute-start.12) | collective-permute-done | bytes 98336 | tf_op jit(solution)/shard_map/ppermute | solution.py:549
  46.1 0.9 %assemble_3.1 = (f32[1280,128]{1,0:T(8,128)S(1)}, f32[1280,128]{1,0:T(8,128)S(1)}, f32[5,4,8,128]{3,2,1,0:T(8,128)S(1)}, f32[5,4,8,128]{3,2,1,0:T(8,128)S(1)}, f...) custom-call(s32[24]{0:T(128)S(1)} %get-tuple-element.53.tags, ...), custom_call_target="tpu_custom_call", output_to_operand_aliasing={{0}: (7, {}), {1}: (8, {}), {2}: (9, {}), {3}: (10, {}), {4... | custom-call | tf_op jit(solution)/shard_map/assemble_3/pallas_call | solution.py:660
  47.0 2.3 %collective-permute-start.15 = (f32[2,5,4,8,128]{4,3,2,1,0:T(8,128)S(1)}, f32[2,5,4,8,128]{4,3,2,1,0:T(8,128)S(1)}, u32[]{:S(2)}, u32[]{:S(2)}) collective-permute-start(f32[2,5,4,8,128]{4,3,2,1,0:T(8,128)S(1)} %get-tuple-element.89), channel_id=1, source_target_pairs={{0,16},{16,0},{1,17},{17,1},{2,18},{18,2},{3,19},{19,3},{4,20},{20... | collective-permute-start | bytes 491528 | tf_op jit(solution)/shard_map/ppermute | solution.py:680
  49.3 0.0 collective-permute-start.17
  49.3 0.5 collective-permute-start.16
  49.8 4.5 %collective-permute-start.13 = (f32[5,4,8,128]{3,2,1,0:T(8,128)S(1)}, f32[5,4,8,128]{3,2,1,0:T(8,128)S(1)}, u32[]{:S(2)}, u32[]{:S(2)}) collective-permute-start(f32[5,4,8,128]{3,2,1,0:T(8,128)S(1)} %get-tuple-element.87.y_one), channel_id=1, source_target_pairs={{0,12},{4,8},{8,4},{12,0},{1,13},{5,9},{9,5},{13,1},{2,14},{6,10},... | collective-permute-start | bytes 245768 | tf_op jit(solution)/shard_map/ppermute | solution.py:685
  54.4 0.0 collective-permute-start.14
  54.4 0.0 collective-permute-done.17.z_next
  54.4 0.0 collective-permute-done.16.z_prev
  54.4 1.5 %sweep_z.2.sofar = f32[1280,128]{1,0:T(8,128)S(1)} custom-call(f32[1280,128]{1,0:T(8,128)S(1)} %get-tuple-element.86.prim, f32[5,32,128]{2,1,0:T(8,128)S(1)} %get-tuple-element.90.z_lo, f32[5,32,128]{2,1,0:T(8,128)S(1)} %get-tuple-element.91.z_hi, f32[5,32,128]{2,1,0:T(8,128)S(1)} %collective-permute-done.16.z_prev, ...), custom_call_target="tpu_custom_call" | custom-call | tf_op jit(solution)/shard_map/sweep_z/pallas_call | solution.py:696
  55.9 0.0 collective-permute-done.15.x_faces
  55.9 0.6 sweep_x.2.sofar
  56.5 0.9 %collective-permute-done.13.got_one = f32[5,4,8,128]{3,2,1,0:T(8,128)S(1)} collective-permute-done((f32[5,4,8,128]{3,2,1,0:T(8,128)S(1)}, f32[5,4,8,128]{3,2,1,0:T(8,128)S(1)}, u32[]{:S(2)}, u32[]{:S(2)}) %collective-permute-start.13) | collective-permute-done | bytes 81952 | tf_op jit(solution)/shard_map/ppermute | solution.py:685
  57.4 2.2 %collective-permute-done.14.got_two = f32[5,4,8,128]{3,2,1,0:T(8,128)S(1)} collective-permute-done((f32[5,4,8,128]{3,2,1,0:T(8,128)S(1)}, f32[5,4,8,128]{3,2,1,0:T(8,128)S(1)}, u32[]{:S(2)}, u32[]{:S(2)}) %collective-permute-start.14) | collective-permute-done | bytes 81952 | tf_op jit(solution)/shard_map/ppermute | solution.py:685
  59.6 1.3 %sweep_y_one.1 = (f32[1280,128]{1,0:T(8,128)S(1)}, f32[1280,128]{1,0:T(8,128)S(1)}, f32[2,5,4,8,128]{4,3,2,1,0:T(8,128)S(1)}, f32[5,4,8,128]{3,2,1,0:T(8,128)S(1...) custom-call(f32[1280,128]{1,0:T(8,128)S(1)} %get-tuple-element.85.field, ...), custom_call_target="tpu_custom_call" | custom-call | tf_op jit(solution)/shard_map/sweep_y_one/pallas_call | solution.py:720
  60.9 1.9 %collective-permute-start.20 = (f32[2,5,4,8,128]{4,3,2,1,0:T(8,128)S(1)}, f32[2,5,4,8,128]{4,3,2,1,0:T(8,128)S(1)}, u32[]{:S(2)}, u32[]{:S(2)}) collective-permute-start(f32[2,5,4,8,128]{4,3,2,1,0:T(8,128)S(1)} %get-tuple-element.96), channel_id=1, source_target_pairs={{0,16},{16,0},{1,17},{17,1},{2,18},{18,2},{3,19},{19,3},{4,20},{20... | collective-permute-start | bytes 491528 | tf_op jit(solution)/shard_map/ppermute | solution.py:680
  62.8 0.0 collective-permute-start.22
  62.8 0.5 collective-permute-start.21
  63.3 1.8 %collective-permute-start.18 = (f32[5,4,8,128]{3,2,1,0:T(8,128)S(1)}, f32[5,4,8,128]{3,2,1,0:T(8,128)S(1)}, u32[]{:S(2)}, u32[]{:S(2)}) collective-permute-start(f32[5,4,8,128]{3,2,1,0:T(8,128)S(1)} %get-tuple-element.94.y_one), channel_id=1, source_target_pairs={{0,12},{4,8},{8,4},{12,0},{1,13},{5,9},{9,5},{13,1},{2,14},{6,10},... | collective-permute-start | bytes 245768 | tf_op jit(solution)/shard_map/ppermute | solution.py:685
  65.1 0.0 collective-permute-start.19
  65.1 0.0 collective-permute-done.22.z_next
  65.1 2.4 %collective-permute-done.21.z_prev = f32[5,32,128]{2,1,0:T(8,128)S(1)} collective-permute-done((f32[5,32,128]{2,1,0:T(8,128)S(1)}, f32[5,32,128]{2,1,0:T(8,128)S(1)}, u32[]{:S(2)}, u32[]{:S(2)}) %collective-permute-start.21) | collective-permute-done | bytes 81952 | tf_op jit(solution)/shard_map/ppermute | solution.py:680
  67.5 1.5 %sweep_z.3.sofar = f32[1280,128]{1,0:T(8,128)S(1)} custom-call(f32[1280,128]{1,0:T(8,128)S(1)} %get-tuple-element.93.prim, f32[5,32,128]{2,1,0:T(8,128)S(1)} %get-tuple-element.97.z_lo, f32[5,32,128]{2,1,0:T(8,128)S(1)} %get-tuple-element.98.z_hi, f32[5,32,128]{2,1,0:T(8,128)S(1)} %collective-permute-done.21.z_prev, ...), custom_call_target="tpu_custom_call" | custom-call | tf_op jit(solution)/shard_map/sweep_z/pallas_call | solution.py:696
  69.0 0.0 collective-permute-done.20.x_faces
  69.0 0.6 sweep_x.3.sofar
  69.6 1.0 %collective-permute-done.18.got_one = f32[5,4,8,128]{3,2,1,0:T(8,128)S(1)} collective-permute-done((f32[5,4,8,128]{3,2,1,0:T(8,128)S(1)}, f32[5,4,8,128]{3,2,1,0:T(8,128)S(1)}, u32[]{:S(2)}, u32[]{:S(2)}) %collective-permute-start.18) | collective-permute-done | bytes 81952 | tf_op jit(solution)/shard_map/ppermute | solution.py:685
  70.6 1.5 %collective-permute-done.19.got_two = f32[5,4,8,128]{3,2,1,0:T(8,128)S(1)} collective-permute-done((f32[5,4,8,128]{3,2,1,0:T(8,128)S(1)}, f32[5,4,8,128]{3,2,1,0:T(8,128)S(1)}, u32[]{:S(2)}, u32[]{:S(2)}) %collective-permute-start.19) | collective-permute-done | bytes 81952 | tf_op jit(solution)/shard_map/ppermute | solution.py:685
  72.0 2.7 %sweep_y_two.1 = (f32[20,256,128]{2,1,0:T(8,128)}, f32[20,256,128]{2,1,0:T(8,128)S(1)}) custom-call(s32[8]{0:T(128)} %copy-done.2, f32[1280,128]{1,0:T(8,128)S(1)} %get-tuple-element.85.field, f32[1280,128]{1,0:T(8,128)S(1)} %get-tuple-element.92.one, f32[1280,128]{1,0:T(8,128)S(1)} %get-tuple-element.93.prim, ...), custom_call_target="tpu_custom_call", output_to_operand_aliasing={{1}: (9, {})} | custom-call | tf_op jit(solution)/shard_map/sweep_y_two/pallas_call | solution.py:731
  (10 shorter events, 0.0 us)
Async XLA Ops:
  0.0 4.4 %copy-start.1 = (s32[3,1,8]{2,1,0:T(1,128)S(1)}, s32[3,1,8]{2,1,0:T(1,128)}, u32[]{:S(2)}) copy-start(s32[3,1,8]{2,1,0:T(1,128)} %send_hbm.1) | copy-start | bytes 292
  0.0 4.4 %copy-start = (f32[32,5,4096]{2,0,1:T(8,128)S(1)}, f32[32,5,4096]{2,0,1:T(8,128)}, u32[]{:S(2)}) copy-start(f32[32,5,4096]{2,0,1:T(8,128)} %param.4) | copy-start | bytes 7864324
  0.0 4.3 %copy-start.4 = (s32[256]{0:T(256)S(1)}, s32[256]{0:T(256)}, u32[]{:S(2)}) copy-start(s32[256]{0:T(256)} %param.7) | copy-start | bytes 3076
  0.0 4.4 %copy-start.3 = (s32[3,1,8]{2,1,0:T(1,128)S(1)}, s32[3,1,8]{2,1,0:T(1,128)}, u32[]{:S(2)}) copy-start(s32[3,1,8]{2,1,0:T(1,128)} %recv.1) | copy-start | bytes 292
  1.3 5.8 %collective-permute-start.1 = (f32[8,24,128]{2,1,0:T(8,128)S(1)}, f32[8,24,128]{2,1,0:T(8,128)S(1)}, u32[]{:S(2)}, u32[]{:S(2)}) collective-permute-start(f32[8,24,128]{2,1,0:T(8,128)S(1)} %pack_first.1), channel_id=1, source_target_pairs={{0,16},{1,17},{2,18},{3,19},{4,20},{5,21},{6,22},{7,23},{8,24},{9,... | collective-permute-start | bytes 294920 | tf_op jit(solution)/shard_map/ppermute | solution.py:549
  4.4 3.3 %copy-start.2 = (s32[8]{0:T(128)}, s32[8]{0:T(128)S(1)}, u32[]{:S(2)}) copy-start(s32[8]{0:T(128)S(1)} %dynamic_slice.3.own.own_there) | copy-start | bytes 100
  5.8 7.2 %collective-permute-start = (f32[8,40,128]{2,1,0:T(8,128)S(1)}, f32[8,40,128]{2,1,0:T(8,128)S(1)}, u32[]{:S(2)}, u32[]{:S(2)}) collective-permute-start(f32[8,40,128]{2,1,0:T(8,128)S(1)} %get-tuple-element.54), channel_id=1, source_target_pairs={{0,16},{1,17},{2,18},{3,19},{4,20},{5,21},{6,22},{7,23},{8,24},{9,... | collective-permute-start | bytes 491528 | tf_op jit(solution)/shard_map/ppermute | solution.py:549
  7.7 10.2 %collective-permute-start.3 = (f32[8,56,128]{2,1,0:T(8,128)S(1)}, f32[8,56,128]{2,1,0:T(8,128)S(1)}, u32[]{:S(2)}, u32[]{:S(2)}) collective-permute-start(f32[8,56,128]{2,1,0:T(8,128)S(1)} %get-tuple-element.60), channel_id=1, source_target_pairs={{0,16},{1,17},{2,18},{3,19},{4,20},{5,21},{6,22},{7,23},{8,24},{9,... | collective-permute-start | bytes 688136 | tf_op jit(solution)/shard_map/ppermute | solution.py:549
  9.7 7.1 %collective-permute-start.4 = (f32[8,24,128]{2,1,0:T(8,128)S(1)}, f32[8,24,128]{2,1,0:T(8,128)S(1)}, u32[]{:S(2)}, u32[]{:S(2)}) collective-permute-start(f32[8,24,128]{2,1,0:T(8,128)S(1)} %get-tuple-element.62), channel_id=1, source_target_pairs={{0,8},{1,9},{2,10},{3,11},{4,12},{5,13},{6,14},{7,15},{8,0},{9,1},... | collective-permute-start | bytes 294920 | tf_op jit(solution)/shard_map/ppermute | solution.py:549
  13.6 7.6 %collective-permute-start.2 = (f32[8,40,128]{2,1,0:T(8,128)S(1)}, f32[8,40,128]{2,1,0:T(8,128)S(1)}, u32[]{:S(2)}, u32[]{:S(2)}) collective-permute-start(f32[8,40,128]{2,1,0:T(8,128)S(1)} %get-tuple-element.59), channel_id=1, source_target_pairs={{0,16},{1,17},{2,18},{3,19},{4,20},{5,21},{6,22},{7,23},{8,24},{9,... | collective-permute-start | bytes 491528 | tf_op jit(solution)/shard_map/ppermute | solution.py:549
  14.2 11.5 %collective-permute-start.5 = (f32[8,40,128]{2,1,0:T(8,128)S(1)}, f32[8,40,128]{2,1,0:T(8,128)S(1)}, u32[]{:S(2)}, u32[]{:S(2)}) collective-permute-start(f32[8,40,128]{2,1,0:T(8,128)S(1)} %get-tuple-element.64), channel_id=1, source_target_pairs={{0,8},{1,9},{2,10},{3,11},{4,12},{5,13},{6,14},{7,15},{8,0},{9,1},... | collective-permute-start | bytes 491528 | tf_op jit(solution)/shard_map/ppermute | solution.py:549
  18.5 12.0 %collective-permute-start.7 = (f32[8,40,128]{2,1,0:T(8,128)S(1)}, f32[8,40,128]{2,1,0:T(8,128)S(1)}, u32[]{:S(2)}, u32[]{:S(2)}) collective-permute-start(f32[8,40,128]{2,1,0:T(8,128)S(1)} %get-tuple-element.67), channel_id=1, source_target_pairs={{0,8},{1,9},{2,10},{3,11},{4,12},{5,13},{6,14},{7,15},{8,0},{9,1},... | collective-permute-start | bytes 491528 | tf_op jit(solution)/shard_map/ppermute | solution.py:549
  26.5 9.8 %collective-permute-start.9 = (f32[8,64,128]{2,1,0:T(8,128)S(1)}, f32[8,64,128]{2,1,0:T(8,128)S(1)}, u32[]{:S(2)}, u32[]{:S(2)}) collective-permute-start(f32[8,64,128]{2,1,0:T(8,128)S(1)} %get-tuple-element.71), channel_id=1, source_target_pairs={{0,2},{1,3},{2,0},{3,1},{4,6},{5,7},{6,4},{7,5},{8,10},{9,11},{10,... | collective-permute-start | bytes 786440 | tf_op jit(solution)/shard_map/ppermute | solution.py:549
  28.0 8.2 %collective-permute-start.6 = (f32[8,32,128]{2,1,0:T(8,128)S(1)}, f32[8,32,128]{2,1,0:T(8,128)S(1)}, u32[]{:S(2)}, u32[]{:S(2)}) collective-permute-start(f32[8,32,128]{2,1,0:T(8,128)S(1)} %get-tuple-element.66), channel_id=1, source_target_pairs={{0,8},{1,9},{2,10},{3,11},{4,12},{5,13},{6,14},{7,15},{8,0},{9,1},... | collective-permute-start | bytes 393224 | tf_op jit(solution)/shard_map/ppermute | solution.py:549
  31.3 9.5 %collective-permute-start.11 = (f32[8,40,128]{2,1,0:T(8,128)S(1)}, f32[8,40,128]{2,1,0:T(8,128)S(1)}, u32[]{:S(2)}, u32[]{:S(2)}) collective-permute-start(f32[8,40,128]{2,1,0:T(8,128)S(1)} %get-tuple-element.74), channel_id=1, source_target_pairs={{0,2},{1,3},{2,0},{3,1},{4,6},{5,7},{6,4},{7,5},{8,10},{9,11},{10,... | collective-permute-start | bytes 491528 | tf_op jit(solution)/shard_map/ppermute | solution.py:549
  32.8 8.0 %collective-permute-start.8 = (f32[8,24,128]{2,1,0:T(8,128)S(1)}, f32[8,24,128]{2,1,0:T(8,128)S(1)}, u32[]{:S(2)}, u32[]{:S(2)}) collective-permute-start(f32[8,24,128]{2,1,0:T(8,128)S(1)} %get-tuple-element.69), channel_id=1, source_target_pairs={{0,8},{1,9},{2,10},{3,11},{4,12},{5,13},{6,14},{7,15},{8,0},{9,1},... | collective-permute-start | bytes 294920 | tf_op jit(solution)/shard_map/ppermute | solution.py:549
  36.9 5.0 %collective-permute-start.10 = (f32[8,32,128]{2,1,0:T(8,128)S(1)}, f32[8,32,128]{2,1,0:T(8,128)S(1)}, u32[]{:S(2)}, u32[]{:S(2)}) collective-permute-start(f32[8,32,128]{2,1,0:T(8,128)S(1)} %get-tuple-element.72), channel_id=1, source_target_pairs={{0,2},{1,3},{2,0},{3,1},{4,6},{5,7},{6,4},{7,5},{8,10},{9,11},{10,... | collective-permute-start | bytes 393224 | tf_op jit(solution)/shard_map/ppermute | solution.py:549
  41.4 4.7 %collective-permute-start.12 = (f32[8,24,128]{2,1,0:T(8,128)S(1)}, f32[8,24,128]{2,1,0:T(8,128)S(1)}, u32[]{:S(2)}, u32[]{:S(2)}) collective-permute-start(f32[8,24,128]{2,1,0:T(8,128)S(1)} %get-tuple-element.75), channel_id=1, source_target_pairs={{0,2},{1,3},{2,0},{3,1},{4,6},{5,7},{6,4},{7,5},{8,10},{9,11},{10,... | collective-permute-start | bytes 294920 | tf_op jit(solution)/shard_map/ppermute | solution.py:549
  47.0 8.9 %collective-permute-start.15 = (f32[2,5,4,8,128]{4,3,2,1,0:T(8,128)S(1)}, f32[2,5,4,8,128]{4,3,2,1,0:T(8,128)S(1)}, u32[]{:S(2)}, u32[]{:S(2)}) collective-permute-start(f32[2,5,4,8,128]{4,3,2,1,0:T(8,128)S(1)} %get-tuple-element.89), channel_id=1, source_target_pairs={{0,16},{16,0},{1,17},{17,1},{2,18},{18,2},{3,19},{19,3},{4,20},{20... | collective-permute-start | bytes 491528 | tf_op jit(solution)/shard_map/ppermute | solution.py:680
  49.3 5.0 %collective-permute-start.17 = (f32[5,32,128]{2,1,0:T(8,128)S(1)}, f32[5,32,128]{2,1,0:T(8,128)S(1)}, u32[]{:S(2)}, u32[]{:S(2)}) collective-permute-start(f32[5,32,128]{2,1,0:T(8,128)S(1)} %get-tuple-element.90.z_lo), channel_id=1, source_target_pairs={{0,3},{1,0},{2,1},{3,2},{4,7},{5,4},{6,5},{7,6},{8,11},{9,8},{10,9... | collective-permute-start | bytes 245768 | tf_op jit(solution)/shard_map/ppermute | solution.py:680
  49.3 5.0 %collective-permute-start.16 = (f32[5,32,128]{2,1,0:T(8,128)S(1)}, f32[5,32,128]{2,1,0:T(8,128)S(1)}, u32[]{:S(2)}, u32[]{:S(2)}) collective-permute-start(f32[5,32,128]{2,1,0:T(8,128)S(1)} %get-tuple-element.91.z_hi), channel_id=1, source_target_pairs={{0,1},{1,2},{2,3},{3,0},{4,5},{5,6},{6,7},{7,4},{8,9},{9,10},{10,1... | collective-permute-start | bytes 245768 | tf_op jit(solution)/shard_map/ppermute | solution.py:680
  49.8 7.6 %collective-permute-start.13 = (f32[5,4,8,128]{3,2,1,0:T(8,128)S(1)}, f32[5,4,8,128]{3,2,1,0:T(8,128)S(1)}, u32[]{:S(2)}, u32[]{:S(2)}) collective-permute-start(f32[5,4,8,128]{3,2,1,0:T(8,128)S(1)} %get-tuple-element.87.y_one), channel_id=1, source_target_pairs={{0,12},{4,8},{8,4},{12,0},{1,13},{5,9},{9,5},{13,1},{2,14},{6,10},... | collective-permute-start | bytes 245768 | tf_op jit(solution)/shard_map/ppermute | solution.py:685
  54.4 5.2 %collective-permute-start.14 = (f32[5,4,8,128]{3,2,1,0:T(8,128)S(1)}, f32[5,4,8,128]{3,2,1,0:T(8,128)S(1)}, u32[]{:S(2)}, u32[]{:S(2)}) collective-permute-start(f32[5,4,8,128]{3,2,1,0:T(8,128)S(1)} %get-tuple-element.88.y_two), channel_id=1, source_target_pairs={{0,4},{4,0},{8,12},{12,8},{1,5},{5,1},{9,13},{13,9},{2,6},{6,2},{1... | collective-permute-start | bytes 245768 | tf_op jit(solution)/shard_map/ppermute | solution.py:685
  60.9 8.1 %collective-permute-start.20 = (f32[2,5,4,8,128]{4,3,2,1,0:T(8,128)S(1)}, f32[2,5,4,8,128]{4,3,2,1,0:T(8,128)S(1)}, u32[]{:S(2)}, u32[]{:S(2)}) collective-permute-start(f32[2,5,4,8,128]{4,3,2,1,0:T(8,128)S(1)} %get-tuple-element.96), channel_id=1, source_target_pairs={{0,16},{16,0},{1,17},{17,1},{2,18},{18,2},{3,19},{19,3},{4,20},{20... | collective-permute-start | bytes 491528 | tf_op jit(solution)/shard_map/ppermute | solution.py:680
  62.8 2.3 %collective-permute-start.22 = (f32[5,32,128]{2,1,0:T(8,128)S(1)}, f32[5,32,128]{2,1,0:T(8,128)S(1)}, u32[]{:S(2)}, u32[]{:S(2)}) collective-permute-start(f32[5,32,128]{2,1,0:T(8,128)S(1)} %get-tuple-element.97.z_lo), channel_id=1, source_target_pairs={{0,3},{1,0},{2,1},{3,2},{4,7},{5,4},{6,5},{7,6},{8,11},{9,8},{10,9... | collective-permute-start | bytes 245768 | tf_op jit(solution)/shard_map/ppermute | solution.py:680
  62.8 4.7 %collective-permute-start.21 = (f32[5,32,128]{2,1,0:T(8,128)S(1)}, f32[5,32,128]{2,1,0:T(8,128)S(1)}, u32[]{:S(2)}, u32[]{:S(2)}) collective-permute-start(f32[5,32,128]{2,1,0:T(8,128)S(1)} %get-tuple-element.98.z_hi), channel_id=1, source_target_pairs={{0,1},{1,2},{2,3},{3,0},{4,5},{5,6},{6,7},{7,4},{8,9},{9,10},{10,1... | collective-permute-start | bytes 245768 | tf_op jit(solution)/shard_map/ppermute | solution.py:680
  63.3 7.3 %collective-permute-start.18 = (f32[5,4,8,128]{3,2,1,0:T(8,128)S(1)}, f32[5,4,8,128]{3,2,1,0:T(8,128)S(1)}, u32[]{:S(2)}, u32[]{:S(2)}) collective-permute-start(f32[5,4,8,128]{3,2,1,0:T(8,128)S(1)} %get-tuple-element.94.y_one), channel_id=1, source_target_pairs={{0,12},{4,8},{8,4},{12,0},{1,13},{5,9},{9,5},{13,1},{2,14},{6,10},... | collective-permute-start | bytes 245768 | tf_op jit(solution)/shard_map/ppermute | solution.py:685
  65.1 6.9 %collective-permute-start.19 = (f32[5,4,8,128]{3,2,1,0:T(8,128)S(1)}, f32[5,4,8,128]{3,2,1,0:T(8,128)S(1)}, u32[]{:S(2)}, u32[]{:S(2)}) collective-permute-start(f32[5,4,8,128]{3,2,1,0:T(8,128)S(1)} %get-tuple-element.95.y_two), channel_id=1, source_target_pairs={{0,4},{4,0},{8,12},{12,8},{1,5},{5,1},{9,13},{13,9},{2,6},{6,2},{1... | collective-permute-start | bytes 245768 | tf_op jit(solution)/shard_map/ppermute | solution.py:685

commit v9 on v8

--- a/solution.py
+++ b/solution.py
@@ -508,7 +508,10 @@
     def copy(part):
         begin = part * span if isinstance(part, int) else pl.multiple_of(part * span, span)
         at = pl.ds(begin, span)
-        return pltpu.make_async_copy(canvas.at[:, at, :], out.at[:, at, :], sems.at[part])
+        return [
+            pltpu.make_async_copy(canvas.at[of, at, :], out.at[of, at, :], sems.at[part, f])
+            for f, of in enumerate(pl.ds(f * groups, groups) for f in FIELDS)
+        ]
 
     def after_slab(q):
         if q == 0:
@@ -518,11 +521,13 @@
             to = pl.ds(q * span + lax.rem(slot, SUB), SUB, stride=SUB)
             for f in FIELDS:
                 canvas[f * groups + slot // SUB, to, :] = result[shape.across(f, q, b), :]
-        copy(q).start()
+        for c in copy(q):
+            c.start()
 
     sweep_y(prim, y_one, y_two, got_one, got_two, sofar, *scratch, shape, finish, after_slab)
     for part in range(shape.slabs):
-        copy(part).wait()
+        for c in copy(part):
+            c.wait()
 
 
 def shards(state, send_slots, recv_slots, owner_slot):
@@ -535,7 +540,7 @@
     groups = slots // SUB
     shape = Shape(rows, edge)
     units = NF * shape.slabs
-    cuts = [split_units(units, shares) for shares in ((3, 5, 7, 5), (3, 5, 5, 4, 3), (8, 5, 4, 3))]
+    cuts = [split_units(units, shares) for shares in ((3, 5, 7, 5), (3, 4, 5, 5, 3), (3, 4, 5, 5, 3))]
     firsts, final = cuts[0], cuts[2]
 
     bit_z = size_z.bit_length() - 2
@@ -628,11 +633,11 @@
     steps = [
         ([(1, 0)], [2], []),
         ([(1, 1)], [3], []),
-        ([(1, 2)], [], [(1, 0)]),
-        ([(1, 3), (2, 0)], [], []),
-        ([(1, 4), (2, 1)], [], []),
-        ([(2, 2)], [], [(2, 0)]),
+        ([(1, 2), (2, 0)], [], []),
+        ([(1, 3), (2, 1)], [], []),
+        ([(1, 4), (2, 2)], [], [(2, 0)]),
         ([(2, 3)], [], [(2, 1)]),
+        ([(2, 4)], [], [(2, 2)]),
     ]
     got[0][0] = swapped(sent[0], 0)
     got[0][1] = swapped(sent[1], 0)
@@ -736,7 +741,7 @@
         scratch_shapes=scratch
         + [
             VMEM(grid.shape, f32),
-            pltpu.SemaphoreType.DMA((shape.slabs,)),
+            pltpu.SemaphoreType.DMA((shape.slabs, NF)),
             SMEM((occ,), jnp.int32),
             pltpu.SemaphoreType.DMA,
         ],

time: 74.9 us -> 73.1 us (0.976)
  waiting for transfers between devices: 27 us -> 24.3 us
    ppermute x13 -> x14, starting transfers between devices: 18.1 us -> 20.8 us  [swapped(): return lax.ppermute(value, AXES, pairs)]
    ppermute x13 -> x14, waiting for transfers between devices: 19 us -> 16.5 us  [swapped(): return lax.ppermute(value, AXES, pairs)]
    ppermute x6, starting transfers between devices: 5.28 us -> 4.18 us  [ring(): lax.ppermute(value, axis, [(i, (i + step) % size) for i in range(size)])]
    ppermute x4, starting transfers between devices: 6.29 us -> 5.36 us  [beside(): return lax.ppermute(value, axis, [(i, j % size) for i, j in pairs])]
  transfers between devices with their start and end apart: 23 -> 24, of which waited for: 14 -> 12; matrix products, arithmetic and copies ran while one was open for 0% -> 0% of each run, Pallas kernels for 16% -> 16%
where the time goes in v9:
time: 73.1 us; the launch traced here: 72.9 us
  starting transfers between devices  30.3 us (41%)
  waiting for transfers between devices  24.3 us (33%)
  Pallas kernels  18 us (25%)
    ppermute x14, starting transfers between devices, swapped(): return lax.ppermute(value, AXES, pairs)  20.8 us
    ppermute x14, waiting for transfers between devices, swapped(): return lax.ppermute(value, AXES, pairs)  16.5 us
    ppermute x4, waiting for transfers between devices, beside(): return lax.ppermute(value, axis, [(i, j % size) for i, j in pairs])  5.44 us
    ppermute x4, starting transfers between devices, beside(): return lax.ppermute(value, axis, [(i, j % size) for i, j in pairs])  5.36 us
    pallas_call x7, Pallas kernels, make(): pl.pallas_call(functools.partial(pick_kernel, plan=plan, held=tuple(found...  4.68 us
    ppermute x6, starting transfers between devices, ring(): lax.ppermute(value, axis, [(i, (i + step) % size) for i in range(size)])  4.18 us
    pallas_call x2, Pallas kernels, flux_sums(): pl.pallas_call(functools.partial(sweep_z_kernel, shape=shape), out_shape=...  3.04 us
    pallas_call x1, Pallas kernels, shards(): pl.pallas_call(functools.partial(sweep_y_two_kernel, shape=shape, occ=occ...  2.8 us
  transfers between devices with their start and end apart: 24, of which 12 were waited for; matrix products, arithmetic and copies ran while one was open for 0% of the time, Pallas kernels for 16%

profile of v9, /device:TPU:0, one launch (start us, length us, event | category | flops | bytes accessed | tf_op | source)
XLA Modules:
  0.0 72.9 jit_solution(3778112858126338242)
XLA Ops:
  0.0 1.2 %pack_first.1 = f32[8,24,128]{2,1,0:T(8,128)S(1)} custom-call(s32[3,1,8]{2,1,0:T(1,128)} %send_hbm.1, f32[5120,128]{1,0:T(8,128)} %bitcast.10), custom_call_target="tpu_custom_call" | custom-call | tf_op jit(solution)/shard_map/pack_first/pallas_call | solution.py:573
  1.3 3.0 %collective-permute-start.1 = (f32[8,24,128]{2,1,0:T(8,128)S(1)}, f32[8,24,128]{2,1,0:T(8,128)S(1)}, u32[]{:S(2)}, u32[]{:S(2)}) collective-permute-start(f32[8,24,128]{2,1,0:T(8,128)S(1)} %pack_first.1), channel_id=1, source_target_pairs={{0,16},{1,17},{2,18},{3,19},{4,20},{5,21},{6,22},{7,23},{8,24},{9,... | collective-permute-start | bytes 294920 | tf_op jit(solution)/shard_map/ppermute | solution.py:554
  4.3 0.1 dynamic_slice.3.own.own_there
  4.4 1.4 %pack_rest.1 = (s32[24]{0:T(128)S(1)}, f32[8,128]{1,0:T(8,128)S(1)}, f32[8,40,128]{2,1,0:T(8,128)S(1)}, f32[8,56,128]{2,1,0:T(8,128)S(1)}, f32[8,40,128]{2,1,0:T(8,128)S(1)}) custom-call(s32[3,1,8]{2,1,0:T(1,128)S(1)} %copy-done.1, s32[3,1,8]{2,1,0:T(1,128)S(1)} %copy-done.3, s32[8]{0:T(128)S(1)} %dynamic_slice.3.own.own_there, f32[5120,128]{1,0:T(8,128)S(1)} %bitcast.11), custom_call_target="tpu_custom_call" | custom-call | tf_op jit(solution)/shard_map/pack_rest/pallas_call | solution.py:586
  5.8 0.6 collective-permute-start
  6.4 0.7 collective-permute-done.1.refs_0_.refs_2_
  7.1 0.6 pick_10.1
  7.7 2.0 %collective-permute-start.3 = (f32[8,56,128]{2,1,0:T(8,128)S(1)}, f32[8,56,128]{2,1,0:T(8,128)S(1)}, u32[]{:S(2)}, u32[]{:S(2)}) collective-permute-start(f32[8,56,128]{2,1,0:T(8,128)S(1)} %get-tuple-element.61), channel_id=1, source_target_pairs={{0,16},{1,17},{2,18},{3,19},{4,20},{5,21},{6,22},{7,23},{8,24},{9,... | collective-permute-start | bytes 688136 | tf_op jit(solution)/shard_map/ppermute | solution.py:554
  9.7 2.6 %collective-permute-start.5 = (f32[8,24,128]{2,1,0:T(8,128)S(1)}, f32[8,24,128]{2,1,0:T(8,128)S(1)}, u32[]{:S(2)}, u32[]{:S(2)}) collective-permute-start(f32[8,24,128]{2,1,0:T(8,128)S(1)} %get-tuple-element.63), channel_id=1, source_target_pairs={{0,8},{1,9},{2,10},{3,11},{4,12},{5,13},{6,14},{7,15},{8,0},{9,1},... | collective-permute-start | bytes 294920 | tf_op jit(solution)/shard_map/ppermute | solution.py:554
  12.3 0.7 collective-permute-done.refs_0_.refs_2_.refs_1_
  13.0 0.6 pick_11.1
  13.6 0.6 collective-permute-start.2
  14.2 2.6 %collective-permute-start.4 = (f32[8,32,128]{2,1,0:T(8,128)S(1)}, f32[8,32,128]{2,1,0:T(8,128)S(1)}, u32[]{:S(2)}, u32[]{:S(2)}) collective-permute-start(f32[8,32,128]{2,1,0:T(8,128)S(1)} %get-tuple-element.62), channel_id=1, source_target_pairs={{0,8},{1,9},{2,10},{3,11},{4,12},{5,13},{6,14},{7,15},{8,0},{9,1},... | collective-permute-start | bytes 393224 | tf_op jit(solution)/shard_map/ppermute | solution.py:554
  16.8 0.0 collective-permute-done.5.refs_3_
  16.8 1.1 %collective-permute-done.3.refs_1_.refs_0_.refs_2_ = f32[8,56,128]{2,1,0:T(8,128)S(1)} collective-permute-done((f32[8,56,128]{2,1,0:T(8,128)S(1)}, f32[8,56,128]{2,1,0:T(8,128)S(1)}, u32[]{:S(2)}, u32[]{:S(2)}) %collective-permute-start.3) | collective-permute-done | bytes 229408 | tf_op jit(solution)/shard_map/ppermute | solution.py:554
  17.9 0.7 pick_12_20.1
  18.6 2.7 %collective-permute-start.7 = (f32[8,40,128]{2,1,0:T(8,128)S(1)}, f32[8,40,128]{2,1,0:T(8,128)S(1)}, u32[]{:S(2)}, u32[]{:S(2)}) collective-permute-start(f32[8,40,128]{2,1,0:T(8,128)S(1)} %get-tuple-element.67), channel_id=1, source_target_pairs={{0,8},{1,9},{2,10},{3,11},{4,12},{5,13},{6,14},{7,15},{8,0},{9,1},... | collective-permute-start | bytes 491528 | tf_op jit(solution)/shard_map/ppermute | solution.py:554
  21.3 1.5 %collective-permute-start.8 = (f32[8,24,128]{2,1,0:T(8,128)S(1)}, f32[8,24,128]{2,1,0:T(8,128)S(1)}, u32[]{:S(2)}, u32[]{:S(2)}) collective-permute-start(f32[8,24,128]{2,1,0:T(8,128)S(1)} %get-tuple-element.69), channel_id=1, source_target_pairs={{0,2},{1,3},{2,0},{3,1},{4,6},{5,7},{6,4},{7,5},{8,10},{9,11},{10,... | collective-permute-start | bytes 294920 | tf_op jit(solution)/shard_map/ppermute | solution.py:554
  22.8 3.7 %collective-permute-done.4.refs_3_.refs_4_ = f32[8,32,128]{2,1,0:T(8,128)S(1)} collective-permute-done((f32[8,32,128]{2,1,0:T(8,128)S(1)}, f32[8,32,128]{2,1,0:T(8,128)S(1)}, u32[]{:S(2)}, u32[]{:S(2)}) %collective-permute-start.4) | collective-permute-done | bytes 131104 | tf_op jit(solution)/shard_map/ppermute | solution.py:554
  26.4 0.0 collective-permute-done.2.refs_1_.refs_0_
  26.4 0.7 pick_13_21.1
  27.2 1.6 %collective-permute-start.10 = (f32[8,32,128]{2,1,0:T(8,128)S(1)}, f32[8,32,128]{2,1,0:T(8,128)S(1)}, u32[]{:S(2)}, u32[]{:S(2)}) collective-permute-start(f32[8,32,128]{2,1,0:T(8,128)S(1)} %get-tuple-element.72), channel_id=1, source_target_pairs={{0,2},{1,3},{2,0},{3,1},{4,6},{5,7},{6,4},{7,5},{8,10},{9,11},{10,... | collective-permute-start | bytes 393224 | tf_op jit(solution)/shard_map/ppermute | solution.py:554
  28.7 0.0 collective-permute-start.6
  28.7 0.0 collective-permute-done.8.refs_5_
  28.7 3.0 %collective-permute-done.7.refs_3_.refs_5_ = f32[8,40,128]{2,1,0:T(8,128)S(1)} collective-permute-done((f32[8,40,128]{2,1,0:T(8,128)S(1)}, f32[8,40,128]{2,1,0:T(8,128)S(1)}, u32[]{:S(2)}, u32[]{:S(2)}) %collective-permute-start.7) | collective-permute-done | bytes 163872 | tf_op jit(solution)/shard_map/ppermute | solution.py:554
  31.7 0.7 pick_14_22.1
  32.4 1.6 %collective-permute-start.12 = (f32[8,40,128]{2,1,0:T(8,128)S(1)}, f32[8,40,128]{2,1,0:T(8,128)S(1)}, u32[]{:S(2)}, u32[]{:S(2)}) collective-permute-start(f32[8,40,128]{2,1,0:T(8,128)S(1)} %get-tuple-element.75), channel_id=1, source_target_pairs={{0,2},{1,3},{2,0},{3,1},{4,6},{5,7},{6,4},{7,5},{8,10},{9,11},{10,... | collective-permute-start | bytes 491528 | tf_op jit(solution)/shard_map/ppermute | solution.py:554
  34.0 0.0 collective-permute-start.9
  34.0 0.0 collective-permute-done.10.refs_4_
  34.0 4.8 %collective-permute-done.6.refs_2_.refs_6_.refs_1_ = f32[8,40,128]{2,1,0:T(8,128)S(1)} collective-permute-done((f32[8,40,128]{2,1,0:T(8,128)S(1)}, f32[8,40,128]{2,1,0:T(8,128)S(1)}, u32[]{:S(2)}, u32[]{:S(2)}) %collective-permute-start.6) | collective-permute-done | bytes 163872 | tf_op jit(solution)/shard_map/ppermute | solution.py:554
  38.8 0.6 pick_23.1
  39.5 0.8 %collective-permute-start.11 = (f32[8,40,128]{2,1,0:T(8,128)S(1)}, f32[8,40,128]{2,1,0:T(8,128)S(1)}, u32[]{:S(2)}, u32[]{:S(2)}) collective-permute-start(f32[8,40,128]{2,1,0:T(8,128)S(1)} %get-tuple-element.73), channel_id=1, source_target_pairs={{0,2},{1,3},{2,0},{3,1},{4,6},{5,7},{6,4},{7,5},{8,10},{9,11},{10,... | collective-permute-start | bytes 491528 | tf_op jit(solution)/shard_map/ppermute | solution.py:554
  40.2 0.0 collective-permute-done.9.refs_1_.refs_2_
  40.3 0.6 pick_24.1
  40.9 1.4 %collective-permute-start.13 = (f32[8,24,128]{2,1,0:T(8,128)S(1)}, f32[8,24,128]{2,1,0:T(8,128)S(1)}, u32[]{:S(2)}, u32[]{:S(2)}) collective-permute-start(f32[8,24,128]{2,1,0:T(8,128)S(1)} %get-tuple-element.76), channel_id=1, source_target_pairs={{0,2},{1,3},{2,0},{3,1},{4,6},{5,7},{6,4},{7,5},{8,10},{9,11},{10,... | collective-permute-start | bytes 294920 | tf_op jit(solution)/shard_map/ppermute | solution.py:554
  42.3 2.6 %collective-permute-done.11.refs_10_.refs_3_ = f32[8,40,128]{2,1,0:T(8,128)S(1)} collective-permute-done((f32[8,40,128]{2,1,0:T(8,128)S(1)}, f32[8,40,128]{2,1,0:T(8,128)S(1)}, u32[]{:S(2)}, u32[]{:S(2)}) %collective-permute-start.11) | collective-permute-done | bytes 163872 | tf_op jit(solution)/shard_map/ppermute | solution.py:554
  44.8 1.5 %assemble_0.1 = (f32[1280,128]{1,0:T(8,128)S(1)}, f32[1280,128]{1,0:T(8,128)S(1)}, f32[5,4,8,128]{3,2,1,0:T(8,128)S(1)}, f32[5,4,8,128]{3,2,1,0:T(8,128)S(1)}, f...) custom-call(s32[24]{0:T(128)S(1)} %get-tuple-element.54.tags, ...), custom_call_target="tpu_custom_call" | custom-call | tf_op jit(solution)/shard_map/assemble_0/pallas_call | solution.py:665
  46.4 0.0 collective-permute-done.13.refs_4_
  46.4 0.9 %assemble_3.1 = (f32[1280,128]{1,0:T(8,128)S(1)}, f32[1280,128]{1,0:T(8,128)S(1)}, f32[5,4,8,128]{3,2,1,0:T(8,128)S(1)}, f32[5,4,8,128]{3,2,1,0:T(8,128)S(1)}, f...) custom-call(s32[24]{0:T(128)S(1)} %get-tuple-element.54.tags, ...), custom_call_target="tpu_custom_call", output_to_operand_aliasing={{0}: (7, {}), {1}: (8, {}), {2}: (9, {}), {3}: (10, {}), {4... | custom-call | tf_op jit(solution)/shard_map/assemble_3/pallas_call | solution.py:665
  47.2 2.9 %collective-permute-start.16 = (f32[2,5,4,8,128]{4,3,2,1,0:T(8,128)S(1)}, f32[2,5,4,8,128]{4,3,2,1,0:T(8,128)S(1)}, u32[]{:S(2)}, u32[]{:S(2)}) collective-permute-start(f32[2,5,4,8,128]{4,3,2,1,0:T(8,128)S(1)} %get-tuple-element.91), channel_id=1, source_target_pairs={{0,16},{16,0},{1,17},{17,1},{2,18},{18,2},{3,19},{19,3},{4,20},{20... | collective-permute-start | bytes 491528 | tf_op jit(solution)/shard_map/ppermute | solution.py:685
  50.1 0.5 collective-permute-start.17
  50.6 3.4 %collective-permute-start.14 = (f32[5,4,8,128]{3,2,1,0:T(8,128)S(1)}, f32[5,4,8,128]{3,2,1,0:T(8,128)S(1)}, u32[]{:S(2)}, u32[]{:S(2)}) collective-permute-start(f32[5,4,8,128]{3,2,1,0:T(8,128)S(1)} %get-tuple-element.89.y_one), channel_id=1, source_target_pairs={{0,12},{4,8},{8,4},{12,0},{1,13},{5,9},{9,5},{13,1},{2,14},{6,10},... | collective-permute-start | bytes 245768 | tf_op jit(solution)/shard_map/ppermute | solution.py:690
  54.0 0.0 collective-permute-start.15
  54.0 0.0 collective-permute-done.18.z_next
  54.0 0.0 collective-permute-done.17.z_prev
  54.0 1.5 %sweep_z.2.sofar = f32[1280,128]{1,0:T(8,128)S(1)} custom-call(f32[1280,128]{1,0:T(8,128)S(1)} %get-tuple-element.88.prim, f32[5,32,128]{2,1,0:T(8,128)S(1)} %get-tuple-element.92.z_lo, f32[5,32,128]{2,1,0:T(8,128)S(1)} %get-tuple-element.93.z_hi, f32[5,32,128]{2,1,0:T(8,128)S(1)} %collective-permute-done.17.z_prev, ...), custom_call_target="tpu_custom_call" | custom-call | tf_op jit(solution)/shard_map/sweep_z/pallas_call | solution.py:701
  55.5 0.0 collective-permute-done.16.x_faces
  55.5 0.6 sweep_x.2.sofar
  56.1 1.6 %collective-permute-done.14.got_one = f32[5,4,8,128]{3,2,1,0:T(8,128)S(1)} collective-permute-done((f32[5,4,8,128]{3,2,1,0:T(8,128)S(1)}, f32[5,4,8,128]{3,2,1,0:T(8,128)S(1)}, u32[]{:S(2)}, u32[]{:S(2)}) %collective-permute-start.14) | collective-permute-done | bytes 81952 | tf_op jit(solution)/shard_map/ppermute | solution.py:690
  57.7 1.7 %collective-permute-done.15.got_two = f32[5,4,8,128]{3,2,1,0:T(8,128)S(1)} collective-permute-done((f32[5,4,8,128]{3,2,1,0:T(8,128)S(1)}, f32[5,4,8,128]{3,2,1,0:T(8,128)S(1)}, u32[]{:S(2)}, u32[]{:S(2)}) %collective-permute-start.15) | collective-permute-done | bytes 81952 | tf_op jit(solution)/shard_map/ppermute | solution.py:690
  59.5 1.3 %sweep_y_one.1 = (f32[1280,128]{1,0:T(8,128)S(1)}, f32[1280,128]{1,0:T(8,128)S(1)}, f32[2,5,4,8,128]{4,3,2,1,0:T(8,128)S(1)}, f32[5,4,8,128]{3,2,1,0:T(8,128)S(1...) custom-call(f32[1280,128]{1,0:T(8,128)S(1)} %get-tuple-element.87.field, ...), custom_call_target="tpu_custom_call" | custom-call | tf_op jit(solution)/shard_map/sweep_y_one/pallas_call | solution.py:725
  60.8 0.3 collective-permute-start.21
  61.1 0.3 collective-permute-start.23
  61.4 0.2 collective-permute-start.22
  61.6 2.0 %collective-permute-start.19 = (f32[5,4,8,128]{3,2,1,0:T(8,128)S(1)}, f32[5,4,8,128]{3,2,1,0:T(8,128)S(1)}, u32[]{:S(2)}, u32[]{:S(2)}) collective-permute-start(f32[5,4,8,128]{3,2,1,0:T(8,128)S(1)} %get-tuple-element.96.y_one), channel_id=1, source_target_pairs={{0,12},{4,8},{8,4},{12,0},{1,13},{5,9},{9,5},{13,1},{2,14},{6,10},... | collective-permute-start | bytes 245768 | tf_op jit(solution)/shard_map/ppermute | solution.py:690
  63.6 0.0 collective-permute-start.20
  63.6 0.0 collective-permute-done.23.z_next
  63.6 2.3 %collective-permute-done.22.z_prev = f32[5,32,128]{2,1,0:T(8,128)S(1)} collective-permute-done((f32[5,32,128]{2,1,0:T(8,128)S(1)}, f32[5,32,128]{2,1,0:T(8,128)S(1)}, u32[]{:S(2)}, u32[]{:S(2)}) %collective-permute-start.22) | collective-permute-done | bytes 81952 | tf_op jit(solution)/shard_map/ppermute | solution.py:685
  65.9 1.5 %sweep_z.3.sofar = f32[1280,128]{1,0:T(8,128)S(1)} custom-call(f32[1280,128]{1,0:T(8,128)S(1)} %get-tuple-element.95.prim, f32[5,32,128]{2,1,0:T(8,128)S(1)} %get-tuple-element.99.z_lo, f32[5,32,128]{2,1,0:T(8,128)S(1)} %get-tuple-element.100.z_hi, f32[5,32,128]{2,1,0:T(8,128)S(1)} %collective-permute-done.22.z_prev, ...), custom_call_target="tpu_custom_call" | custom-call | tf_op jit(solution)/shard_map/sweep_z/pallas_call | solution.py:701
  67.4 0.0 collective-permute-done.21.x_faces
  67.4 0.6 sweep_x.3.sofar
  68.0 0.6 collective-permute-done.19.got_one
  68.7 1.5 %collective-permute-done.20.got_two = f32[5,4,8,128]{3,2,1,0:T(8,128)S(1)} collective-permute-done((f32[5,4,8,128]{3,2,1,0:T(8,128)S(1)}, f32[5,4,8,128]{3,2,1,0:T(8,128)S(1)}, u32[]{:S(2)}, u32[]{:S(2)}) %collective-permute-start.20) | collective-permute-done | bytes 81952 | tf_op jit(solution)/shard_map/ppermute | solution.py:690
  70.1 2.8 %sweep_y_two.1 = (f32[20,256,128]{2,1,0:T(8,128)}, f32[20,256,128]{2,1,0:T(8,128)S(1)}) custom-call(s32[8]{0:T(128)} %copy-done.2, f32[1280,128]{1,0:T(8,128)S(1)} %get-tuple-element.87.field, f32[1280,128]{1,0:T(8,128)S(1)} %get-tuple-element.94.one, f32[1280,128]{1,0:T(8,128)S(1)} %get-tuple-element.95.prim, ...), custom_call_target="tpu_custom_call", output_to_operand_aliasing={{1}: (9, {})} | custom-call | tf_op jit(solution)/shard_map/sweep_y_two/pallas_call | solution.py:736
  (12 shorter events, 0.0 us)
Async XLA Ops:
  0.0 4.4 %copy-start.1 = (s32[3,1,8]{2,1,0:T(1,128)S(1)}, s32[3,1,8]{2,1,0:T(1,128)}, u32[]{:S(2)}) copy-start(s32[3,1,8]{2,1,0:T(1,128)} %send_hbm.1) | copy-start | bytes 292
  0.0 4.4 %copy-start = (f32[32,5,4096]{2,0,1:T(8,128)S(1)}, f32[32,5,4096]{2,0,1:T(8,128)}, u32[]{:S(2)}) copy-start(f32[32,5,4096]{2,0,1:T(8,128)} %param.4) | copy-start | bytes 7864324
  0.0 4.3 %copy-start.4 = (s32[256]{0:T(256)S(1)}, s32[256]{0:T(256)}, u32[]{:S(2)}) copy-start(s32[256]{0:T(256)} %param.7) | copy-start | bytes 3076
  0.0 4.4 %copy-start.3 = (s32[3,1,8]{2,1,0:T(1,128)S(1)}, s32[3,1,8]{2,1,0:T(1,128)}, u32[]{:S(2)}) copy-start(s32[3,1,8]{2,1,0:T(1,128)} %recv.1) | copy-start | bytes 292
  1.3 5.8 %collective-permute-start.1 = (f32[8,24,128]{2,1,0:T(8,128)S(1)}, f32[8,24,128]{2,1,0:T(8,128)S(1)}, u32[]{:S(2)}, u32[]{:S(2)}) collective-permute-start(f32[8,24,128]{2,1,0:T(8,128)S(1)} %pack_first.1), channel_id=1, source_target_pairs={{0,16},{1,17},{2,18},{3,19},{4,20},{5,21},{6,22},{7,23},{8,24},{9,... | collective-permute-start | bytes 294920 | tf_op jit(solution)/shard_map/ppermute | solution.py:554
  4.4 3.3 %copy-start.2 = (s32[8]{0:T(128)}, s32[8]{0:T(128)S(1)}, u32[]{:S(2)}) copy-start(s32[8]{0:T(128)S(1)} %dynamic_slice.3.own.own_there) | copy-start | bytes 100
  5.8 7.2 %collective-permute-start = (f32[8,40,128]{2,1,0:T(8,128)S(1)}, f32[8,40,128]{2,1,0:T(8,128)S(1)}, u32[]{:S(2)}, u32[]{:S(2)}) collective-permute-start(f32[8,40,128]{2,1,0:T(8,128)S(1)} %get-tuple-element.55), channel_id=1, source_target_pairs={{0,16},{1,17},{2,18},{3,19},{4,20},{5,21},{6,22},{7,23},{8,24},{9,... | collective-permute-start | bytes 491528 | tf_op jit(solution)/shard_map/ppermute | solution.py:554
  7.7 10.2 %collective-permute-start.3 = (f32[8,56,128]{2,1,0:T(8,128)S(1)}, f32[8,56,128]{2,1,0:T(8,128)S(1)}, u32[]{:S(2)}, u32[]{:S(2)}) collective-permute-start(f32[8,56,128]{2,1,0:T(8,128)S(1)} %get-tuple-element.61), channel_id=1, source_target_pairs={{0,16},{1,17},{2,18},{3,19},{4,20},{5,21},{6,22},{7,23},{8,24},{9,... | collective-permute-start | bytes 688136 | tf_op jit(solution)/shard_map/ppermute | solution.py:554
  9.7 7.1 %collective-permute-start.5 = (f32[8,24,128]{2,1,0:T(8,128)S(1)}, f32[8,24,128]{2,1,0:T(8,128)S(1)}, u32[]{:S(2)}, u32[]{:S(2)}) collective-permute-start(f32[8,24,128]{2,1,0:T(8,128)S(1)} %get-tuple-element.63), channel_id=1, source_target_pairs={{0,8},{1,9},{2,10},{3,11},{4,12},{5,13},{6,14},{7,15},{8,0},{9,1},... | collective-permute-start | bytes 294920 | tf_op jit(solution)/shard_map/ppermute | solution.py:554
  13.6 12.8 %collective-permute-start.2 = (f32[8,40,128]{2,1,0:T(8,128)S(1)}, f32[8,40,128]{2,1,0:T(8,128)S(1)}, u32[]{:S(2)}, u32[]{:S(2)}) collective-permute-start(f32[8,40,128]{2,1,0:T(8,128)S(1)} %get-tuple-element.60), channel_id=1, source_target_pairs={{0,16},{1,17},{2,18},{3,19},{4,20},{5,21},{6,22},{7,23},{8,24},{9,... | collective-permute-start | bytes 491528 | tf_op jit(solution)/shard_map/ppermute | solution.py:554
  14.2 12.3 %collective-permute-start.4 = (f32[8,32,128]{2,1,0:T(8,128)S(1)}, f32[8,32,128]{2,1,0:T(8,128)S(1)}, u32[]{:S(2)}, u32[]{:S(2)}) collective-permute-start(f32[8,32,128]{2,1,0:T(8,128)S(1)} %get-tuple-element.62), channel_id=1, source_target_pairs={{0,8},{1,9},{2,10},{3,11},{4,12},{5,13},{6,14},{7,15},{8,0},{9,1},... | collective-permute-start | bytes 393224 | tf_op jit(solution)/shard_map/ppermute | solution.py:554
  18.6 13.1 %collective-permute-start.7 = (f32[8,40,128]{2,1,0:T(8,128)S(1)}, f32[8,40,128]{2,1,0:T(8,128)S(1)}, u32[]{:S(2)}, u32[]{:S(2)}) collective-permute-start(f32[8,40,128]{2,1,0:T(8,128)S(1)} %get-tuple-element.67), channel_id=1, source_target_pairs={{0,8},{1,9},{2,10},{3,11},{4,12},{5,13},{6,14},{7,15},{8,0},{9,1},... | collective-permute-start | bytes 491528 | tf_op jit(solution)/shard_map/ppermute | solution.py:554
  21.3 7.5 %collective-permute-start.8 = (f32[8,24,128]{2,1,0:T(8,128)S(1)}, f32[8,24,128]{2,1,0:T(8,128)S(1)}, u32[]{:S(2)}, u32[]{:S(2)}) collective-permute-start(f32[8,24,128]{2,1,0:T(8,128)S(1)} %get-tuple-element.69), channel_id=1, source_target_pairs={{0,2},{1,3},{2,0},{3,1},{4,6},{5,7},{6,4},{7,5},{8,10},{9,11},{10,... | collective-permute-start | bytes 294920 | tf_op jit(solution)/shard_map/ppermute | solution.py:554
  27.2 6.8 %collective-permute-start.10 = (f32[8,32,128]{2,1,0:T(8,128)S(1)}, f32[8,32,128]{2,1,0:T(8,128)S(1)}, u32[]{:S(2)}, u32[]{:S(2)}) collective-permute-start(f32[8,32,128]{2,1,0:T(8,128)S(1)} %get-tuple-element.72), channel_id=1, source_target_pairs={{0,2},{1,3},{2,0},{3,1},{4,6},{5,7},{6,4},{7,5},{8,10},{9,11},{10,... | collective-permute-start | bytes 393224 | tf_op jit(solution)/shard_map/ppermute | solution.py:554
  28.7 10.1 %collective-permute-start.6 = (f32[8,40,128]{2,1,0:T(8,128)S(1)}, f32[8,40,128]{2,1,0:T(8,128)S(1)}, u32[]{:S(2)}, u32[]{:S(2)}) collective-permute-start(f32[8,40,128]{2,1,0:T(8,128)S(1)} %get-tuple-element.66), channel_id=1, source_target_pairs={{0,8},{1,9},{2,10},{3,11},{4,12},{5,13},{6,14},{7,15},{8,0},{9,1},... | collective-permute-start | bytes 491528 | tf_op jit(solution)/shard_map/ppermute | solution.py:554
  32.4 7.8 %collective-permute-start.12 = (f32[8,40,128]{2,1,0:T(8,128)S(1)}, f32[8,40,128]{2,1,0:T(8,128)S(1)}, u32[]{:S(2)}, u32[]{:S(2)}) collective-permute-start(f32[8,40,128]{2,1,0:T(8,128)S(1)} %get-tuple-element.75), channel_id=1, source_target_pairs={{0,2},{1,3},{2,0},{3,1},{4,6},{5,7},{6,4},{7,5},{8,10},{9,11},{10,... | collective-permute-start | bytes 491528 | tf_op jit(solution)/shard_map/ppermute | solution.py:554
  34.0 6.3 %collective-permute-start.9 = (f32[8,24,128]{2,1,0:T(8,128)S(1)}, f32[8,24,128]{2,1,0:T(8,128)S(1)}, u32[]{:S(2)}, u32[]{:S(2)}) collective-permute-start(f32[8,24,128]{2,1,0:T(8,128)S(1)} %get-tuple-element.70), channel_id=1, source_target_pairs={{0,8},{1,9},{2,10},{3,11},{4,12},{5,13},{6,14},{7,15},{8,0},{9,1},... | collective-permute-start | bytes 294920 | tf_op jit(solution)/shard_map/ppermute | solution.py:554
  39.5 5.4 %collective-permute-start.11 = (f32[8,40,128]{2,1,0:T(8,128)S(1)}, f32[8,40,128]{2,1,0:T(8,128)S(1)}, u32[]{:S(2)}, u32[]{:S(2)}) collective-permute-start(f32[8,40,128]{2,1,0:T(8,128)S(1)} %get-tuple-element.73), channel_id=1, source_target_pairs={{0,2},{1,3},{2,0},{3,1},{4,6},{5,7},{6,4},{7,5},{8,10},{9,11},{10,... | collective-permute-start | bytes 491528 | tf_op jit(solution)/shard_map/ppermute | solution.py:554
  40.9 5.5 %collective-permute-start.13 = (f32[8,24,128]{2,1,0:T(8,128)S(1)}, f32[8,24,128]{2,1,0:T(8,128)S(1)}, u32[]{:S(2)}, u32[]{:S(2)}) collective-permute-start(f32[8,24,128]{2,1,0:T(8,128)S(1)} %get-tuple-element.76), channel_id=1, source_target_pairs={{0,2},{1,3},{2,0},{3,1},{4,6},{5,7},{6,4},{7,5},{8,10},{9,11},{10,... | collective-permute-start | bytes 294920 | tf_op jit(solution)/shard_map/ppermute | solution.py:554
  47.2 8.3 %collective-permute-start.16 = (f32[2,5,4,8,128]{4,3,2,1,0:T(8,128)S(1)}, f32[2,5,4,8,128]{4,3,2,1,0:T(8,128)S(1)}, u32[]{:S(2)}, u32[]{:S(2)}) collective-permute-start(f32[2,5,4,8,128]{4,3,2,1,0:T(8,128)S(1)} %get-tuple-element.91), channel_id=1, source_target_pairs={{0,16},{16,0},{1,17},{17,1},{2,18},{18,2},{3,19},{19,3},{4,20},{20... | collective-permute-start | bytes 491528 | tf_op jit(solution)/shard_map/ppermute | solution.py:685
  50.1 3.9 %collective-permute-start.18 = (f32[5,32,128]{2,1,0:T(8,128)S(1)}, f32[5,32,128]{2,1,0:T(8,128)S(1)}, u32[]{:S(2)}, u32[]{:S(2)}) collective-permute-start(f32[5,32,128]{2,1,0:T(8,128)S(1)} %get-tuple-element.92.z_lo), channel_id=1, source_target_pairs={{0,3},{1,0},{2,1},{3,2},{4,7},{5,4},{6,5},{7,6},{8,11},{9,8},{10,9... | collective-permute-start | bytes 245768 | tf_op jit(solution)/shard_map/ppermute | solution.py:685
  50.1 3.9 %collective-permute-start.17 = (f32[5,32,128]{2,1,0:T(8,128)S(1)}, f32[5,32,128]{2,1,0:T(8,128)S(1)}, u32[]{:S(2)}, u32[]{:S(2)}) collective-permute-start(f32[5,32,128]{2,1,0:T(8,128)S(1)} %get-tuple-element.93.z_hi), channel_id=1, source_target_pairs={{0,1},{1,2},{2,3},{3,0},{4,5},{5,6},{6,7},{7,4},{8,9},{9,10},{10,1... | collective-permute-start | bytes 245768 | tf_op jit(solution)/shard_map/ppermute | solution.py:685
  50.6 7.1 %collective-permute-start.14 = (f32[5,4,8,128]{3,2,1,0:T(8,128)S(1)}, f32[5,4,8,128]{3,2,1,0:T(8,128)S(1)}, u32[]{:S(2)}, u32[]{:S(2)}) collective-permute-start(f32[5,4,8,128]{3,2,1,0:T(8,128)S(1)} %get-tuple-element.89.y_one), channel_id=1, source_target_pairs={{0,12},{4,8},{8,4},{12,0},{1,13},{5,9},{9,5},{13,1},{2,14},{6,10},... | collective-permute-start | bytes 245768 | tf_op jit(solution)/shard_map/ppermute | solution.py:690
  54.0 5.5 %collective-permute-start.15 = (f32[5,4,8,128]{3,2,1,0:T(8,128)S(1)}, f32[5,4,8,128]{3,2,1,0:T(8,128)S(1)}, u32[]{:S(2)}, u32[]{:S(2)}) collective-permute-start(f32[5,4,8,128]{3,2,1,0:T(8,128)S(1)} %get-tuple-element.90.y_two), channel_id=1, source_target_pairs={{0,4},{4,0},{8,12},{12,8},{1,5},{5,1},{9,13},{13,9},{2,6},{6,2},{1... | collective-permute-start | bytes 245768 | tf_op jit(solution)/shard_map/ppermute | solution.py:690
  60.8 6.7 %collective-permute-start.21 = (f32[2,5,4,8,128]{4,3,2,1,0:T(8,128)S(1)}, f32[2,5,4,8,128]{4,3,2,1,0:T(8,128)S(1)}, u32[]{:S(2)}, u32[]{:S(2)}) collective-permute-start(f32[2,5,4,8,128]{4,3,2,1,0:T(8,128)S(1)} %get-tuple-element.98), channel_id=1, source_target_pairs={{0,16},{16,0},{1,17},{17,1},{2,18},{18,2},{3,19},{19,3},{4,20},{20... | collective-permute-start | bytes 491528 | tf_op jit(solution)/shard_map/ppermute | solution.py:685
  61.1 2.5 %collective-permute-start.23 = (f32[5,32,128]{2,1,0:T(8,128)S(1)}, f32[5,32,128]{2,1,0:T(8,128)S(1)}, u32[]{:S(2)}, u32[]{:S(2)}) collective-permute-start(f32[5,32,128]{2,1,0:T(8,128)S(1)} %get-tuple-element.99.z_lo), channel_id=1, source_target_pairs={{0,3},{1,0},{2,1},{3,2},{4,7},{5,4},{6,5},{7,6},{8,11},{9,8},{10,9... | collective-permute-start | bytes 245768 | tf_op jit(solution)/shard_map/ppermute | solution.py:685
  61.4 4.6 %collective-permute-start.22 = (f32[5,32,128]{2,1,0:T(8,128)S(1)}, f32[5,32,128]{2,1,0:T(8,128)S(1)}, u32[]{:S(2)}, u32[]{:S(2)}) collective-permute-start(f32[5,32,128]{2,1,0:T(8,128)S(1)} %get-tuple-element.100.z_hi), channel_id=1, source_target_pairs={{0,1},{1,2},{2,3},{3,0},{4,5},{5,6},{6,7},{7,4},{8,9},{9,10},{10,1... | collective-permute-start | bytes 245768 | tf_op jit(solution)/shard_map/ppermute | solution.py:685
  61.6 7.1 %collective-permute-start.19 = (f32[5,4,8,128]{3,2,1,0:T(8,128)S(1)}, f32[5,4,8,128]{3,2,1,0:T(8,128)S(1)}, u32[]{:S(2)}, u32[]{:S(2)}) collective-permute-start(f32[5,4,8,128]{3,2,1,0:T(8,128)S(1)} %get-tuple-element.96.y_one), channel_id=1, source_target_pairs={{0,12},{4,8},{8,4},{12,0},{1,13},{5,9},{9,5},{13,1},{2,14},{6,10},... | collective-permute-start | bytes 245768 | tf_op jit(solution)/shard_map/ppermute | solution.py:690
  63.6 6.5 %collective-permute-start.20 = (f32[5,4,8,128]{3,2,1,0:T(8,128)S(1)}, f32[5,4,8,128]{3,2,1,0:T(8,128)S(1)}, u32[]{:S(2)}, u32[]{:S(2)}) collective-permute-start(f32[5,4,8,128]{3,2,1,0:T(8,128)S(1)} %get-tuple-element.97.y_two), channel_id=1, source_target_pairs={{0,4},{4,0},{8,12},{12,8},{1,5},{5,1},{9,13},{13,9},{2,6},{6,2},{1... | collective-permute-start | bytes 245768 | tf_op jit(solution)/shard_map/ppermute | solution.py:690

commit v10 on v9

--- a/solution.py
+++ b/solution.py
@@ -540,7 +540,7 @@
     groups = slots // SUB
     shape = Shape(rows, edge)
     units = NF * shape.slabs
-    cuts = [split_units(units, shares) for shares in ((3, 5, 7, 5), (3, 4, 5, 5, 3), (3, 4, 5, 5, 3))]
+    cuts = [split_units(units, shares) for shares in ((3, 5, 7, 5), (3, 4, 6, 4, 3), (3, 4, 6, 4, 3))]
     firsts, final = cuts[0], cuts[2]
 
     bit_z = size_z.bit_length() - 2

time: 73.1 us -> 74.2 us (1.015)
    ppermute x4, starting transfers between devices: 5.36 us -> 7.6 us  [beside(): return lax.ppermute(value, axis, [(i, j % size) for i, j in pairs])]
    ppermute x6, starting transfers between devices: 4.18 us -> 3.07 us  [ring(): lax.ppermute(value, axis, [(i, (i + step) % size) for i in range(size)])]
  transfers between devices with their start and end apart: 24 -> 24, of which waited for: 12 -> 14; matrix products, arithmetic and copies ran while one was open for 0% -> 0% of each run, Pallas kernels for 16% -> 16%
where the time goes in v10:
time: 74.2 us; the launch traced here: 74.1 us
  starting transfers between devices  31 us (42%)
  waiting for transfers between devices  24.9 us (34%)
  Pallas kernels  18 us (24%)
    ppermute x14, starting transfers between devices, swapped(): return lax.ppermute(value, AXES, pairs)  20.3 us
    ppermute x14, waiting for transfers between devices, swapped(): return lax.ppermute(value, AXES, pairs)  17.1 us
    ppermute x4, starting transfers between devices, beside(): return lax.ppermute(value, axis, [(i, j % size) for i, j in pairs])  7.6 us
    ppermute x4, waiting for transfers between devices, beside(): return lax.ppermute(value, axis, [(i, j % size) for i, j in pairs])  5.59 us
    pallas_call x7, Pallas kernels, make(): pl.pallas_call(functools.partial(pick_kernel, plan=plan, held=tuple(found...  4.68 us
    ppermute x6, starting transfers between devices, ring(): lax.ppermute(value, axis, [(i, (i + step) % size) for i in range(size)])  3.07 us
    pallas_call x2, Pallas kernels, flux_sums(): pl.pallas_call(functools.partial(sweep_z_kernel, shape=shape), out_shape=...  3.04 us
    pallas_call x1, Pallas kernels, shards(): pl.pallas_call(functools.partial(sweep_y_two_kernel, shape=shape, occ=occ...  2.8 us
  transfers between devices with their start and end apart: 24, of which 14 were waited for; matrix products, arithmetic and copies ran while one was open for 0% of the time, Pallas kernels for 16%

profile of v10, /device:TPU:0, one launch (start us, length us, event | category | flops | bytes accessed | tf_op | source)
XLA Modules:
  0.0 74.1 jit_solution(7577250275724797832)
XLA Ops:
  0.0 1.2 %pack_first.1 = f32[8,24,128]{2,1,0:T(8,128)S(1)} custom-call(s32[3,1,8]{2,1,0:T(1,128)} %send_hbm.1, f32[5120,128]{1,0:T(8,128)} %bitcast.10), custom_call_target="tpu_custom_call" | custom-call | tf_op jit(solution)/shard_map/pack_first/pallas_call | solution.py:573
  1.3 3.0 %collective-permute-start.1 = (f32[8,24,128]{2,1,0:T(8,128)S(1)}, f32[8,24,128]{2,1,0:T(8,128)S(1)}, u32[]{:S(2)}, u32[]{:S(2)}) collective-permute-start(f32[8,24,128]{2,1,0:T(8,128)S(1)} %pack_first.1), channel_id=1, source_target_pairs={{0,16},{1,17},{2,18},{3,19},{4,20},{5,21},{6,22},{7,23},{8,24},{9,... | collective-permute-start | bytes 294920 | tf_op jit(solution)/shard_map/ppermute | solution.py:554
  4.3 0.1 dynamic_slice.3.own.own_there
  4.4 1.4 %pack_rest.1 = (s32[24]{0:T(128)S(1)}, f32[8,128]{1,0:T(8,128)S(1)}, f32[8,40,128]{2,1,0:T(8,128)S(1)}, f32[8,56,128]{2,1,0:T(8,128)S(1)}, f32[8,40,128]{2,1,0:T(8,128)S(1)}) custom-call(s32[3,1,8]{2,1,0:T(1,128)S(1)} %copy-done.1, s32[3,1,8]{2,1,0:T(1,128)S(1)} %copy-done.3, s32[8]{0:T(128)S(1)} %dynamic_slice.3.own.own_there, f32[5120,128]{1,0:T(8,128)S(1)} %bitcast.11), custom_call_target="tpu_custom_call" | custom-call | tf_op jit(solution)/shard_map/pack_rest/pallas_call | solution.py:586
  5.8 0.6 collective-permute-start
  6.4 0.7 collective-permute-done.1.refs_0_.refs_2_
  7.1 0.6 pick_10.1
  7.7 2.0 %collective-permute-start.3 = (f32[8,56,128]{2,1,0:T(8,128)S(1)}, f32[8,56,128]{2,1,0:T(8,128)S(1)}, u32[]{:S(2)}, u32[]{:S(2)}) collective-permute-start(f32[8,56,128]{2,1,0:T(8,128)S(1)} %get-tuple-element.61), channel_id=1, source_target_pairs={{0,16},{1,17},{2,18},{3,19},{4,20},{5,21},{6,22},{7,23},{8,24},{9,... | collective-permute-start | bytes 688136 | tf_op jit(solution)/shard_map/ppermute | solution.py:554
  9.7 2.6 %collective-permute-start.5 = (f32[8,24,128]{2,1,0:T(8,128)S(1)}, f32[8,24,128]{2,1,0:T(8,128)S(1)}, u32[]{:S(2)}, u32[]{:S(2)}) collective-permute-start(f32[8,24,128]{2,1,0:T(8,128)S(1)} %get-tuple-element.63), channel_id=1, source_target_pairs={{0,8},{1,9},{2,10},{3,11},{4,12},{5,13},{6,14},{7,15},{8,0},{9,1},... | collective-permute-start | bytes 294920 | tf_op jit(solution)/shard_map/ppermute | solution.py:554
  12.3 0.7 collective-permute-done.refs_0_.refs_2_.refs_1_
  13.0 0.6 pick_11.1
  13.6 2.7 %collective-permute-start.4 = (f32[8,32,128]{2,1,0:T(8,128)S(1)}, f32[8,32,128]{2,1,0:T(8,128)S(1)}, u32[]{:S(2)}, u32[]{:S(2)}) collective-permute-start(f32[8,32,128]{2,1,0:T(8,128)S(1)} %get-tuple-element.62), channel_id=1, source_target_pairs={{0,8},{1,9},{2,10},{3,11},{4,12},{5,13},{6,14},{7,15},{8,0},{9,1},... | collective-permute-start | bytes 393224 | tf_op jit(solution)/shard_map/ppermute | solution.py:554
  16.3 0.5 collective-permute-start.2
  16.8 1.7 %collective-permute-done.5.refs_3_ = f32[8,24,128]{2,1,0:T(8,128)S(1)} collective-permute-done((f32[8,24,128]{2,1,0:T(8,128)S(1)}, f32[8,24,128]{2,1,0:T(8,128)S(1)}, u32[]{:S(2)}, u32[]{:S(2)}) %collective-permute-start.5) | collective-permute-done | bytes 98336 | tf_op jit(solution)/shard_map/ppermute | solution.py:554
  18.5 0.0 collective-permute-done.3.refs_1_.refs_0_.refs_2_
  18.5 0.7 pick_12_20.1
  19.2 2.1 %collective-permute-start.7 = (f32[8,48,128]{2,1,0:T(8,128)S(1)}, f32[8,48,128]{2,1,0:T(8,128)S(1)}, u32[]{:S(2)}, u32[]{:S(2)}) collective-permute-start(f32[8,48,128]{2,1,0:T(8,128)S(1)} %get-tuple-element.67), channel_id=1, source_target_pairs={{0,8},{1,9},{2,10},{3,11},{4,12},{5,13},{6,14},{7,15},{8,0},{9,1},... | collective-permute-start | bytes 589832 | tf_op jit(solution)/shard_map/ppermute | solution.py:554
  21.3 1.5 %collective-permute-start.8 = (f32[8,24,128]{2,1,0:T(8,128)S(1)}, f32[8,24,128]{2,1,0:T(8,128)S(1)}, u32[]{:S(2)}, u32[]{:S(2)}) collective-permute-start(f32[8,24,128]{2,1,0:T(8,128)S(1)} %get-tuple-element.69), channel_id=1, source_target_pairs={{0,2},{1,3},{2,0},{3,1},{4,6},{5,7},{6,4},{7,5},{8,10},{9,11},{10,... | collective-permute-start | bytes 294920 | tf_op jit(solution)/shard_map/ppermute | solution.py:554
  22.8 2.0 %collective-permute-done.4.refs_3_.refs_4_ = f32[8,32,128]{2,1,0:T(8,128)S(1)} collective-permute-done((f32[8,32,128]{2,1,0:T(8,128)S(1)}, f32[8,32,128]{2,1,0:T(8,128)S(1)}, u32[]{:S(2)}, u32[]{:S(2)}) %collective-permute-start.4) | collective-permute-done | bytes 131104 | tf_op jit(solution)/shard_map/ppermute | solution.py:554
  24.8 0.0 collective-permute-done.2.refs_1_.refs_0_
  24.8 0.7 pick_13_21.1
  25.5 0.1 collective-permute-start.6
  25.6 1.6 %collective-permute-start.10 = (f32[8,32,128]{2,1,0:T(8,128)S(1)}, f32[8,32,128]{2,1,0:T(8,128)S(1)}, u32[]{:S(2)}, u32[]{:S(2)}) collective-permute-start(f32[8,32,128]{2,1,0:T(8,128)S(1)} %get-tuple-element.72), channel_id=1, source_target_pairs={{0,2},{1,3},{2,0},{3,1},{4,6},{5,7},{6,4},{7,5},{8,10},{9,11},{10,... | collective-permute-start | bytes 393224 | tf_op jit(solution)/shard_map/ppermute | solution.py:554
  27.1 0.0 collective-permute-done.8.refs_5_
  27.1 5.1 %collective-permute-done.7.refs_3_.refs_5_ = f32[8,48,128]{2,1,0:T(8,128)S(1)} collective-permute-done((f32[8,48,128]{2,1,0:T(8,128)S(1)}, f32[8,48,128]{2,1,0:T(8,128)S(1)}, u32[]{:S(2)}, u32[]{:S(2)}) %collective-permute-start.7) | collective-permute-done | bytes 196640 | tf_op jit(solution)/shard_map/ppermute | solution.py:554
  32.2 0.7 pick_14_22.1
  33.0 1.6 %collective-permute-start.12 = (f32[8,48,128]{2,1,0:T(8,128)S(1)}, f32[8,48,128]{2,1,0:T(8,128)S(1)}, u32[]{:S(2)}, u32[]{:S(2)}) collective-permute-start(f32[8,48,128]{2,1,0:T(8,128)S(1)} %get-tuple-element.75), channel_id=1, source_target_pairs={{0,2},{1,3},{2,0},{3,1},{4,6},{5,7},{6,4},{7,5},{8,10},{9,11},{10,... | collective-permute-start | bytes 589832 | tf_op jit(solution)/shard_map/ppermute | solution.py:554
  34.5 0.0 collective-permute-start.9
  34.5 0.5 collective-permute-done.6.refs_2_.refs_6_.refs_1_
  35.1 0.0 collective-permute-done.10.refs_4_
  35.1 0.6 pick_23.1
  35.7 1.6 %collective-permute-start.11 = (f32[8,32,128]{2,1,0:T(8,128)S(1)}, f32[8,32,128]{2,1,0:T(8,128)S(1)}, u32[]{:S(2)}, u32[]{:S(2)}) collective-permute-start(f32[8,32,128]{2,1,0:T(8,128)S(1)} %get-tuple-element.73), channel_id=1, source_target_pairs={{0,2},{1,3},{2,0},{3,1},{4,6},{5,7},{6,4},{7,5},{8,10},{9,11},{10,... | collective-permute-start | bytes 393224 | tf_op jit(solution)/shard_map/ppermute | solution.py:554
  37.3 3.8 %collective-permute-done.9.refs_1_.refs_2_ = f32[8,24,128]{2,1,0:T(8,128)S(1)} collective-permute-done((f32[8,24,128]{2,1,0:T(8,128)S(1)}, f32[8,24,128]{2,1,0:T(8,128)S(1)}, u32[]{:S(2)}, u32[]{:S(2)}) %collective-permute-start.9) | collective-permute-done | bytes 98336 | tf_op jit(solution)/shard_map/ppermute | solution.py:554
  41.1 0.0 collective-permute-done.12.refs_3_
  41.1 0.6 pick_24.1
  41.8 0.6 collective-permute-start.13
  42.4 0.2 collective-permute-done.11.refs_10_.refs_3_
  42.6 1.5 %assemble_0.1 = (f32[1280,128]{1,0:T(8,128)S(1)}, f32[1280,128]{1,0:T(8,128)S(1)}, f32[5,4,8,128]{3,2,1,0:T(8,128)S(1)}, f32[5,4,8,128]{3,2,1,0:T(8,128)S(1)}, f...) custom-call(s32[24]{0:T(128)S(1)} %get-tuple-element.54.tags, ...), custom_call_target="tpu_custom_call" | custom-call | tf_op jit(solution)/shard_map/assemble_0/pallas_call | solution.py:665
  44.1 2.3 %collective-permute-done.13.refs_4_ = f32[8,24,128]{2,1,0:T(8,128)S(1)} collective-permute-done((f32[8,24,128]{2,1,0:T(8,128)S(1)}, f32[8,24,128]{2,1,0:T(8,128)S(1)}, u32[]{:S(2)}, u32[]{:S(2)}) %collective-permute-start.13) | collective-permute-done | bytes 98336 | tf_op jit(solution)/shard_map/ppermute | solution.py:554
  46.4 0.9 %assemble_3.1 = (f32[1280,128]{1,0:T(8,128)S(1)}, f32[1280,128]{1,0:T(8,128)S(1)}, f32[5,4,8,128]{3,2,1,0:T(8,128)S(1)}, f32[5,4,8,128]{3,2,1,0:T(8,128)S(1)}, f...) custom-call(s32[24]{0:T(128)S(1)} %get-tuple-element.54.tags, ...), custom_call_target="tpu_custom_call", output_to_operand_aliasing={{0}: (7, {}), {1}: (8, {}), {2}: (9, {}), {3}: (10, {}), {4... | custom-call | tf_op jit(solution)/shard_map/assemble_3/pallas_call | solution.py:665
  47.3 0.1 collective-permute-start.16
  47.4 0.0 collective-permute-start.18
  47.4 0.5 collective-permute-start.17
  47.9 5.7 %collective-permute-start.14 = (f32[5,4,8,128]{3,2,1,0:T(8,128)S(1)}, f32[5,4,8,128]{3,2,1,0:T(8,128)S(1)}, u32[]{:S(2)}, u32[]{:S(2)}) collective-permute-start(f32[5,4,8,128]{3,2,1,0:T(8,128)S(1)} %get-tuple-element.89.y_one), channel_id=1, source_target_pairs={{0,12},{4,8},{8,4},{12,0},{1,13},{5,9},{9,5},{13,1},{2,14},{6,10},... | collective-permute-start | bytes 245768 | tf_op jit(solution)/shard_map/ppermute | solution.py:690
  53.6 0.0 collective-permute-start.15
  53.6 0.0 collective-permute-done.18.z_next
  53.6 1.5 %sweep_z.2.sofar = f32[1280,128]{1,0:T(8,128)S(1)} custom-call(f32[1280,128]{1,0:T(8,128)S(1)} %get-tuple-element.88.prim, f32[5,32,128]{2,1,0:T(8,128)S(1)} %get-tuple-element.92.z_lo, f32[5,32,128]{2,1,0:T(8,128)S(1)} %get-tuple-element.93.z_hi, f32[5,32,128]{2,1,0:T(8,128)S(1)} %collective-permute-done.17.z_prev, ...), custom_call_target="tpu_custom_call" | custom-call | tf_op jit(solution)/shard_map/sweep_z/pallas_call | solution.py:701
  55.2 0.0 collective-permute-done.16.x_faces
  55.2 0.6 sweep_x.2.sofar
  55.8 1.0 %collective-permute-done.14.got_one = f32[5,4,8,128]{3,2,1,0:T(8,128)S(1)} collective-permute-done((f32[5,4,8,128]{3,2,1,0:T(8,128)S(1)}, f32[5,4,8,128]{3,2,1,0:T(8,128)S(1)}, u32[]{:S(2)}, u32[]{:S(2)}) %collective-permute-start.14) | collective-permute-done | bytes 81952 | tf_op jit(solution)/shard_map/ppermute | solution.py:690
  56.8 2.0 %collective-permute-done.15.got_two = f32[5,4,8,128]{3,2,1,0:T(8,128)S(1)} collective-permute-done((f32[5,4,8,128]{3,2,1,0:T(8,128)S(1)}, f32[5,4,8,128]{3,2,1,0:T(8,128)S(1)}, u32[]{:S(2)}, u32[]{:S(2)}) %collective-permute-start.15) | collective-permute-done | bytes 81952 | tf_op jit(solution)/shard_map/ppermute | solution.py:690
  58.8 1.3 %sweep_y_one.1 = (f32[1280,128]{1,0:T(8,128)S(1)}, f32[1280,128]{1,0:T(8,128)S(1)}, f32[2,5,4,8,128]{4,3,2,1,0:T(8,128)S(1)}, f32[5,4,8,128]{3,2,1,0:T(8,128)S(1...) custom-call(f32[1280,128]{1,0:T(8,128)S(1)} %get-tuple-element.87.field, ...), custom_call_target="tpu_custom_call" | custom-call | tf_op jit(solution)/shard_map/sweep_y_one/pallas_call | solution.py:725
  60.0 1.9 %collective-permute-start.21 = (f32[2,5,4,8,128]{4,3,2,1,0:T(8,128)S(1)}, f32[2,5,4,8,128]{4,3,2,1,0:T(8,128)S(1)}, u32[]{:S(2)}, u32[]{:S(2)}) collective-permute-start(f32[2,5,4,8,128]{4,3,2,1,0:T(8,128)S(1)} %get-tuple-element.98), channel_id=1, source_target_pairs={{0,16},{16,0},{1,17},{17,1},{2,18},{18,2},{3,19},{19,3},{4,20},{20... | collective-permute-start | bytes 491528 | tf_op jit(solution)/shard_map/ppermute | solution.py:685
  62.0 0.0 collective-permute-start.23
  62.0 0.5 collective-permute-start.22
  62.5 1.9 %collective-permute-start.19 = (f32[5,4,8,128]{3,2,1,0:T(8,128)S(1)}, f32[5,4,8,128]{3,2,1,0:T(8,128)S(1)}, u32[]{:S(2)}, u32[]{:S(2)}) collective-permute-start(f32[5,4,8,128]{3,2,1,0:T(8,128)S(1)} %get-tuple-element.96.y_one), channel_id=1, source_target_pairs={{0,12},{4,8},{8,4},{12,0},{1,13},{5,9},{9,5},{13,1},{2,14},{6,10},... | collective-permute-start | bytes 245768 | tf_op jit(solution)/shard_map/ppermute | solution.py:690
  64.4 0.0 collective-permute-start.20
  64.4 0.0 collective-permute-done.23.z_next
  64.4 2.2 %collective-permute-done.22.z_prev = f32[5,32,128]{2,1,0:T(8,128)S(1)} collective-permute-done((f32[5,32,128]{2,1,0:T(8,128)S(1)}, f32[5,32,128]{2,1,0:T(8,128)S(1)}, u32[]{:S(2)}, u32[]{:S(2)}) %collective-permute-start.22) | collective-permute-done | bytes 81952 | tf_op jit(solution)/shard_map/ppermute | solution.py:685
  66.6 1.5 %sweep_z.3.sofar = f32[1280,128]{1,0:T(8,128)S(1)} custom-call(f32[1280,128]{1,0:T(8,128)S(1)} %get-tuple-element.95.prim, f32[5,32,128]{2,1,0:T(8,128)S(1)} %get-tuple-element.99.z_lo, f32[5,32,128]{2,1,0:T(8,128)S(1)} %get-tuple-element.100.z_hi, f32[5,32,128]{2,1,0:T(8,128)S(1)} %collective-permute-done.22.z_prev, ...), custom_call_target="tpu_custom_call" | custom-call | tf_op jit(solution)/shard_map/sweep_z/pallas_call | solution.py:701
  68.1 0.6 sweep_x.3.sofar
  68.7 1.0 %collective-permute-done.19.got_one = f32[5,4,8,128]{3,2,1,0:T(8,128)S(1)} collective-permute-done((f32[5,4,8,128]{3,2,1,0:T(8,128)S(1)}, f32[5,4,8,128]{3,2,1,0:T(8,128)S(1)}, u32[]{:S(2)}, u32[]{:S(2)}) %collective-permute-start.19) | collective-permute-done | bytes 81952 | tf_op jit(solution)/shard_map/ppermute | solution.py:690
  69.7 1.6 %collective-permute-done.20.got_two = f32[5,4,8,128]{3,2,1,0:T(8,128)S(1)} collective-permute-done((f32[5,4,8,128]{3,2,1,0:T(8,128)S(1)}, f32[5,4,8,128]{3,2,1,0:T(8,128)S(1)}, u32[]{:S(2)}, u32[]{:S(2)}) %collective-permute-start.20) | collective-permute-done | bytes 81952 | tf_op jit(solution)/shard_map/ppermute | solution.py:690
  71.3 2.8 %sweep_y_two.1 = (f32[20,256,128]{2,1,0:T(8,128)}, f32[20,256,128]{2,1,0:T(8,128)S(1)}) custom-call(s32[8]{0:T(128)} %copy-done.2, f32[1280,128]{1,0:T(8,128)S(1)} %get-tuple-element.87.field, f32[1280,128]{1,0:T(8,128)S(1)} %get-tuple-element.94.one, f32[1280,128]{1,0:T(8,128)S(1)} %get-tuple-element.95.prim, ...), custom_call_target="tpu_custom_call", output_to_operand_aliasing={{1}: (9, {})} | custom-call | tf_op jit(solution)/shard_map/sweep_y_two/pallas_call | solution.py:736
  (12 shorter events, 0.0 us)
Async XLA Ops:
  0.0 4.4 %copy-start.1 = (s32[3,1,8]{2,1,0:T(1,128)S(1)}, s32[3,1,8]{2,1,0:T(1,128)}, u32[]{:S(2)}) copy-start(s32[3,1,8]{2,1,0:T(1,128)} %send_hbm.1) | copy-start | bytes 292
  0.0 4.4 %copy-start = (f32[32,5,4096]{2,0,1:T(8,128)S(1)}, f32[32,5,4096]{2,0,1:T(8,128)}, u32[]{:S(2)}) copy-start(f32[32,5,4096]{2,0,1:T(8,128)} %param.4) | copy-start | bytes 7864324
  0.0 4.3 %copy-start.4 = (s32[256]{0:T(256)S(1)}, s32[256]{0:T(256)}, u32[]{:S(2)}) copy-start(s32[256]{0:T(256)} %param.7) | copy-start | bytes 3076
  0.0 4.4 %copy-start.3 = (s32[3,1,8]{2,1,0:T(1,128)S(1)}, s32[3,1,8]{2,1,0:T(1,128)}, u32[]{:S(2)}) copy-start(s32[3,1,8]{2,1,0:T(1,128)} %recv.1) | copy-start | bytes 292
  1.3 5.8 %collective-permute-start.1 = (f32[8,24,128]{2,1,0:T(8,128)S(1)}, f32[8,24,128]{2,1,0:T(8,128)S(1)}, u32[]{:S(2)}, u32[]{:S(2)}) collective-permute-start(f32[8,24,128]{2,1,0:T(8,128)S(1)} %pack_first.1), channel_id=1, source_target_pairs={{0,16},{1,17},{2,18},{3,19},{4,20},{5,21},{6,22},{7,23},{8,24},{9,... | collective-permute-start | bytes 294920 | tf_op jit(solution)/shard_map/ppermute | solution.py:554
  4.4 3.3 %copy-start.2 = (s32[8]{0:T(128)}, s32[8]{0:T(128)S(1)}, u32[]{:S(2)}) copy-start(s32[8]{0:T(128)S(1)} %dynamic_slice.3.own.own_there) | copy-start | bytes 100
  5.8 7.2 %collective-permute-start = (f32[8,40,128]{2,1,0:T(8,128)S(1)}, f32[8,40,128]{2,1,0:T(8,128)S(1)}, u32[]{:S(2)}, u32[]{:S(2)}) collective-permute-start(f32[8,40,128]{2,1,0:T(8,128)S(1)} %get-tuple-element.55), channel_id=1, source_target_pairs={{0,16},{1,17},{2,18},{3,19},{4,20},{5,21},{6,22},{7,23},{8,24},{9,... | collective-permute-start | bytes 491528 | tf_op jit(solution)/shard_map/ppermute | solution.py:554
  7.7 10.7 %collective-permute-start.3 = (f32[8,56,128]{2,1,0:T(8,128)S(1)}, f32[8,56,128]{2,1,0:T(8,128)S(1)}, u32[]{:S(2)}, u32[]{:S(2)}) collective-permute-start(f32[8,56,128]{2,1,0:T(8,128)S(1)} %get-tuple-element.61), channel_id=1, source_target_pairs={{0,16},{1,17},{2,18},{3,19},{4,20},{5,21},{6,22},{7,23},{8,24},{9,... | collective-permute-start | bytes 688136 | tf_op jit(solution)/shard_map/ppermute | solution.py:554
  9.7 8.8 %collective-permute-start.5 = (f32[8,24,128]{2,1,0:T(8,128)S(1)}, f32[8,24,128]{2,1,0:T(8,128)S(1)}, u32[]{:S(2)}, u32[]{:S(2)}) collective-permute-start(f32[8,24,128]{2,1,0:T(8,128)S(1)} %get-tuple-element.63), channel_id=1, source_target_pairs={{0,8},{1,9},{2,10},{3,11},{4,12},{5,13},{6,14},{7,15},{8,0},{9,1},... | collective-permute-start | bytes 294920 | tf_op jit(solution)/shard_map/ppermute | solution.py:554
  13.6 11.2 %collective-permute-start.4 = (f32[8,32,128]{2,1,0:T(8,128)S(1)}, f32[8,32,128]{2,1,0:T(8,128)S(1)}, u32[]{:S(2)}, u32[]{:S(2)}) collective-permute-start(f32[8,32,128]{2,1,0:T(8,128)S(1)} %get-tuple-element.62), channel_id=1, source_target_pairs={{0,8},{1,9},{2,10},{3,11},{4,12},{5,13},{6,14},{7,15},{8,0},{9,1},... | collective-permute-start | bytes 393224 | tf_op jit(solution)/shard_map/ppermute | solution.py:554
  16.3 8.5 %collective-permute-start.2 = (f32[8,40,128]{2,1,0:T(8,128)S(1)}, f32[8,40,128]{2,1,0:T(8,128)S(1)}, u32[]{:S(2)}, u32[]{:S(2)}) collective-permute-start(f32[8,40,128]{2,1,0:T(8,128)S(1)} %get-tuple-element.60), channel_id=1, source_target_pairs={{0,16},{1,17},{2,18},{3,19},{4,20},{5,21},{6,22},{7,23},{8,24},{9,... | collective-permute-start | bytes 491528 | tf_op jit(solution)/shard_map/ppermute | solution.py:554
  19.2 13.1 %collective-permute-start.7 = (f32[8,48,128]{2,1,0:T(8,128)S(1)}, f32[8,48,128]{2,1,0:T(8,128)S(1)}, u32[]{:S(2)}, u32[]{:S(2)}) collective-permute-start(f32[8,48,128]{2,1,0:T(8,128)S(1)} %get-tuple-element.67), channel_id=1, source_target_pairs={{0,8},{1,9},{2,10},{3,11},{4,12},{5,13},{6,14},{7,15},{8,0},{9,1},... | collective-permute-start | bytes 589832 | tf_op jit(solution)/shard_map/ppermute | solution.py:554
  21.3 5.9 %collective-permute-start.8 = (f32[8,24,128]{2,1,0:T(8,128)S(1)}, f32[8,24,128]{2,1,0:T(8,128)S(1)}, u32[]{:S(2)}, u32[]{:S(2)}) collective-permute-start(f32[8,24,128]{2,1,0:T(8,128)S(1)} %get-tuple-element.69), channel_id=1, source_target_pairs={{0,2},{1,3},{2,0},{3,1},{4,6},{5,7},{6,4},{7,5},{8,10},{9,11},{10,... | collective-permute-start | bytes 294920 | tf_op jit(solution)/shard_map/ppermute | solution.py:554
  25.5 9.6 %collective-permute-start.6 = (f32[8,32,128]{2,1,0:T(8,128)S(1)}, f32[8,32,128]{2,1,0:T(8,128)S(1)}, u32[]{:S(2)}, u32[]{:S(2)}) collective-permute-start(f32[8,32,128]{2,1,0:T(8,128)S(1)} %get-tuple-element.66), channel_id=1, source_target_pairs={{0,8},{1,9},{2,10},{3,11},{4,12},{5,13},{6,14},{7,15},{8,0},{9,1},... | collective-permute-start | bytes 393224 | tf_op jit(solution)/shard_map/ppermute | solution.py:554
  25.6 9.5 %collective-permute-start.10 = (f32[8,32,128]{2,1,0:T(8,128)S(1)}, f32[8,32,128]{2,1,0:T(8,128)S(1)}, u32[]{:S(2)}, u32[]{:S(2)}) collective-permute-start(f32[8,32,128]{2,1,0:T(8,128)S(1)} %get-tuple-element.72), channel_id=1, source_target_pairs={{0,2},{1,3},{2,0},{3,1},{4,6},{5,7},{6,4},{7,5},{8,10},{9,11},{10,... | collective-permute-start | bytes 393224 | tf_op jit(solution)/shard_map/ppermute | solution.py:554
  33.0 8.1 %collective-permute-start.12 = (f32[8,48,128]{2,1,0:T(8,128)S(1)}, f32[8,48,128]{2,1,0:T(8,128)S(1)}, u32[]{:S(2)}, u32[]{:S(2)}) collective-permute-start(f32[8,48,128]{2,1,0:T(8,128)S(1)} %get-tuple-element.75), channel_id=1, source_target_pairs={{0,2},{1,3},{2,0},{3,1},{4,6},{5,7},{6,4},{7,5},{8,10},{9,11},{10,... | collective-permute-start | bytes 589832 | tf_op jit(solution)/shard_map/ppermute | solution.py:554
  34.5 6.6 %collective-permute-start.9 = (f32[8,24,128]{2,1,0:T(8,128)S(1)}, f32[8,24,128]{2,1,0:T(8,128)S(1)}, u32[]{:S(2)}, u32[]{:S(2)}) collective-permute-start(f32[8,24,128]{2,1,0:T(8,128)S(1)} %get-tuple-element.70), channel_id=1, source_target_pairs={{0,8},{1,9},{2,10},{3,11},{4,12},{5,13},{6,14},{7,15},{8,0},{9,1},... | collective-permute-start | bytes 294920 | tf_op jit(solution)/shard_map/ppermute | solution.py:554
  35.7 6.9 %collective-permute-start.11 = (f32[8,32,128]{2,1,0:T(8,128)S(1)}, f32[8,32,128]{2,1,0:T(8,128)S(1)}, u32[]{:S(2)}, u32[]{:S(2)}) collective-permute-start(f32[8,32,128]{2,1,0:T(8,128)S(1)} %get-tuple-element.73), channel_id=1, source_target_pairs={{0,2},{1,3},{2,0},{3,1},{4,6},{5,7},{6,4},{7,5},{8,10},{9,11},{10,... | collective-permute-start | bytes 393224 | tf_op jit(solution)/shard_map/ppermute | solution.py:554
  41.8 4.7 %collective-permute-start.13 = (f32[8,24,128]{2,1,0:T(8,128)S(1)}, f32[8,24,128]{2,1,0:T(8,128)S(1)}, u32[]{:S(2)}, u32[]{:S(2)}) collective-permute-start(f32[8,24,128]{2,1,0:T(8,128)S(1)} %get-tuple-element.76), channel_id=1, source_target_pairs={{0,2},{1,3},{2,0},{3,1},{4,6},{5,7},{6,4},{7,5},{8,10},{9,11},{10,... | collective-permute-start | bytes 294920 | tf_op jit(solution)/shard_map/ppermute | solution.py:554
  47.3 7.9 %collective-permute-start.16 = (f32[2,5,4,8,128]{4,3,2,1,0:T(8,128)S(1)}, f32[2,5,4,8,128]{4,3,2,1,0:T(8,128)S(1)}, u32[]{:S(2)}, u32[]{:S(2)}) collective-permute-start(f32[2,5,4,8,128]{4,3,2,1,0:T(8,128)S(1)} %get-tuple-element.91), channel_id=1, source_target_pairs={{0,16},{16,0},{1,17},{17,1},{2,18},{18,2},{3,19},{19,3},{4,20},{20... | collective-permute-start | bytes 491528 | tf_op jit(solution)/shard_map/ppermute | solution.py:685
  47.4 6.2 %collective-permute-start.18 = (f32[5,32,128]{2,1,0:T(8,128)S(1)}, f32[5,32,128]{2,1,0:T(8,128)S(1)}, u32[]{:S(2)}, u32[]{:S(2)}) collective-permute-start(f32[5,32,128]{2,1,0:T(8,128)S(1)} %get-tuple-element.92.z_lo), channel_id=1, source_target_pairs={{0,3},{1,0},{2,1},{3,2},{4,7},{5,4},{6,5},{7,6},{8,11},{9,8},{10,9... | collective-permute-start | bytes 245768 | tf_op jit(solution)/shard_map/ppermute | solution.py:685
  47.4 6.2 %collective-permute-start.17 = (f32[5,32,128]{2,1,0:T(8,128)S(1)}, f32[5,32,128]{2,1,0:T(8,128)S(1)}, u32[]{:S(2)}, u32[]{:S(2)}) collective-permute-start(f32[5,32,128]{2,1,0:T(8,128)S(1)} %get-tuple-element.93.z_hi), channel_id=1, source_target_pairs={{0,1},{1,2},{2,3},{3,0},{4,5},{5,6},{6,7},{7,4},{8,9},{9,10},{10,1... | collective-permute-start | bytes 245768 | tf_op jit(solution)/shard_map/ppermute | solution.py:685
  47.9 8.9 %collective-permute-start.14 = (f32[5,4,8,128]{3,2,1,0:T(8,128)S(1)}, f32[5,4,8,128]{3,2,1,0:T(8,128)S(1)}, u32[]{:S(2)}, u32[]{:S(2)}) collective-permute-start(f32[5,4,8,128]{3,2,1,0:T(8,128)S(1)} %get-tuple-element.89.y_one), channel_id=1, source_target_pairs={{0,12},{4,8},{8,4},{12,0},{1,13},{5,9},{9,5},{13,1},{2,14},{6,10},... | collective-permute-start | bytes 245768 | tf_op jit(solution)/shard_map/ppermute | solution.py:690
  53.6 5.2 %collective-permute-start.15 = (f32[5,4,8,128]{3,2,1,0:T(8,128)S(1)}, f32[5,4,8,128]{3,2,1,0:T(8,128)S(1)}, u32[]{:S(2)}, u32[]{:S(2)}) collective-permute-start(f32[5,4,8,128]{3,2,1,0:T(8,128)S(1)} %get-tuple-element.90.y_two), channel_id=1, source_target_pairs={{0,4},{4,0},{8,12},{12,8},{1,5},{5,1},{9,13},{13,9},{2,6},{6,2},{1... | collective-permute-start | bytes 245768 | tf_op jit(solution)/shard_map/ppermute | solution.py:690
  60.0 8.1 %collective-permute-start.21 = (f32[2,5,4,8,128]{4,3,2,1,0:T(8,128)S(1)}, f32[2,5,4,8,128]{4,3,2,1,0:T(8,128)S(1)}, u32[]{:S(2)}, u32[]{:S(2)}) collective-permute-start(f32[2,5,4,8,128]{4,3,2,1,0:T(8,128)S(1)} %get-tuple-element.98), channel_id=1, source_target_pairs={{0,16},{16,0},{1,17},{17,1},{2,18},{18,2},{3,19},{19,3},{4,20},{20... | collective-permute-start | bytes 491528 | tf_op jit(solution)/shard_map/ppermute | solution.py:685
  62.0 2.4 %collective-permute-start.23 = (f32[5,32,128]{2,1,0:T(8,128)S(1)}, f32[5,32,128]{2,1,0:T(8,128)S(1)}, u32[]{:S(2)}, u32[]{:S(2)}) collective-permute-start(f32[5,32,128]{2,1,0:T(8,128)S(1)} %get-tuple-element.99.z_lo), channel_id=1, source_target_pairs={{0,3},{1,0},{2,1},{3,2},{4,7},{5,4},{6,5},{7,6},{8,11},{9,8},{10,9... | collective-permute-start | bytes 245768 | tf_op jit(solution)/shard_map/ppermute | solution.py:685
  62.0 4.6 %collective-permute-start.22 = (f32[5,32,128]{2,1,0:T(8,128)S(1)}, f32[5,32,128]{2,1,0:T(8,128)S(1)}, u32[]{:S(2)}, u32[]{:S(2)}) collective-permute-start(f32[5,32,128]{2,1,0:T(8,128)S(1)} %get-tuple-element.100.z_hi), channel_id=1, source_target_pairs={{0,1},{1,2},{2,3},{3,0},{4,5},{5,6},{6,7},{7,4},{8,9},{9,10},{10,1... | collective-permute-start | bytes 245768 | tf_op jit(solution)/shard_map/ppermute | solution.py:685
  62.5 7.2 %collective-permute-start.19 = (f32[5,4,8,128]{3,2,1,0:T(8,128)S(1)}, f32[5,4,8,128]{3,2,1,0:T(8,128)S(1)}, u32[]{:S(2)}, u32[]{:S(2)}) collective-permute-start(f32[5,4,8,128]{3,2,1,0:T(8,128)S(1)} %get-tuple-element.96.y_one), channel_id=1, source_target_pairs={{0,12},{4,8},{8,4},{12,0},{1,13},{5,9},{9,5},{13,1},{2,14},{6,10},... | collective-permute-start | bytes 245768 | tf_op jit(solution)/shard_map/ppermute | solution.py:690
  64.4 6.9 %collective-permute-start.20 = (f32[5,4,8,128]{3,2,1,0:T(8,128)S(1)}, f32[5,4,8,128]{3,2,1,0:T(8,128)S(1)}, u32[]{:S(2)}, u32[]{:S(2)}) collective-permute-start(f32[5,4,8,128]{3,2,1,0:T(8,128)S(1)} %get-tuple-element.97.y_two), channel_id=1, source_target_pairs={{0,4},{4,0},{8,12},{12,8},{1,5},{5,1},{9,13},{13,9},{2,6},{6,2},{1... | collective-permute-start | bytes 245768 | tf_op jit(solution)/shard_map/ppermute | solution.py:690

commit v11 on v10

--- a/solution.py
+++ b/solution.py
@@ -540,7 +540,7 @@
     groups = slots // SUB
     shape = Shape(rows, edge)
     units = NF * shape.slabs
-    cuts = [split_units(units, shares) for shares in ((3, 5, 7, 5), (3, 4, 6, 4, 3), (3, 4, 6, 4, 3))]
+    cuts = [split_units(units, shares) for shares in ((3, 5, 7, 5), (2, 4, 5, 5, 4), (2, 4, 5, 5, 4))]
     firsts, final = cuts[0], cuts[2]
 
     bit_z = size_z.bit_length() - 2

time: 74.2 us -> 75.4 us (1.016)
  waiting for transfers between devices: 24.9 us -> 25.7 us
    ppermute x6, starting transfers between devices: 3.07 us -> 6.11 us  [ring(): lax.ppermute(value, axis, [(i, (i + step) % size) for i in range(size)])]
    ppermute x4, starting transfers between devices: 7.6 us -> 4.83 us  [beside(): return lax.ppermute(value, axis, [(i, j % size) for i, j in pairs])]
    ppermute x14, waiting for transfers between devices: 17.1 us -> 17.9 us  [swapped(): return lax.ppermute(value, AXES, pairs)]
where the time goes in v11:
time: 75.4 us; the launch traced here: 75.3 us
  starting transfers between devices  31.3 us (42%)
  waiting for transfers between devices  25.7 us (34%)
  Pallas kernels  18 us (24%)
    ppermute x14, starting transfers between devices, swapped(): return lax.ppermute(value, AXES, pairs)  20.4 us
    ppermute x14, waiting for transfers between devices, swapped(): return lax.ppermute(value, AXES, pairs)  17.9 us
    ppermute x6, starting transfers between devices, ring(): lax.ppermute(value, axis, [(i, (i + step) % size) for i in range(size)])  6.11 us
    ppermute x4, waiting for transfers between devices, beside(): return lax.ppermute(value, axis, [(i, j % size) for i, j in pairs])  5.24 us
    ppermute x4, starting transfers between devices, beside(): return lax.ppermute(value, axis, [(i, j % size) for i, j in pairs])  4.83 us
    pallas_call x7, Pallas kernels, make(): pl.pallas_call(functools.partial(pick_kernel, plan=plan, held=tuple(found...  4.69 us
    pallas_call x2, Pallas kernels, flux_sums(): pl.pallas_call(functools.partial(sweep_z_kernel, shape=shape), out_shape=...  3.04 us
    pallas_call x1, Pallas kernels, shards(): pl.pallas_call(functools.partial(sweep_y_two_kernel, shape=shape, occ=occ...  2.8 us
  transfers between devices with their start and end apart: 24, of which 14 were waited for; matrix products, arithmetic and copies ran while one was open for 0% of the time, Pallas kernels for 16%

profile of v11, /device:TPU:0, one launch (start us, length us, event | category | flops | bytes accessed | tf_op | source)
XLA Modules:
  0.0 75.3 jit_solution(12056093494872025561)
XLA Ops:
  0.0 1.2 %pack_first.1 = f32[8,24,128]{2,1,0:T(8,128)S(1)} custom-call(s32[3,1,8]{2,1,0:T(1,128)} %send_hbm.1, f32[5120,128]{1,0:T(8,128)} %bitcast.10), custom_call_target="tpu_custom_call" | custom-call | tf_op jit(solution)/shard_map/pack_first/pallas_call | solution.py:573
  1.3 3.0 %collective-permute-start = (f32[8,24,128]{2,1,0:T(8,128)S(1)}, f32[8,24,128]{2,1,0:T(8,128)S(1)}, u32[]{:S(2)}, u32[]{:S(2)}) collective-permute-start(f32[8,24,128]{2,1,0:T(8,128)S(1)} %pack_first.1), channel_id=1, source_target_pairs={{0,16},{1,17},{2,18},{3,19},{4,20},{5,21},{6,22},{7,23},{8,24},{9,... | collective-permute-start | bytes 294920 | tf_op jit(solution)/shard_map/ppermute | solution.py:554
  4.3 0.1 dynamic_slice.3.own.own_there
  4.4 1.4 %pack_rest.1 = (s32[24]{0:T(128)S(1)}, f32[8,128]{1,0:T(8,128)S(1)}, f32[8,40,128]{2,1,0:T(8,128)S(1)}, f32[8,56,128]{2,1,0:T(8,128)S(1)}, f32[8,40,128]{2,1,0:T(8,128)S(1)}) custom-call(s32[3,1,8]{2,1,0:T(1,128)S(1)} %copy-done.1, s32[3,1,8]{2,1,0:T(1,128)S(1)} %copy-done.3, s32[8]{0:T(128)S(1)} %dynamic_slice.3.own.own_there, f32[5120,128]{1,0:T(8,128)S(1)} %bitcast.11), custom_call_target="tpu_custom_call" | custom-call | tf_op jit(solution)/shard_map/pack_rest/pallas_call | solution.py:586
  5.8 0.6 collective-permute-start.1
  6.4 0.7 collective-permute-done.refs_0_.refs_2_
  7.1 0.6 pick_10.1
  7.7 2.0 %collective-permute-start.3 = (f32[8,56,128]{2,1,0:T(8,128)S(1)}, f32[8,56,128]{2,1,0:T(8,128)S(1)}, u32[]{:S(2)}, u32[]{:S(2)}) collective-permute-start(f32[8,56,128]{2,1,0:T(8,128)S(1)} %get-tuple-element.61), channel_id=1, source_target_pairs={{0,16},{1,17},{2,18},{3,19},{4,20},{5,21},{6,22},{7,23},{8,24},{9,... | collective-permute-start | bytes 688136 | tf_op jit(solution)/shard_map/ppermute | solution.py:554
  9.7 2.6 %collective-permute-start.5 = (f32[8,16,128]{2,1,0:T(8,128)S(1)}, f32[8,16,128]{2,1,0:T(8,128)S(1)}, u32[]{:S(2)}, u32[]{:S(2)}) collective-permute-start(f32[8,16,128]{2,1,0:T(8,128)S(1)} %get-tuple-element.63), channel_id=1, source_target_pairs={{0,8},{1,9},{2,10},{3,11},{4,12},{5,13},{6,14},{7,15},{8,0},{9,1},... | collective-permute-start | bytes 196616 | tf_op jit(solution)/shard_map/ppermute | solution.py:554
  12.3 0.7 collective-permute-done.1.refs_1_.refs_0_.refs_3_
  13.0 0.6 pick_11.1
  13.6 0.6 collective-permute-start.2
  14.2 2.6 %collective-permute-start.4 = (f32[8,32,128]{2,1,0:T(8,128)S(1)}, f32[8,32,128]{2,1,0:T(8,128)S(1)}, u32[]{:S(2)}, u32[]{:S(2)}) collective-permute-start(f32[8,32,128]{2,1,0:T(8,128)S(1)} %get-tuple-element.62), channel_id=1, source_target_pairs={{0,8},{1,9},{2,10},{3,11},{4,12},{5,13},{6,14},{7,15},{8,0},{9,1},... | collective-permute-start | bytes 393224 | tf_op jit(solution)/shard_map/ppermute | solution.py:554
  16.8 0.0 collective-permute-done.5.refs_3_
  16.8 1.1 %collective-permute-done.3.refs_1_.refs_0_.refs_2_ = f32[8,56,128]{2,1,0:T(8,128)S(1)} collective-permute-done((f32[8,56,128]{2,1,0:T(8,128)S(1)}, f32[8,56,128]{2,1,0:T(8,128)S(1)}, u32[]{:S(2)}, u32[]{:S(2)}) %collective-permute-start.3) | collective-permute-done | bytes 229408 | tf_op jit(solution)/shard_map/ppermute | solution.py:554
  17.9 0.7 pick_12_20.1
  18.6 2.7 %collective-permute-start.7 = (f32[8,40,128]{2,1,0:T(8,128)S(1)}, f32[8,40,128]{2,1,0:T(8,128)S(1)}, u32[]{:S(2)}, u32[]{:S(2)}) collective-permute-start(f32[8,40,128]{2,1,0:T(8,128)S(1)} %get-tuple-element.67), channel_id=1, source_target_pairs={{0,8},{1,9},{2,10},{3,11},{4,12},{5,13},{6,14},{7,15},{8,0},{9,1},... | collective-permute-start | bytes 491528 | tf_op jit(solution)/shard_map/ppermute | solution.py:554
  21.3 1.5 %collective-permute-start.8 = (f32[8,16,128]{2,1,0:T(8,128)S(1)}, f32[8,16,128]{2,1,0:T(8,128)S(1)}, u32[]{:S(2)}, u32[]{:S(2)}) collective-permute-start(f32[8,16,128]{2,1,0:T(8,128)S(1)} %get-tuple-element.69), channel_id=1, source_target_pairs={{0,2},{1,3},{2,0},{3,1},{4,6},{5,7},{6,4},{7,5},{8,10},{9,11},{10,... | collective-permute-start | bytes 196616 | tf_op jit(solution)/shard_map/ppermute | solution.py:554
  22.8 1.2 %collective-permute-done.4.refs_4_ = f32[8,32,128]{2,1,0:T(8,128)S(1)} collective-permute-done((f32[8,32,128]{2,1,0:T(8,128)S(1)}, f32[8,32,128]{2,1,0:T(8,128)S(1)}, u32[]{:S(2)}, u32[]{:S(2)}) %collective-permute-start.4) | collective-permute-done | bytes 131104 | tf_op jit(solution)/shard_map/ppermute | solution.py:554
  24.0 0.0 collective-permute-done.2.refs_1_.refs_0_
  24.0 0.7 pick_13_21.1
  24.7 1.6 %collective-permute-start.10 = (f32[8,32,128]{2,1,0:T(8,128)S(1)}, f32[8,32,128]{2,1,0:T(8,128)S(1)}, u32[]{:S(2)}, u32[]{:S(2)}) collective-permute-start(f32[8,32,128]{2,1,0:T(8,128)S(1)} %get-tuple-element.72), channel_id=1, source_target_pairs={{0,2},{1,3},{2,0},{3,1},{4,6},{5,7},{6,4},{7,5},{8,10},{9,11},{10,... | collective-permute-start | bytes 393224 | tf_op jit(solution)/shard_map/ppermute | solution.py:554
  26.3 0.0 collective-permute-start.6
  26.3 0.0 collective-permute-done.8.refs_5_
  26.3 4.7 %collective-permute-done.7.refs_3_.refs_5_ = f32[8,40,128]{2,1,0:T(8,128)S(1)} collective-permute-done((f32[8,40,128]{2,1,0:T(8,128)S(1)}, f32[8,40,128]{2,1,0:T(8,128)S(1)}, u32[]{:S(2)}, u32[]{:S(2)}) %collective-permute-start.7) | collective-permute-done | bytes 163872 | tf_op jit(solution)/shard_map/ppermute | solution.py:554
  31.0 0.7 pick_14_22.1
  31.8 1.6 %collective-permute-start.12 = (f32[8,40,128]{2,1,0:T(8,128)S(1)}, f32[8,40,128]{2,1,0:T(8,128)S(1)}, u32[]{:S(2)}, u32[]{:S(2)}) collective-permute-start(f32[8,40,128]{2,1,0:T(8,128)S(1)} %get-tuple-element.75), channel_id=1, source_target_pairs={{0,2},{1,3},{2,0},{3,1},{4,6},{5,7},{6,4},{7,5},{8,10},{9,11},{10,... | collective-permute-start | bytes 491528 | tf_op jit(solution)/shard_map/ppermute | solution.py:554
  33.3 0.0 collective-permute-start.9
  33.3 0.0 collective-permute-done.10.refs_4_
  33.3 0.5 collective-permute-done.6.refs_2_.refs_6_.refs_1_
  33.8 0.6 pick_23.1
  34.4 1.6 %collective-permute-start.11 = (f32[8,40,128]{2,1,0:T(8,128)S(1)}, f32[8,40,128]{2,1,0:T(8,128)S(1)}, u32[]{:S(2)}, u32[]{:S(2)}) collective-permute-start(f32[8,40,128]{2,1,0:T(8,128)S(1)} %get-tuple-element.73), channel_id=1, source_target_pairs={{0,2},{1,3},{2,0},{3,1},{4,6},{5,7},{6,4},{7,5},{8,10},{9,11},{10,... | collective-permute-start | bytes 491528 | tf_op jit(solution)/shard_map/ppermute | solution.py:554
  36.0 5.7 %collective-permute-done.9.refs_1_.refs_2_ = f32[8,32,128]{2,1,0:T(8,128)S(1)} collective-permute-done((f32[8,32,128]{2,1,0:T(8,128)S(1)}, f32[8,32,128]{2,1,0:T(8,128)S(1)}, u32[]{:S(2)}, u32[]{:S(2)}) %collective-permute-start.9) | collective-permute-done | bytes 131104 | tf_op jit(solution)/shard_map/ppermute | solution.py:554
  41.7 0.0 collective-permute-done.12.refs_3_
  41.7 0.6 pick_24.1
  42.3 0.2 collective-permute-start.13
  42.5 0.0 collective-permute-done.11.refs_10_.refs_3_
  42.5 1.5 %assemble_0.1 = (f32[1280,128]{1,0:T(8,128)S(1)}, f32[1280,128]{1,0:T(8,128)S(1)}, f32[5,4,8,128]{3,2,1,0:T(8,128)S(1)}, f32[5,4,8,128]{3,2,1,0:T(8,128)S(1)}, f...) custom-call(s32[24]{0:T(128)S(1)} %get-tuple-element.54.tags, ...), custom_call_target="tpu_custom_call" | custom-call | tf_op jit(solution)/shard_map/assemble_0/pallas_call | solution.py:665
  44.0 3.3 %collective-permute-done.13.refs_4_ = f32[8,32,128]{2,1,0:T(8,128)S(1)} collective-permute-done((f32[8,32,128]{2,1,0:T(8,128)S(1)}, f32[8,32,128]{2,1,0:T(8,128)S(1)}, u32[]{:S(2)}, u32[]{:S(2)}) %collective-permute-start.13) | collective-permute-done | bytes 131104 | tf_op jit(solution)/shard_map/ppermute | solution.py:554
  47.4 0.9 %assemble_3.1 = (f32[1280,128]{1,0:T(8,128)S(1)}, f32[1280,128]{1,0:T(8,128)S(1)}, f32[5,4,8,128]{3,2,1,0:T(8,128)S(1)}, f32[5,4,8,128]{3,2,1,0:T(8,128)S(1)}, f...) custom-call(s32[24]{0:T(128)S(1)} %get-tuple-element.54.tags, ...), custom_call_target="tpu_custom_call", output_to_operand_aliasing={{0}: (7, {}), {1}: (8, {}), {2}: (9, {}), {3}: (10, {}), {4... | custom-call | tf_op jit(solution)/shard_map/assemble_3/pallas_call | solution.py:665
  48.2 3.5 %collective-permute-start.16 = (f32[2,5,4,8,128]{4,3,2,1,0:T(8,128)S(1)}, f32[2,5,4,8,128]{4,3,2,1,0:T(8,128)S(1)}, u32[]{:S(2)}, u32[]{:S(2)}) collective-permute-start(f32[2,5,4,8,128]{4,3,2,1,0:T(8,128)S(1)} %get-tuple-element.91), channel_id=1, source_target_pairs={{0,16},{16,0},{1,17},{17,1},{2,18},{18,2},{3,19},{19,3},{4,20},{20... | collective-permute-start | bytes 491528 | tf_op jit(solution)/shard_map/ppermute | solution.py:685
  51.7 0.0 collective-permute-start.18
  51.7 0.5 collective-permute-start.17
  52.2 2.8 %collective-permute-start.14 = (f32[5,4,8,128]{3,2,1,0:T(8,128)S(1)}, f32[5,4,8,128]{3,2,1,0:T(8,128)S(1)}, u32[]{:S(2)}, u32[]{:S(2)}) collective-permute-start(f32[5,4,8,128]{3,2,1,0:T(8,128)S(1)} %get-tuple-element.89.y_one), channel_id=1, source_target_pairs={{0,12},{4,8},{8,4},{12,0},{1,13},{5,9},{9,5},{13,1},{2,14},{6,10},... | collective-permute-start | bytes 245768 | tf_op jit(solution)/shard_map/ppermute | solution.py:690
  55.0 0.0 collective-permute-done.18.z_next
  55.0 0.5 collective-permute-done.17.z_prev
  55.6 1.5 %sweep_z.2.sofar = f32[1280,128]{1,0:T(8,128)S(1)} custom-call(f32[1280,128]{1,0:T(8,128)S(1)} %get-tuple-element.88.prim, f32[5,32,128]{2,1,0:T(8,128)S(1)} %get-tuple-element.92.z_lo, f32[5,32,128]{2,1,0:T(8,128)S(1)} %get-tuple-element.93.z_hi, f32[5,32,128]{2,1,0:T(8,128)S(1)} %collective-permute-done.17.z_prev, ...), custom_call_target="tpu_custom_call" | custom-call | tf_op jit(solution)/shard_map/sweep_z/pallas_call | solution.py:701
  57.1 0.6 sweep_x.2.sofar
  57.7 1.6 %collective-permute-done.14.got_one = f32[5,4,8,128]{3,2,1,0:T(8,128)S(1)} collective-permute-done((f32[5,4,8,128]{3,2,1,0:T(8,128)S(1)}, f32[5,4,8,128]{3,2,1,0:T(8,128)S(1)}, u32[]{:S(2)}, u32[]{:S(2)}) %collective-permute-start.14) | collective-permute-done | bytes 81952 | tf_op jit(solution)/shard_map/ppermute | solution.py:690
  59.3 1.2 %collective-permute-done.15.got_two = f32[5,4,8,128]{3,2,1,0:T(8,128)S(1)} collective-permute-done((f32[5,4,8,128]{3,2,1,0:T(8,128)S(1)}, f32[5,4,8,128]{3,2,1,0:T(8,128)S(1)}, u32[]{:S(2)}, u32[]{:S(2)}) %collective-permute-start.15) | collective-permute-done | bytes 81952 | tf_op jit(solution)/shard_map/ppermute | solution.py:690
  60.5 1.3 %sweep_y_one.1 = (f32[1280,128]{1,0:T(8,128)S(1)}, f32[1280,128]{1,0:T(8,128)S(1)}, f32[2,5,4,8,128]{4,3,2,1,0:T(8,128)S(1)}, f32[5,4,8,128]{3,2,1,0:T(8,128)S(1...) custom-call(f32[1280,128]{1,0:T(8,128)S(1)} %get-tuple-element.87.field, ...), custom_call_target="tpu_custom_call" | custom-call | tf_op jit(solution)/shard_map/sweep_y_one/pallas_call | solution.py:725
  61.8 1.6 %collective-permute-start.21 = (f32[2,5,4,8,128]{4,3,2,1,0:T(8,128)S(1)}, f32[2,5,4,8,128]{4,3,2,1,0:T(8,128)S(1)}, u32[]{:S(2)}, u32[]{:S(2)}) collective-permute-start(f32[2,5,4,8,128]{4,3,2,1,0:T(8,128)S(1)} %get-tuple-element.98), channel_id=1, source_target_pairs={{0,16},{16,0},{1,17},{17,1},{2,18},{18,2},{3,19},{19,3},{4,20},{20... | collective-permute-start | bytes 491528 | tf_op jit(solution)/shard_map/ppermute | solution.py:685
  63.4 0.0 collective-permute-start.23
  63.4 0.5 collective-permute-start.22
  63.9 2.0 %collective-permute-start.19 = (f32[5,4,8,128]{3,2,1,0:T(8,128)S(1)}, f32[5,4,8,128]{3,2,1,0:T(8,128)S(1)}, u32[]{:S(2)}, u32[]{:S(2)}) collective-permute-start(f32[5,4,8,128]{3,2,1,0:T(8,128)S(1)} %get-tuple-element.96.y_one), channel_id=1, source_target_pairs={{0,12},{4,8},{8,4},{12,0},{1,13},{5,9},{9,5},{13,1},{2,14},{6,10},... | collective-permute-start | bytes 245768 | tf_op jit(solution)/shard_map/ppermute | solution.py:690
  65.9 0.0 collective-permute-start.20
  65.9 0.0 collective-permute-done.23.z_next
  65.9 2.0 %collective-permute-done.22.z_prev = f32[5,32,128]{2,1,0:T(8,128)S(1)} collective-permute-done((f32[5,32,128]{2,1,0:T(8,128)S(1)}, f32[5,32,128]{2,1,0:T(8,128)S(1)}, u32[]{:S(2)}, u32[]{:S(2)}) %collective-permute-start.22) | collective-permute-done | bytes 81952 | tf_op jit(solution)/shard_map/ppermute | solution.py:685
  67.9 1.5 %sweep_z.3.sofar = f32[1280,128]{1,0:T(8,128)S(1)} custom-call(f32[1280,128]{1,0:T(8,128)S(1)} %get-tuple-element.95.prim, f32[5,32,128]{2,1,0:T(8,128)S(1)} %get-tuple-element.99.z_lo, f32[5,32,128]{2,1,0:T(8,128)S(1)} %get-tuple-element.100.z_hi, f32[5,32,128]{2,1,0:T(8,128)S(1)} %collective-permute-done.22.z_prev, ...), custom_call_target="tpu_custom_call" | custom-call | tf_op jit(solution)/shard_map/sweep_z/pallas_call | solution.py:701
  69.4 0.0 collective-permute-done.21.x_faces
  69.4 0.6 sweep_x.3.sofar
  70.0 1.0 %collective-permute-done.19.got_one = f32[5,4,8,128]{3,2,1,0:T(8,128)S(1)} collective-permute-done((f32[5,4,8,128]{3,2,1,0:T(8,128)S(1)}, f32[5,4,8,128]{3,2,1,0:T(8,128)S(1)}, u32[]{:S(2)}, u32[]{:S(2)}) %collective-permute-start.19) | collective-permute-done | bytes 81952 | tf_op jit(solution)/shard_map/ppermute | solution.py:690
  71.0 1.4 %collective-permute-done.20.got_two = f32[5,4,8,128]{3,2,1,0:T(8,128)S(1)} collective-permute-done((f32[5,4,8,128]{3,2,1,0:T(8,128)S(1)}, f32[5,4,8,128]{3,2,1,0:T(8,128)S(1)}, u32[]{:S(2)}, u32[]{:S(2)}) %collective-permute-start.20) | collective-permute-done | bytes 81952 | tf_op jit(solution)/shard_map/ppermute | solution.py:690
  72.5 2.8 %sweep_y_two.1 = (f32[20,256,128]{2,1,0:T(8,128)}, f32[20,256,128]{2,1,0:T(8,128)S(1)}) custom-call(s32[8]{0:T(128)} %copy-done.2, f32[1280,128]{1,0:T(8,128)S(1)} %get-tuple-element.87.field, f32[1280,128]{1,0:T(8,128)S(1)} %get-tuple-element.94.one, f32[1280,128]{1,0:T(8,128)S(1)} %get-tuple-element.95.prim, ...), custom_call_target="tpu_custom_call", output_to_operand_aliasing={{1}: (9, {})} | custom-call | tf_op jit(solution)/shard_map/sweep_y_two/pallas_call | solution.py:736
  (12 shorter events, 0.0 us)
Async XLA Ops:
  0.0 4.4 %copy-start.1 = (s32[3,1,8]{2,1,0:T(1,128)S(1)}, s32[3,1,8]{2,1,0:T(1,128)}, u32[]{:S(2)}) copy-start(s32[3,1,8]{2,1,0:T(1,128)} %send_hbm.1) | copy-start | bytes 292
  0.0 4.4 %copy-start = (f32[32,5,4096]{2,0,1:T(8,128)S(1)}, f32[32,5,4096]{2,0,1:T(8,128)}, u32[]{:S(2)}) copy-start(f32[32,5,4096]{2,0,1:T(8,128)} %param.4) | copy-start | bytes 7864324
  0.0 4.3 %copy-start.4 = (s32[256]{0:T(256)S(1)}, s32[256]{0:T(256)}, u32[]{:S(2)}) copy-start(s32[256]{0:T(256)} %param.7) | copy-start | bytes 3076
  0.0 4.4 %copy-start.3 = (s32[3,1,8]{2,1,0:T(1,128)S(1)}, s32[3,1,8]{2,1,0:T(1,128)}, u32[]{:S(2)}) copy-start(s32[3,1,8]{2,1,0:T(1,128)} %recv.1) | copy-start | bytes 292
  1.3 5.8 %collective-permute-start = (f32[8,24,128]{2,1,0:T(8,128)S(1)}, f32[8,24,128]{2,1,0:T(8,128)S(1)}, u32[]{:S(2)}, u32[]{:S(2)}) collective-permute-start(f32[8,24,128]{2,1,0:T(8,128)S(1)} %pack_first.1), channel_id=1, source_target_pairs={{0,16},{1,17},{2,18},{3,19},{4,20},{5,21},{6,22},{7,23},{8,24},{9,... | collective-permute-start | bytes 294920 | tf_op jit(solution)/shard_map/ppermute | solution.py:554
  4.4 3.3 %copy-start.2 = (s32[8]{0:T(128)}, s32[8]{0:T(128)S(1)}, u32[]{:S(2)}) copy-start(s32[8]{0:T(128)S(1)} %dynamic_slice.3.own.own_there) | copy-start | bytes 100
  5.8 7.2 %collective-permute-start.1 = (f32[8,40,128]{2,1,0:T(8,128)S(1)}, f32[8,40,128]{2,1,0:T(8,128)S(1)}, u32[]{:S(2)}, u32[]{:S(2)}) collective-permute-start(f32[8,40,128]{2,1,0:T(8,128)S(1)} %get-tuple-element.55), channel_id=1, source_target_pairs={{0,16},{1,17},{2,18},{3,19},{4,20},{5,21},{6,22},{7,23},{8,24},{9,... | collective-permute-start | bytes 491528 | tf_op jit(solution)/shard_map/ppermute | solution.py:554
  7.7 10.2 %collective-permute-start.3 = (f32[8,56,128]{2,1,0:T(8,128)S(1)}, f32[8,56,128]{2,1,0:T(8,128)S(1)}, u32[]{:S(2)}, u32[]{:S(2)}) collective-permute-start(f32[8,56,128]{2,1,0:T(8,128)S(1)} %get-tuple-element.61), channel_id=1, source_target_pairs={{0,16},{1,17},{2,18},{3,19},{4,20},{5,21},{6,22},{7,23},{8,24},{9,... | collective-permute-start | bytes 688136 | tf_op jit(solution)/shard_map/ppermute | solution.py:554
  9.7 7.1 %collective-permute-start.5 = (f32[8,16,128]{2,1,0:T(8,128)S(1)}, f32[8,16,128]{2,1,0:T(8,128)S(1)}, u32[]{:S(2)}, u32[]{:S(2)}) collective-permute-start(f32[8,16,128]{2,1,0:T(8,128)S(1)} %get-tuple-element.63), channel_id=1, source_target_pairs={{0,8},{1,9},{2,10},{3,11},{4,12},{5,13},{6,14},{7,15},{8,0},{9,1},... | collective-permute-start | bytes 196616 | tf_op jit(solution)/shard_map/ppermute | solution.py:554
  13.6 10.4 %collective-permute-start.2 = (f32[8,40,128]{2,1,0:T(8,128)S(1)}, f32[8,40,128]{2,1,0:T(8,128)S(1)}, u32[]{:S(2)}, u32[]{:S(2)}) collective-permute-start(f32[8,40,128]{2,1,0:T(8,128)S(1)} %get-tuple-element.60), channel_id=1, source_target_pairs={{0,16},{1,17},{2,18},{3,19},{4,20},{5,21},{6,22},{7,23},{8,24},{9,... | collective-permute-start | bytes 491528 | tf_op jit(solution)/shard_map/ppermute | solution.py:554
  14.2 9.8 %collective-permute-start.4 = (f32[8,32,128]{2,1,0:T(8,128)S(1)}, f32[8,32,128]{2,1,0:T(8,128)S(1)}, u32[]{:S(2)}, u32[]{:S(2)}) collective-permute-start(f32[8,32,128]{2,1,0:T(8,128)S(1)} %get-tuple-element.62), channel_id=1, source_target_pairs={{0,8},{1,9},{2,10},{3,11},{4,12},{5,13},{6,14},{7,15},{8,0},{9,1},... | collective-permute-start | bytes 393224 | tf_op jit(solution)/shard_map/ppermute | solution.py:554
  18.6 12.4 %collective-permute-start.7 = (f32[8,40,128]{2,1,0:T(8,128)S(1)}, f32[8,40,128]{2,1,0:T(8,128)S(1)}, u32[]{:S(2)}, u32[]{:S(2)}) collective-permute-start(f32[8,40,128]{2,1,0:T(8,128)S(1)} %get-tuple-element.67), channel_id=1, source_target_pairs={{0,8},{1,9},{2,10},{3,11},{4,12},{5,13},{6,14},{7,15},{8,0},{9,1},... | collective-permute-start | bytes 491528 | tf_op jit(solution)/shard_map/ppermute | solution.py:554
  21.3 5.0 %collective-permute-start.8 = (f32[8,16,128]{2,1,0:T(8,128)S(1)}, f32[8,16,128]{2,1,0:T(8,128)S(1)}, u32[]{:S(2)}, u32[]{:S(2)}) collective-permute-start(f32[8,16,128]{2,1,0:T(8,128)S(1)} %get-tuple-element.69), channel_id=1, source_target_pairs={{0,2},{1,3},{2,0},{3,1},{4,6},{5,7},{6,4},{7,5},{8,10},{9,11},{10,... | collective-permute-start | bytes 196616 | tf_op jit(solution)/shard_map/ppermute | solution.py:554
  24.7 8.6 %collective-permute-start.10 = (f32[8,32,128]{2,1,0:T(8,128)S(1)}, f32[8,32,128]{2,1,0:T(8,128)S(1)}, u32[]{:S(2)}, u32[]{:S(2)}) collective-permute-start(f32[8,32,128]{2,1,0:T(8,128)S(1)} %get-tuple-element.72), channel_id=1, source_target_pairs={{0,2},{1,3},{2,0},{3,1},{4,6},{5,7},{6,4},{7,5},{8,10},{9,11},{10,... | collective-permute-start | bytes 393224 | tf_op jit(solution)/shard_map/ppermute | solution.py:554
  26.3 7.5 %collective-permute-start.6 = (f32[8,40,128]{2,1,0:T(8,128)S(1)}, f32[8,40,128]{2,1,0:T(8,128)S(1)}, u32[]{:S(2)}, u32[]{:S(2)}) collective-permute-start(f32[8,40,128]{2,1,0:T(8,128)S(1)} %get-tuple-element.66), channel_id=1, source_target_pairs={{0,8},{1,9},{2,10},{3,11},{4,12},{5,13},{6,14},{7,15},{8,0},{9,1},... | collective-permute-start | bytes 491528 | tf_op jit(solution)/shard_map/ppermute | solution.py:554
  31.8 9.9 %collective-permute-start.12 = (f32[8,40,128]{2,1,0:T(8,128)S(1)}, f32[8,40,128]{2,1,0:T(8,128)S(1)}, u32[]{:S(2)}, u32[]{:S(2)}) collective-permute-start(f32[8,40,128]{2,1,0:T(8,128)S(1)} %get-tuple-element.75), channel_id=1, source_target_pairs={{0,2},{1,3},{2,0},{3,1},{4,6},{5,7},{6,4},{7,5},{8,10},{9,11},{10,... | collective-permute-start | bytes 491528 | tf_op jit(solution)/shard_map/ppermute | solution.py:554
  33.3 8.4 %collective-permute-start.9 = (f32[8,32,128]{2,1,0:T(8,128)S(1)}, f32[8,32,128]{2,1,0:T(8,128)S(1)}, u32[]{:S(2)}, u32[]{:S(2)}) collective-permute-start(f32[8,32,128]{2,1,0:T(8,128)S(1)} %get-tuple-element.70), channel_id=1, source_target_pairs={{0,8},{1,9},{2,10},{3,11},{4,12},{5,13},{6,14},{7,15},{8,0},{9,1},... | collective-permute-start | bytes 393224 | tf_op jit(solution)/shard_map/ppermute | solution.py:554
  34.4 8.1 %collective-permute-start.11 = (f32[8,40,128]{2,1,0:T(8,128)S(1)}, f32[8,40,128]{2,1,0:T(8,128)S(1)}, u32[]{:S(2)}, u32[]{:S(2)}) collective-permute-start(f32[8,40,128]{2,1,0:T(8,128)S(1)} %get-tuple-element.73), channel_id=1, source_target_pairs={{0,2},{1,3},{2,0},{3,1},{4,6},{5,7},{6,4},{7,5},{8,10},{9,11},{10,... | collective-permute-start | bytes 491528 | tf_op jit(solution)/shard_map/ppermute | solution.py:554
  42.3 5.0 %collective-permute-start.13 = (f32[8,32,128]{2,1,0:T(8,128)S(1)}, f32[8,32,128]{2,1,0:T(8,128)S(1)}, u32[]{:S(2)}, u32[]{:S(2)}) collective-permute-start(f32[8,32,128]{2,1,0:T(8,128)S(1)} %get-tuple-element.76), channel_id=1, source_target_pairs={{0,2},{1,3},{2,0},{3,1},{4,6},{5,7},{6,4},{7,5},{8,10},{9,11},{10,... | collective-permute-start | bytes 393224 | tf_op jit(solution)/shard_map/ppermute | solution.py:554
  48.2 8.9 %collective-permute-start.16 = (f32[2,5,4,8,128]{4,3,2,1,0:T(8,128)S(1)}, f32[2,5,4,8,128]{4,3,2,1,0:T(8,128)S(1)}, u32[]{:S(2)}, u32[]{:S(2)}) collective-permute-start(f32[2,5,4,8,128]{4,3,2,1,0:T(8,128)S(1)} %get-tuple-element.91), channel_id=1, source_target_pairs={{0,16},{16,0},{1,17},{17,1},{2,18},{18,2},{3,19},{19,3},{4,20},{20... | collective-permute-start | bytes 491528 | tf_op jit(solution)/shard_map/ppermute | solution.py:685
  51.7 3.3 %collective-permute-start.18 = (f32[5,32,128]{2,1,0:T(8,128)S(1)}, f32[5,32,128]{2,1,0:T(8,128)S(1)}, u32[]{:S(2)}, u32[]{:S(2)}) collective-permute-start(f32[5,32,128]{2,1,0:T(8,128)S(1)} %get-tuple-element.92.z_lo), channel_id=1, source_target_pairs={{0,3},{1,0},{2,1},{3,2},{4,7},{5,4},{6,5},{7,6},{8,11},{9,8},{10,9... | collective-permute-start | bytes 245768 | tf_op jit(solution)/shard_map/ppermute | solution.py:685
  51.7 3.9 %collective-permute-start.17 = (f32[5,32,128]{2,1,0:T(8,128)S(1)}, f32[5,32,128]{2,1,0:T(8,128)S(1)}, u32[]{:S(2)}, u32[]{:S(2)}) collective-permute-start(f32[5,32,128]{2,1,0:T(8,128)S(1)} %get-tuple-element.93.z_hi), channel_id=1, source_target_pairs={{0,1},{1,2},{2,3},{3,0},{4,5},{5,6},{6,7},{7,4},{8,9},{9,10},{10,1... | collective-permute-start | bytes 245768 | tf_op jit(solution)/shard_map/ppermute | solution.py:685
  52.2 7.1 %collective-permute-start.14 = (f32[5,4,8,128]{3,2,1,0:T(8,128)S(1)}, f32[5,4,8,128]{3,2,1,0:T(8,128)S(1)}, u32[]{:S(2)}, u32[]{:S(2)}) collective-permute-start(f32[5,4,8,128]{3,2,1,0:T(8,128)S(1)} %get-tuple-element.89.y_one), channel_id=1, source_target_pairs={{0,12},{4,8},{8,4},{12,0},{1,13},{5,9},{9,5},{13,1},{2,14},{6,10},... | collective-permute-start | bytes 245768 | tf_op jit(solution)/shard_map/ppermute | solution.py:690
  55.0 5.5 %collective-permute-start.15 = (f32[5,4,8,128]{3,2,1,0:T(8,128)S(1)}, f32[5,4,8,128]{3,2,1,0:T(8,128)S(1)}, u32[]{:S(2)}, u32[]{:S(2)}) collective-permute-start(f32[5,4,8,128]{3,2,1,0:T(8,128)S(1)} %get-tuple-element.90.y_two), channel_id=1, source_target_pairs={{0,4},{4,0},{8,12},{12,8},{1,5},{5,1},{9,13},{13,9},{2,6},{6,2},{1... | collective-permute-start | bytes 245768 | tf_op jit(solution)/shard_map/ppermute | solution.py:690
  61.8 7.6 %collective-permute-start.21 = (f32[2,5,4,8,128]{4,3,2,1,0:T(8,128)S(1)}, f32[2,5,4,8,128]{4,3,2,1,0:T(8,128)S(1)}, u32[]{:S(2)}, u32[]{:S(2)}) collective-permute-start(f32[2,5,4,8,128]{4,3,2,1,0:T(8,128)S(1)} %get-tuple-element.98), channel_id=1, source_target_pairs={{0,16},{16,0},{1,17},{17,1},{2,18},{18,2},{3,19},{19,3},{4,20},{20... | collective-permute-start | bytes 491528 | tf_op jit(solution)/shard_map/ppermute | solution.py:685
  63.4 2.5 %collective-permute-start.23 = (f32[5,32,128]{2,1,0:T(8,128)S(1)}, f32[5,32,128]{2,1,0:T(8,128)S(1)}, u32[]{:S(2)}, u32[]{:S(2)}) collective-permute-start(f32[5,32,128]{2,1,0:T(8,128)S(1)} %get-tuple-element.99.z_lo), channel_id=1, source_target_pairs={{0,3},{1,0},{2,1},{3,2},{4,7},{5,4},{6,5},{7,6},{8,11},{9,8},{10,9... | collective-permute-start | bytes 245768 | tf_op jit(solution)/shard_map/ppermute | solution.py:685
  63.4 4.5 %collective-permute-start.22 = (f32[5,32,128]{2,1,0:T(8,128)S(1)}, f32[5,32,128]{2,1,0:T(8,128)S(1)}, u32[]{:S(2)}, u32[]{:S(2)}) collective-permute-start(f32[5,32,128]{2,1,0:T(8,128)S(1)} %get-tuple-element.100.z_hi), channel_id=1, source_target_pairs={{0,1},{1,2},{2,3},{3,0},{4,5},{5,6},{6,7},{7,4},{8,9},{9,10},{10,1... | collective-permute-start | bytes 245768 | tf_op jit(solution)/shard_map/ppermute | solution.py:685
  63.9 7.2 %collective-permute-start.19 = (f32[5,4,8,128]{3,2,1,0:T(8,128)S(1)}, f32[5,4,8,128]{3,2,1,0:T(8,128)S(1)}, u32[]{:S(2)}, u32[]{:S(2)}) collective-permute-start(f32[5,4,8,128]{3,2,1,0:T(8,128)S(1)} %get-tuple-element.96.y_one), channel_id=1, source_target_pairs={{0,12},{4,8},{8,4},{12,0},{1,13},{5,9},{9,5},{13,1},{2,14},{6,10},... | collective-permute-start | bytes 245768 | tf_op jit(solution)/shard_map/ppermute | solution.py:690
  65.9 6.6 %collective-permute-start.20 = (f32[5,4,8,128]{3,2,1,0:T(8,128)S(1)}, f32[5,4,8,128]{3,2,1,0:T(8,128)S(1)}, u32[]{:S(2)}, u32[]{:S(2)}) collective-permute-start(f32[5,4,8,128]{3,2,1,0:T(8,128)S(1)} %get-tuple-element.97.y_two), channel_id=1, source_target_pairs={{0,4},{4,0},{8,12},{12,8},{1,5},{5,1},{9,13},{13,9},{2,6},{6,2},{1... | collective-permute-start | bytes 245768 | tf_op jit(solution)/shard_map/ppermute | solution.py:690

commit v12 on v9

--- a/solution.py
+++ b/solution.py
@@ -216,7 +216,7 @@
     def faces(self):
         x = jax.ShapeDtypeStruct((2, NF, self.pad, SUB, LANES), f32)
         y = jax.ShapeDtypeStruct((NF, self.edge // self.fit, SUB, LANES), f32)
-        z = jax.ShapeDtypeStruct((NF, self.rows, LANES), f32)
+        z = jax.ShapeDtypeStruct((NF, SUB, LANES), f32)
         return [x, y, y, z, z]
 
 
@@ -249,11 +249,14 @@
                 hi = jnp.where(mine, above, hi)
         y_one[f, slab] = jnp.where(odd, hi, lo)
         y_two[f, slab] = jnp.where(odd, lo, hi)
-        to = pl.ds(slab * SUB, SUB) if isinstance(slab, int) else pl.ds(
-            pl.multiple_of(slab * SUB, SUB), SUB
-        )
-        z_lo[f, to, :] = prim[shape.across(f, slab, 0), :]
-        z_hi[f, to, :] = prim[shape.across(f, slab, SUB - 1), :]
+        below = lane_roll(prim[shape.across(f, slab, 0), :], 2 * slab)
+        above = lane_roll(prim[shape.across(f, slab, SUB - 1), :], 2 * slab + 2 - shape.edge)
+        if slab:
+            mine = lax.rem(lane, shape.edge) >= 2 * slab
+            below = jnp.where(mine, below, z_lo[f])
+            above = jnp.where(mine, above, z_hi[f])
+        z_lo[f] = below
+        z_hi[f] = above
 
 
 def send_x(shape, prim, faces, low=True, high=True):
@@ -299,15 +302,18 @@
     send_x(shape, prim, x_faces, low=first, high=not first)
 
 
-def sweep_z_kernel(prim, z_lo, z_hi, z_prev, z_next, total, flux_z, right_z, left, right, flux, *, shape):
+def sweep_z_kernel(prim, z_prev, z_next, sofar, total, prev_z, next_z, flux_z, right_z, left, right, flux, *, shape):
     edge, rows = shape.edge, shape.rows
 
     def ghost(a):
         at = pl.ds(a * SUB, SUB)
-        low = [z_lo[f, at, :] for f in FIELDS]
-        high = [z_hi[f, at, :] for f in FIELDS]
-        prev = [z_prev[f, at, :] for f in FIELDS]
-        after = [z_next[f, at, :] for f in FIELDS]
+        low = [prim[shape.across(f, a, 0), :] for f in FIELDS]
+        high = [prim[shape.across(f, a, SUB - 1), :] for f in FIELDS]
+        prev = [lane_roll(z_prev[f], edge - 2 - 2 * a) for f in FIELDS]
+        after = [lane_roll(z_next[f], -2 * a) for f in FIELDS]
+        for f in FIELDS:
+            prev_z[f, at, :] = prev[f]
+            next_z[f, at, :] = after[f]
         below = [lane_roll(v, -(edge - 1)) for v in prev]
         before = [lane_roll(v, -(edge - 2)) for v in prev]
         second = [lane_roll(v, -1) for v in low]
@@ -346,7 +352,7 @@
             for f in FIELDS:
                 at = shape.at(f, row)
                 mine = prim[at, :]
-                shift = half_minmod(mine - down(mine, f, row, z_prev), up(mine, f, row, z_next) - mine)
+                shift = half_minmod(mine - down(mine, f, row, prev_z), up(mine, f, row, next_z) - mine)
                 left[at, :] = mine + shift
                 right[at, :] = mine - shift
 
@@ -362,12 +368,12 @@
             for f in FIELDS:
                 at = shape.at(f, row)
                 mine = flux[at, :]
-                total[at, :] = mine - down(mine, f, row, flux_z)
+                total[at, :] = sofar[at, :] + (mine - down(mine, f, row, flux_z))
 
     in_turn(shape.slabs, slopes, fluxes, differences)
 
 
-def sweep_x_kernel(prim, x_faces, sofar, total, *, shape):
+def sweep_x_kernel(prim, x_faces, total, *, shape):
     halves, edge = shape.halves, shape.edge
 
     def cells(x, h):
@@ -387,7 +393,7 @@
                 if below is not None:
                     for f in FIELDS:
                         at = shape.at(f, (x - 1) * halves + h)
-                        total[at, :] = sofar[at, :] + (flux[f] - below[f])
+                        total[at, :] = flux[f] - below[f]
                 below = flux
             left = plus(ahead[1], shift)
             if x < edge:
@@ -699,23 +705,25 @@
         ghost = VMEM((NF, rows, LANES), f32)
         work = [VMEM(grid.shape, f32)] * 3
         total = pl.pallas_call(
+            functools.partial(sweep_x_kernel, shape=shape),
+            out_shape=grid,
+            in_specs=[whole(VMEM)] * 2,
+            out_specs=whole(VMEM),
+            compiler_params=params(),
+            cost_estimate=cost(1, 1),
+            name="sweep_x",
+        )(prim, x_faces)
+        total = pl.pallas_call(
             functools.partial(sweep_z_kernel, shape=shape),
             out_shape=grid,
-            in_specs=[whole(VMEM)] * 5,
+            in_specs=[whole(VMEM)] * 4,
             out_specs=whole(VMEM),
-            scratch_shapes=[ghost] * 2 + work,
+            scratch_shapes=[ghost] * 4 + work,
+            input_output_aliases={3: 0},
             compiler_params=params(),
+            cost_estimate=cost(1, 1),
             name="sweep_z",
-        )(prim, z_lo, z_hi, z_prev, z_next)
-        total = pl.pallas_call(
-            functools.partial(sweep_x_kernel, shape=shape),
-            out_shape=grid,
-            in_specs=[whole(VMEM)] * 3,
-            out_specs=whole(VMEM),
-            input_output_aliases={2: 0},
-            compiler_params=params(),
-            name="sweep_x",
-        )(prim, x_faces, total)
+        )(prim, z_prev, z_next, total)
         return y_one, y_two, got_one, got_two, total
 
     produced = [grid, grid] + shape.faces()

time: 73.1 us -> 72.3 us (0.989)
  waiting for transfers between devices: 24.3 us -> 19.4 us
  starting transfers between devices: 30.3 us -> 33.2 us
  Pallas kernels: 18 us -> 18.8 us
    ppermute x4, waiting for transfers between devices: 5.44 us -> 0.01 us  [beside(): return lax.ppermute(value, axis, [(i, j % size) for i, j in pairs])]
    ppermute x6, starting transfers between devices: 4.18 us -> 7.11 us  [ring(): lax.ppermute(value, axis, [(i, (i + step) % size) for i in range(size)])]
  transfers between devices with their start and end apart: 24 -> 24, of which waited for: 12 -> 9; matrix products, arithmetic and copies ran while one was open for 0% -> 0% of each run, Pallas kernels for 16% -> 17%
where the time goes in v12:
time: 72.3 us; the launch traced here: 71.7 us
  starting transfers between devices  33.2 us (46%)
  waiting for transfers between devices  19.4 us (27%)
  Pallas kernels  18.8 us (26%)
    ppermute x14, starting transfers between devices, swapped(): return lax.ppermute(value, AXES, pairs)  20.8 us
    ppermute x14, waiting for transfers between devices, swapped(): return lax.ppermute(value, AXES, pairs)  16.5 us
    ppermute x6, starting transfers between devices, ring(): lax.ppermute(value, axis, [(i, (i + step) % size) for i in range(size)])  7.11 us
    ppermute x4, starting transfers between devices, beside(): return lax.ppermute(value, axis, [(i, j % size) for i, j in pairs])  5.31 us
    pallas_call x7, Pallas kernels, make(): pl.pallas_call(functools.partial(pick_kernel, plan=plan, held=tuple(found...  4.68 us
    pallas_call x2, Pallas kernels, flux_sums(): pl.pallas_call(functools.partial(sweep_z_kernel, shape=shape), out_shape=...  3.76 us
    ppermute x6, waiting for transfers between devices, ring(): lax.ppermute(value, axis, [(i, (i + step) % size) for i in range(size)])  2.89 us
    pallas_call x1, Pallas kernels, shards(): pl.pallas_call(functools.partial(sweep_y_two_kernel, shape=shape, occ=occ...  2.8 us
  transfers between devices with their start and end apart: 24, of which 9 were waited for; matrix products, arithmetic and copies ran while one was open for 0% of the time, Pallas kernels for 17%

profile of v12, /device:TPU:0, one launch (start us, length us, event | category | flops | bytes accessed | tf_op | source)
XLA Modules:
  0.0 71.7 jit_solution(7394402855452453304)
XLA Ops:
  0.0 1.2 %pack_first.1 = f32[8,24,128]{2,1,0:T(8,128)S(1)} custom-call(s32[3,1,8]{2,1,0:T(1,128)} %send_hbm.1, f32[5120,128]{1,0:T(8,128)} %bitcast.10), custom_call_target="tpu_custom_call" | custom-call | tf_op jit(solution)/shard_map/pack_first/pallas_call | solution.py:579
  1.3 3.0 %collective-permute-start.1 = (f32[8,24,128]{2,1,0:T(8,128)S(1)}, f32[8,24,128]{2,1,0:T(8,128)S(1)}, u32[]{:S(2)}, u32[]{:S(2)}) collective-permute-start(f32[8,24,128]{2,1,0:T(8,128)S(1)} %pack_first.1), channel_id=1, source_target_pairs={{0,16},{1,17},{2,18},{3,19},{4,20},{5,21},{6,22},{7,23},{8,24},{9,... | collective-permute-start | bytes 294920 | tf_op jit(solution)/shard_map/ppermute | solution.py:560
  4.3 0.1 dynamic_slice.3.own.own_there
  4.4 1.4 %pack_rest.1 = (s32[24]{0:T(128)S(1)}, f32[8,128]{1,0:T(8,128)S(1)}, f32[8,40,128]{2,1,0:T(8,128)S(1)}, f32[8,56,128]{2,1,0:T(8,128)S(1)}, f32[8,40,128]{2,1,0:T(8,128)S(1)}) custom-call(s32[3,1,8]{2,1,0:T(1,128)S(1)} %copy-done.1, s32[3,1,8]{2,1,0:T(1,128)S(1)} %copy-done.3, s32[8]{0:T(128)S(1)} %dynamic_slice.3.own.own_there, f32[5120,128]{1,0:T(8,128)S(1)} %bitcast.11), custom_call_target="tpu_custom_call" | custom-call | tf_op jit(solution)/shard_map/pack_rest/pallas_call | solution.py:592
  5.8 0.6 collective-permute-start
  6.4 0.7 collective-permute-done.1.refs_0_.refs_2_
  7.1 0.6 pick_10.1
  7.7 2.0 %collective-permute-start.3 = (f32[8,56,128]{2,1,0:T(8,128)S(1)}, f32[8,56,128]{2,1,0:T(8,128)S(1)}, u32[]{:S(2)}, u32[]{:S(2)}) collective-permute-start(f32[8,56,128]{2,1,0:T(8,128)S(1)} %get-tuple-element.61), channel_id=1, source_target_pairs={{0,16},{1,17},{2,18},{3,19},{4,20},{5,21},{6,22},{7,23},{8,24},{9,... | collective-permute-start | bytes 688136 | tf_op jit(solution)/shard_map/ppermute | solution.py:560
  9.7 2.6 %collective-permute-start.5 = (f32[8,24,128]{2,1,0:T(8,128)S(1)}, f32[8,24,128]{2,1,0:T(8,128)S(1)}, u32[]{:S(2)}, u32[]{:S(2)}) collective-permute-start(f32[8,24,128]{2,1,0:T(8,128)S(1)} %get-tuple-element.63), channel_id=1, source_target_pairs={{0,8},{1,9},{2,10},{3,11},{4,12},{5,13},{6,14},{7,15},{8,0},{9,1},... | collective-permute-start | bytes 294920 | tf_op jit(solution)/shard_map/ppermute | solution.py:560
  12.3 0.7 collective-permute-done.refs_0_.refs_2_.refs_1_
  13.0 0.6 pick_11.1
  13.6 0.6 collective-permute-start.2
  14.2 2.6 %collective-permute-start.4 = (f32[8,32,128]{2,1,0:T(8,128)S(1)}, f32[8,32,128]{2,1,0:T(8,128)S(1)}, u32[]{:S(2)}, u32[]{:S(2)}) collective-permute-start(f32[8,32,128]{2,1,0:T(8,128)S(1)} %get-tuple-element.62), channel_id=1, source_target_pairs={{0,8},{1,9},{2,10},{3,11},{4,12},{5,13},{6,14},{7,15},{8,0},{9,1},... | collective-permute-start | bytes 393224 | tf_op jit(solution)/shard_map/ppermute | solution.py:560
  16.8 0.0 collective-permute-done.5.refs_3_
  16.8 1.1 %collective-permute-done.3.refs_1_.refs_0_.refs_2_ = f32[8,56,128]{2,1,0:T(8,128)S(1)} collective-permute-done((f32[8,56,128]{2,1,0:T(8,128)S(1)}, f32[8,56,128]{2,1,0:T(8,128)S(1)}, u32[]{:S(2)}, u32[]{:S(2)}) %collective-permute-start.3) | collective-permute-done | bytes 229408 | tf_op jit(solution)/shard_map/ppermute | solution.py:560
  17.9 0.7 pick_12_20.1
  18.6 2.7 %collective-permute-start.7 = (f32[8,40,128]{2,1,0:T(8,128)S(1)}, f32[8,40,128]{2,1,0:T(8,128)S(1)}, u32[]{:S(2)}, u32[]{:S(2)}) collective-permute-start(f32[8,40,128]{2,1,0:T(8,128)S(1)} %get-tuple-element.67), channel_id=1, source_target_pairs={{0,8},{1,9},{2,10},{3,11},{4,12},{5,13},{6,14},{7,15},{8,0},{9,1},... | collective-permute-start | bytes 491528 | tf_op jit(solution)/shard_map/ppermute | solution.py:560
  21.3 1.5 %collective-permute-start.8 = (f32[8,24,128]{2,1,0:T(8,128)S(1)}, f32[8,24,128]{2,1,0:T(8,128)S(1)}, u32[]{:S(2)}, u32[]{:S(2)}) collective-permute-start(f32[8,24,128]{2,1,0:T(8,128)S(1)} %get-tuple-element.69), channel_id=1, source_target_pairs={{0,2},{1,3},{2,0},{3,1},{4,6},{5,7},{6,4},{7,5},{8,10},{9,11},{10,... | collective-permute-start | bytes 294920 | tf_op jit(solution)/shard_map/ppermute | solution.py:560
  22.8 3.7 %collective-permute-done.4.refs_3_.refs_4_ = f32[8,32,128]{2,1,0:T(8,128)S(1)} collective-permute-done((f32[8,32,128]{2,1,0:T(8,128)S(1)}, f32[8,32,128]{2,1,0:T(8,128)S(1)}, u32[]{:S(2)}, u32[]{:S(2)}) %collective-permute-start.4) | collective-permute-done | bytes 131104 | tf_op jit(solution)/shard_map/ppermute | solution.py:560
  26.4 0.0 collective-permute-done.2.refs_1_.refs_0_
  26.4 0.7 %pick_13_21.1 = (f32[8,40,128]{2,1,0:T(8,128)S(1)}, f32[8,32,128]{2,1,0:T(8,128)S(1)}, f32[8,128]{1,0:T(8,128)S(1)}) custom-call(s32[24]{0:T(128)S(1)} %get-tuple-element.54.tags, f32[5120,128]{1,0:T(8,128)S(1)} %bitcast.15, f32[8,56,128]{2,1,0:T(8,128)S(1)} %collective-permute-done.3.refs_1_.refs_0_.refs_2_, ...), custom_call_target="tpu_custom_call", output_to_operand_aliasing={{2}: (6, {})} | custom-call | flops 1000000000 | bytes 1000000000 | tf_op jit(solution)/shard_map/pick_13_21/pallas_call | solution.py:624
  27.2 1.6 %collective-permute-start.10 = (f32[8,32,128]{2,1,0:T(8,128)S(1)}, f32[8,32,128]{2,1,0:T(8,128)S(1)}, u32[]{:S(2)}, u32[]{:S(2)}) collective-permute-start(f32[8,32,128]{2,1,0:T(8,128)S(1)} %get-tuple-element.72), channel_id=1, source_target_pairs={{0,2},{1,3},{2,0},{3,1},{4,6},{5,7},{6,4},{7,5},{8,10},{9,11},{10,... | collective-permute-start | bytes 393224 | tf_op jit(solution)/shard_map/ppermute | solution.py:560
  28.7 0.0 collective-permute-start.6
  28.7 0.0 collective-permute-done.8.refs_5_
  28.7 3.0 %collective-permute-done.7.refs_3_.refs_5_ = f32[8,40,128]{2,1,0:T(8,128)S(1)} collective-permute-done((f32[8,40,128]{2,1,0:T(8,128)S(1)}, f32[8,40,128]{2,1,0:T(8,128)S(1)}, u32[]{:S(2)}, u32[]{:S(2)}) %collective-permute-start.7) | collective-permute-done | bytes 163872 | tf_op jit(solution)/shard_map/ppermute | solution.py:560
  31.7 0.7 %pick_14_22.1 = (f32[8,24,128]{2,1,0:T(8,128)S(1)}, f32[8,40,128]{2,1,0:T(8,128)S(1)}, f32[8,128]{1,0:T(8,128)S(1)}, f32[8,24,128]{2,1,0:T(8,128)S(1)}) custom-call(s32[24]{0:T(128)S(1)} %get-tuple-element.54.tags, f32[5120,128]{1,0:T(8,128)S(1)} %bitcast.16, ...), custom_call_target="tpu_custom_call", output_to_operand_aliasing={{2}: (6, {}), {3}: (7, {})} | custom-call | flops 1000000000 | bytes 1000000000 | tf_op jit(solution)/shard_map/pick_14_22/pallas_call | solution.py:624
  32.4 1.6 %collective-permute-start.12 = (f32[8,40,128]{2,1,0:T(8,128)S(1)}, f32[8,40,128]{2,1,0:T(8,128)S(1)}, u32[]{:S(2)}, u32[]{:S(2)}) collective-permute-start(f32[8,40,128]{2,1,0:T(8,128)S(1)} %get-tuple-element.75), channel_id=1, source_target_pairs={{0,2},{1,3},{2,0},{3,1},{4,6},{5,7},{6,4},{7,5},{8,10},{9,11},{10,... | collective-permute-start | bytes 491528 | tf_op jit(solution)/shard_map/ppermute | solution.py:560
  34.0 0.0 collective-permute-start.9
  34.0 0.0 collective-permute-done.10.refs_4_
  34.0 4.8 %collective-permute-done.6.refs_2_.refs_6_.refs_1_ = f32[8,40,128]{2,1,0:T(8,128)S(1)} collective-permute-done((f32[8,40,128]{2,1,0:T(8,128)S(1)}, f32[8,40,128]{2,1,0:T(8,128)S(1)}, u32[]{:S(2)}, u32[]{:S(2)}) %collective-permute-start.6) | collective-permute-done | bytes 163872 | tf_op jit(solution)/shard_map/ppermute | solution.py:560
  38.8 0.6 pick_23.1
  39.5 0.8 %collective-permute-start.11 = (f32[8,40,128]{2,1,0:T(8,128)S(1)}, f32[8,40,128]{2,1,0:T(8,128)S(1)}, u32[]{:S(2)}, u32[]{:S(2)}) collective-permute-start(f32[8,40,128]{2,1,0:T(8,128)S(1)} %get-tuple-element.73), channel_id=1, source_target_pairs={{0,2},{1,3},{2,0},{3,1},{4,6},{5,7},{6,4},{7,5},{8,10},{9,11},{10,... | collective-permute-start | bytes 491528 | tf_op jit(solution)/shard_map/ppermute | solution.py:560
  40.2 0.0 collective-permute-done.9.refs_1_.refs_2_
  40.2 0.0 collective-permute-done.12.refs_3_
  40.3 0.6 pick_24.1
  40.9 1.4 %collective-permute-start.13 = (f32[8,24,128]{2,1,0:T(8,128)S(1)}, f32[8,24,128]{2,1,0:T(8,128)S(1)}, u32[]{:S(2)}, u32[]{:S(2)}) collective-permute-start(f32[8,24,128]{2,1,0:T(8,128)S(1)} %get-tuple-element.76), channel_id=1, source_target_pairs={{0,2},{1,3},{2,0},{3,1},{4,6},{5,7},{6,4},{7,5},{8,10},{9,11},{10,... | collective-permute-start | bytes 294920 | tf_op jit(solution)/shard_map/ppermute | solution.py:560
  42.3 2.6 %collective-permute-done.11.refs_10_.refs_3_ = f32[8,40,128]{2,1,0:T(8,128)S(1)} collective-permute-done((f32[8,40,128]{2,1,0:T(8,128)S(1)}, f32[8,40,128]{2,1,0:T(8,128)S(1)}, u32[]{:S(2)}, u32[]{:S(2)}) %collective-permute-start.11) | collective-permute-done | bytes 163872 | tf_op jit(solution)/shard_map/ppermute | solution.py:560
  44.8 1.6 %assemble_0.1 = (f32[1280,128]{1,0:T(8,128)S(1)}, f32[1280,128]{1,0:T(8,128)S(1)}, f32[5,4,8,128]{3,2,1,0:T(8,128)S(1)}, f32[5,4,8,128]{3,2,1,0:T(8,128)S(1)}, f...) custom-call(s32[24]{0:T(128)S(1)} %get-tuple-element.54.tags, ...), custom_call_target="tpu_custom_call" | custom-call | tf_op jit(solution)/shard_map/assemble_0/pallas_call | solution.py:671
  46.5 0.0 collective-permute-done.13.refs_4_
  46.5 0.9 %assemble_3.1 = (f32[1280,128]{1,0:T(8,128)S(1)}, f32[1280,128]{1,0:T(8,128)S(1)}, f32[5,4,8,128]{3,2,1,0:T(8,128)S(1)}, f32[5,4,8,128]{3,2,1,0:T(8,128)S(1)}, f...) custom-call(s32[24]{0:T(128)S(1)} %get-tuple-element.54.tags, ...), custom_call_target="tpu_custom_call", output_to_operand_aliasing={{0}: (7, {}), {1}: (8, {}), {2}: (9, {}), {3}: (10, {}), {4... | custom-call | tf_op jit(solution)/shard_map/assemble_3/pallas_call | solution.py:671
  47.4 2.8 %collective-permute-start.18 = (f32[2,5,4,8,128]{4,3,2,1,0:T(8,128)S(1)}, f32[2,5,4,8,128]{4,3,2,1,0:T(8,128)S(1)}, u32[]{:S(2)}, u32[]{:S(2)}) collective-permute-start(f32[2,5,4,8,128]{4,3,2,1,0:T(8,128)S(1)} %get-tuple-element.93), channel_id=1, source_target_pairs={{0,16},{16,0},{1,17},{17,1},{2,18},{18,2},{3,19},{19,3},{4,20},{20... | collective-permute-start | bytes 491528 | tf_op jit(solution)/shard_map/ppermute | solution.py:691
  50.2 3.3 %collective-permute-start.14 = (f32[5,4,8,128]{3,2,1,0:T(8,128)S(1)}, f32[5,4,8,128]{3,2,1,0:T(8,128)S(1)}, u32[]{:S(2)}, u32[]{:S(2)}) collective-permute-start(f32[5,4,8,128]{3,2,1,0:T(8,128)S(1)} %get-tuple-element.89.y_one), channel_id=1, source_target_pairs={{0,12},{4,8},{8,4},{12,0},{1,13},{5,9},{9,5},{13,1},{2,14},{6,10},... | collective-permute-start | bytes 245768 | tf_op jit(solution)/shard_map/ppermute | solution.py:696
  53.5 0.0 collective-permute-start.15
  53.5 0.0 collective-permute-start.16
  53.5 1.7 %collective-permute-start.17 = (f32[5,8,128]{2,1,0:T(8,128)S(1)}, f32[5,8,128]{2,1,0:T(8,128)S(1)}, u32[]{:S(2)}, u32[]{:S(2)}) collective-permute-start(f32[5,8,128]{2,1,0:T(8,128)S(1)} %get-tuple-element.92), channel_id=1, source_target_pairs={{0,3},{1,0},{2,1},{3,2},{4,7},{5,4},{6,5},{7,6},{8,11},{9,8},{10,9... | collective-permute-start | bytes 61448 | tf_op jit(solution)/shard_map/ppermute | solution.py:691
  55.2 0.0 collective-permute-done.18.x_faces
  55.2 0.6 sweep_x.2.sofar
  55.8 0.9 %collective-permute-done.16.z_prev = f32[5,8,128]{2,1,0:T(8,128)S(1)} collective-permute-done((f32[5,8,128]{2,1,0:T(8,128)S(1)}, f32[5,8,128]{2,1,0:T(8,128)S(1)}, u32[]{:S(2)}, u32[]{:S(2)}) %collective-permute-start.16) | collective-permute-done | bytes 20512 | tf_op jit(solution)/shard_map/ppermute | solution.py:691
  56.7 0.0 collective-permute-done.17.z_next
  56.7 1.9 %sweep_z.2.sofar = f32[1280,128]{1,0:T(8,128)S(1)} custom-call(f32[1280,128]{1,0:T(8,128)S(1)} %get-tuple-element.88.prim, f32[5,8,128]{2,1,0:T(8,128)S(1)} %collective-permute-done.16.z_prev, f32[5,8,128]{2,1,0:T(8,128)S(1)} %collective-permute-done.17.z_next, f32[1280,128]{1,0:T(8,128)S(1)} %sweep_x.2.sofar), custom_call_target="tpu_custom_call", output_to_operand_aliasing={{}: (3, {})} | custom-call | flops 1 | bytes 1 | tf_op jit(solution)/shard_map/sweep_z/pallas_call | solution.py:716
  58.6 0.0 collective-permute-done.14.got_one
  58.6 0.0 collective-permute-done.15.got_two
  58.6 1.3 %sweep_y_one.1 = (f32[1280,128]{1,0:T(8,128)S(1)}, f32[1280,128]{1,0:T(8,128)S(1)}, f32[2,5,4,8,128]{4,3,2,1,0:T(8,128)S(1)}, f32[5,4,8,128]{3,2,1,0:T(8,128)S(1...) custom-call(f32[1280,128]{1,0:T(8,128)S(1)} %get-tuple-element.87.field, ...), custom_call_target="tpu_custom_call" | custom-call | tf_op jit(solution)/shard_map/sweep_y_one/pallas_call | solution.py:733
  60.0 0.8 %collective-permute-start.23 = (f32[2,5,4,8,128]{4,3,2,1,0:T(8,128)S(1)}, f32[2,5,4,8,128]{4,3,2,1,0:T(8,128)S(1)}, u32[]{:S(2)}, u32[]{:S(2)}) collective-permute-start(f32[2,5,4,8,128]{4,3,2,1,0:T(8,128)S(1)} %get-tuple-element.100), channel_id=1, source_target_pairs={{0,16},{16,0},{1,17},{17,1},{2,18},{18,2},{3,19},{19,3},{4,20},{20... | collective-permute-start | bytes 491528 | tf_op jit(solution)/shard_map/ppermute | solution.py:691
  60.8 1.9 %collective-permute-start.19 = (f32[5,4,8,128]{3,2,1,0:T(8,128)S(1)}, f32[5,4,8,128]{3,2,1,0:T(8,128)S(1)}, u32[]{:S(2)}, u32[]{:S(2)}) collective-permute-start(f32[5,4,8,128]{3,2,1,0:T(8,128)S(1)} %get-tuple-element.96.y_one), channel_id=1, source_target_pairs={{0,12},{4,8},{8,4},{12,0},{1,13},{5,9},{9,5},{13,1},{2,14},{6,10},... | collective-permute-start | bytes 245768 | tf_op jit(solution)/shard_map/ppermute | solution.py:696
  62.7 0.1 collective-permute-start.20
  62.8 0.8 %collective-permute-start.21 = (f32[5,8,128]{2,1,0:T(8,128)S(1)}, f32[5,8,128]{2,1,0:T(8,128)S(1)}, u32[]{:S(2)}, u32[]{:S(2)}) collective-permute-start(f32[5,8,128]{2,1,0:T(8,128)S(1)} %get-tuple-element.98), channel_id=1, source_target_pairs={{0,1},{1,2},{2,3},{3,0},{4,5},{5,6},{6,7},{7,4},{8,9},{9,10},{10,1... | collective-permute-start | bytes 61448 | tf_op jit(solution)/shard_map/ppermute | solution.py:691
  63.6 0.9 %collective-permute-start.22 = (f32[5,8,128]{2,1,0:T(8,128)S(1)}, f32[5,8,128]{2,1,0:T(8,128)S(1)}, u32[]{:S(2)}, u32[]{:S(2)}) collective-permute-start(f32[5,8,128]{2,1,0:T(8,128)S(1)} %get-tuple-element.99), channel_id=1, source_target_pairs={{0,3},{1,0},{2,1},{3,2},{4,7},{5,4},{6,5},{7,6},{8,11},{9,8},{10,9... | collective-permute-start | bytes 61448 | tf_op jit(solution)/shard_map/ppermute | solution.py:691
  64.5 2.0 %collective-permute-done.23.x_faces = f32[2,5,4,8,128]{4,3,2,1,0:T(8,128)S(1)} collective-permute-done((f32[2,5,4,8,128]{4,3,2,1,0:T(8,128)S(1)}, f32[2,5,4,8,128]{4,3,2,1,0:T(8,128)S(1)}, u32[]{:S(2)}, u32[]{:S(2)}) %collective-permute-start.23) | collective-permute-done | bytes 163872 | tf_op jit(solution)/shard_map/ppermute | solution.py:691
  66.5 0.6 sweep_x.3.sofar
  67.0 0.0 collective-permute-done.22.z_next
  67.1 1.9 %sweep_z.3.sofar = f32[1280,128]{1,0:T(8,128)S(1)} custom-call(f32[1280,128]{1,0:T(8,128)S(1)} %get-tuple-element.95.prim, f32[5,8,128]{2,1,0:T(8,128)S(1)} %collective-permute-done.21.z_prev, f32[5,8,128]{2,1,0:T(8,128)S(1)} %collective-permute-done.22.z_next, f32[1280,128]{1,0:T(8,128)S(1)} %sweep_x.3.sofar), custom_call_target="tpu_custom_call", output_to_operand_aliasing={{}: (3, {})} | custom-call | flops 1 | bytes 1 | tf_op jit(solution)/shard_map/sweep_z/pallas_call | solution.py:716
  68.9 0.0 collective-permute-done.19.got_one
  68.9 2.8 %sweep_y_two.1 = (f32[20,256,128]{2,1,0:T(8,128)}, f32[20,256,128]{2,1,0:T(8,128)S(1)}) custom-call(s32[8]{0:T(128)} %copy-done.2, f32[1280,128]{1,0:T(8,128)S(1)} %get-tuple-element.87.field, f32[1280,128]{1,0:T(8,128)S(1)} %get-tuple-element.94.one, f32[1280,128]{1,0:T(8,128)S(1)} %get-tuple-element.95.prim, ...), custom_call_target="tpu_custom_call", output_to_operand_aliasing={{1}: (9, {})} | custom-call | tf_op jit(solution)/shard_map/sweep_y_two/pallas_call | solution.py:744
  (12 shorter events, 0.0 us)
Async XLA Ops:
  0.0 4.4 %copy-start.1 = (s32[3,1,8]{2,1,0:T(1,128)S(1)}, s32[3,1,8]{2,1,0:T(1,128)}, u32[]{:S(2)}) copy-start(s32[3,1,8]{2,1,0:T(1,128)} %send_hbm.1) | copy-start | bytes 292
  0.0 4.4 %copy-start = (f32[32,5,4096]{2,0,1:T(8,128)S(1)}, f32[32,5,4096]{2,0,1:T(8,128)}, u32[]{:S(2)}) copy-start(f32[32,5,4096]{2,0,1:T(8,128)} %param.4) | copy-start | bytes 7864324
  0.0 4.3 %copy-start.4 = (s32[256]{0:T(256)S(1)}, s32[256]{0:T(256)}, u32[]{:S(2)}) copy-start(s32[256]{0:T(256)} %param.7) | copy-start | bytes 3076
  0.0 4.4 %copy-start.3 = (s32[3,1,8]{2,1,0:T(1,128)S(1)}, s32[3,1,8]{2,1,0:T(1,128)}, u32[]{:S(2)}) copy-start(s32[3,1,8]{2,1,0:T(1,128)} %recv.1) | copy-start | bytes 292
  1.3 5.8 %collective-permute-start.1 = (f32[8,24,128]{2,1,0:T(8,128)S(1)}, f32[8,24,128]{2,1,0:T(8,128)S(1)}, u32[]{:S(2)}, u32[]{:S(2)}) collective-permute-start(f32[8,24,128]{2,1,0:T(8,128)S(1)} %pack_first.1), channel_id=1, source_target_pairs={{0,16},{1,17},{2,18},{3,19},{4,20},{5,21},{6,22},{7,23},{8,24},{9,... | collective-permute-start | bytes 294920 | tf_op jit(solution)/shard_map/ppermute | solution.py:560
  4.4 3.3 %copy-start.2 = (s32[8]{0:T(128)}, s32[8]{0:T(128)S(1)}, u32[]{:S(2)}) copy-start(s32[8]{0:T(128)S(1)} %dynamic_slice.3.own.own_there) | copy-start | bytes 100
  5.8 7.2 %collective-permute-start = (f32[8,40,128]{2,1,0:T(8,128)S(1)}, f32[8,40,128]{2,1,0:T(8,128)S(1)}, u32[]{:S(2)}, u32[]{:S(2)}) collective-permute-start(f32[8,40,128]{2,1,0:T(8,128)S(1)} %get-tuple-element.55), channel_id=1, source_target_pairs={{0,16},{1,17},{2,18},{3,19},{4,20},{5,21},{6,22},{7,23},{8,24},{9,... | collective-permute-start | bytes 491528 | tf_op jit(solution)/shard_map/ppermute | solution.py:560
  7.7 10.2 %collective-permute-start.3 = (f32[8,56,128]{2,1,0:T(8,128)S(1)}, f32[8,56,128]{2,1,0:T(8,128)S(1)}, u32[]{:S(2)}, u32[]{:S(2)}) collective-permute-start(f32[8,56,128]{2,1,0:T(8,128)S(1)} %get-tuple-element.61), channel_id=1, source_target_pairs={{0,16},{1,17},{2,18},{3,19},{4,20},{5,21},{6,22},{7,23},{8,24},{9,... | collective-permute-start | bytes 688136 | tf_op jit(solution)/shard_map/ppermute | solution.py:560
  9.7 7.1 %collective-permute-start.5 = (f32[8,24,128]{2,1,0:T(8,128)S(1)}, f32[8,24,128]{2,1,0:T(8,128)S(1)}, u32[]{:S(2)}, u32[]{:S(2)}) collective-permute-start(f32[8,24,128]{2,1,0:T(8,128)S(1)} %get-tuple-element.63), channel_id=1, source_target_pairs={{0,8},{1,9},{2,10},{3,11},{4,12},{5,13},{6,14},{7,15},{8,0},{9,1},... | collective-permute-start | bytes 294920 | tf_op jit(solution)/shard_map/ppermute | solution.py:560
  13.6 12.8 %collective-permute-start.2 = (f32[8,40,128]{2,1,0:T(8,128)S(1)}, f32[8,40,128]{2,1,0:T(8,128)S(1)}, u32[]{:S(2)}, u32[]{:S(2)}) collective-permute-start(f32[8,40,128]{2,1,0:T(8,128)S(1)} %get-tuple-element.60), channel_id=1, source_target_pairs={{0,16},{1,17},{2,18},{3,19},{4,20},{5,21},{6,22},{7,23},{8,24},{9,... | collective-permute-start | bytes 491528 | tf_op jit(solution)/shard_map/ppermute | solution.py:560
  14.2 12.3 %collective-permute-start.4 = (f32[8,32,128]{2,1,0:T(8,128)S(1)}, f32[8,32,128]{2,1,0:T(8,128)S(1)}, u32[]{:S(2)}, u32[]{:S(2)}) collective-permute-start(f32[8,32,128]{2,1,0:T(8,128)S(1)} %get-tuple-element.62), channel_id=1, source_target_pairs={{0,8},{1,9},{2,10},{3,11},{4,12},{5,13},{6,14},{7,15},{8,0},{9,1},... | collective-permute-start | bytes 393224 | tf_op jit(solution)/shard_map/ppermute | solution.py:560
  18.6 13.1 %collective-permute-start.7 = (f32[8,40,128]{2,1,0:T(8,128)S(1)}, f32[8,40,128]{2,1,0:T(8,128)S(1)}, u32[]{:S(2)}, u32[]{:S(2)}) collective-permute-start(f32[8,40,128]{2,1,0:T(8,128)S(1)} %get-tuple-element.67), channel_id=1, source_target_pairs={{0,8},{1,9},{2,10},{3,11},{4,12},{5,13},{6,14},{7,15},{8,0},{9,1},... | collective-permute-start | bytes 491528 | tf_op jit(solution)/shard_map/ppermute | solution.py:560
  21.3 7.5 %collective-permute-start.8 = (f32[8,24,128]{2,1,0:T(8,128)S(1)}, f32[8,24,128]{2,1,0:T(8,128)S(1)}, u32[]{:S(2)}, u32[]{:S(2)}) collective-permute-start(f32[8,24,128]{2,1,0:T(8,128)S(1)} %get-tuple-element.69), channel_id=1, source_target_pairs={{0,2},{1,3},{2,0},{3,1},{4,6},{5,7},{6,4},{7,5},{8,10},{9,11},{10,... | collective-permute-start | bytes 294920 | tf_op jit(solution)/shard_map/ppermute | solution.py:560
  27.2 6.8 %collective-permute-start.10 = (f32[8,32,128]{2,1,0:T(8,128)S(1)}, f32[8,32,128]{2,1,0:T(8,128)S(1)}, u32[]{:S(2)}, u32[]{:S(2)}) collective-permute-start(f32[8,32,128]{2,1,0:T(8,128)S(1)} %get-tuple-element.72), channel_id=1, source_target_pairs={{0,2},{1,3},{2,0},{3,1},{4,6},{5,7},{6,4},{7,5},{8,10},{9,11},{10,... | collective-permute-start | bytes 393224 | tf_op jit(solution)/shard_map/ppermute | solution.py:560
  28.7 10.1 %collective-permute-start.6 = (f32[8,40,128]{2,1,0:T(8,128)S(1)}, f32[8,40,128]{2,1,0:T(8,128)S(1)}, u32[]{:S(2)}, u32[]{:S(2)}) collective-permute-start(f32[8,40,128]{2,1,0:T(8,128)S(1)} %get-tuple-element.66), channel_id=1, source_target_pairs={{0,8},{1,9},{2,10},{3,11},{4,12},{5,13},{6,14},{7,15},{8,0},{9,1},... | collective-permute-start | bytes 491528 | tf_op jit(solution)/shard_map/ppermute | solution.py:560
  32.4 7.8 %collective-permute-start.12 = (f32[8,40,128]{2,1,0:T(8,128)S(1)}, f32[8,40,128]{2,1,0:T(8,128)S(1)}, u32[]{:S(2)}, u32[]{:S(2)}) collective-permute-start(f32[8,40,128]{2,1,0:T(8,128)S(1)} %get-tuple-element.75), channel_id=1, source_target_pairs={{0,2},{1,3},{2,0},{3,1},{4,6},{5,7},{6,4},{7,5},{8,10},{9,11},{10,... | collective-permute-start | bytes 491528 | tf_op jit(solution)/shard_map/ppermute | solution.py:560
  34.0 6.3 %collective-permute-start.9 = (f32[8,24,128]{2,1,0:T(8,128)S(1)}, f32[8,24,128]{2,1,0:T(8,128)S(1)}, u32[]{:S(2)}, u32[]{:S(2)}) collective-permute-start(f32[8,24,128]{2,1,0:T(8,128)S(1)} %get-tuple-element.70), channel_id=1, source_target_pairs={{0,8},{1,9},{2,10},{3,11},{4,12},{5,13},{6,14},{7,15},{8,0},{9,1},... | collective-permute-start | bytes 294920 | tf_op jit(solution)/shard_map/ppermute | solution.py:560
  39.5 5.4 %collective-permute-start.11 = (f32[8,40,128]{2,1,0:T(8,128)S(1)}, f32[8,40,128]{2,1,0:T(8,128)S(1)}, u32[]{:S(2)}, u32[]{:S(2)}) collective-permute-start(f32[8,40,128]{2,1,0:T(8,128)S(1)} %get-tuple-element.73), channel_id=1, source_target_pairs={{0,2},{1,3},{2,0},{3,1},{4,6},{5,7},{6,4},{7,5},{8,10},{9,11},{10,... | collective-permute-start | bytes 491528 | tf_op jit(solution)/shard_map/ppermute | solution.py:560
  40.9 5.6 %collective-permute-start.13 = (f32[8,24,128]{2,1,0:T(8,128)S(1)}, f32[8,24,128]{2,1,0:T(8,128)S(1)}, u32[]{:S(2)}, u32[]{:S(2)}) collective-permute-start(f32[8,24,128]{2,1,0:T(8,128)S(1)} %get-tuple-element.76), channel_id=1, source_target_pairs={{0,2},{1,3},{2,0},{3,1},{4,6},{5,7},{6,4},{7,5},{8,10},{9,11},{10,... | collective-permute-start | bytes 294920 | tf_op jit(solution)/shard_map/ppermute | solution.py:560
  47.4 7.9 %collective-permute-start.18 = (f32[2,5,4,8,128]{4,3,2,1,0:T(8,128)S(1)}, f32[2,5,4,8,128]{4,3,2,1,0:T(8,128)S(1)}, u32[]{:S(2)}, u32[]{:S(2)}) collective-permute-start(f32[2,5,4,8,128]{4,3,2,1,0:T(8,128)S(1)} %get-tuple-element.93), channel_id=1, source_target_pairs={{0,16},{16,0},{1,17},{17,1},{2,18},{18,2},{3,19},{19,3},{4,20},{20... | collective-permute-start | bytes 491528 | tf_op jit(solution)/shard_map/ppermute | solution.py:691
  50.2 8.4 %collective-permute-start.14 = (f32[5,4,8,128]{3,2,1,0:T(8,128)S(1)}, f32[5,4,8,128]{3,2,1,0:T(8,128)S(1)}, u32[]{:S(2)}, u32[]{:S(2)}) collective-permute-start(f32[5,4,8,128]{3,2,1,0:T(8,128)S(1)} %get-tuple-element.89.y_one), channel_id=1, source_target_pairs={{0,12},{4,8},{8,4},{12,0},{1,13},{5,9},{9,5},{13,1},{2,14},{6,10},... | collective-permute-start | bytes 245768 | tf_op jit(solution)/shard_map/ppermute | solution.py:696
  53.5 5.2 %collective-permute-start.15 = (f32[5,4,8,128]{3,2,1,0:T(8,128)S(1)}, f32[5,4,8,128]{3,2,1,0:T(8,128)S(1)}, u32[]{:S(2)}, u32[]{:S(2)}) collective-permute-start(f32[5,4,8,128]{3,2,1,0:T(8,128)S(1)} %get-tuple-element.90.y_two), channel_id=1, source_target_pairs={{0,4},{4,0},{8,12},{12,8},{1,5},{5,1},{9,13},{13,9},{2,6},{6,2},{1... | collective-permute-start | bytes 245768 | tf_op jit(solution)/shard_map/ppermute | solution.py:696
  53.5 3.2 %collective-permute-start.16 = (f32[5,8,128]{2,1,0:T(8,128)S(1)}, f32[5,8,128]{2,1,0:T(8,128)S(1)}, u32[]{:S(2)}, u32[]{:S(2)}) collective-permute-start(f32[5,8,128]{2,1,0:T(8,128)S(1)} %get-tuple-element.91), channel_id=1, source_target_pairs={{0,1},{1,2},{2,3},{3,0},{4,5},{5,6},{6,7},{7,4},{8,9},{9,10},{10,1... | collective-permute-start | bytes 61448 | tf_op jit(solution)/shard_map/ppermute | solution.py:691
  53.5 3.2 %collective-permute-start.17 = (f32[5,8,128]{2,1,0:T(8,128)S(1)}, f32[5,8,128]{2,1,0:T(8,128)S(1)}, u32[]{:S(2)}, u32[]{:S(2)}) collective-permute-start(f32[5,8,128]{2,1,0:T(8,128)S(1)} %get-tuple-element.92), channel_id=1, source_target_pairs={{0,3},{1,0},{2,1},{3,2},{4,7},{5,4},{6,5},{7,6},{8,11},{9,8},{10,9... | collective-permute-start | bytes 61448 | tf_op jit(solution)/shard_map/ppermute | solution.py:691
  60.0 6.5 %collective-permute-start.23 = (f32[2,5,4,8,128]{4,3,2,1,0:T(8,128)S(1)}, f32[2,5,4,8,128]{4,3,2,1,0:T(8,128)S(1)}, u32[]{:S(2)}, u32[]{:S(2)}) collective-permute-start(f32[2,5,4,8,128]{4,3,2,1,0:T(8,128)S(1)} %get-tuple-element.100), channel_id=1, source_target_pairs={{0,16},{16,0},{1,17},{17,1},{2,18},{18,2},{3,19},{19,3},{4,20},{20... | collective-permute-start | bytes 491528 | tf_op jit(solution)/shard_map/ppermute | solution.py:691
  60.8 8.2 %collective-permute-start.19 = (f32[5,4,8,128]{3,2,1,0:T(8,128)S(1)}, f32[5,4,8,128]{3,2,1,0:T(8,128)S(1)}, u32[]{:S(2)}, u32[]{:S(2)}) collective-permute-start(f32[5,4,8,128]{3,2,1,0:T(8,128)S(1)} %get-tuple-element.96.y_one), channel_id=1, source_target_pairs={{0,12},{4,8},{8,4},{12,0},{1,13},{5,9},{9,5},{13,1},{2,14},{6,10},... | collective-permute-start | bytes 245768 | tf_op jit(solution)/shard_map/ppermute | solution.py:696
  62.7 6.2 %collective-permute-start.20 = (f32[5,4,8,128]{3,2,1,0:T(8,128)S(1)}, f32[5,4,8,128]{3,2,1,0:T(8,128)S(1)}, u32[]{:S(2)}, u32[]{:S(2)}) collective-permute-start(f32[5,4,8,128]{3,2,1,0:T(8,128)S(1)} %get-tuple-element.97.y_two), channel_id=1, source_target_pairs={{0,4},{4,0},{8,12},{12,8},{1,5},{5,1},{9,13},{13,9},{2,6},{6,2},{1... | collective-permute-start | bytes 245768 | tf_op jit(solution)/shard_map/ppermute | solution.py:696
  62.8 4.3 %collective-permute-start.21 = (f32[5,8,128]{2,1,0:T(8,128)S(1)}, f32[5,8,128]{2,1,0:T(8,128)S(1)}, u32[]{:S(2)}, u32[]{:S(2)}) collective-permute-start(f32[5,8,128]{2,1,0:T(8,128)S(1)} %get-tuple-element.98), channel_id=1, source_target_pairs={{0,1},{1,2},{2,3},{3,0},{4,5},{5,6},{6,7},{7,4},{8,9},{9,10},{10,1... | collective-permute-start | bytes 61448 | tf_op jit(solution)/shard_map/ppermute | solution.py:691
  63.6 3.5 %collective-permute-start.22 = (f32[5,8,128]{2,1,0:T(8,128)S(1)}, f32[5,8,128]{2,1,0:T(8,128)S(1)}, u32[]{:S(2)}, u32[]{:S(2)}) collective-permute-start(f32[5,8,128]{2,1,0:T(8,128)S(1)} %get-tuple-element.99), channel_id=1, source_target_pairs={{0,3},{1,0},{2,1},{3,2},{4,7},{5,4},{6,5},{7,6},{8,11},{9,8},{10,9... | collective-permute-start | bytes 61448 | tf_op jit(solution)/shard_map/ppermute | solution.py:691

commit v13 on v12

--- a/solution.py
+++ b/solution.py
@@ -546,7 +546,7 @@
     groups = slots // SUB
     shape = Shape(rows, edge)
     units = NF * shape.slabs
-    cuts = [split_units(units, shares) for shares in ((3, 5, 7, 5), (3, 4, 5, 5, 3), (3, 4, 5, 5, 3))]
+    cuts = [split_units(units, shares) for shares in ((3, 5, 7, 5), (3, 4, 5, 4, 4), (3, 4, 5, 4, 4))]
     firsts, final = cuts[0], cuts[2]
 
     bit_z = size_z.bit_length() - 2

time: 72.3 us -> 72.8 us (level)
  starting transfers between devices: 33.2 us -> 35.2 us
  waiting for transfers between devices: 19.4 us -> 18.4 us
    ppermute x4, starting transfers between devices: 5.31 us -> 7.79 us  [beside(): return lax.ppermute(value, axis, [(i, j % size) for i, j in pairs])]
    ppermute x14, waiting for transfers between devices: 16.5 us -> 14.9 us  [swapped(): return lax.ppermute(value, AXES, pairs)]
    ppermute x6, starting transfers between devices: 7.11 us -> 6.27 us  [ring(): lax.ppermute(value, axis, [(i, (i + step) % size) for i in range(size)])]
where the time goes in v13:
time: 72.8 us; the launch traced here: 72.7 us
  starting transfers between devices  35.2 us (48%)
  Pallas kernels  18.8 us (26%)
  waiting for transfers between devices  18.4 us (25%)
    ppermute x14, starting transfers between devices, swapped(): return lax.ppermute(value, AXES, pairs)  21.2 us
    ppermute x14, waiting for transfers between devices, swapped(): return lax.ppermute(value, AXES, pairs)  14.9 us
    ppermute x4, starting transfers between devices, beside(): return lax.ppermute(value, axis, [(i, j % size) for i, j in pairs])  7.79 us
    ppermute x6, starting transfers between devices, ring(): lax.ppermute(value, axis, [(i, (i + step) % size) for i in range(size)])  6.27 us
    pallas_call x7, Pallas kernels, make(): pl.pallas_call(functools.partial(pick_kernel, plan=plan, held=tuple(found...  4.68 us
    pallas_call x2, Pallas kernels, flux_sums(): pl.pallas_call(functools.partial(sweep_z_kernel, shape=shape), out_shape=...  3.76 us
    ppermute x6, waiting for transfers between devices, ring(): lax.ppermute(value, axis, [(i, (i + step) % size) for i in range(size)])  3.47 us
    pallas_call x1, Pallas kernels, shards(): pl.pallas_call(functools.partial(sweep_y_two_kernel, shape=shape, occ=occ...  2.8 us
  transfers between devices with their start and end apart: 24, of which 9 were waited for; matrix products, arithmetic and copies ran while one was open for 0% of the time, Pallas kernels for 17%

profile of v13, /device:TPU:0, one launch (start us, length us, event | category | flops | bytes accessed | tf_op | source)
XLA Modules:
  0.0 72.7 jit_solution(8215572957627462985)
XLA Ops:
  0.0 1.2 %pack_first.1 = f32[8,24,128]{2,1,0:T(8,128)S(1)} custom-call(s32[3,1,8]{2,1,0:T(1,128)} %send_hbm.1, f32[5120,128]{1,0:T(8,128)} %bitcast.10), custom_call_target="tpu_custom_call" | custom-call | tf_op jit(solution)/shard_map/pack_first/pallas_call | solution.py:579
  1.3 3.0 %collective-permute-start.1 = (f32[8,24,128]{2,1,0:T(8,128)S(1)}, f32[8,24,128]{2,1,0:T(8,128)S(1)}, u32[]{:S(2)}, u32[]{:S(2)}) collective-permute-start(f32[8,24,128]{2,1,0:T(8,128)S(1)} %pack_first.1), channel_id=1, source_target_pairs={{0,16},{1,17},{2,18},{3,19},{4,20},{5,21},{6,22},{7,23},{8,24},{9,... | collective-permute-start | bytes 294920 | tf_op jit(solution)/shard_map/ppermute | solution.py:560
  4.3 0.1 dynamic_slice.3.own.own_there
  4.4 1.4 %pack_rest.1 = (s32[24]{0:T(128)S(1)}, f32[8,128]{1,0:T(8,128)S(1)}, f32[8,40,128]{2,1,0:T(8,128)S(1)}, f32[8,56,128]{2,1,0:T(8,128)S(1)}, f32[8,40,128]{2,1,0:T(8,128)S(1)}) custom-call(s32[3,1,8]{2,1,0:T(1,128)S(1)} %copy-done.1, s32[3,1,8]{2,1,0:T(1,128)S(1)} %copy-done.3, s32[8]{0:T(128)S(1)} %dynamic_slice.3.own.own_there, f32[5120,128]{1,0:T(8,128)S(1)} %bitcast.11), custom_call_target="tpu_custom_call" | custom-call | tf_op jit(solution)/shard_map/pack_rest/pallas_call | solution.py:592
  5.8 0.6 collective-permute-start
  6.4 0.7 collective-permute-done.1.refs_0_.refs_2_
  7.1 0.6 pick_10.1
  7.7 2.0 %collective-permute-start.3 = (f32[8,56,128]{2,1,0:T(8,128)S(1)}, f32[8,56,128]{2,1,0:T(8,128)S(1)}, u32[]{:S(2)}, u32[]{:S(2)}) collective-permute-start(f32[8,56,128]{2,1,0:T(8,128)S(1)} %get-tuple-element.61), channel_id=1, source_target_pairs={{0,16},{1,17},{2,18},{3,19},{4,20},{5,21},{6,22},{7,23},{8,24},{9,... | collective-permute-start | bytes 688136 | tf_op jit(solution)/shard_map/ppermute | solution.py:560
  9.7 2.6 %collective-permute-start.5 = (f32[8,24,128]{2,1,0:T(8,128)S(1)}, f32[8,24,128]{2,1,0:T(8,128)S(1)}, u32[]{:S(2)}, u32[]{:S(2)}) collective-permute-start(f32[8,24,128]{2,1,0:T(8,128)S(1)} %get-tuple-element.63), channel_id=1, source_target_pairs={{0,8},{1,9},{2,10},{3,11},{4,12},{5,13},{6,14},{7,15},{8,0},{9,1},... | collective-permute-start | bytes 294920 | tf_op jit(solution)/shard_map/ppermute | solution.py:560
  12.3 0.7 collective-permute-done.refs_0_.refs_2_.refs_1_
  13.0 0.6 pick_11.1
  13.6 0.6 collective-permute-start.2
  14.2 2.6 %collective-permute-start.4 = (f32[8,32,128]{2,1,0:T(8,128)S(1)}, f32[8,32,128]{2,1,0:T(8,128)S(1)}, u32[]{:S(2)}, u32[]{:S(2)}) collective-permute-start(f32[8,32,128]{2,1,0:T(8,128)S(1)} %get-tuple-element.62), channel_id=1, source_target_pairs={{0,8},{1,9},{2,10},{3,11},{4,12},{5,13},{6,14},{7,15},{8,0},{9,1},... | collective-permute-start | bytes 393224 | tf_op jit(solution)/shard_map/ppermute | solution.py:560
  16.8 0.0 collective-permute-done.5.refs_3_
  16.8 1.1 %collective-permute-done.3.refs_1_.refs_0_.refs_2_ = f32[8,56,128]{2,1,0:T(8,128)S(1)} collective-permute-done((f32[8,56,128]{2,1,0:T(8,128)S(1)}, f32[8,56,128]{2,1,0:T(8,128)S(1)}, u32[]{:S(2)}, u32[]{:S(2)}) %collective-permute-start.3) | collective-permute-done | bytes 229408 | tf_op jit(solution)/shard_map/ppermute | solution.py:560
  17.9 0.7 pick_12_20.1
  18.6 2.7 %collective-permute-start.7 = (f32[8,40,128]{2,1,0:T(8,128)S(1)}, f32[8,40,128]{2,1,0:T(8,128)S(1)}, u32[]{:S(2)}, u32[]{:S(2)}) collective-permute-start(f32[8,40,128]{2,1,0:T(8,128)S(1)} %get-tuple-element.67), channel_id=1, source_target_pairs={{0,8},{1,9},{2,10},{3,11},{4,12},{5,13},{6,14},{7,15},{8,0},{9,1},... | collective-permute-start | bytes 491528 | tf_op jit(solution)/shard_map/ppermute | solution.py:560
  21.3 1.5 %collective-permute-start.8 = (f32[8,24,128]{2,1,0:T(8,128)S(1)}, f32[8,24,128]{2,1,0:T(8,128)S(1)}, u32[]{:S(2)}, u32[]{:S(2)}) collective-permute-start(f32[8,24,128]{2,1,0:T(8,128)S(1)} %get-tuple-element.69), channel_id=1, source_target_pairs={{0,2},{1,3},{2,0},{3,1},{4,6},{5,7},{6,4},{7,5},{8,10},{9,11},{10,... | collective-permute-start | bytes 294920 | tf_op jit(solution)/shard_map/ppermute | solution.py:560
  22.8 3.7 %collective-permute-done.4.refs_3_.refs_4_ = f32[8,32,128]{2,1,0:T(8,128)S(1)} collective-permute-done((f32[8,32,128]{2,1,0:T(8,128)S(1)}, f32[8,32,128]{2,1,0:T(8,128)S(1)}, u32[]{:S(2)}, u32[]{:S(2)}) %collective-permute-start.4) | collective-permute-done | bytes 131104 | tf_op jit(solution)/shard_map/ppermute | solution.py:560
  26.4 0.0 collective-permute-done.2.refs_1_.refs_0_
  26.4 0.7 pick_13_21.1
  27.2 0.1 collective-permute-start.6
  27.2 1.6 %collective-permute-start.10 = (f32[8,32,128]{2,1,0:T(8,128)S(1)}, f32[8,32,128]{2,1,0:T(8,128)S(1)}, u32[]{:S(2)}, u32[]{:S(2)}) collective-permute-start(f32[8,32,128]{2,1,0:T(8,128)S(1)} %get-tuple-element.72), channel_id=1, source_target_pairs={{0,2},{1,3},{2,0},{3,1},{4,6},{5,7},{6,4},{7,5},{8,10},{9,11},{10,... | collective-permute-start | bytes 393224 | tf_op jit(solution)/shard_map/ppermute | solution.py:560
  28.8 0.0 collective-permute-done.8.refs_5_
  28.8 2.5 %collective-permute-done.7.refs_3_.refs_5_ = f32[8,40,128]{2,1,0:T(8,128)S(1)} collective-permute-done((f32[8,40,128]{2,1,0:T(8,128)S(1)}, f32[8,40,128]{2,1,0:T(8,128)S(1)}, u32[]{:S(2)}, u32[]{:S(2)}) %collective-permute-start.7) | collective-permute-done | bytes 163872 | tf_op jit(solution)/shard_map/ppermute | solution.py:560
  31.4 0.7 pick_14_22.1
  32.1 1.6 %collective-permute-start.12 = (f32[8,40,128]{2,1,0:T(8,128)S(1)}, f32[8,40,128]{2,1,0:T(8,128)S(1)}, u32[]{:S(2)}, u32[]{:S(2)}) collective-permute-start(f32[8,40,128]{2,1,0:T(8,128)S(1)} %get-tuple-element.75), channel_id=1, source_target_pairs={{0,2},{1,3},{2,0},{3,1},{4,6},{5,7},{6,4},{7,5},{8,10},{9,11},{10,... | collective-permute-start | bytes 491528 | tf_op jit(solution)/shard_map/ppermute | solution.py:560
  33.6 0.0 collective-permute-start.9
  33.6 0.0 collective-permute-done.6.refs_2_.refs_6_.refs_1_
  33.6 0.0 collective-permute-done.10.refs_4_
  33.6 0.6 pick_23.1
  34.3 1.0 %collective-permute-start.11 = (f32[8,32,128]{2,1,0:T(8,128)S(1)}, f32[8,32,128]{2,1,0:T(8,128)S(1)}, u32[]{:S(2)}, u32[]{:S(2)}) collective-permute-start(f32[8,32,128]{2,1,0:T(8,128)S(1)} %get-tuple-element.73), channel_id=1, source_target_pairs={{0,2},{1,3},{2,0},{3,1},{4,6},{5,7},{6,4},{7,5},{8,10},{9,11},{10,... | collective-permute-start | bytes 393224 | tf_op jit(solution)/shard_map/ppermute | solution.py:560
  35.3 4.2 %collective-permute-done.9.refs_1_.refs_2_ = f32[8,32,128]{2,1,0:T(8,128)S(1)} collective-permute-done((f32[8,32,128]{2,1,0:T(8,128)S(1)}, f32[8,32,128]{2,1,0:T(8,128)S(1)}, u32[]{:S(2)}, u32[]{:S(2)}) %collective-permute-start.9) | collective-permute-done | bytes 131104 | tf_op jit(solution)/shard_map/ppermute | solution.py:560
  39.5 0.0 collective-permute-done.12.refs_3_
  39.5 0.6 pick_24.1
  40.2 1.4 %collective-permute-start.13 = (f32[8,32,128]{2,1,0:T(8,128)S(1)}, f32[8,32,128]{2,1,0:T(8,128)S(1)}, u32[]{:S(2)}, u32[]{:S(2)}) collective-permute-start(f32[8,32,128]{2,1,0:T(8,128)S(1)} %get-tuple-element.76), channel_id=1, source_target_pairs={{0,2},{1,3},{2,0},{3,1},{4,6},{5,7},{6,4},{7,5},{8,10},{9,11},{10,... | collective-permute-start | bytes 393224 | tf_op jit(solution)/shard_map/ppermute | solution.py:560
  41.6 1.6 %assemble_0.1 = (f32[1280,128]{1,0:T(8,128)S(1)}, f32[1280,128]{1,0:T(8,128)S(1)}, f32[5,4,8,128]{3,2,1,0:T(8,128)S(1)}, f32[5,4,8,128]{3,2,1,0:T(8,128)S(1)}, f...) custom-call(s32[24]{0:T(128)S(1)} %get-tuple-element.54.tags, ...), custom_call_target="tpu_custom_call" | custom-call | tf_op jit(solution)/shard_map/assemble_0/pallas_call | solution.py:671
  43.2 2.0 %collective-permute-done.13.refs_4_ = f32[8,32,128]{2,1,0:T(8,128)S(1)} collective-permute-done((f32[8,32,128]{2,1,0:T(8,128)S(1)}, f32[8,32,128]{2,1,0:T(8,128)S(1)}, u32[]{:S(2)}, u32[]{:S(2)}) %collective-permute-start.13) | collective-permute-done | bytes 131104 | tf_op jit(solution)/shard_map/ppermute | solution.py:560
  45.2 0.9 %assemble_3.1 = (f32[1280,128]{1,0:T(8,128)S(1)}, f32[1280,128]{1,0:T(8,128)S(1)}, f32[5,4,8,128]{3,2,1,0:T(8,128)S(1)}, f32[5,4,8,128]{3,2,1,0:T(8,128)S(1)}, f...) custom-call(s32[24]{0:T(128)S(1)} %get-tuple-element.54.tags, ...), custom_call_target="tpu_custom_call", output_to_operand_aliasing={{0}: (7, {}), {1}: (8, {}), {2}: (9, {}), {3}: (10, {}), {4... | custom-call | tf_op jit(solution)/shard_map/assemble_3/pallas_call | solution.py:671
  46.1 2.0 %collective-permute-start.18 = (f32[2,5,4,8,128]{4,3,2,1,0:T(8,128)S(1)}, f32[2,5,4,8,128]{4,3,2,1,0:T(8,128)S(1)}, u32[]{:S(2)}, u32[]{:S(2)}) collective-permute-start(f32[2,5,4,8,128]{4,3,2,1,0:T(8,128)S(1)} %get-tuple-element.93), channel_id=1, source_target_pairs={{0,16},{16,0},{1,17},{17,1},{2,18},{18,2},{3,19},{19,3},{4,20},{20... | collective-permute-start | bytes 491528 | tf_op jit(solution)/shard_map/ppermute | solution.py:691
  48.1 5.8 %collective-permute-start.14 = (f32[5,4,8,128]{3,2,1,0:T(8,128)S(1)}, f32[5,4,8,128]{3,2,1,0:T(8,128)S(1)}, u32[]{:S(2)}, u32[]{:S(2)}) collective-permute-start(f32[5,4,8,128]{3,2,1,0:T(8,128)S(1)} %get-tuple-element.89.y_one), channel_id=1, source_target_pairs={{0,12},{4,8},{8,4},{12,0},{1,13},{5,9},{9,5},{13,1},{2,14},{6,10},... | collective-permute-start | bytes 245768 | tf_op jit(solution)/shard_map/ppermute | solution.py:696
  53.8 0.0 collective-permute-start.15
  53.8 0.0 collective-permute-start.16
  53.8 1.7 %collective-permute-start.17 = (f32[5,8,128]{2,1,0:T(8,128)S(1)}, f32[5,8,128]{2,1,0:T(8,128)S(1)}, u32[]{:S(2)}, u32[]{:S(2)}) collective-permute-start(f32[5,8,128]{2,1,0:T(8,128)S(1)} %get-tuple-element.92), channel_id=1, source_target_pairs={{0,3},{1,0},{2,1},{3,2},{4,7},{5,4},{6,5},{7,6},{8,11},{9,8},{10,9... | collective-permute-start | bytes 61448 | tf_op jit(solution)/shard_map/ppermute | solution.py:691
  55.6 0.0 collective-permute-done.18.x_faces
  55.6 0.6 sweep_x.2.sofar
  56.1 0.9 %collective-permute-done.16.z_prev = f32[5,8,128]{2,1,0:T(8,128)S(1)} collective-permute-done((f32[5,8,128]{2,1,0:T(8,128)S(1)}, f32[5,8,128]{2,1,0:T(8,128)S(1)}, u32[]{:S(2)}, u32[]{:S(2)}) %collective-permute-start.16) | collective-permute-done | bytes 20512 | tf_op jit(solution)/shard_map/ppermute | solution.py:691
  57.0 0.0 collective-permute-done.17.z_next
  57.1 1.9 %sweep_z.2.sofar = f32[1280,128]{1,0:T(8,128)S(1)} custom-call(f32[1280,128]{1,0:T(8,128)S(1)} %get-tuple-element.88.prim, f32[5,8,128]{2,1,0:T(8,128)S(1)} %collective-permute-done.16.z_prev, f32[5,8,128]{2,1,0:T(8,128)S(1)} %collective-permute-done.17.z_next, f32[1280,128]{1,0:T(8,128)S(1)} %sweep_x.2.sofar), custom_call_target="tpu_custom_call", output_to_operand_aliasing={{}: (3, {})} | custom-call | flops 1 | bytes 1 | tf_op jit(solution)/shard_map/sweep_z/pallas_call | solution.py:716
  59.0 0.0 collective-permute-done.14.got_one
  59.0 0.0 collective-permute-done.15.got_two
  59.0 1.3 %sweep_y_one.1 = (f32[1280,128]{1,0:T(8,128)S(1)}, f32[1280,128]{1,0:T(8,128)S(1)}, f32[2,5,4,8,128]{4,3,2,1,0:T(8,128)S(1)}, f32[5,4,8,128]{3,2,1,0:T(8,128)S(1...) custom-call(f32[1280,128]{1,0:T(8,128)S(1)} %get-tuple-element.87.field, ...), custom_call_target="tpu_custom_call" | custom-call | tf_op jit(solution)/shard_map/sweep_y_one/pallas_call | solution.py:733
  60.3 0.8 %collective-permute-start.23 = (f32[2,5,4,8,128]{4,3,2,1,0:T(8,128)S(1)}, f32[2,5,4,8,128]{4,3,2,1,0:T(8,128)S(1)}, u32[]{:S(2)}, u32[]{:S(2)}) collective-permute-start(f32[2,5,4,8,128]{4,3,2,1,0:T(8,128)S(1)} %get-tuple-element.100), channel_id=1, source_target_pairs={{0,16},{16,0},{1,17},{17,1},{2,18},{18,2},{3,19},{19,3},{4,20},{20... | collective-permute-start | bytes 491528 | tf_op jit(solution)/shard_map/ppermute | solution.py:691
  61.1 1.9 %collective-permute-start.19 = (f32[5,4,8,128]{3,2,1,0:T(8,128)S(1)}, f32[5,4,8,128]{3,2,1,0:T(8,128)S(1)}, u32[]{:S(2)}, u32[]{:S(2)}) collective-permute-start(f32[5,4,8,128]{3,2,1,0:T(8,128)S(1)} %get-tuple-element.96.y_one), channel_id=1, source_target_pairs={{0,12},{4,8},{8,4},{12,0},{1,13},{5,9},{9,5},{13,1},{2,14},{6,10},... | collective-permute-start | bytes 245768 | tf_op jit(solution)/shard_map/ppermute | solution.py:696
  63.1 0.1 collective-permute-start.20
  63.1 0.1 collective-permute-start.21
  63.2 1.7 %collective-permute-start.22 = (f32[5,8,128]{2,1,0:T(8,128)S(1)}, f32[5,8,128]{2,1,0:T(8,128)S(1)}, u32[]{:S(2)}, u32[]{:S(2)}) collective-permute-start(f32[5,8,128]{2,1,0:T(8,128)S(1)} %get-tuple-element.99), channel_id=1, source_target_pairs={{0,3},{1,0},{2,1},{3,2},{4,7},{5,4},{6,5},{7,6},{8,11},{9,8},{10,9... | collective-permute-start | bytes 61448 | tf_op jit(solution)/shard_map/ppermute | solution.py:691
  64.9 2.5 %collective-permute-done.23.x_faces = f32[2,5,4,8,128]{4,3,2,1,0:T(8,128)S(1)} collective-permute-done((f32[2,5,4,8,128]{4,3,2,1,0:T(8,128)S(1)}, f32[2,5,4,8,128]{4,3,2,1,0:T(8,128)S(1)}, u32[]{:S(2)}, u32[]{:S(2)}) %collective-permute-start.23) | collective-permute-done | bytes 163872 | tf_op jit(solution)/shard_map/ppermute | solution.py:691
  67.4 0.6 sweep_x.3.sofar
  68.0 0.0 collective-permute-done.21.z_prev
  68.0 0.0 collective-permute-done.22.z_next
  68.0 1.9 %sweep_z.3.sofar = f32[1280,128]{1,0:T(8,128)S(1)} custom-call(f32[1280,128]{1,0:T(8,128)S(1)} %get-tuple-element.95.prim, f32[5,8,128]{2,1,0:T(8,128)S(1)} %collective-permute-done.21.z_prev, f32[5,8,128]{2,1,0:T(8,128)S(1)} %collective-permute-done.22.z_next, f32[1280,128]{1,0:T(8,128)S(1)} %sweep_x.3.sofar), custom_call_target="tpu_custom_call", output_to_operand_aliasing={{}: (3, {})} | custom-call | flops 1 | bytes 1 | tf_op jit(solution)/shard_map/sweep_z/pallas_call | solution.py:716
  69.9 0.0 collective-permute-done.19.got_one
  69.9 2.8 %sweep_y_two.1 = (f32[20,256,128]{2,1,0:T(8,128)}, f32[20,256,128]{2,1,0:T(8,128)S(1)}) custom-call(s32[8]{0:T(128)} %copy-done.2, f32[1280,128]{1,0:T(8,128)S(1)} %get-tuple-element.87.field, f32[1280,128]{1,0:T(8,128)S(1)} %get-tuple-element.94.one, f32[1280,128]{1,0:T(8,128)S(1)} %get-tuple-element.95.prim, ...), custom_call_target="tpu_custom_call", output_to_operand_aliasing={{1}: (9, {})} | custom-call | tf_op jit(solution)/shard_map/sweep_y_two/pallas_call | solution.py:744
  (12 shorter events, 0.0 us)
Async XLA Ops:
  0.0 4.4 %copy-start.1 = (s32[3,1,8]{2,1,0:T(1,128)S(1)}, s32[3,1,8]{2,1,0:T(1,128)}, u32[]{:S(2)}) copy-start(s32[3,1,8]{2,1,0:T(1,128)} %send_hbm.1) | copy-start | bytes 292
  0.0 4.4 %copy-start = (f32[32,5,4096]{2,0,1:T(8,128)S(1)}, f32[32,5,4096]{2,0,1:T(8,128)}, u32[]{:S(2)}) copy-start(f32[32,5,4096]{2,0,1:T(8,128)} %param.4) | copy-start | bytes 7864324
  0.0 4.3 %copy-start.4 = (s32[256]{0:T(256)S(1)}, s32[256]{0:T(256)}, u32[]{:S(2)}) copy-start(s32[256]{0:T(256)} %param.7) | copy-start | bytes 3076
  0.0 4.4 %copy-start.3 = (s32[3,1,8]{2,1,0:T(1,128)S(1)}, s32[3,1,8]{2,1,0:T(1,128)}, u32[]{:S(2)}) copy-start(s32[3,1,8]{2,1,0:T(1,128)} %recv.1) | copy-start | bytes 292
  1.3 5.8 %collective-permute-start.1 = (f32[8,24,128]{2,1,0:T(8,128)S(1)}, f32[8,24,128]{2,1,0:T(8,128)S(1)}, u32[]{:S(2)}, u32[]{:S(2)}) collective-permute-start(f32[8,24,128]{2,1,0:T(8,128)S(1)} %pack_first.1), channel_id=1, source_target_pairs={{0,16},{1,17},{2,18},{3,19},{4,20},{5,21},{6,22},{7,23},{8,24},{9,... | collective-permute-start | bytes 294920 | tf_op jit(solution)/shard_map/ppermute | solution.py:560
  4.4 3.3 %copy-start.2 = (s32[8]{0:T(128)}, s32[8]{0:T(128)S(1)}, u32[]{:S(2)}) copy-start(s32[8]{0:T(128)S(1)} %dynamic_slice.3.own.own_there) | copy-start | bytes 100
  5.8 7.2 %collective-permute-start = (f32[8,40,128]{2,1,0:T(8,128)S(1)}, f32[8,40,128]{2,1,0:T(8,128)S(1)}, u32[]{:S(2)}, u32[]{:S(2)}) collective-permute-start(f32[8,40,128]{2,1,0:T(8,128)S(1)} %get-tuple-element.55), channel_id=1, source_target_pairs={{0,16},{1,17},{2,18},{3,19},{4,20},{5,21},{6,22},{7,23},{8,24},{9,... | collective-permute-start | bytes 491528 | tf_op jit(solution)/shard_map/ppermute | solution.py:560
  7.7 10.2 %collective-permute-start.3 = (f32[8,56,128]{2,1,0:T(8,128)S(1)}, f32[8,56,128]{2,1,0:T(8,128)S(1)}, u32[]{:S(2)}, u32[]{:S(2)}) collective-permute-start(f32[8,56,128]{2,1,0:T(8,128)S(1)} %get-tuple-element.61), channel_id=1, source_target_pairs={{0,16},{1,17},{2,18},{3,19},{4,20},{5,21},{6,22},{7,23},{8,24},{9,... | collective-permute-start | bytes 688136 | tf_op jit(solution)/shard_map/ppermute | solution.py:560
  9.7 7.1 %collective-permute-start.5 = (f32[8,24,128]{2,1,0:T(8,128)S(1)}, f32[8,24,128]{2,1,0:T(8,128)S(1)}, u32[]{:S(2)}, u32[]{:S(2)}) collective-permute-start(f32[8,24,128]{2,1,0:T(8,128)S(1)} %get-tuple-element.63), channel_id=1, source_target_pairs={{0,8},{1,9},{2,10},{3,11},{4,12},{5,13},{6,14},{7,15},{8,0},{9,1},... | collective-permute-start | bytes 294920 | tf_op jit(solution)/shard_map/ppermute | solution.py:560
  13.6 12.8 %collective-permute-start.2 = (f32[8,40,128]{2,1,0:T(8,128)S(1)}, f32[8,40,128]{2,1,0:T(8,128)S(1)}, u32[]{:S(2)}, u32[]{:S(2)}) collective-permute-start(f32[8,40,128]{2,1,0:T(8,128)S(1)} %get-tuple-element.60), channel_id=1, source_target_pairs={{0,16},{1,17},{2,18},{3,19},{4,20},{5,21},{6,22},{7,23},{8,24},{9,... | collective-permute-start | bytes 491528 | tf_op jit(solution)/shard_map/ppermute | solution.py:560
  14.2 12.3 %collective-permute-start.4 = (f32[8,32,128]{2,1,0:T(8,128)S(1)}, f32[8,32,128]{2,1,0:T(8,128)S(1)}, u32[]{:S(2)}, u32[]{:S(2)}) collective-permute-start(f32[8,32,128]{2,1,0:T(8,128)S(1)} %get-tuple-element.62), channel_id=1, source_target_pairs={{0,8},{1,9},{2,10},{3,11},{4,12},{5,13},{6,14},{7,15},{8,0},{9,1},... | collective-permute-start | bytes 393224 | tf_op jit(solution)/shard_map/ppermute | solution.py:560
  18.6 12.7 %collective-permute-start.7 = (f32[8,40,128]{2,1,0:T(8,128)S(1)}, f32[8,40,128]{2,1,0:T(8,128)S(1)}, u32[]{:S(2)}, u32[]{:S(2)}) collective-permute-start(f32[8,40,128]{2,1,0:T(8,128)S(1)} %get-tuple-element.67), channel_id=1, source_target_pairs={{0,8},{1,9},{2,10},{3,11},{4,12},{5,13},{6,14},{7,15},{8,0},{9,1},... | collective-permute-start | bytes 491528 | tf_op jit(solution)/shard_map/ppermute | solution.py:560
  21.3 7.5 %collective-permute-start.8 = (f32[8,24,128]{2,1,0:T(8,128)S(1)}, f32[8,24,128]{2,1,0:T(8,128)S(1)}, u32[]{:S(2)}, u32[]{:S(2)}) collective-permute-start(f32[8,24,128]{2,1,0:T(8,128)S(1)} %get-tuple-element.69), channel_id=1, source_target_pairs={{0,2},{1,3},{2,0},{3,1},{4,6},{5,7},{6,4},{7,5},{8,10},{9,11},{10,... | collective-permute-start | bytes 294920 | tf_op jit(solution)/shard_map/ppermute | solution.py:560
  27.2 6.5 %collective-permute-start.6 = (f32[8,32,128]{2,1,0:T(8,128)S(1)}, f32[8,32,128]{2,1,0:T(8,128)S(1)}, u32[]{:S(2)}, u32[]{:S(2)}) collective-permute-start(f32[8,32,128]{2,1,0:T(8,128)S(1)} %get-tuple-element.66), channel_id=1, source_target_pairs={{0,8},{1,9},{2,10},{3,11},{4,12},{5,13},{6,14},{7,15},{8,0},{9,1},... | collective-permute-start | bytes 393224 | tf_op jit(solution)/shard_map/ppermute | solution.py:560
  27.2 6.4 %collective-permute-start.10 = (f32[8,32,128]{2,1,0:T(8,128)S(1)}, f32[8,32,128]{2,1,0:T(8,128)S(1)}, u32[]{:S(2)}, u32[]{:S(2)}) collective-permute-start(f32[8,32,128]{2,1,0:T(8,128)S(1)} %get-tuple-element.72), channel_id=1, source_target_pairs={{0,2},{1,3},{2,0},{3,1},{4,6},{5,7},{6,4},{7,5},{8,10},{9,11},{10,... | collective-permute-start | bytes 393224 | tf_op jit(solution)/shard_map/ppermute | solution.py:560
  32.1 7.4 %collective-permute-start.12 = (f32[8,40,128]{2,1,0:T(8,128)S(1)}, f32[8,40,128]{2,1,0:T(8,128)S(1)}, u32[]{:S(2)}, u32[]{:S(2)}) collective-permute-start(f32[8,40,128]{2,1,0:T(8,128)S(1)} %get-tuple-element.75), channel_id=1, source_target_pairs={{0,2},{1,3},{2,0},{3,1},{4,6},{5,7},{6,4},{7,5},{8,10},{9,11},{10,... | collective-permute-start | bytes 491528 | tf_op jit(solution)/shard_map/ppermute | solution.py:560
  33.6 5.9 %collective-permute-start.9 = (f32[8,32,128]{2,1,0:T(8,128)S(1)}, f32[8,32,128]{2,1,0:T(8,128)S(1)}, u32[]{:S(2)}, u32[]{:S(2)}) collective-permute-start(f32[8,32,128]{2,1,0:T(8,128)S(1)} %get-tuple-element.70), channel_id=1, source_target_pairs={{0,8},{1,9},{2,10},{3,11},{4,12},{5,13},{6,14},{7,15},{8,0},{9,1},... | collective-permute-start | bytes 393224 | tf_op jit(solution)/shard_map/ppermute | solution.py:560
  34.3 7.3 %collective-permute-start.11 = (f32[8,32,128]{2,1,0:T(8,128)S(1)}, f32[8,32,128]{2,1,0:T(8,128)S(1)}, u32[]{:S(2)}, u32[]{:S(2)}) collective-permute-start(f32[8,32,128]{2,1,0:T(8,128)S(1)} %get-tuple-element.73), channel_id=1, source_target_pairs={{0,2},{1,3},{2,0},{3,1},{4,6},{5,7},{6,4},{7,5},{8,10},{9,11},{10,... | collective-permute-start | bytes 393224 | tf_op jit(solution)/shard_map/ppermute | solution.py:560
  40.2 5.0 %collective-permute-start.13 = (f32[8,32,128]{2,1,0:T(8,128)S(1)}, f32[8,32,128]{2,1,0:T(8,128)S(1)}, u32[]{:S(2)}, u32[]{:S(2)}) collective-permute-start(f32[8,32,128]{2,1,0:T(8,128)S(1)} %get-tuple-element.76), channel_id=1, source_target_pairs={{0,2},{1,3},{2,0},{3,1},{4,6},{5,7},{6,4},{7,5},{8,10},{9,11},{10,... | collective-permute-start | bytes 393224 | tf_op jit(solution)/shard_map/ppermute | solution.py:560
  46.1 9.5 %collective-permute-start.18 = (f32[2,5,4,8,128]{4,3,2,1,0:T(8,128)S(1)}, f32[2,5,4,8,128]{4,3,2,1,0:T(8,128)S(1)}, u32[]{:S(2)}, u32[]{:S(2)}) collective-permute-start(f32[2,5,4,8,128]{4,3,2,1,0:T(8,128)S(1)} %get-tuple-element.93), channel_id=1, source_target_pairs={{0,16},{16,0},{1,17},{17,1},{2,18},{18,2},{3,19},{19,3},{4,20},{20... | collective-permute-start | bytes 491528 | tf_op jit(solution)/shard_map/ppermute | solution.py:691
  48.1 10.9 %collective-permute-start.14 = (f32[5,4,8,128]{3,2,1,0:T(8,128)S(1)}, f32[5,4,8,128]{3,2,1,0:T(8,128)S(1)}, u32[]{:S(2)}, u32[]{:S(2)}) collective-permute-start(f32[5,4,8,128]{3,2,1,0:T(8,128)S(1)} %get-tuple-element.89.y_one), channel_id=1, source_target_pairs={{0,12},{4,8},{8,4},{12,0},{1,13},{5,9},{9,5},{13,1},{2,14},{6,10},... | collective-permute-start | bytes 245768 | tf_op jit(solution)/shard_map/ppermute | solution.py:696
  53.8 5.2 %collective-permute-start.15 = (f32[5,4,8,128]{3,2,1,0:T(8,128)S(1)}, f32[5,4,8,128]{3,2,1,0:T(8,128)S(1)}, u32[]{:S(2)}, u32[]{:S(2)}) collective-permute-start(f32[5,4,8,128]{3,2,1,0:T(8,128)S(1)} %get-tuple-element.90.y_two), channel_id=1, source_target_pairs={{0,4},{4,0},{8,12},{12,8},{1,5},{5,1},{9,13},{13,9},{2,6},{6,2},{1... | collective-permute-start | bytes 245768 | tf_op jit(solution)/shard_map/ppermute | solution.py:696
  53.8 3.2 %collective-permute-start.16 = (f32[5,8,128]{2,1,0:T(8,128)S(1)}, f32[5,8,128]{2,1,0:T(8,128)S(1)}, u32[]{:S(2)}, u32[]{:S(2)}) collective-permute-start(f32[5,8,128]{2,1,0:T(8,128)S(1)} %get-tuple-element.91), channel_id=1, source_target_pairs={{0,1},{1,2},{2,3},{3,0},{4,5},{5,6},{6,7},{7,4},{8,9},{9,10},{10,1... | collective-permute-start | bytes 61448 | tf_op jit(solution)/shard_map/ppermute | solution.py:691
  53.8 3.2 %collective-permute-start.17 = (f32[5,8,128]{2,1,0:T(8,128)S(1)}, f32[5,8,128]{2,1,0:T(8,128)S(1)}, u32[]{:S(2)}, u32[]{:S(2)}) collective-permute-start(f32[5,8,128]{2,1,0:T(8,128)S(1)} %get-tuple-element.92), channel_id=1, source_target_pairs={{0,3},{1,0},{2,1},{3,2},{4,7},{5,4},{6,5},{7,6},{8,11},{9,8},{10,9... | collective-permute-start | bytes 61448 | tf_op jit(solution)/shard_map/ppermute | solution.py:691
  60.3 7.1 %collective-permute-start.23 = (f32[2,5,4,8,128]{4,3,2,1,0:T(8,128)S(1)}, f32[2,5,4,8,128]{4,3,2,1,0:T(8,128)S(1)}, u32[]{:S(2)}, u32[]{:S(2)}) collective-permute-start(f32[2,5,4,8,128]{4,3,2,1,0:T(8,128)S(1)} %get-tuple-element.100), channel_id=1, source_target_pairs={{0,16},{16,0},{1,17},{17,1},{2,18},{18,2},{3,19},{19,3},{4,20},{20... | collective-permute-start | bytes 491528 | tf_op jit(solution)/shard_map/ppermute | solution.py:691
  61.1 8.8 %collective-permute-start.19 = (f32[5,4,8,128]{3,2,1,0:T(8,128)S(1)}, f32[5,4,8,128]{3,2,1,0:T(8,128)S(1)}, u32[]{:S(2)}, u32[]{:S(2)}) collective-permute-start(f32[5,4,8,128]{3,2,1,0:T(8,128)S(1)} %get-tuple-element.96.y_one), channel_id=1, source_target_pairs={{0,12},{4,8},{8,4},{12,0},{1,13},{5,9},{9,5},{13,1},{2,14},{6,10},... | collective-permute-start | bytes 245768 | tf_op jit(solution)/shard_map/ppermute | solution.py:696
  63.1 6.8 %collective-permute-start.20 = (f32[5,4,8,128]{3,2,1,0:T(8,128)S(1)}, f32[5,4,8,128]{3,2,1,0:T(8,128)S(1)}, u32[]{:S(2)}, u32[]{:S(2)}) collective-permute-start(f32[5,4,8,128]{3,2,1,0:T(8,128)S(1)} %get-tuple-element.97.y_two), channel_id=1, source_target_pairs={{0,4},{4,0},{8,12},{12,8},{1,5},{5,1},{9,13},{13,9},{2,6},{6,2},{1... | collective-permute-start | bytes 245768 | tf_op jit(solution)/shard_map/ppermute | solution.py:696
  63.1 4.8 %collective-permute-start.21 = (f32[5,8,128]{2,1,0:T(8,128)S(1)}, f32[5,8,128]{2,1,0:T(8,128)S(1)}, u32[]{:S(2)}, u32[]{:S(2)}) collective-permute-start(f32[5,8,128]{2,1,0:T(8,128)S(1)} %get-tuple-element.98), channel_id=1, source_target_pairs={{0,1},{1,2},{2,3},{3,0},{4,5},{5,6},{6,7},{7,4},{8,9},{9,10},{10,1... | collective-permute-start | bytes 61448 | tf_op jit(solution)/shard_map/ppermute | solution.py:691
  63.2 4.8 %collective-permute-start.22 = (f32[5,8,128]{2,1,0:T(8,128)S(1)}, f32[5,8,128]{2,1,0:T(8,128)S(1)}, u32[]{:S(2)}, u32[]{:S(2)}) collective-permute-start(f32[5,8,128]{2,1,0:T(8,128)S(1)} %get-tuple-element.99), channel_id=1, source_target_pairs={{0,3},{1,0},{2,1},{3,2},{4,7},{5,4},{6,5},{7,6},{8,11},{9,8},{10,9... | collective-permute-start | bytes 61448 | tf_op jit(solution)/shard_map/ppermute | solution.py:691
